TPU v7x, 32 devices: a whole 2x2x4 slice. The times are simulated.
32 devices in a mesh: kgrp: 4 (over y, x), energy: 8 (over z, core).
Axes of the slice: x: 2, y: 2, z: 4, core: 2. Of those that a mesh axis runs over, the one named last changes fastest.
Arguments:
- greens: float32 [2, 2, 2, 256, 1024], P(None, None, None, 'kgrp', 'energy'), may hold values from -6 to 6
- current: float32 [2, 2, 2, 256, 1024], P(None, None, None, ('kgrp', 'energy')), may hold values from -6 to 6
- past_inputs: float32 [5, 2, 2, 2, 256, 1024], P(None, None, None, None, ('kgrp', 'energy')), may hold values from -6 to 6
- past_residuals: float32 [5, 2, 2, 2, 256, 1024], P(None, None, None, None, ('kgrp', 'energy')), may hold values from -40 to 40
- slot_order: int32 [5], replicated, may hold values from 0 to 4, each once
- neighbour: int32 [256, 5], P('kgrp'), may hold values from 0 to 255, as said below
- momentum_class: int32 [256], P('kgrp'), may hold values from 0 to 3
- stencil_weight: float32 [5], replicated, may hold values from 0.1 to 0.4
- acoustic_coupling: float32 [4], replicated, may hold values from 0.3 to 1.5
- optical_coupling: float32 [2], replicated, may hold values from 0.2 to 0.6
- occupation: float32 [2], replicated, may hold values from 0.1 to 1
- phonon_shift: int32 [2], replicated, may hold values from 32 to 96, as said below
Outputs:
- mixed: float32 [2, 2, 2, 256, 1024], P(None, None, None, ('kgrp', 'energy'))
Inputs may be any that keep to these rules, and one draw needn't show every extreme that they name: `neighbour`: each index names a momentum of the row's own group of 64 consecutive momenta or of the group just before or after it, counted periodically over all groups. `phonon_shift`: the larger of the two shifts is exactly 96.
All inputs are finite; a program needn't handle non-finite values.
Results may differ from a plain program's by a relative error of at most 0.000053.
Values sent between devices are 32-bit elements; how exact they have to be, the bound alone decides.
No kernel may reach another device: no remote copies, remote signals or barrier semaphores. Data moves between devices by JAX's collectives and lax.ppermute only.
A program may use at most 64 MiB of HBM per device.

v0:
```python
import jax
import jax.numpy as jnp
from jax import lax
from jax.experimental import pallas as pl
from jax.experimental.pallas import tpu as pltpu
from jax.sharding import PartitionSpec as P

HIST = 5
LANES = 128

mixing_share = 0.5
ridge_share = 0.1

VMEM = pl.BlockSpec(memory_space=pltpu.VMEM)
SMEM = pl.BlockSpec(memory_space=pltpu.SMEM)
PARAMS = pltpu.CompilerParams(vmem_limit_bytes=16 * 1024 * 1024)

NEAR, FAR = 0, 1

PAIRS = [(i, j) for i in range(1, HIST + 1) for j in range(i, HIST + 1)]
SPOTS = {pair: v for v, pair in enumerate(PAIRS)}
for _j in range(HIST + 1):
    SPOTS[(0, _j)] = 16 + _j


def split(value):
    high = value.astype(jnp.bfloat16)
    return high, (value - high.astype(jnp.float32)).astype(jnp.bfloat16)


def product(left, right):
    dot = lambda a, b: jnp.dot(a, b, preferred_element_type=jnp.float32)
    return dot(left[0], right[0]) + (dot(left[0], right[1]) + dot(left[1], right[0]))


def prepare_kernel(total_k, own, neighbour, weight, stencil_hi, stencil_lo, part):
    comps, group_len, slice_len = own.shape
    group_id = lax.axis_index("kgrp")
    parts = lax.axis_size("energy")
    rows = group_len // parts
    targets = neighbour[...]
    place = lax.axis_index("energy")
    bit = 1
    while bit < parts:
        span = bit * rows
        blocks = [targets[at : at + span] for at in range(0, group_len, span)]
        flipped = [blocks[b ^ 1] for b in range(len(blocks))]
        targets = jnp.where(place & bit != 0, jnp.concatenate(flipped, axis=0), targets)
        bit *= 2
    local = (targets - group_id * group_len + (group_len + total_k)) % total_k
    spot = lax.broadcasted_iota(jnp.int32, (group_len, 3 * group_len), 1)
    stencil = jnp.zeros(spot.shape, jnp.float32)
    for n in range(local.shape[1]):
        stencil = stencil + jnp.where(spot == local[:, n : n + 1], weight[n], 0.0)
    before, after = stencil[:, :group_len], stencil[:, 2 * group_len :]
    swapped = paired(total_k // group_len) & (group_id % 2 == 1)
    near, far = jnp.where(swapped, before, after), jnp.where(swapped, after, before)
    stencil_hi[...], stencil_lo[...] = split(jnp.concatenate([near, far], axis=1))
    centre = split(stencil[:, group_len : 2 * group_len])
    for c in range(0, comps, 2):
        result = product(centre, split(jnp.concatenate([own[c], own[c + 1]], axis=1)))
        part[c] = result[:, :slice_len]
        part[c + 1] = result[:, slice_len:]


def prepare(own, neighbour, weight, total_k):
    group_len = own.shape[1]
    sides = jax.ShapeDtypeStruct((group_len, 2 * group_len), jnp.bfloat16)
    return pl.pallas_call(
        lambda *refs: prepare_kernel(total_k, *refs),
        out_shape=(sides, sides, jax.ShapeDtypeStruct(own.shape, jnp.float32)),
        in_specs=[VMEM, VMEM, SMEM],
        out_specs=(VMEM, VMEM, VMEM),
        compiler_params=PARAMS,
        cost_estimate=pl.CostEstimate(
            flops=6 * own.size * group_len, bytes_accessed=8 * own.size, transcendentals=0
        ),
        name="prepare",
    )(own, neighbour, weight)


def smear_kernel(side, count, *refs):
    blocks, (stencil_hi, stencil_lo, part), out = refs[:count], refs[count : count + 3], refs[count + 3 :]
    _, group_len, slice_len = blocks[0].shape
    at = slice(side * group_len, (side + 1) * group_len)
    stencil = (stencil_hi[:, at], stencil_lo[:, at])
    rows = group_len // len(out)
    first = 0
    for block in blocks:
        for c in range(0, block.shape[0], 2):
            result = product(stencil, split(jnp.concatenate([block[c], block[c + 1]], axis=1)))
            for p in range(2):
                at = first + c + p
                smeared = part[at] + result[:, p * slice_len : (p + 1) * slice_len]
                if side == NEAR:
                    out[0][at] = smeared
                    continue
                for m in range(len(out)):
                    out[m][at * rows : (at + 1) * rows, :] = smeared[m * rows : (m + 1) * rows]
        first += block.shape[0]


def smear(side, blocks, stencil_hi, stencil_lo, part, parts):
    comps, group_len, slice_len = part.shape
    if side == NEAR:
        out_shape = [jax.ShapeDtypeStruct(part.shape, jnp.float32)]
    else:
        out_shape = [jax.ShapeDtypeStruct((comps * group_len // parts, slice_len), jnp.float32)] * parts
    return pl.pallas_call(
        lambda *refs: smear_kernel(side, len(blocks), *refs),
        out_shape=out_shape,
        in_specs=[VMEM] * (len(blocks) + 3),
        out_specs=[VMEM] * len(out_shape),
        compiler_params=PARAMS,
        cost_estimate=pl.CostEstimate(
            flops=6 * part.size * group_len, bytes_accessed=12 * part.size, transcendentals=0
        ),
        name="smear",
    )(*blocks, stencil_hi, stencil_lo, part)


def paired(groups):
    return groups == 4


def exchange(own, groups):
    if not paired(groups):
        forward = [(i, (i + 1) % groups) for i in range(groups)]
        backward = [(target, source) for source, target in forward]
        return [lax.ppermute(own, "kgrp", backward)], [lax.ppermute(own, "kgrp", forward)]
    half = own.shape[0] // 2
    across = lambda block, flip: lax.ppermute(block, "kgrp", [(i, i ^ flip) for i in range(groups)])
    near = [across(own[:half], 1), across(own[half:], 1)]
    return near, [across(near[0], 2), across(own[half:], 3)]


def spread(values, shape):
    row = lax.broadcasted_iota(jnp.int32, shape, 0)
    lane = lax.broadcasted_iota(jnp.int32, shape, 1)
    tile = jnp.zeros(shape, jnp.float32)
    for spot, value in values:
        tile = jnp.where((row == spot % 8) & (lane == spot // 8), value, tile)
    return tile


def total(acc):
    return jnp.sum(jnp.sum(acc, axis=0, keepdims=True), axis=1, keepdims=True)


def history_kernel(past_inputs, past_residuals, slots, aged, tile):
    _, rows, width = past_inputs.shape
    acc = [jnp.zeros((8, LANES), jnp.float32) for _ in PAIRS]
    for top in range(0, rows, 8):
        def column(t, acc, top=top):
            at = pl.ds(pl.multiple_of(t * LANES, LANES), LANES)
            old = []
            for j in range(HIST):
                res = past_residuals[slots[j], top : top + 8, at]
                aged[j, top : top + 8, at] = (
                    past_inputs[slots[j], top : top + 8, at] + mixing_share * res
                )
                old.append(res)
            return [a + old[i - 1] * old[j - 1] for a, (i, j) in zip(acc, PAIRS)]
        acc = lax.fori_loop(0, width // LANES, column, acc, unroll=4)
    tile[...] = spread([(v, total(a)) for v, a in enumerate(acc)], tile.shape)


def history(past_inputs, past_residuals, slots):
    size = past_inputs.size
    return pl.pallas_call(
        history_kernel,
        out_shape=(
            jax.ShapeDtypeStruct(past_inputs.shape, jnp.float32),
            jax.ShapeDtypeStruct((8, LANES), jnp.float32),
        ),
        in_specs=[VMEM, VMEM, SMEM],
        out_specs=(VMEM, VMEM),
        compiler_params=PARAMS,
        cost_estimate=pl.CostEstimate(flops=8 * size, bytes_accessed=12 * size, transcendentals=0),
        name="history",
    )(past_inputs, past_residuals, slots)


def residual_kernel(rows, parts, *refs):
    received = refs[:parts]
    (current, past_residuals, old_tile, slots, classes, acoustic, optical, number, shift,
     fresh, tile, smeared) = refs[parts:]
    _, height, slice_len = smeared.shape
    place = lax.axis_index("energy")
    for m in range(parts):
        smeared[place ^ m] = received[m][...]
    first = place * rows
    row = lax.broadcasted_iota(jnp.int32, (8, slice_len), 0) % rows
    lane = lax.broadcasted_iota(jnp.int32, (8, slice_len), 1)
    coupling = jnp.zeros((8, slice_len), jnp.float32)
    for i in range(rows):
        coupling = jnp.where(row == i, acoustic[classes[first + i]], coupling)
    modes = []
    for m in range(2):
        s = shift[m]
        modes.append((s, lane < slice_len - s, lane >= s, optical[m] * (number[m] + 1.0), optical[m] * number[m]))
    zero = jnp.zeros((8, slice_len), jnp.float32)
    acc = [zero] * (HIST + 1)
    for top in range(0, height, 8):
        at = slice(top, top + 8)
        source = [smeared[e, at, :] for e in range(parts)]
        sigma = [coupling * x for x in source]
        lesser = top < height // 2
        for s, keep_up, keep_down, emitted, absorbed in modes:
            up = [pltpu.roll(x, slice_len - s, 1) for x in source] + [zero]
            down = [zero] + [pltpu.roll(x, s, 1) for x in source]
            gain_up, gain_down = (emitted, absorbed) if lesser else (absorbed, emitted)
            for e in range(parts):
                above = jnp.where(keep_up, up[e], up[e + 1])
                below = jnp.where(keep_down, down[e + 1], down[e])
                sigma[e] = sigma[e] + (gain_up * above + gain_down * below)
        for e in range(parts):
            where = (at, slice(e * slice_len, (e + 1) * slice_len))
            new = sigma[e] - current[where]
            fresh[where] = new
            acc[0] = acc[0] + new * new
            for j in range(HIST):
                acc[j + 1] = acc[j + 1] + new * past_residuals[(slots[j],) + where]
    mine = jnp.concatenate([jnp.sum(a, axis=0, keepdims=True) for a in acc] + [zero[: 8 - HIST - 1]], axis=0)
    mine = jnp.sum(mine, axis=1, keepdims=True)
    lane = lax.broadcasted_iota(jnp.int32, old_tile.shape, 1)
    tile[...] = jnp.broadcast_to(jnp.where(lane == 2, mine, old_tile[...])[None], tile.shape)


def residual(smeared, current, past_residuals, old_tile, slots, classes, acoustic, optical, number, shift, rows, copies):
    return pl.pallas_call(
        lambda *refs: residual_kernel(rows, len(smeared), *refs),
        out_shape=(
            jax.ShapeDtypeStruct(current.shape, jnp.float32),
            jax.ShapeDtypeStruct((copies, 8, LANES), jnp.float32),
        ),
        in_specs=[VMEM] * (len(smeared) + 3) + [SMEM] * 6,
        out_specs=(VMEM, VMEM),
        scratch_shapes=[pltpu.VMEM((len(smeared),) + smeared[0].shape, jnp.float32)],
        compiler_params=PARAMS,
        name="residual",
    )(*smeared, current, past_residuals, old_tile, slots, classes, acoustic, optical, number, shift)


def solve(products):
    prod = lambda i, j: products[(min(i, j), max(i, j))]
    n = HIST
    system = [
        [prod(i, j) - prod(i, j + 1) - prod(i + 1, j) + prod(i + 1, j + 1) for j in range(n)]
        for i in range(n)
    ]
    target = [prod(i, 0) - prod(i + 1, 0) for i in range(n)]
    trace = system[0][0]
    for i in range(1, n):
        trace = trace + system[i][i]
    ridge = ridge_share * trace / n + 1e-06
    for i in range(n):
        system[i][i] = system[i][i] + ridge
    inverse = [None] * n
    for k in range(n):
        inverse[k] = 1.0 / system[k][k]
        for i in range(k + 1, n):
            factor = system[k][i] * inverse[k]
            for j in range(i, n):
                system[i][j] = system[i][j] - factor * system[k][j]
            target[i] = target[i] - factor * target[k]
    gamma = [None] * n
    for k in range(n - 1, -1, -1):
        value = target[k]
        for j in range(k + 1, n):
            value = value - system[k][j] * gamma[j]
        gamma[k] = value * inverse[k]
    weights = [1.0 - gamma[0]]
    for j in range(1, n):
        weights.append(gamma[j - 1] - gamma[j])
    weights.append(gamma[n - 1])
    return weights


def mix_kernel(entries, tiles, fresh, current, aged, out, wide):
    summed = jnp.sum(tiles[...], axis=0) / entries
    for lane in range(wide.shape[0]):
        wide[lane] = jnp.broadcast_to(summed[:, lane : lane + 1], (8, LANES))
    products = {
        pair: jnp.broadcast_to(wide[spot // 8, spot % 8 : spot % 8 + 1, :], (8, LANES))
        for pair, spot in SPOTS.items()
    }
    weights = solve(products)
    rows, width = fresh.shape
    for top in range(0, rows, 8):
        for left in range(0, width, LANES):
            at = (slice(top, top + 8), slice(left, left + LANES))
            mixed = weights[0] * (current[at] + mixing_share * fresh[at])
            for j in range(HIST):
                mixed = mixed + weights[j + 1] * aged[(j,) + at]
            out[at] = mixed


def mix(tiles, fresh, current, aged, entries):
    return pl.pallas_call(
        lambda *refs: mix_kernel(entries, *refs),
        out_shape=jax.ShapeDtypeStruct(fresh.shape, jnp.float32),
        in_specs=[VMEM] * 4,
        out_specs=VMEM,
        scratch_shapes=[pltpu.VMEM((3, 8, LANES), jnp.float32)],
        compiler_params=PARAMS,
        name="mix",
    )(tiles, fresh, current, aged)


def per_device(
    greens,
    current,
    past_inputs,
    past_residuals,
    slot_order,
    neighbour,
    momentum_class,
    stencil_weight,
    acoustic_coupling,
    optical_coupling,
    occupation,
    phonon_shift,
):
    group_len, slice_len = greens.shape[3:]
    rows, width = current.shape[3:]
    groups = lax.axis_size("kgrp")
    parts = lax.axis_size("energy")
    own = greens.reshape(-1, group_len, slice_len)
    height = own.shape[0] * rows

    sides = exchange(own, groups)

    flat = current.reshape(height, width)
    old_in = past_inputs.reshape(HIST, height, width)
    old_res = past_residuals.reshape(HIST, height, width)
    stencil_hi, stencil_lo, smeared = prepare(own, neighbour, stencil_weight, groups * group_len)
    aged, old_tile = history(old_in, old_res, slot_order)
    (smeared,) = smear(NEAR, sides[NEAR], stencil_hi, stencil_lo, smeared, parts)
    smeared = list(smear(FAR, sides[FAR], stencil_hi, stencil_lo, smeared, parts))
    for m in range(parts - 1, 0, -1):
        smeared[m] = lax.ppermute(smeared[m], "energy", [(e, e ^ m) for e in range(parts)])
    fresh, tile = residual(
        smeared, flat, old_res, old_tile, slot_order, momentum_class, acoustic_coupling,
        optical_coupling, occupation, phonon_shift, rows, groups * parts,
    )
    tiles = lax.all_to_all(tile, ("kgrp", "energy"), split_axis=0, concat_axis=0, tiled=True)
    entries = float(flat.size * groups * parts)
    return mix(tiles, fresh, flat, aged, entries).reshape(current.shape)


def solution(mesh):
    return jax.shard_map(
        per_device,
        mesh=mesh,
        in_specs=(
            P(None, None, None, "kgrp", "energy"),
            P(None, None, None, ("kgrp", "energy"), None),
            P(None, None, None, None, ("kgrp", "energy"), None),
            P(None, None, None, None, ("kgrp", "energy"), None),
            P(),
            P("kgrp", None),
            P("kgrp"),
            P(),
            P(),
            P(),
            P(),
            P(),
        ),
        out_specs=P(None, None, None, ("kgrp", "energy"), None),
        check_vma=False,
    )
```

profile of v0, /device:TPU:0, one launch (start us, length us, event | category | flops | bytes accessed | tf_op | source)
XLA Modules:
  0.0 42.1 jit_solution(6937307740135301646)
XLA Ops:
  0.0 0.0 copy-start
  0.0 1.1 %fusion = (f32[1,2,2,64,128]{4,3,2,1,0:T(8,128)S(1)}, f32[1,2,2,64,128]{4,3,2,1,0:T(8,128)S(1)}) fusion(f32[2,2,2,64,128]{4,3,2,1,0:T(8,128)} %param.12), kind=kLoop, calls=%fused_computation | loop fusion | bytes 524288 | tf_op jit(solution)/shard_map/slice | solution.py:134
  1.1 3.0 %collective-permute-start = (f32[4,64,128]{2,1,0:T(8,128)S(1)}, f32[4,64,128]{2,1,0:T(8,128)S(1)}, u32[]{:S(2)}, u32[]{:S(2)}) collective-permute-start(f32[4,64,128]{2,1,0:T(8,128)S(1)} %bitcast.15), channel_id=1, source_target_pairs={{0,8},{8,0},{16,24},{24,16},{1,9},{9,1},{17,25},{25,17},{2,10},{10... | collective-permute-start | bytes 393224 | tf_op jit(solution)/shard_map/ppermute | solution.py:132
  4.1 0.1 collective-permute-start.3
  4.2 2.9 %collective-permute-start.2 = (f32[4,64,128]{2,1,0:T(8,128)S(1)}, f32[4,64,128]{2,1,0:T(8,128)S(1)}, u32[]{:S(2)}, u32[]{:S(2)}) collective-permute-start(f32[4,64,128]{2,1,0:T(8,128)S(1)} %bitcast.14), channel_id=1, source_target_pairs={{0,24},{8,16},{16,8},{24,0},{1,25},{9,17},{17,9},{25,1},{2,26},{10... | collective-permute-start | bytes 393224 | tf_op jit(solution)/shard_map/ppermute | solution.py:132
  7.1 1.3 %collective-permute-done.refs_0_ = f32[4,64,128]{2,1,0:T(8,128)S(1)} collective-permute-done((f32[4,64,128]{2,1,0:T(8,128)S(1)}, f32[4,64,128]{2,1,0:T(8,128)S(1)}, u32[]{:S(2)}, u32[]{:S(2)}) %collective-permute-start) | collective-permute-done | bytes 131104 | tf_op jit(solution)/shard_map/ppermute | solution.py:132
  8.4 2.1 %collective-permute-start.1 = (f32[4,64,128]{2,1,0:T(8,128)S(1)}, f32[4,64,128]{2,1,0:T(8,128)S(1)}, u32[]{:S(2)}, u32[]{:S(2)}) collective-permute-start(f32[4,64,128]{2,1,0:T(8,128)S(1)} %collective-permute-done.refs_0_), channel_id=1, source_target_pairs={{0,16},{8,24},{16,0},{24,8},{1,17},{9,25},{17,1},{25,9},{2,18},{10... | collective-permute-start | bytes 393224 | tf_op jit(solution)/shard_map/ppermute | solution.py:132
  10.5 0.8 %copy.13.refs_1_ = s32[64,5]{1,0:T(8,128)S(1)} copy(s32[64,5]{0,1:T(8,128)} %param.17) | data formatting | bytes 2560 | tf_op args[5]
  11.3 0.0 copy-start.2
  11.3 0.9 %copy-done.2 = f32[2,2,2,64,128]{4,3,2,1,0:T(8,128)S(1)} copy-done((f32[2,2,2,64,128]{4,3,2,1,0:T(8,128)S(1)}, f32[2,2,2,64,128]{4,3,2,1,0:T(8,128)}, u32[]{:S(2)}) %copy-start.2) | copy-done | bytes 262168
  12.2 0.0 copy-start.5
  12.2 0.7 %copy-done.5 = f32[5]{0:T(128)S(1)} copy-done((f32[5]{0:T(128)S(1)}, f32[5]{0:T(128)}, u32[]{:S(2)}) %copy-start.5) | copy-done | bytes 44
  12.9 0.0 copy-start.4
  12.9 1.0 %prepare.1 = (bf16[64,128]{1,0:T(8,128)(2,1)S(1)}, bf16[64,128]{1,0:T(8,128)(2,1)S(1)}, f32[8,64,128]{2,1,0:T(8,128)S(1)}) custom-call(f32[8,64,128]{2,1,0:T(8,128)S(1)} %bitcast.10, s32[64,5]{1,0:T(8,128)S(1)} %copy.13.refs_1_, f32[5]{0:T(128)S(1)} %copy-done.5), custom_call_target="tpu_custom_call" | custom-call | flops 25165824 | bytes 524288 | tf_op jit(solution)/shard_map/prepare/pallas_call | solution.py:69
  13.9 0.0 collective-permute-done.3.refs_1_
  13.9 0.2 smear.2.refs_4_
  14.1 0.4 collective-permute-done.2.refs_1_
  14.5 0.9 %collective-permute-done.1.refs_0_ = f32[4,64,128]{2,1,0:T(8,128)S(1)} collective-permute-done((f32[4,64,128]{2,1,0:T(8,128)S(1)}, f32[4,64,128]{2,1,0:T(8,128)S(1)}, u32[]{:S(2)}, u32[]{:S(2)}) %collective-permute-start.1) | collective-permute-done | bytes 131104 | tf_op jit(solution)/shard_map/ppermute | solution.py:132
  15.5 0.3 smear.3
  15.8 0.1 collective-permute-start.4
  15.9 1.9 %collective-permute-start.5 = (f32[64,128]{1,0:T(8,128)S(1)}, f32[64,128]{1,0:T(8,128)S(1)}, u32[]{:S(2)}, u32[]{:S(2)}) collective-permute-start(f32[64,128]{1,0:T(8,128)S(1)} %get-tuple-element.25), channel_id=1, source_target_pairs={{0,2},{1,3},{2,0},{3,1},{4,6},{5,7},{6,4},{7,5},{8,10},{9,11},{10,... | collective-permute-start | bytes 98312 | tf_op jit(solution)/shard_map/ppermute | solution.py:342
  17.7 0.1 collective-permute-start.6
  17.8 2.8 %collective-permute-start.7 = (f32[64,128]{1,0:T(8,128)S(1)}, f32[64,128]{1,0:T(8,128)S(1)}, u32[]{:S(2)}, u32[]{:S(2)}) collective-permute-start(f32[64,128]{1,0:T(8,128)S(1)} %get-tuple-element.27), channel_id=1, source_target_pairs={{0,4},{1,5},{2,6},{3,7},{4,0},{5,1},{6,2},{7,3},{8,12},{9,13},{10,... | collective-permute-start | bytes 98312 | tf_op jit(solution)/shard_map/ppermute | solution.py:342
  20.6 0.0 collective-permute-start.8
  20.6 0.0 collective-permute-done.4.refs_1_
  20.6 3.6 %collective-permute-start.9 = (f32[64,128]{1,0:T(8,128)S(1)}, f32[64,128]{1,0:T(8,128)S(1)}, u32[]{:S(2)}, u32[]{:S(2)}) collective-permute-start(f32[64,128]{1,0:T(8,128)S(1)} %get-tuple-element.29), channel_id=1, source_target_pairs={{0,6},{1,7},{2,4},{3,5},{4,2},{5,3},{6,0},{7,1},{8,14},{9,15},{10,... | collective-permute-start | bytes 98312 | tf_op jit(solution)/shard_map/ppermute | solution.py:342
  24.2 0.0 collective-permute-done.5.refs_2_
  24.2 0.1 collective-permute-start.10
  24.3 0.0 copy-done
  24.3 0.0 copy-done.4
  24.3 1.3 %copy-done.1 = f32[5,2,2,2,8,1024]{5,4,3,2,1,0:T(8,128)S(1)} copy-done((f32[5,2,2,2,8,1024]{5,4,3,2,1,0:T(8,128)S(1)}, f32[5,2,2,2,8,1024]{5,4,3,2,1,0:T(8,128)}, u32[]{:S(2)}) %copy-start.1) | copy-done | bytes 1310744
  25.6 0.0 copy-start.9
  25.6 0.0 copy-start.10
  25.6 1.3 %history.1 = (f32[5,64,1024]{2,1,0:T(8,128)S(1)}, f32[8,128]{1,0:T(8,128)S(1)}) custom-call(f32[5,64,1024]{2,1,0:T(8,128)S(1)} %bitcast.9, f32[5,64,1024]{2,1,0:T(8,128)S(1)} %bitcast.7, s32[5]{0:T(128)S(1)} %copy-done.4), custom_call_target="tpu_custom_call" | custom-call | flops 2621440 | bytes 3932160 | tf_op jit(solution)/shard_map/history/pallas_call | solution.py:170
  26.9 0.0 collective-permute-done.6.refs_3_
  26.9 0.0 collective-permute-done.7.refs_4_
  26.9 0.0 collective-permute-done.8.refs_5_
  27.0 0.0 collective-permute-done.9.refs_6_
  27.0 2.3 %collective-permute-done.10.refs_7_ = f32[64,128]{1,0:T(8,128)S(1)} collective-permute-done((f32[64,128]{1,0:T(8,128)S(1)}, f32[64,128]{1,0:T(8,128)S(1)}, u32[]{:S(2)}, u32[]{:S(2)}) %collective-permute-start.10) | collective-permute-done | bytes 32800 | tf_op jit(solution)/shard_map/ppermute | solution.py:342
  29.3 0.0 copy-done.3
  29.3 0.0 copy-done.6
  29.3 0.0 copy-done.7
  29.3 0.0 copy-done.8
  29.3 0.0 copy-done.9
  29.3 0.0 copy-done.10
  29.4 1.1 %residual.1 = (f32[64,1024]{1,0:T(8,128)S(1)}, f32[32,8,128]{2,1,0:T(8,128)S(1)}) custom-call(f32[64,128]{1,0:T(8,128)S(1)} %get-tuple-element.23.refs_0_, f32[64,128]{1,0:T(8,128)S(1)} %collective-permute-done.4.refs_1_, f32[64,128]{1,0:T(8,128)S(1)} %collective-permute-done.5.refs_2_, f32[64,128]{1,0:T(8,128)S(1)} %collective-permute-done.6.refs_3_, ...), custom_call_target="tpu_custom_call" | custom-call | tf_op jit(solution)/shard_map/residual/pallas_call | solution.py:231
  30.4 10.7 %all_to_all.5.refs_0_ = f32[32,8,128]{2,1,0:T(8,128)S(1)} all-to-all(f32[32,8,128]{2,1,0:T(8,128)S(1)} %get-tuple-element.32), channel_id=1, replica_groups=mesh['kgrp'=4,'energy'=8] {'kgrp','energy'}, dimensions={0} | all-to-all | bytes 262144 | tf_op jit(solution)/shard_map/all_to_all | solution.py:347
  41.1 1.0 %mix.1 = f32[64,1024]{1,0:T(8,128)} custom-call(f32[32,8,128]{2,1,0:T(8,128)S(1)} %all_to_all.5.refs_0_, f32[64,1024]{1,0:T(8,128)S(1)} %get-tuple-element.33.refs_1_, f32[64,1024]{1,0:T(8,128)S(1)} %bitcast.12, f32[5,64,1024]{2,1,0:T(8,128)S(1)} %get-tuple-element.34.refs_3_), custom_call_target="tpu_custom_call" | custom-call | tf_op jit(solution)/shard_map/mix/pallas_call | solution.py:300
  (5 shorter events, 0.0 us)
Async XLA Ops:
  0.0 24.3 %copy-start = (f32[5,2,2,2,8,1024]{5,4,3,2,1,0:T(8,128)S(1)}, f32[5,2,2,2,8,1024]{5,4,3,2,1,0:T(8,128)}, u32[]{:S(2)}) copy-start(f32[5,2,2,2,8,1024]{5,4,3,2,1,0:T(8,128)} %param.15) | copy-start | bytes 3932164
  1.1 7.3 %collective-permute-start = (f32[4,64,128]{2,1,0:T(8,128)S(1)}, f32[4,64,128]{2,1,0:T(8,128)S(1)}, u32[]{:S(2)}, u32[]{:S(2)}) collective-permute-start(f32[4,64,128]{2,1,0:T(8,128)S(1)} %bitcast.15), channel_id=1, source_target_pairs={{0,8},{8,0},{16,24},{24,16},{1,9},{9,1},{17,25},{25,17},{2,10},{10... | collective-permute-start | bytes 393224 | tf_op jit(solution)/shard_map/ppermute | solution.py:132
  4.1 9.8 %collective-permute-start.3 = (f32[4,64,128]{2,1,0:T(8,128)S(1)}, f32[4,64,128]{2,1,0:T(8,128)S(1)}, u32[]{:S(2)}, u32[]{:S(2)}) collective-permute-start(f32[4,64,128]{2,1,0:T(8,128)S(1)} %bitcast.13), channel_id=1, source_target_pairs={{0,8},{8,0},{16,24},{24,16},{1,9},{9,1},{17,25},{25,17},{2,10},{10... | collective-permute-start | bytes 393224 | tf_op jit(solution)/shard_map/ppermute | solution.py:132
  4.2 10.3 %collective-permute-start.2 = (f32[4,64,128]{2,1,0:T(8,128)S(1)}, f32[4,64,128]{2,1,0:T(8,128)S(1)}, u32[]{:S(2)}, u32[]{:S(2)}) collective-permute-start(f32[4,64,128]{2,1,0:T(8,128)S(1)} %bitcast.14), channel_id=1, source_target_pairs={{0,24},{8,16},{16,8},{24,0},{1,25},{9,17},{17,9},{25,1},{2,26},{10... | collective-permute-start | bytes 393224 | tf_op jit(solution)/shard_map/ppermute | solution.py:132
  8.4 7.0 %collective-permute-start.1 = (f32[4,64,128]{2,1,0:T(8,128)S(1)}, f32[4,64,128]{2,1,0:T(8,128)S(1)}, u32[]{:S(2)}, u32[]{:S(2)}) collective-permute-start(f32[4,64,128]{2,1,0:T(8,128)S(1)} %collective-permute-done.refs_0_), channel_id=1, source_target_pairs={{0,16},{8,24},{16,0},{24,8},{1,17},{9,25},{17,1},{25,9},{2,18},{10... | collective-permute-start | bytes 393224 | tf_op jit(solution)/shard_map/ppermute | solution.py:132
  11.3 0.9 %copy-start.2 = (f32[2,2,2,64,128]{4,3,2,1,0:T(8,128)S(1)}, f32[2,2,2,64,128]{4,3,2,1,0:T(8,128)}, u32[]{:S(2)}) copy-start(f32[2,2,2,64,128]{4,3,2,1,0:T(8,128)} %param.12) | copy-start | bytes 786436
  12.2 0.7 %copy-start.5 = (f32[5]{0:T(128)S(1)}, f32[5]{0:T(128)}, u32[]{:S(2)}) copy-start(f32[5]{0:T(128)} %refs_2_.1) | copy-start | bytes 64
  12.9 11.4 %copy-start.4 = (s32[5]{0:T(128)S(1)}, s32[5]{0:T(128)}, u32[]{:S(2)}) copy-start(s32[5]{0:T(128)} %refs_11_.1) | copy-start | bytes 64
  15.8 4.8 %collective-permute-start.4 = (f32[64,128]{1,0:T(8,128)S(1)}, f32[64,128]{1,0:T(8,128)S(1)}, u32[]{:S(2)}, u32[]{:S(2)}) collective-permute-start(f32[64,128]{1,0:T(8,128)S(1)} %get-tuple-element.24), channel_id=1, source_target_pairs={{0,1},{1,0},{2,3},{3,2},{4,5},{5,4},{6,7},{7,6},{8,9},{9,8},{10,11... | collective-permute-start | bytes 98312 | tf_op jit(solution)/shard_map/ppermute | solution.py:342
  15.9 8.3 %collective-permute-start.5 = (f32[64,128]{1,0:T(8,128)S(1)}, f32[64,128]{1,0:T(8,128)S(1)}, u32[]{:S(2)}, u32[]{:S(2)}) collective-permute-start(f32[64,128]{1,0:T(8,128)S(1)} %get-tuple-element.25), channel_id=1, source_target_pairs={{0,2},{1,3},{2,0},{3,1},{4,6},{5,7},{6,4},{7,5},{8,10},{9,11},{10,... | collective-permute-start | bytes 98312 | tf_op jit(solution)/shard_map/ppermute | solution.py:342
  17.7 9.2 %collective-permute-start.6 = (f32[64,128]{1,0:T(8,128)S(1)}, f32[64,128]{1,0:T(8,128)S(1)}, u32[]{:S(2)}, u32[]{:S(2)}) collective-permute-start(f32[64,128]{1,0:T(8,128)S(1)} %get-tuple-element.26), channel_id=1, source_target_pairs={{0,3},{1,2},{2,1},{3,0},{4,7},{5,6},{6,5},{7,4},{8,11},{9,10},{10,... | collective-permute-start | bytes 98312 | tf_op jit(solution)/shard_map/ppermute | solution.py:342
  17.8 9.1 %collective-permute-start.7 = (f32[64,128]{1,0:T(8,128)S(1)}, f32[64,128]{1,0:T(8,128)S(1)}, u32[]{:S(2)}, u32[]{:S(2)}) collective-permute-start(f32[64,128]{1,0:T(8,128)S(1)} %get-tuple-element.27), channel_id=1, source_target_pairs={{0,4},{1,5},{2,6},{3,7},{4,0},{5,1},{6,2},{7,3},{8,12},{9,13},{10,... | collective-permute-start | bytes 98312 | tf_op jit(solution)/shard_map/ppermute | solution.py:342
  20.6 6.4 %collective-permute-start.8 = (f32[64,128]{1,0:T(8,128)S(1)}, f32[64,128]{1,0:T(8,128)S(1)}, u32[]{:S(2)}, u32[]{:S(2)}) collective-permute-start(f32[64,128]{1,0:T(8,128)S(1)} %get-tuple-element.28), channel_id=1, source_target_pairs={{0,5},{1,4},{2,7},{3,6},{4,1},{5,0},{6,3},{7,2},{8,13},{9,12},{10,... | collective-permute-start | bytes 98312 | tf_op jit(solution)/shard_map/ppermute | solution.py:342
  20.6 6.4 %collective-permute-start.9 = (f32[64,128]{1,0:T(8,128)S(1)}, f32[64,128]{1,0:T(8,128)S(1)}, u32[]{:S(2)}, u32[]{:S(2)}) collective-permute-start(f32[64,128]{1,0:T(8,128)S(1)} %get-tuple-element.29), channel_id=1, source_target_pairs={{0,6},{1,7},{2,4},{3,5},{4,2},{5,3},{6,0},{7,1},{8,14},{9,15},{10,... | collective-permute-start | bytes 98312 | tf_op jit(solution)/shard_map/ppermute | solution.py:342
  24.2 5.1 %collective-permute-start.10 = (f32[64,128]{1,0:T(8,128)S(1)}, f32[64,128]{1,0:T(8,128)S(1)}, u32[]{:S(2)}, u32[]{:S(2)}) collective-permute-start(f32[64,128]{1,0:T(8,128)S(1)} %get-tuple-element.30), channel_id=1, source_target_pairs={{0,7},{1,6},{2,5},{3,4},{4,3},{5,2},{6,1},{7,0},{8,15},{9,14},{10,... | collective-permute-start | bytes 98312 | tf_op jit(solution)/shard_map/ppermute | solution.py:342
  24.3 1.3 %copy-start.1 = (f32[5,2,2,2,8,1024]{5,4,3,2,1,0:T(8,128)S(1)}, f32[5,2,2,2,8,1024]{5,4,3,2,1,0:T(8,128)}, u32[]{:S(2)}) copy-start(f32[5,2,2,2,8,1024]{5,4,3,2,1,0:T(8,128)} %param.14) | copy-start | bytes 3932164
  25.6 3.7 %copy-start.3 = (f32[2,2,2,8,1024]{4,3,2,1,0:T(8,128)S(1)}, f32[2,2,2,8,1024]{4,3,2,1,0:T(8,128)}, u32[]{:S(2)}) copy-start(f32[2,2,2,8,1024]{4,3,2,1,0:T(8,128)} %param.13) | copy-start | bytes 786436
  25.6 3.7 %copy-start.6 = (s32[64]{0:T(128)S(1)}, s32[64]{0:T(128)}, u32[]{:S(2)}) copy-start(s32[64]{0:T(128)} %refs_12_.1) | copy-start | bytes 772
  25.6 3.7 %copy-start.7 = (f32[4]{0:T(128)S(1)}, f32[4]{0:T(128)}, u32[]{:S(2)}) copy-start(f32[4]{0:T(128)} %refs_13_.1) | copy-start | bytes 52
  25.6 3.7 %copy-start.8 = (f32[2]{0:T(128)S(1)}, f32[2]{0:T(128)}, u32[]{:S(2)}) copy-start(f32[2]{0:T(128)} %refs_14_.1) | copy-start | bytes 28
  25.6 3.7 %copy-start.9 = (f32[2]{0:T(128)S(1)}, f32[2]{0:T(128)}, u32[]{:S(2)}) copy-start(f32[2]{0:T(128)} %refs_15_.1) | copy-start | bytes 28
  25.6 3.7 %copy-start.10 = (s32[2]{0:T(128)S(1)}, s32[2]{0:T(128)}, u32[]{:S(2)}) copy-start(s32[2]{0:T(128)} %refs_16_.1) | copy-start | bytes 28
where the time goes:
time: 42.4 us; the launch traced here: 42.1 us
  starting transfers between devices  16.6 us (39%)
  blocking collectives  10.7 us (25%)
  waiting for transfers between devices  5.05 us (12%)
  Pallas kernels  4.85 us (11%)
  local copies, waits for them, and re-layouts  4.82 us (11%)
    all_to_all x1, blocking collectives, per_device(): lax.all_to_all(tile, ('kgrp', 'energy'), split_axis=0, concat_axis=0, til...  10.7 us
    ppermute x7, starting transfers between devices, per_device(): lax.ppermute(smeared[m], 'energy', [(e, e ^ m) for e in range(parts)])  8.49 us
    ppermute x4, starting transfers between devices, exchange(): lax.ppermute(block, 'kgrp', [(i, i ^ flip) for i in range(groups)])  8.07 us
    unnamed x23, local copies, waits for them, and re-layouts  3.73 us
    ppermute x4, waiting for transfers between devices, exchange(): lax.ppermute(block, 'kgrp', [(i, i ^ flip) for i in range(groups)])  2.68 us
    ppermute x7, waiting for transfers between devices, per_device(): lax.ppermute(smeared[m], 'energy', [(e, e ^ m) for e in range(parts)])  2.37 us
    pallas_call x1, Pallas kernels, history(): pl.pallas_call(history_kernel, out_shape=(jax.ShapeDtypeStruct(past_input...  1.27 us
    slice x1, local copies, waits for them, and re-layouts, exchange(): return (near, [across(near[0], 2), across(own[half:], 3)])  1.09 us
  transfers between devices with their start and end apart: 11, of which 4 were waited for; matrix products, arithmetic and copies ran while one was open for 2% of the time, Pallas kernels for 6%

commit v1 on v0

--- a/solution.py
+++ b/solution.py
@@ -33,12 +33,14 @@
     return dot(left[0], right[0]) + (dot(left[0], right[1]) + dot(left[1], right[0]))
 
 
-def prepare_kernel(total_k, own, neighbour, weight, stencil_hi, stencil_lo, part):
+def prepare_kernel(total_k, own, neighbour, weight, stencil_hi, stencil_lo, part, tail):
     comps, group_len, slice_len = own.shape
     group_id = lax.axis_index("kgrp")
     parts = lax.axis_size("energy")
     rows = group_len // parts
-    targets = neighbour[...]
+    slots, _ = neighbour.shape
+    padded = jnp.concatenate([neighbour[...], jnp.zeros((8 - slots, group_len), jnp.int32)], axis=0)
+    targets = jnp.transpose(padded)
     place = lax.axis_index("energy")
     bit = 1
     while bit < parts:
@@ -50,7 +52,7 @@
     local = (targets - group_id * group_len + (group_len + total_k)) % total_k
     spot = lax.broadcasted_iota(jnp.int32, (group_len, 3 * group_len), 1)
     stencil = jnp.zeros(spot.shape, jnp.float32)
-    for n in range(local.shape[1]):
+    for n in range(slots):
         stencil = stencil + jnp.where(spot == local[:, n : n + 1], weight[n], 0.0)
     before, after = stencil[:, :group_len], stencil[:, 2 * group_len :]
     swapped = paired(total_k // group_len) & (group_id % 2 == 1)
@@ -59,6 +61,9 @@
     centre = split(stencil[:, group_len : 2 * group_len])
     for c in range(0, comps, 2):
         result = product(centre, split(jnp.concatenate([own[c], own[c + 1]], axis=1)))
+        if c >= comps - tail.shape[0]:
+            at = c - comps + tail.shape[0]
+            tail[at], tail[at + 1] = own[c], own[c + 1]
         part[c] = result[:, :slice_len]
         part[c + 1] = result[:, slice_len:]
 
@@ -66,21 +71,23 @@
 def prepare(own, neighbour, weight, total_k):
     group_len = own.shape[1]
     sides = jax.ShapeDtypeStruct((group_len, 2 * group_len), jnp.bfloat16)
+    tail = jax.ShapeDtypeStruct((own.shape[0] // 2,) + own.shape[1:], jnp.float32)
     return pl.pallas_call(
         lambda *refs: prepare_kernel(total_k, *refs),
-        out_shape=(sides, sides, jax.ShapeDtypeStruct(own.shape, jnp.float32)),
+        out_shape=(sides, sides, jax.ShapeDtypeStruct(own.shape, jnp.float32), tail),
         in_specs=[VMEM, VMEM, SMEM],
-        out_specs=(VMEM, VMEM, VMEM),
+        out_specs=(VMEM,) * 4,
         compiler_params=PARAMS,
         cost_estimate=pl.CostEstimate(
             flops=6 * own.size * group_len, bytes_accessed=8 * own.size, transcendentals=0
         ),
         name="prepare",
-    )(own, neighbour, weight)
+    )(own, jnp.transpose(neighbour), weight)
 
 
 def smear_kernel(side, count, *refs):
-    blocks, (stencil_hi, stencil_lo, part), out = refs[:count], refs[count : count + 3], refs[count + 3 :]
+    blocks, (stencil_hi, stencil_lo, part, _) = refs[:count], refs[count : count + 4]
+    out = refs[count + 4 :]
     _, group_len, slice_len = blocks[0].shape
     at = slice(side * group_len, (side + 1) * group_len)
     stencil = (stencil_hi[:, at], stencil_lo[:, at])
@@ -100,7 +107,7 @@
         first += block.shape[0]
 
 
-def smear(side, blocks, stencil_hi, stencil_lo, part, parts):
+def smear(side, blocks, stencil_hi, stencil_lo, part, after, parts):
     comps, group_len, slice_len = part.shape
     if side == NEAR:
         out_shape = [jax.ShapeDtypeStruct(part.shape, jnp.float32)]
@@ -109,29 +116,28 @@
     return pl.pallas_call(
         lambda *refs: smear_kernel(side, len(blocks), *refs),
         out_shape=out_shape,
-        in_specs=[VMEM] * (len(blocks) + 3),
+        in_specs=[VMEM] * (len(blocks) + 4),
         out_specs=[VMEM] * len(out_shape),
         compiler_params=PARAMS,
         cost_estimate=pl.CostEstimate(
             flops=6 * part.size * group_len, bytes_accessed=12 * part.size, transcendentals=0
         ),
         name="smear",
-    )(*blocks, stencil_hi, stencil_lo, part)
+    )(*blocks, stencil_hi, stencil_lo, part, after)
 
 
 def paired(groups):
     return groups == 4
 
 
-def exchange(own, groups):
+def exchange(own, tail, groups):
     if not paired(groups):
         forward = [(i, (i + 1) % groups) for i in range(groups)]
         backward = [(target, source) for source, target in forward]
         return [lax.ppermute(own, "kgrp", backward)], [lax.ppermute(own, "kgrp", forward)]
-    half = own.shape[0] // 2
     across = lambda block, flip: lax.ppermute(block, "kgrp", [(i, i ^ flip) for i in range(groups)])
-    near = [across(own[:half], 1), across(own[half:], 1)]
-    return near, [across(near[0], 2), across(own[half:], 3)]
+    head = across(own[: own.shape[0] - tail.shape[0]], 1)
+    return [head, across(tail, 1)], [across(head, 2), across(tail, 3)]
 
 
 def spread(values, shape):
@@ -329,15 +335,16 @@
     own = greens.reshape(-1, group_len, slice_len)
     height = own.shape[0] * rows
 
-    sides = exchange(own, groups)
-
     flat = current.reshape(height, width)
     old_in = past_inputs.reshape(HIST, height, width)
     old_res = past_residuals.reshape(HIST, height, width)
-    stencil_hi, stencil_lo, smeared = prepare(own, neighbour, stencil_weight, groups * group_len)
+    stencil_hi, stencil_lo, smeared, tail = prepare(
+        own, neighbour, stencil_weight, groups * group_len
+    )
+    sides = exchange(own, tail, groups)
     aged, old_tile = history(old_in, old_res, slot_order)
-    (smeared,) = smear(NEAR, sides[NEAR], stencil_hi, stencil_lo, smeared, parts)
-    smeared = list(smear(FAR, sides[FAR], stencil_hi, stencil_lo, smeared, parts))
+    (smeared,) = smear(NEAR, sides[NEAR], stencil_hi, stencil_lo, smeared, old_tile, parts)
+    smeared = list(smear(FAR, sides[FAR], stencil_hi, stencil_lo, smeared, old_tile, parts))
     for m in range(parts - 1, 0, -1):
         smeared[m] = lax.ppermute(smeared[m], "energy", [(e, e ^ m) for e in range(parts)])
     fresh, tile = residual(

time: 42.4 us -> 44 us (1.038)
  waiting for transfers between devices: 5.05 us -> 6.85 us
  local copies, waits for them, and re-layouts: 4.82 us -> 6.54 us
  starting transfers between devices: 16.6 us -> 15.3 us
  blocking collectives: 10.7 us -> 9.88 us
    ppermute x7, waiting for transfers between devices: 2.37 us -> 5.11 us  [per_device(): lax.ppermute(smeared[m], 'energy', [(e, e ^ m) for e in range(parts)])]
    unnamed x23 -> x28, local copies, waits for them, and re-layouts: 3.73 us -> 5.62 us
    ppermute x4, starting transfers between devices: 8.07 us -> 6.56 us  [exchange(): lax.ppermute(block, 'kgrp', [(i, i ^ flip) for i in range(groups)])]
    ppermute x4, waiting for transfers between devices: 2.68 us -> 1.73 us  [exchange(): lax.ppermute(block, 'kgrp', [(i, i ^ flip) for i in range(groups)])]
    all_to_all x1, blocking collectives: 10.7 us -> 9.88 us  [per_device(): lax.all_to_all(tile, ('kgrp', 'energy'), split_axis=0, concat_axis=0, til...]
  transfers between devices with their start and end apart: 11 -> 11, of which waited for: 4 -> 6; matrix products, arithmetic and copies ran while one was open for 2% -> 0% of each run, Pallas kernels for 6% -> 6%
where the time goes in v1:
time: 44 us; the launch traced here: 43.7 us
  starting transfers between devices  15.3 us (35%)
  blocking collectives  9.88 us (22%)
  waiting for transfers between devices  6.85 us (16%)
  local copies, waits for them, and re-layouts  6.54 us (15%)
  Pallas kernels  4.93 us (11%)
    all_to_all x1, blocking collectives, per_device(): lax.all_to_all(tile, ('kgrp', 'energy'), split_axis=0, concat_axis=0, til...  9.88 us
    ppermute x7, starting transfers between devices, per_device(): lax.ppermute(smeared[m], 'energy', [(e, e ^ m) for e in range(parts)])  8.77 us
    ppermute x4, starting transfers between devices, exchange(): lax.ppermute(block, 'kgrp', [(i, i ^ flip) for i in range(groups)])  6.56 us
    unnamed x28, local copies, waits for them, and re-layouts  5.62 us
    ppermute x7, waiting for transfers between devices, per_device(): lax.ppermute(smeared[m], 'energy', [(e, e ^ m) for e in range(parts)])  5.11 us
    ppermute x4, waiting for transfers between devices, exchange(): lax.ppermute(block, 'kgrp', [(i, i ^ flip) for i in range(groups)])  1.73 us
    pallas_call x1, Pallas kernels, history(): pl.pallas_call(history_kernel, out_shape=(jax.ShapeDtypeStruct(past_input...  1.27 us
    pallas_call x1, Pallas kernels, residual(): pl.pallas_call(lambda *refs: residual_kernel(rows, len(smeared), *refs),...  1.07 us
  transfers between devices with their start and end apart: 11, of which 6 were waited for; matrix products, arithmetic and copies ran while one was open for 0% of the time, Pallas kernels for 6%

profile of v1, /device:TPU:0, one launch (start us, length us, event | category | flops | bytes accessed | tf_op | source)
XLA Modules:
  0.0 43.7 jit_solution(12161807640602650250)
XLA Ops:
  0.0 0.9 %slice.6 = f32[1,2,2,64,128]{4,3,2,1,0:T(8,128)S(1)} slice(f32[2,2,2,64,128]{4,3,2,1,0:T(8,128)} %param.12), slice={[0:1], [0:2], [0:2], [0:64], [0:128]} | slice | bytes 262144 | tf_op jit(solution)/shard_map/slice | solution.py:139
  0.9 3.0 %collective-permute-start = (f32[4,64,128]{2,1,0:T(8,128)S(1)}, f32[4,64,128]{2,1,0:T(8,128)S(1)}, u32[]{:S(2)}, u32[]{:S(2)}) collective-permute-start(f32[4,64,128]{2,1,0:T(8,128)S(1)} %bitcast.14), channel_id=1, source_target_pairs={{0,8},{8,0},{16,24},{24,16},{1,9},{9,1},{17,25},{25,17},{2,10},{10... | collective-permute-start | bytes 393224 | tf_op jit(solution)/shard_map/ppermute | solution.py:138
  3.9 0.9 %copy-done.4 = f32[2,2,2,64,128]{4,3,2,1,0:T(8,128)S(1)} copy-done((f32[2,2,2,64,128]{4,3,2,1,0:T(8,128)S(1)}, f32[2,2,2,64,128]{4,3,2,1,0:T(8,128)}, u32[]{:S(2)}) %copy-start.4) | copy-done | bytes 262168
  4.9 0.7 %copy-done.5 = s32[64,5]{0,1:T(8,128)S(1)} copy-done((s32[64,5]{0,1:T(8,128)S(1)}, s32[64,5]{0,1:T(8,128)}, u32[]{:S(2)}) %copy-start.5) | copy-done | bytes 1304
  5.6 0.7 %copy-done.8 = f32[5]{0:T(128)S(1)} copy-done((f32[5]{0:T(128)S(1)}, f32[5]{0:T(128)}, u32[]{:S(2)}) %copy-start.8) | copy-done | bytes 44
  6.2 1.1 %prepare.1 = (bf16[64,128]{1,0:T(8,128)(2,1)S(1)}, bf16[64,128]{1,0:T(8,128)(2,1)S(1)}, f32[8,64,128]{2,1,0:T(8,128)S(1)}, f32[4,64,128]{2,1,0:T(8,128)S(1)}) custom-call(f32[8,64,128]{2,1,0:T(8,128)S(1)} %bitcast.12, s32[5,64]{1,0:T(8,128)S(1)} %bitcast.13, f32[5]{0:T(128)S(1)} %copy-done.8), custom_call_target="tpu_custom_call" | custom-call | flops 25165824 | bytes 524288 | tf_op jit(solution)/shard_map/prepare/pallas_call | solution.py:75
  7.3 0.1 collective-permute-start.3
  7.4 3.0 %collective-permute-start.2 = (f32[4,64,128]{2,1,0:T(8,128)S(1)}, f32[4,64,128]{2,1,0:T(8,128)S(1)}, u32[]{:S(2)}, u32[]{:S(2)}) collective-permute-start(f32[4,64,128]{2,1,0:T(8,128)S(1)} %get-tuple-element.21), channel_id=1, source_target_pairs={{0,24},{8,16},{16,8},{24,0},{1,25},{9,17},{17,9},{25,1},{2,26},{10... | collective-permute-start | bytes 393224 | tf_op jit(solution)/shard_map/ppermute | solution.py:138
  10.3 0.0 collective-permute-done.refs_0_
  10.3 0.5 %collective-permute-start.1 = (f32[4,64,128]{2,1,0:T(8,128)S(1)}, f32[4,64,128]{2,1,0:T(8,128)S(1)}, u32[]{:S(2)}, u32[]{:S(2)}) collective-permute-start(f32[4,64,128]{2,1,0:T(8,128)S(1)} %collective-permute-done.refs_0_), channel_id=1, source_target_pairs={{0,16},{8,24},{16,0},{24,8},{1,17},{9,25},{17,1},{25,9},{2,18},{10... | collective-permute-start | bytes 393224 | tf_op jit(solution)/shard_map/ppermute | solution.py:138
  10.8 1.3 %copy-done = f32[5,2,2,2,8,1024]{5,4,3,2,1,0:T(8,128)S(1)} copy-done((f32[5,2,2,2,8,1024]{5,4,3,2,1,0:T(8,128)S(1)}, f32[5,2,2,2,8,1024]{5,4,3,2,1,0:T(8,128)}, u32[]{:S(2)}) %copy-start) | copy-done | bytes 1310744
  12.2 1.3 %copy-done.2 = f32[5,2,2,2,8,1024]{5,4,3,2,1,0:T(8,128)S(1)} copy-done((f32[5,2,2,2,8,1024]{5,4,3,2,1,0:T(8,128)S(1)}, f32[5,2,2,2,8,1024]{5,4,3,2,1,0:T(8,128)}, u32[]{:S(2)}) %copy-start.2) | copy-done | bytes 1310744
  13.5 0.7 %copy-done.6 = s32[5]{0:T(128)S(1)} copy-done((s32[5]{0:T(128)S(1)}, s32[5]{0:T(128)}, u32[]{:S(2)}) %copy-start.6) | copy-done | bytes 44
  14.1 1.3 %history.1 = (f32[5,64,1024]{2,1,0:T(8,128)S(1)}, f32[8,128]{1,0:T(8,128)S(1)}) custom-call(f32[5,64,1024]{2,1,0:T(8,128)S(1)} %bitcast.9, f32[5,64,1024]{2,1,0:T(8,128)S(1)} %bitcast.7, s32[5]{0:T(128)S(1)} %copy-done.6), custom_call_target="tpu_custom_call" | custom-call | flops 2621440 | bytes 3932160 | tf_op jit(solution)/shard_map/history/pallas_call | solution.py:176
  15.4 0.0 copy-start.1
  15.4 0.0 copy-start.7
  15.4 0.0 copy-start.9
  15.4 0.0 copy-start.10
  15.5 0.0 copy-start.11
  15.5 0.0 copy-start.12
  15.5 0.0 copy-start.13
  15.5 0.0 collective-permute-done.3.refs_1_
  15.5 0.2 smear.2.refs_4_
  15.7 0.4 collective-permute-done.2.refs_1_
  16.2 1.3 %collective-permute-done.1.refs_0_ = f32[4,64,128]{2,1,0:T(8,128)S(1)} collective-permute-done((f32[4,64,128]{2,1,0:T(8,128)S(1)}, f32[4,64,128]{2,1,0:T(8,128)S(1)}, u32[]{:S(2)}, u32[]{:S(2)}) %collective-permute-start.1) | collective-permute-done | bytes 131104 | tf_op jit(solution)/shard_map/ppermute | solution.py:138
  17.5 0.3 smear.3
  17.8 2.3 %collective-permute-start.10 = (f32[64,128]{1,0:T(8,128)S(1)}, f32[64,128]{1,0:T(8,128)S(1)}, u32[]{:S(2)}, u32[]{:S(2)}) collective-permute-start(f32[64,128]{1,0:T(8,128)S(1)} %get-tuple-element.33), channel_id=1, source_target_pairs={{0,7},{1,6},{2,5},{3,4},{4,3},{5,2},{6,1},{7,0},{8,15},{9,14},{10,... | collective-permute-start | bytes 98312 | tf_op jit(solution)/shard_map/ppermute | solution.py:349
  20.1 1.4 %collective-permute-start.4 = (f32[64,128]{1,0:T(8,128)S(1)}, f32[64,128]{1,0:T(8,128)S(1)}, u32[]{:S(2)}, u32[]{:S(2)}) collective-permute-start(f32[64,128]{1,0:T(8,128)S(1)} %get-tuple-element.27), channel_id=1, source_target_pairs={{0,1},{1,0},{2,3},{3,2},{4,5},{5,4},{6,7},{7,6},{8,9},{9,8},{10,11... | collective-permute-start | bytes 98312 | tf_op jit(solution)/shard_map/ppermute | solution.py:349
  21.6 0.0 collective-permute-start.5
  21.6 1.4 %collective-permute-start.6 = (f32[64,128]{1,0:T(8,128)S(1)}, f32[64,128]{1,0:T(8,128)S(1)}, u32[]{:S(2)}, u32[]{:S(2)}) collective-permute-start(f32[64,128]{1,0:T(8,128)S(1)} %get-tuple-element.29), channel_id=1, source_target_pairs={{0,3},{1,2},{2,1},{3,0},{4,7},{5,6},{6,5},{7,4},{8,11},{9,10},{10,... | collective-permute-start | bytes 98312 | tf_op jit(solution)/shard_map/ppermute | solution.py:349
  22.9 0.0 collective-permute-start.7
  22.9 0.1 collective-permute-done.10.refs_7_
  23.0 3.0 %collective-permute-start.8 = (f32[64,128]{1,0:T(8,128)S(1)}, f32[64,128]{1,0:T(8,128)S(1)}, u32[]{:S(2)}, u32[]{:S(2)}) collective-permute-start(f32[64,128]{1,0:T(8,128)S(1)} %get-tuple-element.31), channel_id=1, source_target_pairs={{0,5},{1,4},{2,7},{3,6},{4,1},{5,0},{6,3},{7,2},{8,13},{9,12},{10,... | collective-permute-start | bytes 98312 | tf_op jit(solution)/shard_map/ppermute | solution.py:349
  26.0 0.0 collective-permute-done.4.refs_1_
  26.0 0.7 %collective-permute-start.9 = (f32[64,128]{1,0:T(8,128)S(1)}, f32[64,128]{1,0:T(8,128)S(1)}, u32[]{:S(2)}, u32[]{:S(2)}) collective-permute-start(f32[64,128]{1,0:T(8,128)S(1)} %get-tuple-element.32), channel_id=1, source_target_pairs={{0,6},{1,7},{2,4},{3,5},{4,2},{5,3},{6,0},{7,1},{8,14},{9,15},{10,... | collective-permute-start | bytes 98312 | tf_op jit(solution)/shard_map/ppermute | solution.py:349
  26.6 0.0 collective-permute-done.5.refs_2_
  26.6 0.0 collective-permute-done.6.refs_3_
  26.6 2.5 %collective-permute-done.7.refs_4_ = f32[64,128]{1,0:T(8,128)S(1)} collective-permute-done((f32[64,128]{1,0:T(8,128)S(1)}, f32[64,128]{1,0:T(8,128)S(1)}, u32[]{:S(2)}, u32[]{:S(2)}) %collective-permute-start.7) | collective-permute-done | bytes 32800 | tf_op jit(solution)/shard_map/ppermute | solution.py:349
  29.1 0.4 collective-permute-done.8.refs_5_
  29.5 2.2 %collective-permute-done.9.refs_6_ = f32[64,128]{1,0:T(8,128)S(1)} collective-permute-done((f32[64,128]{1,0:T(8,128)S(1)}, f32[64,128]{1,0:T(8,128)S(1)}, u32[]{:S(2)}, u32[]{:S(2)}) %collective-permute-start.9) | collective-permute-done | bytes 32800 | tf_op jit(solution)/shard_map/ppermute | solution.py:349
  31.7 0.0 copy-done.3
  31.7 0.0 copy-done.1
  31.7 0.0 copy-done.7
  31.7 0.0 copy-done.9
  31.7 0.0 copy-done.10
  31.7 1.1 %residual.1 = (f32[64,1024]{1,0:T(8,128)S(1)}, f32[32,8,128]{2,1,0:T(8,128)S(1)}) custom-call(f32[64,128]{1,0:T(8,128)S(1)} %get-tuple-element.26.refs_0_, f32[64,128]{1,0:T(8,128)S(1)} %collective-permute-done.4.refs_1_, f32[64,128]{1,0:T(8,128)S(1)} %collective-permute-done.5.refs_2_, f32[64,128]{1,0:T(8,128)S(1)} %collective-permute-done.6.refs_3_, ...), custom_call_target="tpu_custom_call" | custom-call | tf_op jit(solution)/shard_map/residual/pallas_call | solution.py:237
  32.8 9.9 %all_to_all.5.refs_0_ = f32[32,8,128]{2,1,0:T(8,128)S(1)} all-to-all(f32[32,8,128]{2,1,0:T(8,128)S(1)} %get-tuple-element.34), channel_id=1, replica_groups=mesh['kgrp'=4,'energy'=8] {'kgrp','energy'}, dimensions={0} | all-to-all | bytes 262144 | tf_op jit(solution)/shard_map/all_to_all | solution.py:354
  42.7 1.0 %mix.1 = f32[64,1024]{1,0:T(8,128)} custom-call(f32[32,8,128]{2,1,0:T(8,128)S(1)} %all_to_all.5.refs_0_, f32[64,1024]{1,0:T(8,128)S(1)} %get-tuple-element.35.refs_1_, f32[64,1024]{1,0:T(8,128)S(1)} %bitcast.11, f32[5,64,1024]{2,1,0:T(8,128)S(1)} %get-tuple-element.36.refs_3_), custom_call_target="tpu_custom_call" | custom-call | tf_op jit(solution)/shard_map/mix/pallas_call | solution.py:306
  (10 shorter events, 0.0 us)
Async XLA Ops:
  0.9 9.4 %collective-permute-start = (f32[4,64,128]{2,1,0:T(8,128)S(1)}, f32[4,64,128]{2,1,0:T(8,128)S(1)}, u32[]{:S(2)}, u32[]{:S(2)}) collective-permute-start(f32[4,64,128]{2,1,0:T(8,128)S(1)} %bitcast.14), channel_id=1, source_target_pairs={{0,8},{8,0},{16,24},{24,16},{1,9},{9,1},{17,25},{25,17},{2,10},{10... | collective-permute-start | bytes 393224 | tf_op jit(solution)/shard_map/ppermute | solution.py:138
  3.9 0.9 %copy-start.4 = (f32[2,2,2,64,128]{4,3,2,1,0:T(8,128)S(1)}, f32[2,2,2,64,128]{4,3,2,1,0:T(8,128)}, u32[]{:S(2)}) copy-start(f32[2,2,2,64,128]{4,3,2,1,0:T(8,128)} %param.12) | copy-start | bytes 786436
  4.9 0.7 %copy-start.5 = (s32[64,5]{0,1:T(8,128)S(1)}, s32[64,5]{0,1:T(8,128)}, u32[]{:S(2)}) copy-start(s32[64,5]{0,1:T(8,128)} %param.17) | copy-start | bytes 3844
  5.6 0.7 %copy-start.8 = (f32[5]{0:T(128)S(1)}, f32[5]{0:T(128)}, u32[]{:S(2)}) copy-start(f32[5]{0:T(128)} %refs_2_.1) | copy-start | bytes 64
  7.3 8.2 %collective-permute-start.3 = (f32[4,64,128]{2,1,0:T(8,128)S(1)}, f32[4,64,128]{2,1,0:T(8,128)S(1)}, u32[]{:S(2)}, u32[]{:S(2)}) collective-permute-start(f32[4,64,128]{2,1,0:T(8,128)S(1)} %get-tuple-element.21), channel_id=1, source_target_pairs={{0,8},{8,0},{16,24},{24,16},{1,9},{9,1},{17,25},{25,17},{2,10},{10... | collective-permute-start | bytes 393224 | tf_op jit(solution)/shard_map/ppermute | solution.py:138
  7.4 8.8 %collective-permute-start.2 = (f32[4,64,128]{2,1,0:T(8,128)S(1)}, f32[4,64,128]{2,1,0:T(8,128)S(1)}, u32[]{:S(2)}, u32[]{:S(2)}) collective-permute-start(f32[4,64,128]{2,1,0:T(8,128)S(1)} %get-tuple-element.21), channel_id=1, source_target_pairs={{0,24},{8,16},{16,8},{24,0},{1,25},{9,17},{17,9},{25,1},{2,26},{10... | collective-permute-start | bytes 393224 | tf_op jit(solution)/shard_map/ppermute | solution.py:138
  10.3 7.1 %collective-permute-start.1 = (f32[4,64,128]{2,1,0:T(8,128)S(1)}, f32[4,64,128]{2,1,0:T(8,128)S(1)}, u32[]{:S(2)}, u32[]{:S(2)}) collective-permute-start(f32[4,64,128]{2,1,0:T(8,128)S(1)} %collective-permute-done.refs_0_), channel_id=1, source_target_pairs={{0,16},{8,24},{16,0},{24,8},{1,17},{9,25},{17,1},{25,9},{2,18},{10... | collective-permute-start | bytes 393224 | tf_op jit(solution)/shard_map/ppermute | solution.py:138
  10.8 1.3 %copy-start = (f32[5,2,2,2,8,1024]{5,4,3,2,1,0:T(8,128)S(1)}, f32[5,2,2,2,8,1024]{5,4,3,2,1,0:T(8,128)}, u32[]{:S(2)}) copy-start(f32[5,2,2,2,8,1024]{5,4,3,2,1,0:T(8,128)} %param.15) | copy-start | bytes 3932164
  12.2 1.3 %copy-start.2 = (f32[5,2,2,2,8,1024]{5,4,3,2,1,0:T(8,128)S(1)}, f32[5,2,2,2,8,1024]{5,4,3,2,1,0:T(8,128)}, u32[]{:S(2)}) copy-start(f32[5,2,2,2,8,1024]{5,4,3,2,1,0:T(8,128)} %param.14) | copy-start | bytes 3932164
  13.5 0.7 %copy-start.6 = (s32[5]{0:T(128)S(1)}, s32[5]{0:T(128)}, u32[]{:S(2)}) copy-start(s32[5]{0:T(128)} %refs_11_.1) | copy-start | bytes 64
  14.1 17.5 %copy-start.3 = (f32[2,2,2,8,1024]{4,3,2,1,0:T(8,128)S(1)}, f32[2,2,2,8,1024]{4,3,2,1,0:T(8,128)}, u32[]{:S(2)}) copy-start(f32[2,2,2,8,1024]{4,3,2,1,0:T(8,128)} %param.13) | copy-start | bytes 786436
  15.4 16.3 %copy-start.1 = (f32[5,2,2,2,8,1024]{5,4,3,2,1,0:T(8,128)S(1)}, f32[5,2,2,2,8,1024]{5,4,3,2,1,0:T(8,128)}, u32[]{:S(2)}) copy-start(f32[5,2,2,2,8,1024]{5,4,3,2,1,0:T(8,128)} %param.15) | copy-start | bytes 3932164
  15.4 16.3 %copy-start.7 = (s32[5]{0:T(128)S(1)}, s32[5]{0:T(128)}, u32[]{:S(2)}) copy-start(s32[5]{0:T(128)} %refs_11_.1) | copy-start | bytes 64
  15.4 16.3 %copy-start.9 = (s32[64]{0:T(128)S(1)}, s32[64]{0:T(128)}, u32[]{:S(2)}) copy-start(s32[64]{0:T(128)} %refs_12_.1) | copy-start | bytes 772
  15.4 16.3 %copy-start.10 = (f32[4]{0:T(128)S(1)}, f32[4]{0:T(128)}, u32[]{:S(2)}) copy-start(f32[4]{0:T(128)} %refs_13_.1) | copy-start | bytes 52
  15.5 16.3 %copy-start.11 = (f32[2]{0:T(128)S(1)}, f32[2]{0:T(128)}, u32[]{:S(2)}) copy-start(f32[2]{0:T(128)} %refs_14_.1) | copy-start | bytes 28
  15.5 16.2 %copy-start.12 = (f32[2]{0:T(128)S(1)}, f32[2]{0:T(128)}, u32[]{:S(2)}) copy-start(f32[2]{0:T(128)} %refs_15_.1) | copy-start | bytes 28
  15.5 16.2 %copy-start.13 = (s32[2]{0:T(128)S(1)}, s32[2]{0:T(128)}, u32[]{:S(2)}) copy-start(s32[2]{0:T(128)} %refs_16_.1) | copy-start | bytes 28
  17.8 5.2 %collective-permute-start.10 = (f32[64,128]{1,0:T(8,128)S(1)}, f32[64,128]{1,0:T(8,128)S(1)}, u32[]{:S(2)}, u32[]{:S(2)}) collective-permute-start(f32[64,128]{1,0:T(8,128)S(1)} %get-tuple-element.33), channel_id=1, source_target_pairs={{0,7},{1,6},{2,5},{3,4},{4,3},{5,2},{6,1},{7,0},{8,15},{9,14},{10,... | collective-permute-start | bytes 98312 | tf_op jit(solution)/shard_map/ppermute | solution.py:349
  20.1 5.8 %collective-permute-start.4 = (f32[64,128]{1,0:T(8,128)S(1)}, f32[64,128]{1,0:T(8,128)S(1)}, u32[]{:S(2)}, u32[]{:S(2)}) collective-permute-start(f32[64,128]{1,0:T(8,128)S(1)} %get-tuple-element.27), channel_id=1, source_target_pairs={{0,1},{1,0},{2,3},{3,2},{4,5},{5,4},{6,7},{7,6},{8,9},{9,8},{10,11... | collective-permute-start | bytes 98312 | tf_op jit(solution)/shard_map/ppermute | solution.py:349
  21.6 5.1 %collective-permute-start.5 = (f32[64,128]{1,0:T(8,128)S(1)}, f32[64,128]{1,0:T(8,128)S(1)}, u32[]{:S(2)}, u32[]{:S(2)}) collective-permute-start(f32[64,128]{1,0:T(8,128)S(1)} %get-tuple-element.28), channel_id=1, source_target_pairs={{0,2},{1,3},{2,0},{3,1},{4,6},{5,7},{6,4},{7,5},{8,10},{9,11},{10,... | collective-permute-start | bytes 98312 | tf_op jit(solution)/shard_map/ppermute | solution.py:349
  21.6 5.1 %collective-permute-start.6 = (f32[64,128]{1,0:T(8,128)S(1)}, f32[64,128]{1,0:T(8,128)S(1)}, u32[]{:S(2)}, u32[]{:S(2)}) collective-permute-start(f32[64,128]{1,0:T(8,128)S(1)} %get-tuple-element.29), channel_id=1, source_target_pairs={{0,3},{1,2},{2,1},{3,0},{4,7},{5,6},{6,5},{7,4},{8,11},{9,10},{10,... | collective-permute-start | bytes 98312 | tf_op jit(solution)/shard_map/ppermute | solution.py:349
  22.9 6.2 %collective-permute-start.7 = (f32[64,128]{1,0:T(8,128)S(1)}, f32[64,128]{1,0:T(8,128)S(1)}, u32[]{:S(2)}, u32[]{:S(2)}) collective-permute-start(f32[64,128]{1,0:T(8,128)S(1)} %get-tuple-element.30), channel_id=1, source_target_pairs={{0,4},{1,5},{2,6},{3,7},{4,0},{5,1},{6,2},{7,3},{8,12},{9,13},{10,... | collective-permute-start | bytes 98312 | tf_op jit(solution)/shard_map/ppermute | solution.py:349
  23.0 6.5 %collective-permute-start.8 = (f32[64,128]{1,0:T(8,128)S(1)}, f32[64,128]{1,0:T(8,128)S(1)}, u32[]{:S(2)}, u32[]{:S(2)}) collective-permute-start(f32[64,128]{1,0:T(8,128)S(1)} %get-tuple-element.31), channel_id=1, source_target_pairs={{0,5},{1,4},{2,7},{3,6},{4,1},{5,0},{6,3},{7,2},{8,13},{9,12},{10,... | collective-permute-start | bytes 98312 | tf_op jit(solution)/shard_map/ppermute | solution.py:349
  26.0 5.7 %collective-permute-start.9 = (f32[64,128]{1,0:T(8,128)S(1)}, f32[64,128]{1,0:T(8,128)S(1)}, u32[]{:S(2)}, u32[]{:S(2)}) collective-permute-start(f32[64,128]{1,0:T(8,128)S(1)} %get-tuple-element.32), channel_id=1, source_target_pairs={{0,6},{1,7},{2,4},{3,5},{4,2},{5,3},{6,0},{7,1},{8,14},{9,15},{10,... | collective-permute-start | bytes 98312 | tf_op jit(solution)/shard_map/ppermute | solution.py:349

commit v2 on v1

--- a/solution.py
+++ b/solution.py
@@ -33,7 +33,7 @@
     return dot(left[0], right[0]) + (dot(left[0], right[1]) + dot(left[1], right[0]))
 
 
-def prepare_kernel(total_k, own, neighbour, weight, stencil_hi, stencil_lo, part, tail):
+def prepare_kernel(total_k, own, neighbour, weight, stencil_hi, stencil_lo, part):
     comps, group_len, slice_len = own.shape
     group_id = lax.axis_index("kgrp")
     parts = lax.axis_size("energy")
@@ -61,9 +61,6 @@
     centre = split(stencil[:, group_len : 2 * group_len])
     for c in range(0, comps, 2):
         result = product(centre, split(jnp.concatenate([own[c], own[c + 1]], axis=1)))
-        if c >= comps - tail.shape[0]:
-            at = c - comps + tail.shape[0]
-            tail[at], tail[at + 1] = own[c], own[c + 1]
         part[c] = result[:, :slice_len]
         part[c + 1] = result[:, slice_len:]
 
@@ -71,12 +68,11 @@
 def prepare(own, neighbour, weight, total_k):
     group_len = own.shape[1]
     sides = jax.ShapeDtypeStruct((group_len, 2 * group_len), jnp.bfloat16)
-    tail = jax.ShapeDtypeStruct((own.shape[0] // 2,) + own.shape[1:], jnp.float32)
     return pl.pallas_call(
         lambda *refs: prepare_kernel(total_k, *refs),
-        out_shape=(sides, sides, jax.ShapeDtypeStruct(own.shape, jnp.float32), tail),
+        out_shape=(sides, sides, jax.ShapeDtypeStruct(own.shape, jnp.float32)),
         in_specs=[VMEM, VMEM, SMEM],
-        out_specs=(VMEM,) * 4,
+        out_specs=(VMEM,) * 3,
         compiler_params=PARAMS,
         cost_estimate=pl.CostEstimate(
             flops=6 * own.size * group_len, bytes_accessed=8 * own.size, transcendentals=0
@@ -91,7 +87,6 @@
     _, group_len, slice_len = blocks[0].shape
     at = slice(side * group_len, (side + 1) * group_len)
     stencil = (stencil_hi[:, at], stencil_lo[:, at])
-    rows = group_len // len(out)
     first = 0
     for block in blocks:
         for c in range(0, block.shape[0], 2):
@@ -102,8 +97,10 @@
                 if side == NEAR:
                     out[0][at] = smeared
                     continue
-                for m in range(len(out)):
-                    out[m][at * rows : (at + 1) * rows, :] = smeared[m * rows : (m + 1) * rows]
+                chips, height, _ = out[0].shape
+                rows = height // part.shape[0]
+                for m in range(2 * chips):
+                    out[m % 2][m // 2, at * rows : (at + 1) * rows, :] = smeared[m * rows : (m + 1) * rows]
         first += block.shape[0]
 
 
@@ -112,7 +109,8 @@
     if side == NEAR:
         out_shape = [jax.ShapeDtypeStruct(part.shape, jnp.float32)]
     else:
-        out_shape = [jax.ShapeDtypeStruct((comps * group_len // parts, slice_len), jnp.float32)] * parts
+        shape = (parts // 2, comps * group_len // parts, slice_len)
+        out_shape = [jax.ShapeDtypeStruct(shape, jnp.float32)] * 2
     return pl.pallas_call(
         lambda *refs: smear_kernel(side, len(blocks), *refs),
         out_shape=out_shape,
@@ -126,18 +124,37 @@
     )(*blocks, stencil_hi, stencil_lo, part, after)
 
 
+def join_kernel(own, swapped, *out):
+    for chip, block in enumerate(out, 1):
+        block[0], block[1] = own[chip], swapped[chip]
+
+
+def join(own, swapped):
+    chips, height, slice_len = own.shape
+    shape = jax.ShapeDtypeStruct((2, height, slice_len), jnp.float32)
+    return pl.pallas_call(
+        join_kernel,
+        out_shape=[shape] * (chips - 1),
+        in_specs=[VMEM] * 2,
+        out_specs=[VMEM] * (chips - 1),
+        compiler_params=PARAMS,
+        name="join",
+    )(own, swapped)
+
+
 def paired(groups):
     return groups == 4
 
 
-def exchange(own, tail, groups):
+def exchange(own, groups):
     if not paired(groups):
         forward = [(i, (i + 1) % groups) for i in range(groups)]
         backward = [(target, source) for source, target in forward]
         return [lax.ppermute(own, "kgrp", backward)], [lax.ppermute(own, "kgrp", forward)]
     across = lambda block, flip: lax.ppermute(block, "kgrp", [(i, i ^ flip) for i in range(groups)])
-    head = across(own[: own.shape[0] - tail.shape[0]], 1)
-    return [head, across(tail, 1)], [across(head, 2), across(tail, 3)]
+    half = own.shape[0] // 2
+    near = [across(own[:half], 1), across(own[half:], 1)]
+    return near, [across(near[0], 2), across(own[half:], 3)]
 
 
 def spread(values, shape):
@@ -187,14 +204,15 @@
     )(past_inputs, past_residuals, slots)
 
 
-def residual_kernel(rows, parts, *refs):
-    received = refs[:parts]
+def residual_kernel(rows, count, own, swapped, *refs):
+    received = refs[:count]
     (current, past_residuals, old_tile, slots, classes, acoustic, optical, number, shift,
-     fresh, tile, smeared) = refs[parts:]
-    _, height, slice_len = smeared.shape
+     fresh, tile, smeared) = refs[count:]
+    parts, height, slice_len = smeared.shape
     place = lax.axis_index("energy")
-    for m in range(parts):
-        smeared[place ^ m] = received[m][...]
+    smeared[place], smeared[place ^ 1] = own[0], swapped[0]
+    for chip, block in enumerate(received, 1):
+        smeared[place ^ (2 * chip)], smeared[place ^ (2 * chip + 1)] = block[0], block[1]
     first = place * rows
     row = lax.broadcasted_iota(jnp.int32, (8, slice_len), 0) % rows
     lane = lax.broadcasted_iota(jnp.int32, (8, slice_len), 1)
@@ -233,19 +251,19 @@
     tile[...] = jnp.broadcast_to(jnp.where(lane == 2, mine, old_tile[...])[None], tile.shape)
 
 
-def residual(smeared, current, past_residuals, old_tile, slots, classes, acoustic, optical, number, shift, rows, copies):
+def residual(kept, swapped, smeared, current, past_residuals, old_tile, slots, classes, acoustic, optical, number, shift, rows, copies):
     return pl.pallas_call(
         lambda *refs: residual_kernel(rows, len(smeared), *refs),
         out_shape=(
             jax.ShapeDtypeStruct(current.shape, jnp.float32),
             jax.ShapeDtypeStruct((copies, 8, LANES), jnp.float32),
         ),
-        in_specs=[VMEM] * (len(smeared) + 3) + [SMEM] * 6,
+        in_specs=[VMEM] * (len(smeared) + 5) + [SMEM] * 6,
         out_specs=(VMEM, VMEM),
-        scratch_shapes=[pltpu.VMEM((len(smeared),) + smeared[0].shape, jnp.float32)],
+        scratch_shapes=[pltpu.VMEM((2 * kept.shape[0],) + kept.shape[1:], jnp.float32)],
         compiler_params=PARAMS,
         name="residual",
-    )(*smeared, current, past_residuals, old_tile, slots, classes, acoustic, optical, number, shift)
+    )(kept, swapped, *smeared, current, past_residuals, old_tile, slots, classes, acoustic, optical, number, shift)
 
 
 def solve(products):
@@ -338,17 +356,16 @@
     flat = current.reshape(height, width)
     old_in = past_inputs.reshape(HIST, height, width)
     old_res = past_residuals.reshape(HIST, height, width)
-    stencil_hi, stencil_lo, smeared, tail = prepare(
-        own, neighbour, stencil_weight, groups * group_len
-    )
-    sides = exchange(own, tail, groups)
+    sides = exchange(own, groups)
+    stencil_hi, stencil_lo, smeared = prepare(own, neighbour, stencil_weight, groups * group_len)
     aged, old_tile = history(old_in, old_res, slot_order)
     (smeared,) = smear(NEAR, sides[NEAR], stencil_hi, stencil_lo, smeared, old_tile, parts)
-    smeared = list(smear(FAR, sides[FAR], stencil_hi, stencil_lo, smeared, old_tile, parts))
-    for m in range(parts - 1, 0, -1):
-        smeared[m] = lax.ppermute(smeared[m], "energy", [(e, e ^ m) for e in range(parts)])
+    kept, given = smear(FAR, sides[FAR], stencil_hi, stencil_lo, smeared, old_tile, parts)
+    meet = lambda block, m: lax.ppermute(block, "energy", [(e, e ^ m) for e in range(parts)])
+    swapped = meet(given, 1)
+    smeared = [meet(block, 2 * chip) for chip, block in enumerate(join(kept, swapped), 1)]
     fresh, tile = residual(
-        smeared, flat, old_res, old_tile, slot_order, momentum_class, acoustic_coupling,
+        kept, swapped, smeared, flat, old_res, old_tile, slot_order, momentum_class, acoustic_coupling,
         optical_coupling, occupation, phonon_shift, rows, groups * parts,
     )
     tiles = lax.all_to_all(tile, ("kgrp", "energy"), split_axis=0, concat_axis=0, tiled=True)

time: 44 us -> 42.2 us (0.959)
  starting transfers between devices: 15.3 us -> 12.6 us
  local copies, waits for them, and re-layouts: 6.54 us -> 4.33 us
  waiting for transfers between devices: 6.85 us -> 8.63 us
  blocking collectives: 9.88 us -> 11.3 us
    ppermute x7 -> x4, starting transfers between devices: 8.77 us -> 4.52 us  [per_device(): lax.ppermute(block, 'energy', [(e, e ^ m) for e in range(parts)])]
    unnamed x28 -> x26, local copies, waits for them, and re-layouts: 5.62 us -> 3.34 us
    ppermute x7 -> x4, waiting for transfers between devices: 5.11 us -> 7.28 us  [per_device(): lax.ppermute(block, 'energy', [(e, e ^ m) for e in range(parts)])]
    ppermute x4, starting transfers between devices: 6.56 us -> 8.07 us  [exchange(): lax.ppermute(block, 'kgrp', [(i, i ^ flip) for i in range(groups)])]
    all_to_all x1, blocking collectives: 9.88 us -> 11.3 us  [per_device(): lax.all_to_all(tile, ('kgrp', 'energy'), split_axis=0, concat_axis=0, til...]
  transfers between devices with their start and end apart: 11 -> 8, of which waited for: 6 -> 4; matrix products, arithmetic and copies ran while one was open for 0% -> 0% of each run, Pallas kernels for 6% -> 6%
where the time goes in v2:
time: 42.2 us; the launch traced here: 42 us
  starting transfers between devices  12.6 us (30%)
  blocking collectives  11.3 us (27%)
  waiting for transfers between devices  8.63 us (20%)
  Pallas kernels  4.94 us (12%)
  local copies, waits for them, and re-layouts  4.33 us (10%)
    all_to_all x1, blocking collectives, per_device(): lax.all_to_all(tile, ('kgrp', 'energy'), split_axis=0, concat_axis=0, til...  11.3 us
    ppermute x4, starting transfers between devices, exchange(): lax.ppermute(block, 'kgrp', [(i, i ^ flip) for i in range(groups)])  8.07 us
    ppermute x4, waiting for transfers between devices, per_device(): lax.ppermute(block, 'energy', [(e, e ^ m) for e in range(parts)])  7.28 us
    ppermute x4, starting transfers between devices, per_device(): lax.ppermute(block, 'energy', [(e, e ^ m) for e in range(parts)])  4.52 us
    unnamed x26, local copies, waits for them, and re-layouts  3.34 us
    ppermute x4, waiting for transfers between devices, exchange(): lax.ppermute(block, 'kgrp', [(i, i ^ flip) for i in range(groups)])  1.35 us
    pallas_call x1, Pallas kernels, history(): pl.pallas_call(history_kernel, out_shape=(jax.ShapeDtypeStruct(past_input...  1.27 us
    pallas_call x1, Pallas kernels, prepare(): pl.pallas_call(lambda *refs: prepare_kernel(total_k, *refs), out_shape=(s...  1.06 us
  transfers between devices with their start and end apart: 8, of which 4 were waited for; matrix products, arithmetic and copies ran while one was open for 0% of the time, Pallas kernels for 6%

profile of v2, /device:TPU:0, one launch (start us, length us, event | category | flops | bytes accessed | tf_op | source)
XLA Modules:
  0.0 42.0 jit_solution(5327784454998444144)
XLA Ops:
  0.0 1.0 %fusion = (f32[1,2,2,64,128]{4,3,2,1,0:T(8,128)S(1)}, f32[1,2,2,64,128]{4,3,2,1,0:T(8,128)S(1)}) fusion(f32[2,2,2,64,128]{4,3,2,1,0:T(8,128)} %param.12), kind=kLoop, calls=%fused_computation | loop fusion | bytes 524288 | tf_op jit(solution)/shard_map/slice | solution.py:157
  1.0 3.0 %collective-permute-start = (f32[4,64,128]{2,1,0:T(8,128)S(1)}, f32[4,64,128]{2,1,0:T(8,128)S(1)}, u32[]{:S(2)}, u32[]{:S(2)}) collective-permute-start(f32[4,64,128]{2,1,0:T(8,128)S(1)} %bitcast.17), channel_id=1, source_target_pairs={{0,8},{8,0},{16,24},{24,16},{1,9},{9,1},{17,25},{25,17},{2,10},{10... | collective-permute-start | bytes 393224 | tf_op jit(solution)/shard_map/ppermute | solution.py:154
  4.0 0.1 collective-permute-start.3
  4.1 2.9 %collective-permute-start.2 = (f32[4,64,128]{2,1,0:T(8,128)S(1)}, f32[4,64,128]{2,1,0:T(8,128)S(1)}, u32[]{:S(2)}, u32[]{:S(2)}) collective-permute-start(f32[4,64,128]{2,1,0:T(8,128)S(1)} %bitcast.16), channel_id=1, source_target_pairs={{0,24},{8,16},{16,8},{24,0},{1,25},{9,17},{17,9},{25,1},{2,26},{10... | collective-permute-start | bytes 393224 | tf_op jit(solution)/shard_map/ppermute | solution.py:154
  7.0 1.3 %collective-permute-done.refs_0_ = f32[4,64,128]{2,1,0:T(8,128)S(1)} collective-permute-done((f32[4,64,128]{2,1,0:T(8,128)S(1)}, f32[4,64,128]{2,1,0:T(8,128)S(1)}, u32[]{:S(2)}, u32[]{:S(2)}) %collective-permute-start) | collective-permute-done | bytes 131104 | tf_op jit(solution)/shard_map/ppermute | solution.py:154
  8.3 2.1 %collective-permute-start.1 = (f32[4,64,128]{2,1,0:T(8,128)S(1)}, f32[4,64,128]{2,1,0:T(8,128)S(1)}, u32[]{:S(2)}, u32[]{:S(2)}) collective-permute-start(f32[4,64,128]{2,1,0:T(8,128)S(1)} %collective-permute-done.refs_0_), channel_id=1, source_target_pairs={{0,16},{8,24},{16,0},{24,8},{1,17},{9,25},{17,1},{25,9},{2,18},{10... | collective-permute-start | bytes 393224 | tf_op jit(solution)/shard_map/ppermute | solution.py:154
  10.4 0.0 copy-start
  10.4 1.3 %copy-done = f32[5,2,2,2,8,1024]{5,4,3,2,1,0:T(8,128)S(1)} copy-done((f32[5,2,2,2,8,1024]{5,4,3,2,1,0:T(8,128)S(1)}, f32[5,2,2,2,8,1024]{5,4,3,2,1,0:T(8,128)}, u32[]{:S(2)}) %copy-start) | copy-done | bytes 1310744
  11.7 0.0 copy-start.2
  11.7 1.3 %copy-done.2 = f32[5,2,2,2,8,1024]{5,4,3,2,1,0:T(8,128)S(1)} copy-done((f32[5,2,2,2,8,1024]{5,4,3,2,1,0:T(8,128)S(1)}, f32[5,2,2,2,8,1024]{5,4,3,2,1,0:T(8,128)}, u32[]{:S(2)}) %copy-start.2) | copy-done | bytes 1310744
  13.0 0.0 copy-start.6
  13.0 0.7 %copy-done.6 = s32[5]{0:T(128)S(1)} copy-done((s32[5]{0:T(128)S(1)}, s32[5]{0:T(128)}, u32[]{:S(2)}) %copy-start.6) | copy-done | bytes 44
  13.7 0.0 copy-start.4
  13.7 1.3 %history.1 = (f32[5,64,1024]{2,1,0:T(8,128)S(1)}, f32[8,128]{1,0:T(8,128)S(1)}) custom-call(f32[5,64,1024]{2,1,0:T(8,128)S(1)} %bitcast.10, f32[5,64,1024]{2,1,0:T(8,128)S(1)} %bitcast.8, s32[5]{0:T(128)S(1)} %copy-done.6), custom_call_target="tpu_custom_call" | custom-call | flops 2621440 | bytes 3932160 | tf_op jit(solution)/shard_map/history/pallas_call | solution.py:193
  15.0 0.0 copy-start.1
  15.0 0.0 copy-start.3
  15.0 0.0 copy-start.8
  15.0 0.0 copy-start.9
  15.0 0.0 copy-start.10
  15.0 0.0 copy-start.11
  15.0 0.0 copy-start.12
  15.1 0.0 copy-done.4
  15.1 0.0 copy-done.5
  15.1 0.0 copy-done.7
  15.1 1.1 %prepare.1 = (bf16[64,128]{1,0:T(8,128)(2,1)S(1)}, bf16[64,128]{1,0:T(8,128)(2,1)S(1)}, f32[8,64,128]{2,1,0:T(8,128)S(1)}) custom-call(f32[8,64,128]{2,1,0:T(8,128)S(1)} %bitcast.13, s32[5,64]{1,0:T(8,128)S(1)} %bitcast.14, f32[5]{0:T(128)S(1)} %copy-done.7), custom_call_target="tpu_custom_call" | custom-call | flops 25165824 | bytes 524288 | tf_op jit(solution)/shard_map/prepare/pallas_call | solution.py:71
  16.2 0.0 collective-permute-done.3.refs_1_
  16.2 0.2 smear.2.refs_4_
  16.4 0.0 collective-permute-done.2.refs_1_
  16.4 0.0 collective-permute-done.1.refs_0_
  16.4 0.3 smear.3
  16.7 0.1 collective-permute-start.4
  16.8 1.3 %collective-permute-done.4.swapped.refs_1_ = f32[4,64,128]{2,1,0:T(8,128)S(1)} collective-permute-done((f32[4,64,128]{2,1,0:T(8,128)S(1)}, f32[4,64,128]{2,1,0:T(8,128)S(1)}, u32[]{:S(2)}, u32[]{:S(2)}) %collective-permute-start.4) | collective-permute-done | bytes 131104 | tf_op jit(solution)/shard_map/ppermute | solution.py:364
  18.2 1.6 %collective-permute-start.5 = (f32[2,64,128]{2,1,0:T(8,128)S(1)}, f32[2,64,128]{2,1,0:T(8,128)S(1)}, u32[]{:S(2)}, u32[]{:S(2)}) collective-permute-start(f32[2,64,128]{2,1,0:T(8,128)S(1)} %get-tuple-element.23), channel_id=1, source_target_pairs={{0,2},{1,3},{2,0},{3,1},{4,6},{5,7},{6,4},{7,5},{8,10},{9,11},{10,... | collective-permute-start | bytes 196616 | tf_op jit(solution)/shard_map/ppermute | solution.py:364
  19.8 2.6 %collective-permute-start.6 = (f32[2,64,128]{2,1,0:T(8,128)S(1)}, f32[2,64,128]{2,1,0:T(8,128)S(1)}, u32[]{:S(2)}, u32[]{:S(2)}) collective-permute-start(f32[2,64,128]{2,1,0:T(8,128)S(1)} %get-tuple-element.24), channel_id=1, source_target_pairs={{0,4},{1,5},{2,6},{3,7},{4,0},{5,1},{6,2},{7,3},{8,12},{9,13},{10,... | collective-permute-start | bytes 196616 | tf_op jit(solution)/shard_map/ppermute | solution.py:364
  22.4 0.2 collective-permute-start.7
  22.6 0.0 collective-permute-done.5.refs_2_
  22.6 4.7 %collective-permute-done.6.refs_3_ = f32[2,64,128]{2,1,0:T(8,128)S(1)} collective-permute-done((f32[2,64,128]{2,1,0:T(8,128)S(1)}, f32[2,64,128]{2,1,0:T(8,128)S(1)}, u32[]{:S(2)}, u32[]{:S(2)}) %collective-permute-start.6) | collective-permute-done | bytes 65568 | tf_op jit(solution)/shard_map/ppermute | solution.py:364
  27.4 1.2 %collective-permute-done.7.refs_4_ = f32[2,64,128]{2,1,0:T(8,128)S(1)} collective-permute-done((f32[2,64,128]{2,1,0:T(8,128)S(1)}, f32[2,64,128]{2,1,0:T(8,128)S(1)}, u32[]{:S(2)}, u32[]{:S(2)}) %collective-permute-start.7) | collective-permute-done | bytes 65568 | tf_op jit(solution)/shard_map/ppermute | solution.py:364
  28.6 0.0 copy-done.1
  28.6 0.0 copy-done.3
  28.6 0.0 copy-done.8
  28.6 0.0 copy-done.9
  28.6 0.0 copy-done.10
  28.6 0.0 copy-done.11
  28.6 0.0 copy-done.12
  28.6 1.1 %residual.1 = (f32[64,1024]{1,0:T(8,128)S(1)}, f32[32,8,128]{2,1,0:T(8,128)S(1)}) custom-call(f32[4,64,128]{2,1,0:T(8,128)S(1)} %get-tuple-element.21.own.refs_0_, f32[4,64,128]{2,1,0:T(8,128)S(1)} %collective-permute-done.4.swapped.refs_1_, f32[2,64,128]{2,1,0:T(8,128)S(1)} %collective-permute-done.5.refs_2_, ...), custom_call_target="tpu_custom_call" | custom-call | tf_op jit(solution)/shard_map/residual/pallas_call | solution.py:255
  29.7 11.3 %all_to_all.5.refs_0_ = f32[32,8,128]{2,1,0:T(8,128)S(1)} all-to-all(f32[32,8,128]{2,1,0:T(8,128)S(1)} %get-tuple-element.26), channel_id=1, replica_groups=mesh['kgrp'=4,'energy'=8] {'kgrp','energy'}, dimensions={0} | all-to-all | bytes 262144 | tf_op jit(solution)/shard_map/all_to_all | solution.py:371
  41.0 1.0 %mix.1 = f32[64,1024]{1,0:T(8,128)} custom-call(f32[32,8,128]{2,1,0:T(8,128)S(1)} %all_to_all.5.refs_0_, f32[64,1024]{1,0:T(8,128)S(1)} %get-tuple-element.27.refs_1_, f32[64,1024]{1,0:T(8,128)S(1)} %bitcast.12, f32[5,64,1024]{2,1,0:T(8,128)S(1)} %get-tuple-element.28.refs_3_), custom_call_target="tpu_custom_call" | custom-call | tf_op jit(solution)/shard_map/mix/pallas_call | solution.py:324
  (3 shorter events, 0.0 us)
Async XLA Ops:
  1.0 7.3 %collective-permute-start = (f32[4,64,128]{2,1,0:T(8,128)S(1)}, f32[4,64,128]{2,1,0:T(8,128)S(1)}, u32[]{:S(2)}, u32[]{:S(2)}) collective-permute-start(f32[4,64,128]{2,1,0:T(8,128)S(1)} %bitcast.17), channel_id=1, source_target_pairs={{0,8},{8,0},{16,24},{24,16},{1,9},{9,1},{17,25},{25,17},{2,10},{10... | collective-permute-start | bytes 393224 | tf_op jit(solution)/shard_map/ppermute | solution.py:154
  4.0 12.2 %collective-permute-start.3 = (f32[4,64,128]{2,1,0:T(8,128)S(1)}, f32[4,64,128]{2,1,0:T(8,128)S(1)}, u32[]{:S(2)}, u32[]{:S(2)}) collective-permute-start(f32[4,64,128]{2,1,0:T(8,128)S(1)} %bitcast.15), channel_id=1, source_target_pairs={{0,8},{8,0},{16,24},{24,16},{1,9},{9,1},{17,25},{25,17},{2,10},{10... | collective-permute-start | bytes 393224 | tf_op jit(solution)/shard_map/ppermute | solution.py:154
  4.1 12.4 %collective-permute-start.2 = (f32[4,64,128]{2,1,0:T(8,128)S(1)}, f32[4,64,128]{2,1,0:T(8,128)S(1)}, u32[]{:S(2)}, u32[]{:S(2)}) collective-permute-start(f32[4,64,128]{2,1,0:T(8,128)S(1)} %bitcast.16), channel_id=1, source_target_pairs={{0,24},{8,16},{16,8},{24,0},{1,25},{9,17},{17,9},{25,1},{2,26},{10... | collective-permute-start | bytes 393224 | tf_op jit(solution)/shard_map/ppermute | solution.py:154
  8.3 8.1 %collective-permute-start.1 = (f32[4,64,128]{2,1,0:T(8,128)S(1)}, f32[4,64,128]{2,1,0:T(8,128)S(1)}, u32[]{:S(2)}, u32[]{:S(2)}) collective-permute-start(f32[4,64,128]{2,1,0:T(8,128)S(1)} %collective-permute-done.refs_0_), channel_id=1, source_target_pairs={{0,16},{8,24},{16,0},{24,8},{1,17},{9,25},{17,1},{25,9},{2,18},{10... | collective-permute-start | bytes 393224 | tf_op jit(solution)/shard_map/ppermute | solution.py:154
  10.4 1.3 %copy-start = (f32[5,2,2,2,8,1024]{5,4,3,2,1,0:T(8,128)S(1)}, f32[5,2,2,2,8,1024]{5,4,3,2,1,0:T(8,128)}, u32[]{:S(2)}) copy-start(f32[5,2,2,2,8,1024]{5,4,3,2,1,0:T(8,128)} %param.15) | copy-start | bytes 3932164
  11.7 1.3 %copy-start.2 = (f32[5,2,2,2,8,1024]{5,4,3,2,1,0:T(8,128)S(1)}, f32[5,2,2,2,8,1024]{5,4,3,2,1,0:T(8,128)}, u32[]{:S(2)}) copy-start(f32[5,2,2,2,8,1024]{5,4,3,2,1,0:T(8,128)} %param.14) | copy-start | bytes 3932164
  13.0 0.7 %copy-start.6 = (s32[5]{0:T(128)S(1)}, s32[5]{0:T(128)}, u32[]{:S(2)}) copy-start(s32[5]{0:T(128)} %refs_8_.1) | copy-start | bytes 64
  13.7 1.4 %copy-start.4 = (f32[2,2,2,64,128]{4,3,2,1,0:T(8,128)S(1)}, f32[2,2,2,64,128]{4,3,2,1,0:T(8,128)}, u32[]{:S(2)}) copy-start(f32[2,2,2,64,128]{4,3,2,1,0:T(8,128)} %param.12) | copy-start | bytes 786436
  13.7 1.4 %copy-start.5 = (s32[64,5]{0,1:T(8,128)S(1)}, s32[64,5]{0,1:T(8,128)}, u32[]{:S(2)}) copy-start(s32[64,5]{0,1:T(8,128)} %param.17) | copy-start | bytes 3844
  13.7 1.4 %copy-start.7 = (f32[5]{0:T(128)S(1)}, f32[5]{0:T(128)}, u32[]{:S(2)}) copy-start(f32[5]{0:T(128)} %refs_2_.1) | copy-start | bytes 64
  15.0 13.6 %copy-start.1 = (f32[5,2,2,2,8,1024]{5,4,3,2,1,0:T(8,128)S(1)}, f32[5,2,2,2,8,1024]{5,4,3,2,1,0:T(8,128)}, u32[]{:S(2)}) copy-start(f32[5,2,2,2,8,1024]{5,4,3,2,1,0:T(8,128)} %param.15) | copy-start | bytes 3932164
  15.0 13.6 %copy-start.3 = (f32[2,2,2,8,1024]{4,3,2,1,0:T(8,128)S(1)}, f32[2,2,2,8,1024]{4,3,2,1,0:T(8,128)}, u32[]{:S(2)}) copy-start(f32[2,2,2,8,1024]{4,3,2,1,0:T(8,128)} %param.13) | copy-start | bytes 786436
  15.0 13.6 %copy-start.8 = (s32[64]{0:T(128)S(1)}, s32[64]{0:T(128)}, u32[]{:S(2)}) copy-start(s32[64]{0:T(128)} %refs_9_.1) | copy-start | bytes 772
  15.0 13.6 %copy-start.9 = (f32[4]{0:T(128)S(1)}, f32[4]{0:T(128)}, u32[]{:S(2)}) copy-start(f32[4]{0:T(128)} %refs_10_.1) | copy-start | bytes 52
  15.0 13.6 %copy-start.10 = (f32[2]{0:T(128)S(1)}, f32[2]{0:T(128)}, u32[]{:S(2)}) copy-start(f32[2]{0:T(128)} %refs_11_.1) | copy-start | bytes 28
  15.0 13.6 %copy-start.11 = (f32[2]{0:T(128)S(1)}, f32[2]{0:T(128)}, u32[]{:S(2)}) copy-start(f32[2]{0:T(128)} %refs_12_.1) | copy-start | bytes 28
  15.0 13.6 %copy-start.12 = (s32[2]{0:T(128)S(1)}, s32[2]{0:T(128)}, u32[]{:S(2)}) copy-start(s32[2]{0:T(128)} %refs_13_.1) | copy-start | bytes 28
  16.7 1.4 %collective-permute-start.4 = (f32[4,64,128]{2,1,0:T(8,128)S(1)}, f32[4,64,128]{2,1,0:T(8,128)S(1)}, u32[]{:S(2)}, u32[]{:S(2)}) collective-permute-start(f32[4,64,128]{2,1,0:T(8,128)S(1)} %get-tuple-element.22), channel_id=1, source_target_pairs={{0,1},{1,0},{2,3},{3,2},{4,5},{5,4},{6,7},{7,6},{8,9},{9,8},{10,11... | collective-permute-start | bytes 393224 | tf_op jit(solution)/shard_map/ppermute | solution.py:364
  18.2 4.5 %collective-permute-start.5 = (f32[2,64,128]{2,1,0:T(8,128)S(1)}, f32[2,64,128]{2,1,0:T(8,128)S(1)}, u32[]{:S(2)}, u32[]{:S(2)}) collective-permute-start(f32[2,64,128]{2,1,0:T(8,128)S(1)} %get-tuple-element.23), channel_id=1, source_target_pairs={{0,2},{1,3},{2,0},{3,1},{4,6},{5,7},{6,4},{7,5},{8,10},{9,11},{10,... | collective-permute-start | bytes 196616 | tf_op jit(solution)/shard_map/ppermute | solution.py:364
  19.8 7.5 %collective-permute-start.6 = (f32[2,64,128]{2,1,0:T(8,128)S(1)}, f32[2,64,128]{2,1,0:T(8,128)S(1)}, u32[]{:S(2)}, u32[]{:S(2)}) collective-permute-start(f32[2,64,128]{2,1,0:T(8,128)S(1)} %get-tuple-element.24), channel_id=1, source_target_pairs={{0,4},{1,5},{2,6},{3,7},{4,0},{5,1},{6,2},{7,3},{8,12},{9,13},{10,... | collective-permute-start | bytes 196616 | tf_op jit(solution)/shard_map/ppermute | solution.py:364
  22.4 6.2 %collective-permute-start.7 = (f32[2,64,128]{2,1,0:T(8,128)S(1)}, f32[2,64,128]{2,1,0:T(8,128)S(1)}, u32[]{:S(2)}, u32[]{:S(2)}) collective-permute-start(f32[2,64,128]{2,1,0:T(8,128)S(1)} %get-tuple-element.25), channel_id=1, source_target_pairs={{0,6},{1,7},{2,4},{3,5},{4,2},{5,3},{6,0},{7,1},{8,14},{9,15},{10,... | collective-permute-start | bytes 196616 | tf_op jit(solution)/shard_map/ppermute | solution.py:364

commit v3 on v2

--- a/solution.py
+++ b/solution.py
@@ -15,7 +15,7 @@
 SMEM = pl.BlockSpec(memory_space=pltpu.SMEM)
 PARAMS = pltpu.CompilerParams(vmem_limit_bytes=16 * 1024 * 1024)
 
-NEAR, FAR = 0, 1
+CHUNKS = 2
 
 PAIRS = [(i, j) for i in range(1, HIST + 1) for j in range(i, HIST + 1)]
 SPOTS = {pair: v for v, pair in enumerate(PAIRS)}
@@ -33,7 +33,7 @@
     return dot(left[0], right[0]) + (dot(left[0], right[1]) + dot(left[1], right[0]))
 
 
-def prepare_kernel(total_k, own, neighbour, weight, stencil_hi, stencil_lo, part):
+def prepare_kernel(total_k, own, neighbour, weight, _, stencil_hi, stencil_lo, part):
     comps, group_len, slice_len = own.shape
     group_id = lax.axis_index("kgrp")
     parts = lax.axis_size("energy")
@@ -65,63 +65,55 @@
         part[c + 1] = result[:, slice_len:]
 
 
-def prepare(own, neighbour, weight, total_k):
+def prepare(own, neighbour, weight, after, total_k):
     group_len = own.shape[1]
     sides = jax.ShapeDtypeStruct((group_len, 2 * group_len), jnp.bfloat16)
     return pl.pallas_call(
         lambda *refs: prepare_kernel(total_k, *refs),
         out_shape=(sides, sides, jax.ShapeDtypeStruct(own.shape, jnp.float32)),
-        in_specs=[VMEM, VMEM, SMEM],
+        in_specs=[VMEM, VMEM, SMEM, VMEM],
         out_specs=(VMEM,) * 3,
         compiler_params=PARAMS,
         cost_estimate=pl.CostEstimate(
             flops=6 * own.size * group_len, bytes_accessed=8 * own.size, transcendentals=0
         ),
         name="prepare",
-    )(own, jnp.transpose(neighbour), weight)
-
-
-def smear_kernel(side, count, *refs):
-    blocks, (stencil_hi, stencil_lo, part, _) = refs[:count], refs[count : count + 4]
-    out = refs[count + 4 :]
-    _, group_len, slice_len = blocks[0].shape
-    at = slice(side * group_len, (side + 1) * group_len)
-    stencil = (stencil_hi[:, at], stencil_lo[:, at])
-    first = 0
-    for block in blocks:
-        for c in range(0, block.shape[0], 2):
-            result = product(stencil, split(jnp.concatenate([block[c], block[c + 1]], axis=1)))
-            for p in range(2):
-                at = first + c + p
-                smeared = part[at] + result[:, p * slice_len : (p + 1) * slice_len]
-                if side == NEAR:
-                    out[0][at] = smeared
-                    continue
-                chips, height, _ = out[0].shape
-                rows = height // part.shape[0]
-                for m in range(2 * chips):
-                    out[m % 2][m // 2, at * rows : (at + 1) * rows, :] = smeared[m * rows : (m + 1) * rows]
-        first += block.shape[0]
-
-
-def smear(side, blocks, stencil_hi, stencil_lo, part, after, parts):
-    comps, group_len, slice_len = part.shape
-    if side == NEAR:
-        out_shape = [jax.ShapeDtypeStruct(part.shape, jnp.float32)]
-    else:
-        shape = (parts // 2, comps * group_len // parts, slice_len)
-        out_shape = [jax.ShapeDtypeStruct(shape, jnp.float32)] * 2
-    return pl.pallas_call(
-        lambda *refs: smear_kernel(side, len(blocks), *refs),
-        out_shape=out_shape,
-        in_specs=[VMEM] * (len(blocks) + 4),
-        out_specs=[VMEM] * len(out_shape),
+    )(own, jnp.transpose(neighbour), weight, after)
+
+
+def smear_kernel(first, near, far, stencil_hi, stencil_lo, part, *refs):
+    *_, kept, given = refs
+    comps, _, slice_len = near.shape
+    chips, height, _ = kept.shape
+    rows = height // comps
+    stencil = (stencil_hi[...], stencil_lo[...])
+    for c in range(0, comps, 2):
+        block = jnp.concatenate(
+            [jnp.concatenate([side[c], side[c + 1]], axis=1) for side in (near, far)], axis=0
+        )
+        result = product(stencil, split(block))
+        for p in range(2):
+            smeared = part[first + c + p] + result[:, p * slice_len : (p + 1) * slice_len]
+            at = slice((c + p) * rows, (c + p + 1) * rows)
+            for m in range(2 * chips):
+                out = given if m % 2 else kept
+                out[m // 2, at, :] = smeared[m * rows : (m + 1) * rows]
+
+
+def smear(first, near, far, stencil_hi, stencil_lo, part, after, parts):
+    comps, group_len, slice_len = near.shape
+    shape = (parts // 2, comps * group_len // parts, slice_len)
+    return pl.pallas_call(
+        lambda *refs: smear_kernel(first, *refs),
+        out_shape=[jax.ShapeDtypeStruct(shape, jnp.float32)] * 2,
+        in_specs=[VMEM] * 5 + [pl.BlockSpec(memory_space=pl.ANY)] * len(after),
+        out_specs=[VMEM] * 2,
         compiler_params=PARAMS,
         cost_estimate=pl.CostEstimate(
-            flops=6 * part.size * group_len, bytes_accessed=12 * part.size, transcendentals=0
+            flops=12 * near.size * group_len, bytes_accessed=16 * near.size, transcendentals=0
         ),
         name="smear",
-    )(*blocks, stencil_hi, stencil_lo, part, after)
+    )(near, far, stencil_hi, stencil_lo, part, *after)
 
 
 def join_kernel(own, swapped, *out):
@@ -146,15 +138,14 @@
     return groups == 4
 
 
-def exchange(own, groups):
-    if not paired(groups):
-        forward = [(i, (i + 1) % groups) for i in range(groups)]
-        backward = [(target, source) for source, target in forward]
-        return [lax.ppermute(own, "kgrp", backward)], [lax.ppermute(own, "kgrp", forward)]
-    across = lambda block, flip: lax.ppermute(block, "kgrp", [(i, i ^ flip) for i in range(groups)])
-    half = own.shape[0] // 2
-    near = [across(own[:half], 1), across(own[half:], 1)]
-    return near, [across(near[0], 2), across(own[half:], 3)]
+def exchange(block, groups):
+    if paired(groups):
+        near = [(i, i ^ 1) for i in range(groups)]
+        far = [(i, i ^ 3) for i in range(groups)]
+    else:
+        far = [(i, (i + 1) % groups) for i in range(groups)]
+        near = [(target, source) for source, target in far]
+    return lax.ppermute(block, "kgrp", near), lax.ppermute(block, "kgrp", far)
 
 
 def spread(values, shape):
@@ -204,15 +195,20 @@
     )(past_inputs, past_residuals, slots)
 
 
-def residual_kernel(rows, count, own, swapped, *refs):
-    received = refs[:count]
+def residual_kernel(rows, count, *refs):
+    arrived = refs[: CHUNKS * count]
     (current, past_residuals, old_tile, slots, classes, acoustic, optical, number, shift,
-     fresh, tile, smeared) = refs[count:]
+     fresh, tile, smeared) = refs[CHUNKS * count :]
     parts, height, slice_len = smeared.shape
+    span = height // CHUNKS
     place = lax.axis_index("energy")
-    smeared[place], smeared[place ^ 1] = own[0], swapped[0]
-    for chip, block in enumerate(received, 1):
-        smeared[place ^ (2 * chip)], smeared[place ^ (2 * chip + 1)] = block[0], block[1]
+    for chunk in range(CHUNKS):
+        own, swapped, *received = arrived[chunk * count : (chunk + 1) * count]
+        at = slice(chunk * span, (chunk + 1) * span)
+        smeared[place, at], smeared[place ^ 1, at] = own[0], swapped[0]
+        for chip, block in enumerate(received, 1):
+            smeared[place ^ (2 * chip), at] = block[0]
+            smeared[place ^ (2 * chip + 1), at] = block[1]
     first = place * rows
     row = lax.broadcasted_iota(jnp.int32, (8, slice_len), 0) % rows
     lane = lax.broadcasted_iota(jnp.int32, (8, slice_len), 1)
@@ -251,19 +247,21 @@
     tile[...] = jnp.broadcast_to(jnp.where(lane == 2, mine, old_tile[...])[None], tile.shape)
 
 
-def residual(kept, swapped, smeared, current, past_residuals, old_tile, slots, classes, acoustic, optical, number, shift, rows, copies):
-    return pl.pallas_call(
-        lambda *refs: residual_kernel(rows, len(smeared), *refs),
+def residual(arrived, current, past_residuals, old_tile, slots, classes, acoustic, optical, number, shift, rows, copies):
+    count = len(arrived) // CHUNKS
+    chips, span, slice_len = arrived[0].shape
+    return pl.pallas_call(
+        lambda *refs: residual_kernel(rows, count, *refs),
         out_shape=(
             jax.ShapeDtypeStruct(current.shape, jnp.float32),
             jax.ShapeDtypeStruct((copies, 8, LANES), jnp.float32),
         ),
-        in_specs=[VMEM] * (len(smeared) + 5) + [SMEM] * 6,
+        in_specs=[VMEM] * (len(arrived) + 3) + [SMEM] * 6,
         out_specs=(VMEM, VMEM),
-        scratch_shapes=[pltpu.VMEM((2 * kept.shape[0],) + kept.shape[1:], jnp.float32)],
+        scratch_shapes=[pltpu.VMEM((2 * chips, CHUNKS * span, slice_len), jnp.float32)],
         compiler_params=PARAMS,
         name="residual",
-    )(kept, swapped, *smeared, current, past_residuals, old_tile, slots, classes, acoustic, optical, number, shift)
+    )(*arrived, current, past_residuals, old_tile, slots, classes, acoustic, optical, number, shift)
 
 
 def solve(products):
@@ -356,16 +354,26 @@
     flat = current.reshape(height, width)
     old_in = past_inputs.reshape(HIST, height, width)
     old_res = past_residuals.reshape(HIST, height, width)
-    sides = exchange(own, groups)
-    stencil_hi, stencil_lo, smeared = prepare(own, neighbour, stencil_weight, groups * group_len)
+    span = own.shape[0] // CHUNKS
+    sides = [exchange(own[c * span : (c + 1) * span], groups) for c in range(CHUNKS)]
+
+    flat = current.reshape(height, width)
+    old_in = past_inputs.reshape(HIST, height, width)
+    old_res = past_residuals.reshape(HIST, height, width)
     aged, old_tile = history(old_in, old_res, slot_order)
-    (smeared,) = smear(NEAR, sides[NEAR], stencil_hi, stencil_lo, smeared, old_tile, parts)
-    kept, given = smear(FAR, sides[FAR], stencil_hi, stencil_lo, smeared, old_tile, parts)
+    stencil_hi, stencil_lo, part = prepare(
+        own, neighbour, stencil_weight, old_tile, groups * group_len
+    )
     meet = lambda block, m: lax.ppermute(block, "energy", [(e, e ^ m) for e in range(parts)])
-    swapped = meet(given, 1)
-    smeared = [meet(block, 2 * chip) for chip, block in enumerate(join(kept, swapped), 1)]
+    arrived = []
+    for chunk, (near, far) in enumerate(sides):
+        after = arrived[2:]
+        kept, given = smear(chunk * span, near, far, stencil_hi, stencil_lo, part, after, parts)
+        swapped = meet(given, 1)
+        joined = join(kept, swapped)
+        arrived += [kept, swapped] + [meet(block, 2 * chip) for chip, block in enumerate(joined, 1)]
     fresh, tile = residual(
-        kept, swapped, smeared, flat, old_res, old_tile, slot_order, momentum_class, acoustic_coupling,
+        arrived, flat, old_res, old_tile, slot_order, momentum_class, acoustic_coupling,
         optical_coupling, occupation, phonon_shift, rows, groups * parts,
     )
     tiles = lax.all_to_all(tile, ("kgrp", "energy"), split_axis=0, concat_axis=0, tiled=True)

time: 42.2 us -> 46.7 us (1.11)
  waiting for transfers between devices: 8.63 us -> 10.6 us
  starting transfers between devices: 12.6 us -> 14.4 us
  blocking collectives: 11.3 us -> 12.2 us
    ppermute x4 -> x8, starting transfers between devices: 4.52 us -> 8.37 us  [per_device(): lax.ppermute(block, 'energy', [(e, e ^ m) for e in range(parts)])]
    ppermute x4 -> x8, waiting for transfers between devices: 7.28 us -> 10.5 us  [per_device(): lax.ppermute(block, 'energy', [(e, e ^ m) for e in range(parts)])]
    ppermute x4, starting transfers between devices: 8.07 us -> 6.01 us  [exchange(): return (lax.ppermute(block, 'kgrp', near), lax.ppermute(block, 'kgrp', far))]
    ppermute x4, waiting for transfers between devices: 1.35 us -> 0.01 us  [exchange(): return (lax.ppermute(block, 'kgrp', near), lax.ppermute(block, 'kgrp', far))]
    all_to_all x1, blocking collectives: 11.3 us -> 12.2 us  [per_device(): lax.all_to_all(tile, ('kgrp', 'energy'), split_axis=0, concat_axis=0, til...]
  transfers between devices with their start and end apart: 8 -> 12, of which waited for: 4 -> 6; matrix products, arithmetic and copies ran while one was open for 0% -> 0% of each run, Pallas kernels for 6% -> 5%
where the time goes in v3:
time: 46.7 us; the launch traced here: 46.5 us
  starting transfers between devices  14.4 us (31%)
  blocking collectives  12.2 us (26%)
  waiting for transfers between devices  10.6 us (23%)
  Pallas kernels  4.82 us (10%)
  local copies, waits for them, and re-layouts  4.33 us (9%)
    all_to_all x1, blocking collectives, per_device(): lax.all_to_all(tile, ('kgrp', 'energy'), split_axis=0, concat_axis=0, til...  12.2 us
    ppermute x8, waiting for transfers between devices, per_device(): lax.ppermute(block, 'energy', [(e, e ^ m) for e in range(parts)])  10.5 us
    ppermute x8, starting transfers between devices, per_device(): lax.ppermute(block, 'energy', [(e, e ^ m) for e in range(parts)])  8.37 us
    ppermute x4, starting transfers between devices, exchange(): return (lax.ppermute(block, 'kgrp', near), lax.ppermute(block, 'kgrp', far))  6.01 us
    unnamed x26, local copies, waits for them, and re-layouts  3.34 us
    pallas_call x1, Pallas kernels, history(): pl.pallas_call(history_kernel, out_shape=(jax.ShapeDtypeStruct(past_input...  1.27 us
    pallas_call x1, Pallas kernels, prepare(): pl.pallas_call(lambda *refs: prepare_kernel(total_k, *refs), out_shape=(s...  1.07 us
    pallas_call x1, Pallas kernels, residual(): pl.pallas_call(lambda *refs: residual_kernel(rows, count, *refs), out_sha...  1.06 us
  transfers between devices with their start and end apart: 12, of which 6 were waited for; matrix products, arithmetic and copies ran while one was open for 0% of the time, Pallas kernels for 5%

profile of v3, /device:TPU:0, one launch (start us, length us, event | category | flops | bytes accessed | tf_op | source)
XLA Modules:
  0.0 46.5 jit_solution(16447529782224452950)
XLA Ops:
  0.0 1.0 %fusion = (f32[1,2,2,64,128]{4,3,2,1,0:T(8,128)S(1)}, f32[1,2,2,64,128]{4,3,2,1,0:T(8,128)S(1)}) fusion(f32[2,2,2,64,128]{4,3,2,1,0:T(8,128)} %param.12), kind=kLoop, calls=%fused_computation | loop fusion | bytes 524288 | tf_op jit(solution)/shard_map/slice | solution.py:358
  1.0 3.0 %collective-permute-start = (f32[4,64,128]{2,1,0:T(8,128)S(1)}, f32[4,64,128]{2,1,0:T(8,128)S(1)}, u32[]{:S(2)}, u32[]{:S(2)}) collective-permute-start(f32[4,64,128]{2,1,0:T(8,128)S(1)} %bitcast.17), channel_id=1, source_target_pairs={{0,8},{8,0},{16,24},{24,16},{1,9},{9,1},{17,25},{25,17},{2,10},{10... | collective-permute-start | bytes 393224 | tf_op jit(solution)/shard_map/ppermute | solution.py:148
  4.0 1.5 %collective-permute-start.1 = (f32[4,64,128]{2,1,0:T(8,128)S(1)}, f32[4,64,128]{2,1,0:T(8,128)S(1)}, u32[]{:S(2)}, u32[]{:S(2)}) collective-permute-start(f32[4,64,128]{2,1,0:T(8,128)S(1)} %bitcast.18), channel_id=1, source_target_pairs={{0,24},{8,16},{16,8},{24,0},{1,25},{9,17},{17,9},{25,1},{2,26},{10... | collective-permute-start | bytes 393224 | tf_op jit(solution)/shard_map/ppermute | solution.py:148
  5.5 1.5 %collective-permute-start.6 = (f32[4,64,128]{2,1,0:T(8,128)S(1)}, f32[4,64,128]{2,1,0:T(8,128)S(1)}, u32[]{:S(2)}, u32[]{:S(2)}) collective-permute-start(f32[4,64,128]{2,1,0:T(8,128)S(1)} %bitcast.15), channel_id=1, source_target_pairs={{0,8},{8,0},{16,24},{24,16},{1,9},{9,1},{17,25},{25,17},{2,10},{10... | collective-permute-start | bytes 393224 | tf_op jit(solution)/shard_map/ppermute | solution.py:148
  7.0 0.0 collective-permute-start.7
  7.0 1.3 %copy-done = f32[5,2,2,2,8,1024]{5,4,3,2,1,0:T(8,128)S(1)} copy-done((f32[5,2,2,2,8,1024]{5,4,3,2,1,0:T(8,128)S(1)}, f32[5,2,2,2,8,1024]{5,4,3,2,1,0:T(8,128)}, u32[]{:S(2)}) %copy-start) | copy-done | bytes 1310744
  8.3 1.3 %copy-done.2 = f32[5,2,2,2,8,1024]{5,4,3,2,1,0:T(8,128)S(1)} copy-done((f32[5,2,2,2,8,1024]{5,4,3,2,1,0:T(8,128)S(1)}, f32[5,2,2,2,8,1024]{5,4,3,2,1,0:T(8,128)}, u32[]{:S(2)}) %copy-start.2) | copy-done | bytes 1310744
  9.6 0.7 %copy-done.6 = s32[5]{0:T(128)S(1)} copy-done((s32[5]{0:T(128)S(1)}, s32[5]{0:T(128)}, u32[]{:S(2)}) %copy-start.6) | copy-done | bytes 44
  10.3 1.3 %history.1 = (f32[5,64,1024]{2,1,0:T(8,128)S(1)}, f32[8,128]{1,0:T(8,128)S(1)}) custom-call(f32[5,64,1024]{2,1,0:T(8,128)S(1)} %bitcast.10, f32[5,64,1024]{2,1,0:T(8,128)S(1)} %bitcast.8, s32[5]{0:T(128)S(1)} %copy-done.6), custom_call_target="tpu_custom_call" | custom-call | flops 2621440 | bytes 3932160 | tf_op jit(solution)/shard_map/history/pallas_call | solution.py:184
  11.6 0.0 copy-start.1
  11.6 0.0 copy-start.3
  11.6 0.0 copy-start.8
  11.6 0.0 copy-start.9
  11.6 0.0 copy-start.10
  11.6 0.0 copy-start.11
  11.6 0.0 copy-start.12
  11.7 0.0 copy-done.4
  11.7 0.0 copy-done.5
  11.7 0.0 copy-done.7
  11.7 1.1 %prepare.1 = (bf16[64,128]{1,0:T(8,128)(2,1)S(1)}, bf16[64,128]{1,0:T(8,128)(2,1)S(1)}, f32[8,64,128]{2,1,0:T(8,128)S(1)}) custom-call(f32[8,64,128]{2,1,0:T(8,128)S(1)} %bitcast.13, s32[5,64]{1,0:T(8,128)S(1)} %bitcast.14, f32[5]{0:T(128)S(1)} %copy-done.7, f32[8,128]{1,0:T(8,128)S(1)} %get-tuple-element.22.refs_3_.refs_12_), custom_call_target="tpu_custom_call" | custom-call | flops 25165824 | bytes 524288 | tf_op jit(solution)/shard_map/prepare/pallas_call | solution.py:71
  12.8 0.0 collective-permute-done.refs_0_
  12.8 0.0 collective-permute-done.1.refs_1_
  12.8 0.2 smear.2
  13.0 0.1 collective-permute-start.2
  13.1 1.2 %collective-permute-done.2.swapped.refs_1_ = f32[4,32,128]{2,1,0:T(8,128)S(1)} collective-permute-done((f32[4,32,128]{2,1,0:T(8,128)S(1)}, f32[4,32,128]{2,1,0:T(8,128)S(1)}, u32[]{:S(2)}, u32[]{:S(2)}) %collective-permute-start.2) | collective-permute-done | bytes 65568 | tf_op jit(solution)/shard_map/ppermute | solution.py:367
  14.3 2.1 %collective-permute-start.3 = (f32[2,32,128]{2,1,0:T(8,128)S(1)}, f32[2,32,128]{2,1,0:T(8,128)S(1)}, u32[]{:S(2)}, u32[]{:S(2)}) collective-permute-start(f32[2,32,128]{2,1,0:T(8,128)S(1)} %get-tuple-element.28), channel_id=1, source_target_pairs={{0,2},{1,3},{2,0},{3,1},{4,6},{5,7},{6,4},{7,5},{8,10},{9,11},{10,... | collective-permute-start | bytes 98312 | tf_op jit(solution)/shard_map/ppermute | solution.py:367
  16.4 2.6 %collective-permute-start.4 = (f32[2,32,128]{2,1,0:T(8,128)S(1)}, f32[2,32,128]{2,1,0:T(8,128)S(1)}, u32[]{:S(2)}, u32[]{:S(2)}) collective-permute-start(f32[2,32,128]{2,1,0:T(8,128)S(1)} %get-tuple-element.29), channel_id=1, source_target_pairs={{0,4},{1,5},{2,6},{3,7},{4,0},{5,1},{6,2},{7,3},{8,12},{9,13},{10,... | collective-permute-start | bytes 98312 | tf_op jit(solution)/shard_map/ppermute | solution.py:367
  19.0 0.0 collective-permute-start.5
  19.0 0.0 collective-permute-done.6.refs_0_
  19.0 0.0 collective-permute-done.7.refs_1_
  19.0 0.0 collective-permute-done.3.refs_5_.refs_2_
  19.0 2.8 %collective-permute-done.4.refs_6_.refs_3_ = f32[2,32,128]{2,1,0:T(8,128)S(1)} collective-permute-done((f32[2,32,128]{2,1,0:T(8,128)S(1)}, f32[2,32,128]{2,1,0:T(8,128)S(1)}, u32[]{:S(2)}, u32[]{:S(2)}) %collective-permute-start.4) | collective-permute-done | bytes 32800 | tf_op jit(solution)/shard_map/ppermute | solution.py:367
  21.8 2.9 %collective-permute-done.5.refs_7_.refs_4_ = f32[2,32,128]{2,1,0:T(8,128)S(1)} collective-permute-done((f32[2,32,128]{2,1,0:T(8,128)S(1)}, f32[2,32,128]{2,1,0:T(8,128)S(1)}, u32[]{:S(2)}, u32[]{:S(2)}) %collective-permute-start.5) | collective-permute-done | bytes 32800 | tf_op jit(solution)/shard_map/ppermute | solution.py:367
  24.7 0.2 smear.3
  24.9 0.1 collective-permute-start.8
  25.0 1.2 %collective-permute-done.8.swapped.refs_6_ = f32[4,32,128]{2,1,0:T(8,128)S(1)} collective-permute-done((f32[4,32,128]{2,1,0:T(8,128)S(1)}, f32[4,32,128]{2,1,0:T(8,128)S(1)}, u32[]{:S(2)}, u32[]{:S(2)}) %collective-permute-start.8) | collective-permute-done | bytes 65568 | tf_op jit(solution)/shard_map/ppermute | solution.py:367
  26.3 0.1 collective-permute-start.10
  26.3 1.0 %collective-permute-start.11 = (f32[2,32,128]{2,1,0:T(8,128)S(1)}, f32[2,32,128]{2,1,0:T(8,128)S(1)}, u32[]{:S(2)}, u32[]{:S(2)}) collective-permute-start(f32[2,32,128]{2,1,0:T(8,128)S(1)} %get-tuple-element.35), channel_id=1, source_target_pairs={{0,6},{1,7},{2,4},{3,5},{4,2},{5,3},{6,0},{7,1},{8,14},{9,15},{10,... | collective-permute-start | bytes 98312 | tf_op jit(solution)/shard_map/ppermute | solution.py:367
  27.3 2.5 %collective-permute-start.9 = (f32[2,32,128]{2,1,0:T(8,128)S(1)}, f32[2,32,128]{2,1,0:T(8,128)S(1)}, u32[]{:S(2)}, u32[]{:S(2)}) collective-permute-start(f32[2,32,128]{2,1,0:T(8,128)S(1)} %get-tuple-element.33), channel_id=1, source_target_pairs={{0,2},{1,3},{2,0},{3,1},{4,6},{5,7},{6,4},{7,5},{8,10},{9,11},{10,... | collective-permute-start | bytes 98312 | tf_op jit(solution)/shard_map/ppermute | solution.py:367
  29.8 1.7 %collective-permute-done.10.refs_8_ = f32[2,32,128]{2,1,0:T(8,128)S(1)} collective-permute-done((f32[2,32,128]{2,1,0:T(8,128)S(1)}, f32[2,32,128]{2,1,0:T(8,128)S(1)}, u32[]{:S(2)}, u32[]{:S(2)}) %collective-permute-start.10) | collective-permute-done | bytes 32800 | tf_op jit(solution)/shard_map/ppermute | solution.py:367
  31.5 0.7 %collective-permute-done.11.refs_9_ = f32[2,32,128]{2,1,0:T(8,128)S(1)} collective-permute-done((f32[2,32,128]{2,1,0:T(8,128)S(1)}, f32[2,32,128]{2,1,0:T(8,128)S(1)}, u32[]{:S(2)}, u32[]{:S(2)}) %collective-permute-start.11) | collective-permute-done | bytes 32800 | tf_op jit(solution)/shard_map/ppermute | solution.py:367
  32.2 0.0 collective-permute-done.9.refs_7_
  32.2 0.0 copy-done.1
  32.2 0.0 copy-done.3
  32.2 0.0 copy-done.8
  32.2 1.1 %residual.1 = (f32[64,1024]{1,0:T(8,128)S(1)}, f32[32,8,128]{2,1,0:T(8,128)S(1)}) custom-call(f32[4,32,128]{2,1,0:T(8,128)S(1)} %get-tuple-element.26.own.refs_0_, f32[4,32,128]{2,1,0:T(8,128)S(1)} %collective-permute-done.2.swapped.refs_1_, f32[2,32,128]{2,1,0:T(8,128)S(1)} %collective-permute-done.3.refs_5_.refs_2_, ...), custom_call_target="tpu_custom_call" | custom-call | tf_op jit(solution)/shard_map/residual/pallas_call | solution.py:253
  33.3 12.2 %all_to_all.5.refs_0_ = f32[32,8,128]{2,1,0:T(8,128)S(1)} all-to-all(f32[32,8,128]{2,1,0:T(8,128)S(1)} %get-tuple-element.36), channel_id=1, replica_groups=mesh['kgrp'=4,'energy'=8] {'kgrp','energy'}, dimensions={0} | all-to-all | bytes 262144 | tf_op jit(solution)/shard_map/all_to_all | solution.py:379
  45.5 1.0 %mix.1 = f32[64,1024]{1,0:T(8,128)} custom-call(f32[32,8,128]{2,1,0:T(8,128)S(1)} %all_to_all.5.refs_0_, f32[64,1024]{1,0:T(8,128)S(1)} %get-tuple-element.37.refs_1_, f32[64,1024]{1,0:T(8,128)S(1)} %bitcast.12, f32[5,64,1024]{2,1,0:T(8,128)S(1)} %get-tuple-element.38.refs_3_), custom_call_target="tpu_custom_call" | custom-call | tf_op jit(solution)/shard_map/mix/pallas_call | solution.py:322
  (12 shorter events, 0.0 us)
Async XLA Ops:
  1.0 11.8 %collective-permute-start = (f32[4,64,128]{2,1,0:T(8,128)S(1)}, f32[4,64,128]{2,1,0:T(8,128)S(1)}, u32[]{:S(2)}, u32[]{:S(2)}) collective-permute-start(f32[4,64,128]{2,1,0:T(8,128)S(1)} %bitcast.17), channel_id=1, source_target_pairs={{0,8},{8,0},{16,24},{24,16},{1,9},{9,1},{17,25},{25,17},{2,10},{10... | collective-permute-start | bytes 393224 | tf_op jit(solution)/shard_map/ppermute | solution.py:148
  4.0 8.8 %collective-permute-start.1 = (f32[4,64,128]{2,1,0:T(8,128)S(1)}, f32[4,64,128]{2,1,0:T(8,128)S(1)}, u32[]{:S(2)}, u32[]{:S(2)}) collective-permute-start(f32[4,64,128]{2,1,0:T(8,128)S(1)} %bitcast.18), channel_id=1, source_target_pairs={{0,24},{8,16},{16,8},{24,0},{1,25},{9,17},{17,9},{25,1},{2,26},{10... | collective-permute-start | bytes 393224 | tf_op jit(solution)/shard_map/ppermute | solution.py:148
  5.5 13.5 %collective-permute-start.6 = (f32[4,64,128]{2,1,0:T(8,128)S(1)}, f32[4,64,128]{2,1,0:T(8,128)S(1)}, u32[]{:S(2)}, u32[]{:S(2)}) collective-permute-start(f32[4,64,128]{2,1,0:T(8,128)S(1)} %bitcast.15), channel_id=1, source_target_pairs={{0,8},{8,0},{16,24},{24,16},{1,9},{9,1},{17,25},{25,17},{2,10},{10... | collective-permute-start | bytes 393224 | tf_op jit(solution)/shard_map/ppermute | solution.py:148
  7.0 12.0 %collective-permute-start.7 = (f32[4,64,128]{2,1,0:T(8,128)S(1)}, f32[4,64,128]{2,1,0:T(8,128)S(1)}, u32[]{:S(2)}, u32[]{:S(2)}) collective-permute-start(f32[4,64,128]{2,1,0:T(8,128)S(1)} %bitcast.16), channel_id=1, source_target_pairs={{0,24},{8,16},{16,8},{24,0},{1,25},{9,17},{17,9},{25,1},{2,26},{10... | collective-permute-start | bytes 393224 | tf_op jit(solution)/shard_map/ppermute | solution.py:148
  7.0 1.3 %copy-start = (f32[5,2,2,2,8,1024]{5,4,3,2,1,0:T(8,128)S(1)}, f32[5,2,2,2,8,1024]{5,4,3,2,1,0:T(8,128)}, u32[]{:S(2)}) copy-start(f32[5,2,2,2,8,1024]{5,4,3,2,1,0:T(8,128)} %param.15) | copy-start | bytes 3932164
  8.3 1.3 %copy-start.2 = (f32[5,2,2,2,8,1024]{5,4,3,2,1,0:T(8,128)S(1)}, f32[5,2,2,2,8,1024]{5,4,3,2,1,0:T(8,128)}, u32[]{:S(2)}) copy-start(f32[5,2,2,2,8,1024]{5,4,3,2,1,0:T(8,128)} %param.14) | copy-start | bytes 3932164
  9.6 0.7 %copy-start.6 = (s32[5]{0:T(128)S(1)}, s32[5]{0:T(128)}, u32[]{:S(2)}) copy-start(s32[5]{0:T(128)} %refs_13_.1) | copy-start | bytes 64
  10.3 1.4 %copy-start.4 = (f32[2,2,2,64,128]{4,3,2,1,0:T(8,128)S(1)}, f32[2,2,2,64,128]{4,3,2,1,0:T(8,128)}, u32[]{:S(2)}) copy-start(f32[2,2,2,64,128]{4,3,2,1,0:T(8,128)} %param.12) | copy-start | bytes 786436
  10.3 1.4 %copy-start.5 = (s32[64,5]{0,1:T(8,128)S(1)}, s32[64,5]{0,1:T(8,128)}, u32[]{:S(2)}) copy-start(s32[64,5]{0,1:T(8,128)} %param.17) | copy-start | bytes 3844
  10.3 1.4 %copy-start.7 = (f32[5]{0:T(128)S(1)}, f32[5]{0:T(128)}, u32[]{:S(2)}) copy-start(f32[5]{0:T(128)} %refs_2_.1) | copy-start | bytes 64
  11.6 20.6 %copy-start.1 = (f32[5,2,2,2,8,1024]{5,4,3,2,1,0:T(8,128)S(1)}, f32[5,2,2,2,8,1024]{5,4,3,2,1,0:T(8,128)}, u32[]{:S(2)}) copy-start(f32[5,2,2,2,8,1024]{5,4,3,2,1,0:T(8,128)} %param.15) | copy-start | bytes 3932164
  11.6 20.6 %copy-start.3 = (f32[2,2,2,8,1024]{4,3,2,1,0:T(8,128)S(1)}, f32[2,2,2,8,1024]{4,3,2,1,0:T(8,128)}, u32[]{:S(2)}) copy-start(f32[2,2,2,8,1024]{4,3,2,1,0:T(8,128)} %param.13) | copy-start | bytes 786436
  11.6 20.6 %copy-start.8 = (s32[64]{0:T(128)S(1)}, s32[64]{0:T(128)}, u32[]{:S(2)}) copy-start(s32[64]{0:T(128)} %refs_14_.1) | copy-start | bytes 772
  11.6 20.6 %copy-start.9 = (f32[4]{0:T(128)S(1)}, f32[4]{0:T(128)}, u32[]{:S(2)}) copy-start(f32[4]{0:T(128)} %refs_15_.1) | copy-start | bytes 52
  11.6 20.6 %copy-start.10 = (f32[2]{0:T(128)S(1)}, f32[2]{0:T(128)}, u32[]{:S(2)}) copy-start(f32[2]{0:T(128)} %refs_16_.1) | copy-start | bytes 28
  11.6 20.6 %copy-start.11 = (f32[2]{0:T(128)S(1)}, f32[2]{0:T(128)}, u32[]{:S(2)}) copy-start(f32[2]{0:T(128)} %refs_17_.1) | copy-start | bytes 28
  11.6 20.6 %copy-start.12 = (s32[2]{0:T(128)S(1)}, s32[2]{0:T(128)}, u32[]{:S(2)}) copy-start(s32[2]{0:T(128)} %refs_18_.1) | copy-start | bytes 28
  13.0 1.3 %collective-permute-start.2 = (f32[4,32,128]{2,1,0:T(8,128)S(1)}, f32[4,32,128]{2,1,0:T(8,128)S(1)}, u32[]{:S(2)}, u32[]{:S(2)}) collective-permute-start(f32[4,32,128]{2,1,0:T(8,128)S(1)} %get-tuple-element.27), channel_id=1, source_target_pairs={{0,1},{1,0},{2,3},{3,2},{4,5},{5,4},{6,7},{7,6},{8,9},{9,8},{10,11... | collective-permute-start | bytes 196616 | tf_op jit(solution)/shard_map/ppermute | solution.py:367
  14.3 4.7 %collective-permute-start.3 = (f32[2,32,128]{2,1,0:T(8,128)S(1)}, f32[2,32,128]{2,1,0:T(8,128)S(1)}, u32[]{:S(2)}, u32[]{:S(2)}) collective-permute-start(f32[2,32,128]{2,1,0:T(8,128)S(1)} %get-tuple-element.28), channel_id=1, source_target_pairs={{0,2},{1,3},{2,0},{3,1},{4,6},{5,7},{6,4},{7,5},{8,10},{9,11},{10,... | collective-permute-start | bytes 98312 | tf_op jit(solution)/shard_map/ppermute | solution.py:367
  16.4 5.4 %collective-permute-start.4 = (f32[2,32,128]{2,1,0:T(8,128)S(1)}, f32[2,32,128]{2,1,0:T(8,128)S(1)}, u32[]{:S(2)}, u32[]{:S(2)}) collective-permute-start(f32[2,32,128]{2,1,0:T(8,128)S(1)} %get-tuple-element.29), channel_id=1, source_target_pairs={{0,4},{1,5},{2,6},{3,7},{4,0},{5,1},{6,2},{7,3},{8,12},{9,13},{10,... | collective-permute-start | bytes 98312 | tf_op jit(solution)/shard_map/ppermute | solution.py:367
  19.0 5.7 %collective-permute-start.5 = (f32[2,32,128]{2,1,0:T(8,128)S(1)}, f32[2,32,128]{2,1,0:T(8,128)S(1)}, u32[]{:S(2)}, u32[]{:S(2)}) collective-permute-start(f32[2,32,128]{2,1,0:T(8,128)S(1)} %get-tuple-element.30), channel_id=1, source_target_pairs={{0,6},{1,7},{2,4},{3,5},{4,2},{5,3},{6,0},{7,1},{8,14},{9,15},{10,... | collective-permute-start | bytes 98312 | tf_op jit(solution)/shard_map/ppermute | solution.py:367
  24.9 1.3 %collective-permute-start.8 = (f32[4,32,128]{2,1,0:T(8,128)S(1)}, f32[4,32,128]{2,1,0:T(8,128)S(1)}, u32[]{:S(2)}, u32[]{:S(2)}) collective-permute-start(f32[4,32,128]{2,1,0:T(8,128)S(1)} %get-tuple-element.32), channel_id=1, source_target_pairs={{0,1},{1,0},{2,3},{3,2},{4,5},{5,4},{6,7},{7,6},{8,9},{9,8},{10,11... | collective-permute-start | bytes 196616 | tf_op jit(solution)/shard_map/ppermute | solution.py:367
  26.3 5.2 %collective-permute-start.10 = (f32[2,32,128]{2,1,0:T(8,128)S(1)}, f32[2,32,128]{2,1,0:T(8,128)S(1)}, u32[]{:S(2)}, u32[]{:S(2)}) collective-permute-start(f32[2,32,128]{2,1,0:T(8,128)S(1)} %get-tuple-element.34), channel_id=1, source_target_pairs={{0,4},{1,5},{2,6},{3,7},{4,0},{5,1},{6,2},{7,3},{8,12},{9,13},{10,... | collective-permute-start | bytes 98312 | tf_op jit(solution)/shard_map/ppermute | solution.py:367
  26.3 5.8 %collective-permute-start.11 = (f32[2,32,128]{2,1,0:T(8,128)S(1)}, f32[2,32,128]{2,1,0:T(8,128)S(1)}, u32[]{:S(2)}, u32[]{:S(2)}) collective-permute-start(f32[2,32,128]{2,1,0:T(8,128)S(1)} %get-tuple-element.35), channel_id=1, source_target_pairs={{0,6},{1,7},{2,4},{3,5},{4,2},{5,3},{6,0},{7,1},{8,14},{9,15},{10,... | collective-permute-start | bytes 98312 | tf_op jit(solution)/shard_map/ppermute | solution.py:367
  27.3 4.8 %collective-permute-start.9 = (f32[2,32,128]{2,1,0:T(8,128)S(1)}, f32[2,32,128]{2,1,0:T(8,128)S(1)}, u32[]{:S(2)}, u32[]{:S(2)}) collective-permute-start(f32[2,32,128]{2,1,0:T(8,128)S(1)} %get-tuple-element.33), channel_id=1, source_target_pairs={{0,2},{1,3},{2,0},{3,1},{4,6},{5,7},{6,4},{7,5},{8,10},{9,11},{10,... | collective-permute-start | bytes 98312 | tf_op jit(solution)/shard_map/ppermute | solution.py:367

commit v4 on v2

--- a/solution.py
+++ b/solution.py
@@ -82,8 +82,7 @@
 
 
 def smear_kernel(side, count, *refs):
-    blocks, (stencil_hi, stencil_lo, part, _) = refs[:count], refs[count : count + 4]
-    out = refs[count + 4 :]
+    blocks, (stencil_hi, stencil_lo, part), out = refs[:count], refs[count : count + 3], refs[count + 3 :]
     _, group_len, slice_len = blocks[0].shape
     at = slice(side * group_len, (side + 1) * group_len)
     stencil = (stencil_hi[:, at], stencil_lo[:, at])
@@ -104,7 +103,7 @@
         first += block.shape[0]
 
 
-def smear(side, blocks, stencil_hi, stencil_lo, part, after, parts):
+def smear(side, blocks, stencil_hi, stencil_lo, part, parts):
     comps, group_len, slice_len = part.shape
     if side == NEAR:
         out_shape = [jax.ShapeDtypeStruct(part.shape, jnp.float32)]
@@ -114,14 +113,14 @@
     return pl.pallas_call(
         lambda *refs: smear_kernel(side, len(blocks), *refs),
         out_shape=out_shape,
-        in_specs=[VMEM] * (len(blocks) + 4),
+        in_specs=[VMEM] * (len(blocks) + 3),
         out_specs=[VMEM] * len(out_shape),
         compiler_params=PARAMS,
         cost_estimate=pl.CostEstimate(
             flops=6 * part.size * group_len, bytes_accessed=12 * part.size, transcendentals=0
         ),
         name="smear",
-    )(*blocks, stencil_hi, stencil_lo, part, after)
+    )(*blocks, stencil_hi, stencil_lo, part)
 
 
 def join_kernel(own, swapped, *out):
@@ -158,19 +157,29 @@
 
 
 def spread(values, shape):
-    row = lax.broadcasted_iota(jnp.int32, shape, 0)
     lane = lax.broadcasted_iota(jnp.int32, shape, 1)
-    tile = jnp.zeros(shape, jnp.float32)
+    row = jnp.zeros(shape, jnp.float32)
     for spot, value in values:
-        tile = jnp.where((row == spot % 8) & (lane == spot // 8), value, tile)
-    return tile
+        row = jnp.where(lane == spot, value, row)
+    return row
 
 
 def total(acc):
     return jnp.sum(jnp.sum(acc, axis=0, keepdims=True), axis=1, keepdims=True)
 
 
-def history_kernel(past_inputs, past_residuals, slots, aged, tile):
+def history_kernel(
+    total_rows, past_inputs, past_residuals, slots, classes, acoustic, optical, number, aged, line, gains,
+):
+    first = lax.axis_index("energy") * total_rows
+    row = lax.broadcasted_iota(jnp.int32, (8, LANES), 0) % total_rows
+    coupling = jnp.zeros((8, LANES), jnp.float32)
+    for i in range(total_rows):
+        coupling = jnp.where(row == i, acoustic[classes[first + i]], coupling)
+    gains[0] = coupling
+    for m in range(2):
+        gains[2 * m + 1] = jnp.full((8, LANES), optical[m] * (number[m] + 1.0))
+        gains[2 * m + 2] = jnp.full((8, LANES), optical[m] * number[m])
     _, rows, width = past_inputs.shape
     acc = [jnp.zeros((8, LANES), jnp.float32) for _ in PAIRS]
     for top in range(0, rows, 8):
@@ -185,44 +194,40 @@
                 old.append(res)
             return [a + old[i - 1] * old[j - 1] for a, (i, j) in zip(acc, PAIRS)]
         acc = lax.fori_loop(0, width // LANES, column, acc, unroll=4)
-    tile[...] = spread([(v, total(a)) for v, a in enumerate(acc)], tile.shape)
-
-
-def history(past_inputs, past_residuals, slots):
+    line[...] = spread([(v, total(a)) for v, a in enumerate(acc)], line.shape)
+
+
+def history(past_inputs, past_residuals, scalars, rows):
     size = past_inputs.size
     return pl.pallas_call(
-        history_kernel,
+        lambda *refs: history_kernel(rows, *refs),
         out_shape=(
             jax.ShapeDtypeStruct(past_inputs.shape, jnp.float32),
-            jax.ShapeDtypeStruct((8, LANES), jnp.float32),
+            jax.ShapeDtypeStruct((1, LANES), jnp.float32),
+            jax.ShapeDtypeStruct((5, 8, LANES), jnp.float32),
         ),
-        in_specs=[VMEM, VMEM, SMEM],
-        out_specs=(VMEM, VMEM),
+        in_specs=[VMEM, VMEM] + [SMEM] * 5,
+        out_specs=(VMEM,) * 3,
         compiler_params=PARAMS,
         cost_estimate=pl.CostEstimate(flops=8 * size, bytes_accessed=12 * size, transcendentals=0),
         name="history",
-    )(past_inputs, past_residuals, slots)
-
-
-def residual_kernel(rows, count, own, swapped, *refs):
+    )(past_inputs, past_residuals, *scalars)
+
+
+def residual_kernel(count, own, swapped, *refs):
     received = refs[:count]
-    (current, past_residuals, old_tile, slots, classes, acoustic, optical, number, shift,
-     fresh, tile, smeared) = refs[count:]
+    current, past_residuals, old_line, gains, slots, shift, fresh, lines, smeared = refs[count:]
     parts, height, slice_len = smeared.shape
     place = lax.axis_index("energy")
     smeared[place], smeared[place ^ 1] = own[0], swapped[0]
     for chip, block in enumerate(received, 1):
         smeared[place ^ (2 * chip)], smeared[place ^ (2 * chip + 1)] = block[0], block[1]
-    first = place * rows
-    row = lax.broadcasted_iota(jnp.int32, (8, slice_len), 0) % rows
     lane = lax.broadcasted_iota(jnp.int32, (8, slice_len), 1)
-    coupling = jnp.zeros((8, slice_len), jnp.float32)
-    for i in range(rows):
-        coupling = jnp.where(row == i, acoustic[classes[first + i]], coupling)
-    modes = []
-    for m in range(2):
-        s = shift[m]
-        modes.append((s, lane < slice_len - s, lane >= s, optical[m] * (number[m] + 1.0), optical[m] * number[m]))
+    coupling = gains[0]
+    modes = [
+        (shift[m], lane < slice_len - shift[m], lane >= shift[m], gains[2 * m + 1], gains[2 * m + 2])
+        for m in range(2)
+    ]
     zero = jnp.zeros((8, slice_len), jnp.float32)
     acc = [zero] * (HIST + 1)
     for top in range(0, height, 8):
@@ -247,23 +252,25 @@
                 acc[j + 1] = acc[j + 1] + new * past_residuals[(slots[j],) + where]
     mine = jnp.concatenate([jnp.sum(a, axis=0, keepdims=True) for a in acc] + [zero[: 8 - HIST - 1]], axis=0)
     mine = jnp.sum(mine, axis=1, keepdims=True)
-    lane = lax.broadcasted_iota(jnp.int32, old_tile.shape, 1)
-    tile[...] = jnp.broadcast_to(jnp.where(lane == 2, mine, old_tile[...])[None], tile.shape)
-
-
-def residual(kept, swapped, smeared, current, past_residuals, old_tile, slots, classes, acoustic, optical, number, shift, rows, copies):
-    return pl.pallas_call(
-        lambda *refs: residual_kernel(rows, len(smeared), *refs),
+    spot = lax.broadcasted_iota(jnp.int32, (8, LANES), 0) + SPOTS[(0, 0)]
+    mine = jnp.where(lax.broadcasted_iota(jnp.int32, (8, LANES), 1) == spot, mine, 0.0)
+    mine = old_line[...] + jnp.sum(mine, axis=0, keepdims=True)
+    lines[...] = jnp.broadcast_to(mine[None], lines.shape)
+
+
+def residual(kept, swapped, smeared, current, past_residuals, old_line, gains, slots, shift, copies):
+    return pl.pallas_call(
+        lambda *refs: residual_kernel(len(smeared), *refs),
         out_shape=(
             jax.ShapeDtypeStruct(current.shape, jnp.float32),
-            jax.ShapeDtypeStruct((copies, 8, LANES), jnp.float32),
+            jax.ShapeDtypeStruct((copies, 1, LANES), jnp.float32),
         ),
-        in_specs=[VMEM] * (len(smeared) + 5) + [SMEM] * 6,
+        in_specs=[VMEM] * (len(smeared) + 6) + [SMEM] * 2,
         out_specs=(VMEM, VMEM),
         scratch_shapes=[pltpu.VMEM((2 * kept.shape[0],) + kept.shape[1:], jnp.float32)],
         compiler_params=PARAMS,
         name="residual",
-    )(kept, swapped, *smeared, current, past_residuals, old_tile, slots, classes, acoustic, optical, number, shift)
+    )(kept, swapped, *smeared, current, past_residuals, old_line, gains, slots, shift)
 
 
 def solve(products):
@@ -301,10 +308,13 @@
     return weights
 
 
-def mix_kernel(entries, tiles, fresh, current, aged, out, wide):
-    summed = jnp.sum(tiles[...], axis=0) / entries
-    for lane in range(wide.shape[0]):
-        wide[lane] = jnp.broadcast_to(summed[:, lane : lane + 1], (8, LANES))
+def mix_kernel(entries, lines, fresh, current, aged, out, wide):
+    summed = jnp.sum(lines[...], axis=0) / entries
+    row = lax.broadcasted_iota(jnp.int32, (8, LANES), 0)
+    lane = lax.broadcasted_iota(jnp.int32, (8, LANES), 1)
+    for part in range(wide.shape[0]):
+        own = jnp.where(lane == row + 8 * part, summed, 0.0)
+        wide[part] = jnp.broadcast_to(jnp.sum(own, axis=1, keepdims=True), (8, LANES))
     products = {
         pair: jnp.broadcast_to(wide[spot // 8, spot % 8 : spot % 8 + 1, :], (8, LANES))
         for pair, spot in SPOTS.items()
@@ -320,7 +330,7 @@
             out[at] = mixed
 
 
-def mix(tiles, fresh, current, aged, entries):
+def mix(lines, fresh, current, aged, entries):
     return pl.pallas_call(
         lambda *refs: mix_kernel(entries, *refs),
         out_shape=jax.ShapeDtypeStruct(fresh.shape, jnp.float32),
@@ -329,7 +339,7 @@
         scratch_shapes=[pltpu.VMEM((3, 8, LANES), jnp.float32)],
         compiler_params=PARAMS,
         name="mix",
-    )(tiles, fresh, current, aged)
+    )(lines, fresh, current, aged)
 
 
 def per_device(
@@ -358,19 +368,19 @@
     old_res = past_residuals.reshape(HIST, height, width)
     sides = exchange(own, groups)
     stencil_hi, stencil_lo, smeared = prepare(own, neighbour, stencil_weight, groups * group_len)
-    aged, old_tile = history(old_in, old_res, slot_order)
-    (smeared,) = smear(NEAR, sides[NEAR], stencil_hi, stencil_lo, smeared, old_tile, parts)
-    kept, given = smear(FAR, sides[FAR], stencil_hi, stencil_lo, smeared, old_tile, parts)
+    scalars = (slot_order, momentum_class, acoustic_coupling, optical_coupling, occupation)
+    aged, old_line, gains = history(old_in, old_res, scalars, rows)
+    (smeared,) = smear(NEAR, sides[NEAR], stencil_hi, stencil_lo, smeared, parts)
+    kept, given = smear(FAR, sides[FAR], stencil_hi, stencil_lo, smeared, parts)
     meet = lambda block, m: lax.ppermute(block, "energy", [(e, e ^ m) for e in range(parts)])
     swapped = meet(given, 1)
     smeared = [meet(block, 2 * chip) for chip, block in enumerate(join(kept, swapped), 1)]
-    fresh, tile = residual(
-        kept, swapped, smeared, flat, old_res, old_tile, slot_order, momentum_class, acoustic_coupling,
-        optical_coupling, occupation, phonon_shift, rows, groups * parts,
+    fresh, lines = residual(
+        kept, swapped, smeared, flat, old_res, old_line, gains, slot_order, phonon_shift, groups * parts
     )
-    tiles = lax.all_to_all(tile, ("kgrp", "energy"), split_axis=0, concat_axis=0, tiled=True)
+    lines = lax.all_to_all(lines, ("kgrp", "energy"), split_axis=0, concat_axis=0, tiled=True)
     entries = float(flat.size * groups * parts)
-    return mix(tiles, fresh, flat, aged, entries).reshape(current.shape)
+    return mix(lines, fresh, flat, aged, entries).reshape(current.shape)
 
 
 def solution(mesh):

time: 42.2 us -> 40.7 us (0.964)
  waiting for transfers between devices: 8.63 us -> 7.45 us
  blocking collectives: 11.3 us -> 10.5 us
    ppermute x4, waiting for transfers between devices: 7.28 us -> 4.8 us  [per_device(): lax.ppermute(block, 'energy', [(e, e ^ m) for e in range(parts)])]
    ppermute x4, waiting for transfers between devices: 1.35 us -> 2.64 us  [exchange(): lax.ppermute(block, 'kgrp', [(i, i ^ flip) for i in range(groups)])]
    all_to_all x1, blocking collectives: 11.3 us -> 10.5 us  [per_device(): lax.all_to_all(lines, ('kgrp', 'energy'), split_axis=0, concat_axis=0, ti...]
    unnamed x26 -> x24, local copies, waits for them, and re-layouts: 3.34 us -> 3.63 us
  transfers between devices with their start and end apart: 8 -> 8, of which waited for: 4 -> 6; matrix products, arithmetic and copies ran while one was open for 0% -> 0% of each run, Pallas kernels for 6% -> 6%
where the time goes in v4:
time: 40.7 us; the launch traced here: 40.4 us
  starting transfers between devices  12.6 us (31%)
  blocking collectives  10.5 us (26%)
  waiting for transfers between devices  7.45 us (18%)
  Pallas kernels  4.98 us (12%)
  local copies, waits for them, and re-layouts  4.72 us (12%)
    all_to_all x1, blocking collectives, per_device(): lax.all_to_all(lines, ('kgrp', 'energy'), split_axis=0, concat_axis=0, ti...  10.5 us
    ppermute x4, starting transfers between devices, exchange(): lax.ppermute(block, 'kgrp', [(i, i ^ flip) for i in range(groups)])  8.07 us
    ppermute x4, waiting for transfers between devices, per_device(): lax.ppermute(block, 'energy', [(e, e ^ m) for e in range(parts)])  4.8 us
    ppermute x4, starting transfers between devices, per_device(): lax.ppermute(block, 'energy', [(e, e ^ m) for e in range(parts)])  4.55 us
    unnamed x24, local copies, waits for them, and re-layouts  3.63 us
    ppermute x4, waiting for transfers between devices, exchange(): lax.ppermute(block, 'kgrp', [(i, i ^ flip) for i in range(groups)])  2.64 us
    pallas_call x1, Pallas kernels, history(): pl.pallas_call(lambda *refs: history_kernel(rows, *refs), out_shape=(jax....  1.31 us
    slice x1, local copies, waits for them, and re-layouts, exchange(): return (near, [across(near[0], 2), across(own[half:], 3)])  1.09 us
  transfers between devices with their start and end apart: 8, of which 6 were waited for; matrix products, arithmetic and copies ran while one was open for 0% of the time, Pallas kernels for 6%

profile of v4, /device:TPU:0, one launch (start us, length us, event | category | flops | bytes accessed | tf_op | source)
XLA Modules:
  0.0 40.4 jit_solution(8253295707310684049)
XLA Ops:
  0.0 0.0 copy-start
  0.0 1.1 %fusion = (f32[1,2,2,64,128]{4,3,2,1,0:T(8,128)S(1)}, f32[1,2,2,64,128]{4,3,2,1,0:T(8,128)S(1)}) fusion(f32[2,2,2,64,128]{4,3,2,1,0:T(8,128)} %param.12), kind=kLoop, calls=%fused_computation | loop fusion | bytes 524288 | tf_op jit(solution)/shard_map/slice | solution.py:156
  1.1 3.0 %collective-permute-start = (f32[4,64,128]{2,1,0:T(8,128)S(1)}, f32[4,64,128]{2,1,0:T(8,128)S(1)}, u32[]{:S(2)}, u32[]{:S(2)}) collective-permute-start(f32[4,64,128]{2,1,0:T(8,128)S(1)} %bitcast.17), channel_id=1, source_target_pairs={{0,8},{8,0},{16,24},{24,16},{1,9},{9,1},{17,25},{25,17},{2,10},{10... | collective-permute-start | bytes 393224 | tf_op jit(solution)/shard_map/ppermute | solution.py:153
  4.1 0.1 collective-permute-start.3
  4.2 2.9 %collective-permute-start.2 = (f32[4,64,128]{2,1,0:T(8,128)S(1)}, f32[4,64,128]{2,1,0:T(8,128)S(1)}, u32[]{:S(2)}, u32[]{:S(2)}) collective-permute-start(f32[4,64,128]{2,1,0:T(8,128)S(1)} %bitcast.16), channel_id=1, source_target_pairs={{0,24},{8,16},{16,8},{24,0},{1,25},{9,17},{17,9},{25,1},{2,26},{10... | collective-permute-start | bytes 393224 | tf_op jit(solution)/shard_map/ppermute | solution.py:153
  7.1 1.3 %collective-permute-done.refs_0_ = f32[4,64,128]{2,1,0:T(8,128)S(1)} collective-permute-done((f32[4,64,128]{2,1,0:T(8,128)S(1)}, f32[4,64,128]{2,1,0:T(8,128)S(1)}, u32[]{:S(2)}, u32[]{:S(2)}) %collective-permute-start) | collective-permute-done | bytes 131104 | tf_op jit(solution)/shard_map/ppermute | solution.py:153
  8.4 2.1 %collective-permute-start.1 = (f32[4,64,128]{2,1,0:T(8,128)S(1)}, f32[4,64,128]{2,1,0:T(8,128)S(1)}, u32[]{:S(2)}, u32[]{:S(2)}) collective-permute-start(f32[4,64,128]{2,1,0:T(8,128)S(1)} %collective-permute-done.refs_0_), channel_id=1, source_target_pairs={{0,16},{8,24},{16,0},{24,8},{1,17},{9,25},{17,1},{25,9},{2,18},{10... | collective-permute-start | bytes 393224 | tf_op jit(solution)/shard_map/ppermute | solution.py:153
  10.5 0.0 copy-start.2
  10.5 0.9 %copy-done.2 = f32[2,2,2,64,128]{4,3,2,1,0:T(8,128)S(1)} copy-done((f32[2,2,2,64,128]{4,3,2,1,0:T(8,128)S(1)}, f32[2,2,2,64,128]{4,3,2,1,0:T(8,128)}, u32[]{:S(2)}) %copy-start.2) | copy-done | bytes 262168
  11.5 0.0 copy-start.4
  11.5 0.7 %copy-done.4 = s32[64,5]{0,1:T(8,128)S(1)} copy-done((s32[64,5]{0,1:T(8,128)S(1)}, s32[64,5]{0,1:T(8,128)}, u32[]{:S(2)}) %copy-start.4) | copy-done | bytes 1304
  12.2 0.0 copy-start.6
  12.2 0.7 %copy-done.6 = f32[5]{0:T(128)S(1)} copy-done((f32[5]{0:T(128)S(1)}, f32[5]{0:T(128)}, u32[]{:S(2)}) %copy-start.6) | copy-done | bytes 44
  12.8 0.0 copy-start.5
  12.8 0.0 copy-start.7
  12.8 0.0 copy-start.8
  12.8 0.0 copy-start.9
  12.8 0.0 copy-start.10
  12.8 1.1 %prepare.1 = (bf16[64,128]{1,0:T(8,128)(2,1)S(1)}, bf16[64,128]{1,0:T(8,128)(2,1)S(1)}, f32[8,64,128]{2,1,0:T(8,128)S(1)}) custom-call(f32[8,64,128]{2,1,0:T(8,128)S(1)} %bitcast.11, s32[5,64]{1,0:T(8,128)S(1)} %bitcast.14, f32[5]{0:T(128)S(1)} %copy-done.6), custom_call_target="tpu_custom_call" | custom-call | flops 25165824 | bytes 524288 | tf_op jit(solution)/shard_map/prepare/pallas_call | solution.py:71
  13.9 0.0 collective-permute-done.3.refs_1_
  13.9 0.3 smear.2.refs_4_
  14.2 0.4 collective-permute-done.2.refs_1_
  14.5 0.9 %collective-permute-done.1.refs_0_ = f32[4,64,128]{2,1,0:T(8,128)S(1)} collective-permute-done((f32[4,64,128]{2,1,0:T(8,128)S(1)}, f32[4,64,128]{2,1,0:T(8,128)S(1)}, u32[]{:S(2)}, u32[]{:S(2)}) %collective-permute-start.1) | collective-permute-done | bytes 131104 | tf_op jit(solution)/shard_map/ppermute | solution.py:153
  15.5 0.3 smear.3
  15.8 0.1 collective-permute-start.4
  15.9 1.3 %collective-permute-done.4.swapped.refs_1_ = f32[4,64,128]{2,1,0:T(8,128)S(1)} collective-permute-done((f32[4,64,128]{2,1,0:T(8,128)S(1)}, f32[4,64,128]{2,1,0:T(8,128)S(1)}, u32[]{:S(2)}, u32[]{:S(2)}) %collective-permute-start.4) | collective-permute-done | bytes 131104 | tf_op jit(solution)/shard_map/ppermute | solution.py:375
  17.2 1.9 %collective-permute-start.5 = (f32[2,64,128]{2,1,0:T(8,128)S(1)}, f32[2,64,128]{2,1,0:T(8,128)S(1)}, u32[]{:S(2)}, u32[]{:S(2)}) collective-permute-start(f32[2,64,128]{2,1,0:T(8,128)S(1)} %get-tuple-element.23), channel_id=1, source_target_pairs={{0,2},{1,3},{2,0},{3,1},{4,6},{5,7},{6,4},{7,5},{8,10},{9,11},{10,... | collective-permute-start | bytes 196616 | tf_op jit(solution)/shard_map/ppermute | solution.py:375
  19.1 2.6 %collective-permute-start.6 = (f32[2,64,128]{2,1,0:T(8,128)S(1)}, f32[2,64,128]{2,1,0:T(8,128)S(1)}, u32[]{:S(2)}, u32[]{:S(2)}) collective-permute-start(f32[2,64,128]{2,1,0:T(8,128)S(1)} %get-tuple-element.24), channel_id=1, source_target_pairs={{0,4},{1,5},{2,6},{3,7},{4,0},{5,1},{6,2},{7,3},{8,12},{9,13},{10,... | collective-permute-start | bytes 196616 | tf_op jit(solution)/shard_map/ppermute | solution.py:375
  21.7 0.0 collective-permute-start.7
  21.7 0.0 copy-done
  21.7 0.0 copy-done.5
  21.7 0.0 copy-done.7
  21.7 0.0 copy-done.8
  21.7 0.0 copy-done.9
  21.7 0.0 copy-done.10
  21.7 0.0 copy-start.1
  21.7 1.3 %copy-done.1 = f32[5,2,2,2,8,1024]{5,4,3,2,1,0:T(8,128)S(1)} copy-done((f32[5,2,2,2,8,1024]{5,4,3,2,1,0:T(8,128)S(1)}, f32[5,2,2,2,8,1024]{5,4,3,2,1,0:T(8,128)}, u32[]{:S(2)}) %copy-start.1) | copy-done | bytes 1310744
  23.1 0.0 copy-start.3
  23.1 0.0 copy-start.11
  23.1 1.3 %history.1 = (f32[5,64,1024]{2,1,0:T(8,128)S(1)}, f32[1,128]{1,0:T(1,128)S(1)}, f32[5,8,128]{2,1,0:T(8,128)S(1)}) custom-call(f32[5,64,1024]{2,1,0:T(8,128)S(1)} %bitcast.10, f32[5,64,1024]{2,1,0:T(8,128)S(1)} %bitcast.8, s32[5]{0:T(128)S(1)} %copy-done.5, s32[64]{0:T(128)S(1)} %copy-done.7, f32[4]{0:T(128)S(1)} %copy-done.8, f32[2]{0:T(128)S(1)} %copy-done.9, ...), custom_call_target="tpu_custom_call" | custom-call | flops 2621440 | bytes 3932160 | tf_op jit(solution)/shard_map/history/pallas_call | solution.py:202
  24.4 0.0 collective-permute-done.5.refs_2_
  24.4 2.3 %collective-permute-done.6.refs_3_ = f32[2,64,128]{2,1,0:T(8,128)S(1)} collective-permute-done((f32[2,64,128]{2,1,0:T(8,128)S(1)}, f32[2,64,128]{2,1,0:T(8,128)S(1)}, u32[]{:S(2)}, u32[]{:S(2)}) %collective-permute-start.6) | collective-permute-done | bytes 65568 | tf_op jit(solution)/shard_map/ppermute | solution.py:375
  26.6 1.2 %collective-permute-done.7.refs_4_ = f32[2,64,128]{2,1,0:T(8,128)S(1)} collective-permute-done((f32[2,64,128]{2,1,0:T(8,128)S(1)}, f32[2,64,128]{2,1,0:T(8,128)S(1)}, u32[]{:S(2)}, u32[]{:S(2)}) %collective-permute-start.7) | collective-permute-done | bytes 65568 | tf_op jit(solution)/shard_map/ppermute | solution.py:375
  27.9 0.0 copy-done.3
  27.9 0.0 copy-done.11
  27.9 1.0 %residual.1 = (f32[64,1024]{1,0:T(8,128)S(1)}, f32[32,1,128]{2,1,0:T(1,128)S(1)}) custom-call(f32[4,64,128]{2,1,0:T(8,128)S(1)} %get-tuple-element.21.own.refs_0_, f32[4,64,128]{2,1,0:T(8,128)S(1)} %collective-permute-done.4.swapped.refs_1_, f32[2,64,128]{2,1,0:T(8,128)S(1)} %collective-permute-done.5.refs_2_, ...), custom_call_target="tpu_custom_call" | custom-call | tf_op jit(solution)/shard_map/residual/pallas_call | solution.py:262
  28.9 10.5 %all_to_all.5.refs_0_ = f32[32,1,128]{2,1,0:T(1,128)S(1)} all-to-all(f32[32,1,128]{2,1,0:T(1,128)S(1)} %get-tuple-element.28), channel_id=1, replica_groups=mesh['kgrp'=4,'energy'=8] {'kgrp','energy'}, dimensions={0} | all-to-all | bytes 32768 | tf_op jit(solution)/shard_map/all_to_all | solution.py:381
  39.4 1.0 %mix.1 = f32[64,1024]{1,0:T(8,128)} custom-call(f32[32,1,128]{2,1,0:T(1,128)S(1)} %all_to_all.5.refs_0_, f32[64,1024]{1,0:T(8,128)S(1)} %get-tuple-element.29.refs_1_, f32[64,1024]{1,0:T(8,128)S(1)} %bitcast.13, f32[5,64,1024]{2,1,0:T(8,128)S(1)} %get-tuple-element.30.refs_3_), custom_call_target="tpu_custom_call" | custom-call | tf_op jit(solution)/shard_map/mix/pallas_call | solution.py:334
  (1 shorter events, 0.0 us)
Async XLA Ops:
  0.0 21.7 %copy-start = (f32[5,2,2,2,8,1024]{5,4,3,2,1,0:T(8,128)S(1)}, f32[5,2,2,2,8,1024]{5,4,3,2,1,0:T(8,128)}, u32[]{:S(2)}) copy-start(f32[5,2,2,2,8,1024]{5,4,3,2,1,0:T(8,128)} %param.15) | copy-start | bytes 3932164
  1.1 7.3 %collective-permute-start = (f32[4,64,128]{2,1,0:T(8,128)S(1)}, f32[4,64,128]{2,1,0:T(8,128)S(1)}, u32[]{:S(2)}, u32[]{:S(2)}) collective-permute-start(f32[4,64,128]{2,1,0:T(8,128)S(1)} %bitcast.17), channel_id=1, source_target_pairs={{0,8},{8,0},{16,24},{24,16},{1,9},{9,1},{17,25},{25,17},{2,10},{10... | collective-permute-start | bytes 393224 | tf_op jit(solution)/shard_map/ppermute | solution.py:153
  4.1 9.8 %collective-permute-start.3 = (f32[4,64,128]{2,1,0:T(8,128)S(1)}, f32[4,64,128]{2,1,0:T(8,128)S(1)}, u32[]{:S(2)}, u32[]{:S(2)}) collective-permute-start(f32[4,64,128]{2,1,0:T(8,128)S(1)} %bitcast.15), channel_id=1, source_target_pairs={{0,8},{8,0},{16,24},{24,16},{1,9},{9,1},{17,25},{25,17},{2,10},{10... | collective-permute-start | bytes 393224 | tf_op jit(solution)/shard_map/ppermute | solution.py:153
  4.2 10.3 %collective-permute-start.2 = (f32[4,64,128]{2,1,0:T(8,128)S(1)}, f32[4,64,128]{2,1,0:T(8,128)S(1)}, u32[]{:S(2)}, u32[]{:S(2)}) collective-permute-start(f32[4,64,128]{2,1,0:T(8,128)S(1)} %bitcast.16), channel_id=1, source_target_pairs={{0,24},{8,16},{16,8},{24,0},{1,25},{9,17},{17,9},{25,1},{2,26},{10... | collective-permute-start | bytes 393224 | tf_op jit(solution)/shard_map/ppermute | solution.py:153
  8.4 7.0 %collective-permute-start.1 = (f32[4,64,128]{2,1,0:T(8,128)S(1)}, f32[4,64,128]{2,1,0:T(8,128)S(1)}, u32[]{:S(2)}, u32[]{:S(2)}) collective-permute-start(f32[4,64,128]{2,1,0:T(8,128)S(1)} %collective-permute-done.refs_0_), channel_id=1, source_target_pairs={{0,16},{8,24},{16,0},{24,8},{1,17},{9,25},{17,1},{25,9},{2,18},{10... | collective-permute-start | bytes 393224 | tf_op jit(solution)/shard_map/ppermute | solution.py:153
  10.5 0.9 %copy-start.2 = (f32[2,2,2,64,128]{4,3,2,1,0:T(8,128)S(1)}, f32[2,2,2,64,128]{4,3,2,1,0:T(8,128)}, u32[]{:S(2)}) copy-start(f32[2,2,2,64,128]{4,3,2,1,0:T(8,128)} %param.12) | copy-start | bytes 786436
  11.5 0.7 %copy-start.4 = (s32[64,5]{0,1:T(8,128)S(1)}, s32[64,5]{0,1:T(8,128)}, u32[]{:S(2)}) copy-start(s32[64,5]{0,1:T(8,128)} %param.17) | copy-start | bytes 3844
  12.2 0.7 %copy-start.6 = (f32[5]{0:T(128)S(1)}, f32[5]{0:T(128)}, u32[]{:S(2)}) copy-start(f32[5]{0:T(128)} %refs_2_.2) | copy-start | bytes 64
  12.8 8.9 %copy-start.5 = (s32[5]{0:T(128)S(1)}, s32[5]{0:T(128)}, u32[]{:S(2)}) copy-start(s32[5]{0:T(128)} %refs_9_.1) | copy-start | bytes 64
  12.8 8.9 %copy-start.7 = (s32[64]{0:T(128)S(1)}, s32[64]{0:T(128)}, u32[]{:S(2)}) copy-start(s32[64]{0:T(128)} %refs_3_.1) | copy-start | bytes 772
  12.8 8.9 %copy-start.8 = (f32[4]{0:T(128)S(1)}, f32[4]{0:T(128)}, u32[]{:S(2)}) copy-start(f32[4]{0:T(128)} %refs_4_.1) | copy-start | bytes 52
  12.8 8.9 %copy-start.9 = (f32[2]{0:T(128)S(1)}, f32[2]{0:T(128)}, u32[]{:S(2)}) copy-start(f32[2]{0:T(128)} %refs_5_.1) | copy-start | bytes 28
  12.8 8.9 %copy-start.10 = (f32[2]{0:T(128)S(1)}, f32[2]{0:T(128)}, u32[]{:S(2)}) copy-start(f32[2]{0:T(128)} %refs_6_.1) | copy-start | bytes 28
  15.8 1.4 %collective-permute-start.4 = (f32[4,64,128]{2,1,0:T(8,128)S(1)}, f32[4,64,128]{2,1,0:T(8,128)S(1)}, u32[]{:S(2)}, u32[]{:S(2)}) collective-permute-start(f32[4,64,128]{2,1,0:T(8,128)S(1)} %get-tuple-element.22), channel_id=1, source_target_pairs={{0,1},{1,0},{2,3},{3,2},{4,5},{5,4},{6,7},{7,6},{8,9},{9,8},{10,11... | collective-permute-start | bytes 393224 | tf_op jit(solution)/shard_map/ppermute | solution.py:375
  17.2 7.2 %collective-permute-start.5 = (f32[2,64,128]{2,1,0:T(8,128)S(1)}, f32[2,64,128]{2,1,0:T(8,128)S(1)}, u32[]{:S(2)}, u32[]{:S(2)}) collective-permute-start(f32[2,64,128]{2,1,0:T(8,128)S(1)} %get-tuple-element.23), channel_id=1, source_target_pairs={{0,2},{1,3},{2,0},{3,1},{4,6},{5,7},{6,4},{7,5},{8,10},{9,11},{10,... | collective-permute-start | bytes 196616 | tf_op jit(solution)/shard_map/ppermute | solution.py:375
  19.1 7.5 %collective-permute-start.6 = (f32[2,64,128]{2,1,0:T(8,128)S(1)}, f32[2,64,128]{2,1,0:T(8,128)S(1)}, u32[]{:S(2)}, u32[]{:S(2)}) collective-permute-start(f32[2,64,128]{2,1,0:T(8,128)S(1)} %get-tuple-element.24), channel_id=1, source_target_pairs={{0,4},{1,5},{2,6},{3,7},{4,0},{5,1},{6,2},{7,3},{8,12},{9,13},{10,... | collective-permute-start | bytes 196616 | tf_op jit(solution)/shard_map/ppermute | solution.py:375
  21.7 6.2 %collective-permute-start.7 = (f32[2,64,128]{2,1,0:T(8,128)S(1)}, f32[2,64,128]{2,1,0:T(8,128)S(1)}, u32[]{:S(2)}, u32[]{:S(2)}) collective-permute-start(f32[2,64,128]{2,1,0:T(8,128)S(1)} %get-tuple-element.25), channel_id=1, source_target_pairs={{0,6},{1,7},{2,4},{3,5},{4,2},{5,3},{6,0},{7,1},{8,14},{9,15},{10,... | collective-permute-start | bytes 196616 | tf_op jit(solution)/shard_map/ppermute | solution.py:375
  21.7 1.3 %copy-start.1 = (f32[5,2,2,2,8,1024]{5,4,3,2,1,0:T(8,128)S(1)}, f32[5,2,2,2,8,1024]{5,4,3,2,1,0:T(8,128)}, u32[]{:S(2)}) copy-start(f32[5,2,2,2,8,1024]{5,4,3,2,1,0:T(8,128)} %param.14) | copy-start | bytes 3932164
  23.1 4.8 %copy-start.3 = (f32[2,2,2,8,1024]{4,3,2,1,0:T(8,128)S(1)}, f32[2,2,2,8,1024]{4,3,2,1,0:T(8,128)}, u32[]{:S(2)}) copy-start(f32[2,2,2,8,1024]{4,3,2,1,0:T(8,128)} %param.13) | copy-start | bytes 786436
  23.1 4.8 %copy-start.11 = (s32[2]{0:T(128)S(1)}, s32[2]{0:T(128)}, u32[]{:S(2)}) copy-start(s32[2]{0:T(128)} %refs_10_.1) | copy-start | bytes 28

commit v5 on v4

--- a/solution.py
+++ b/solution.py
@@ -81,46 +81,71 @@
     )(own, jnp.transpose(neighbour), weight)
 
 
-def smear_kernel(side, count, *refs):
-    blocks, (stencil_hi, stencil_lo, part), out = refs[:count], refs[count : count + 3], refs[count + 3 :]
-    _, group_len, slice_len = blocks[0].shape
+def smeared_pairs(side, first, block, stencil_hi, stencil_lo, part):
+    comps, group_len, slice_len = block.shape
     at = slice(side * group_len, (side + 1) * group_len)
     stencil = (stencil_hi[:, at], stencil_lo[:, at])
-    first = 0
+    for c in range(0, comps, 2):
+        result = product(stencil, split(jnp.concatenate([block[c], block[c + 1]], axis=1)))
+        for p in range(2):
+            yield c + p, part[first + c + p] + result[:, p * slice_len : (p + 1) * slice_len]
+
+
+def add_side_kernel(side, first, *refs):
+    *blocks, stencil_hi, stencil_lo, part, out = refs
+    done = 0
     for block in blocks:
-        for c in range(0, block.shape[0], 2):
-            result = product(stencil, split(jnp.concatenate([block[c], block[c + 1]], axis=1)))
-            for p in range(2):
-                at = first + c + p
-                smeared = part[at] + result[:, p * slice_len : (p + 1) * slice_len]
-                if side == NEAR:
-                    out[0][at] = smeared
-                    continue
-                chips, height, _ = out[0].shape
-                rows = height // part.shape[0]
-                for m in range(2 * chips):
-                    out[m % 2][m // 2, at * rows : (at + 1) * rows, :] = smeared[m * rows : (m + 1) * rows]
-        first += block.shape[0]
-
-
-def smear(side, blocks, stencil_hi, stencil_lo, part, parts):
+        for c, smeared in smeared_pairs(side, first + done, block, stencil_hi, stencil_lo, part):
+            out[done + c] = smeared
+        done += block.shape[0]
+
+
+def add_side(side, first, blocks, stencil_hi, stencil_lo, part):
+    shape = (sum(block.shape[0] for block in blocks),) + part.shape[1:]
+    return pl.pallas_call(
+        lambda *refs: add_side_kernel(side, first, *refs),
+        out_shape=jax.ShapeDtypeStruct(shape, jnp.float32),
+        in_specs=[VMEM] * (len(blocks) + 3),
+        out_specs=VMEM,
+        compiler_params=PARAMS,
+        cost_estimate=pl.CostEstimate(
+            flops=6 * part.size * part.shape[1], bytes_accessed=12 * part.size, transcendentals=0
+        ),
+        name="add_side",
+    )(*blocks, stencil_hi, stencil_lo, part)
+
+
+def finish_kernel(side, block, stencil_hi, stencil_lo, part, *refs):
+    *ready, kept, given = refs
+    chips, height, _ = kept.shape
+    comps = part.shape[0]
+    rows = height // comps
+
+    def place(c, smeared):
+        for m in range(2 * chips):
+            out = given if m % 2 else kept
+            out[m // 2, c * rows : (c + 1) * rows, :] = smeared[m * rows : (m + 1) * rows]
+
+    for c, smeared in smeared_pairs(side, 0, block, stencil_hi, stencil_lo, part):
+        place(c, smeared)
+    for c in range(block.shape[0], comps):
+        place(c, ready[0][c - block.shape[0]])
+
+
+def finish(side, block, stencil_hi, stencil_lo, part, ready, parts):
     comps, group_len, slice_len = part.shape
-    if side == NEAR:
-        out_shape = [jax.ShapeDtypeStruct(part.shape, jnp.float32)]
-    else:
-        shape = (parts // 2, comps * group_len // parts, slice_len)
-        out_shape = [jax.ShapeDtypeStruct(shape, jnp.float32)] * 2
-    return pl.pallas_call(
-        lambda *refs: smear_kernel(side, len(blocks), *refs),
-        out_shape=out_shape,
-        in_specs=[VMEM] * (len(blocks) + 3),
-        out_specs=[VMEM] * len(out_shape),
+    shape = (parts // 2, comps * group_len // parts, slice_len)
+    return pl.pallas_call(
+        lambda *refs: finish_kernel(side, *refs),
+        out_shape=[jax.ShapeDtypeStruct(shape, jnp.float32)] * 2,
+        in_specs=[VMEM] * (len(ready) + 4),
+        out_specs=[VMEM] * 2,
         compiler_params=PARAMS,
         cost_estimate=pl.CostEstimate(
             flops=6 * part.size * group_len, bytes_accessed=12 * part.size, transcendentals=0
         ),
-        name="smear",
-    )(*blocks, stencil_hi, stencil_lo, part)
+        name="finish",
+    )(block, stencil_hi, stencil_lo, part, *ready)
 
 
 def join_kernel(own, swapped, *out):
@@ -143,6 +168,21 @@
 
 def paired(groups):
     return groups == 4
+
+
+def hold_kernel(block, _, out):
+    out[...] = block[...]
+
+
+def hold(block, until):
+    return pl.pallas_call(
+        hold_kernel,
+        out_shape=jax.ShapeDtypeStruct(block.shape, jnp.float32),
+        in_specs=[VMEM, pl.BlockSpec(memory_space=pl.ANY)],
+        out_specs=VMEM,
+        compiler_params=PARAMS,
+        name="hold",
+    )(block, until)
 
 
 def exchange(own, groups):
@@ -153,7 +193,7 @@
     across = lambda block, flip: lax.ppermute(block, "kgrp", [(i, i ^ flip) for i in range(groups)])
     half = own.shape[0] // 2
     near = [across(own[:half], 1), across(own[half:], 1)]
-    return near, [across(near[0], 2), across(own[half:], 3)]
+    return near, [across(hold(own[:half], near[1]), 3), across(near[1], 2)]
 
 
 def spread(values, shape):
@@ -366,12 +406,14 @@
     flat = current.reshape(height, width)
     old_in = past_inputs.reshape(HIST, height, width)
     old_res = past_residuals.reshape(HIST, height, width)
-    sides = exchange(own, groups)
+    near, far = exchange(own, groups)
     stencil_hi, stencil_lo, smeared = prepare(own, neighbour, stencil_weight, groups * group_len)
     scalars = (slot_order, momentum_class, acoustic_coupling, optical_coupling, occupation)
     aged, old_line, gains = history(old_in, old_res, scalars, rows)
-    (smeared,) = smear(NEAR, sides[NEAR], stencil_hi, stencil_lo, smeared, parts)
-    kept, given = smear(FAR, sides[FAR], stencil_hi, stencil_lo, smeared, parts)
+    smeared = add_side(NEAR, 0, near, stencil_hi, stencil_lo, smeared)
+    direct, *forwarded = far
+    ready = [add_side(FAR, direct.shape[0], forwarded, stencil_hi, stencil_lo, smeared)] if forwarded else []
+    kept, given = finish(FAR, direct, stencil_hi, stencil_lo, smeared, ready, parts)
     meet = lambda block, m: lax.ppermute(block, "energy", [(e, e ^ m) for e in range(parts)])
     swapped = meet(given, 1)
     smeared = [meet(block, 2 * chip) for chip, block in enumerate(join(kept, swapped), 1)]

time: 40.7 us -> 41 us (level)
  waiting for transfers between devices: 7.45 us -> 10.7 us
  starting transfers between devices: 12.6 us -> 11.2 us
  local copies, waits for them, and re-layouts: 4.72 us -> 3.32 us
    ppermute x4, waiting for transfers between devices: 2.64 us -> 4.77 us  [exchange(): lax.ppermute(block, 'kgrp', [(i, i ^ flip) for i in range(groups)])]
    ppermute x4, starting transfers between devices: 8.07 us -> 6.67 us  [exchange(): lax.ppermute(block, 'kgrp', [(i, i ^ flip) for i in range(groups)])]
    unnamed x24, local copies, waits for them, and re-layouts: 3.63 us -> 2.33 us
    ppermute x4, waiting for transfers between devices: 4.8 us -> 5.88 us  [per_device(): lax.ppermute(block, 'energy', [(e, e ^ m) for e in range(parts)])]
  transfers between devices with their start and end apart: 8 -> 8, of which waited for: 6 -> 5; matrix products, arithmetic and copies ran while one was open for 0% -> 0% of each run, Pallas kernels for 6% -> 7%
where the time goes in v5:
time: 41 us; the launch traced here: 40.8 us
  starting transfers between devices  11.2 us (27%)
  waiting for transfers between devices  10.7 us (26%)
  blocking collectives  10.3 us (25%)
  Pallas kernels  5.17 us (13%)
  local copies, waits for them, and re-layouts  3.32 us (8%)
    all_to_all x1, blocking collectives, per_device(): lax.all_to_all(lines, ('kgrp', 'energy'), split_axis=0, concat_axis=0, ti...  10.3 us
    ppermute x4, starting transfers between devices, exchange(): lax.ppermute(block, 'kgrp', [(i, i ^ flip) for i in range(groups)])  6.67 us
    ppermute x4, waiting for transfers between devices, per_device(): lax.ppermute(block, 'energy', [(e, e ^ m) for e in range(parts)])  5.88 us
    ppermute x4, waiting for transfers between devices, exchange(): lax.ppermute(block, 'kgrp', [(i, i ^ flip) for i in range(groups)])  4.77 us
    ppermute x4, starting transfers between devices, per_device(): lax.ppermute(block, 'energy', [(e, e ^ m) for e in range(parts)])  4.52 us
    unnamed x24, local copies, waits for them, and re-layouts  2.33 us
    pallas_call x1, Pallas kernels, history(): pl.pallas_call(lambda *refs: history_kernel(rows, *refs), out_shape=(jax....  1.31 us
    pallas_call x1, Pallas kernels, prepare(): pl.pallas_call(lambda *refs: prepare_kernel(total_k, *refs), out_shape=(s...  1.06 us
  transfers between devices with their start and end apart: 8, of which 5 were waited for; matrix products, arithmetic and copies ran while one was open for 0% of the time, Pallas kernels for 7%

profile of v5, /device:TPU:0, one launch (start us, length us, event | category | flops | bytes accessed | tf_op | source)
XLA Modules:
  0.0 40.8 jit_solution(6522104801810825891)
XLA Ops:
  0.0 1.0 %fusion = (f32[1,2,2,64,128]{4,3,2,1,0:T(8,128)S(1)}, f32[1,2,2,64,128]{4,3,2,1,0:T(8,128)S(1)}) fusion(f32[2,2,2,64,128]{4,3,2,1,0:T(8,128)} %param.12), kind=kLoop, calls=%fused_computation | loop fusion | bytes 524288 | tf_op jit(solution)/shard_map/slice | solution.py:195
  1.0 3.0 %collective-permute-start = (f32[4,64,128]{2,1,0:T(8,128)S(1)}, f32[4,64,128]{2,1,0:T(8,128)S(1)}, u32[]{:S(2)}, u32[]{:S(2)}) collective-permute-start(f32[4,64,128]{2,1,0:T(8,128)S(1)} %bitcast.17), channel_id=1, source_target_pairs={{0,8},{8,0},{16,24},{24,16},{1,9},{9,1},{17,25},{25,17},{2,10},{10... | collective-permute-start | bytes 393224 | tf_op jit(solution)/shard_map/ppermute | solution.py:193
  4.0 0.1 collective-permute-start.2
  4.1 4.2 %collective-permute-done._.refs_1_ = f32[4,64,128]{2,1,0:T(8,128)S(1)} collective-permute-done((f32[4,64,128]{2,1,0:T(8,128)S(1)}, f32[4,64,128]{2,1,0:T(8,128)S(1)}, u32[]{:S(2)}, u32[]{:S(2)}) %collective-permute-start) | collective-permute-done | bytes 131104 | tf_op jit(solution)/shard_map/ppermute | solution.py:193
  8.3 2.1 %collective-permute-start.3 = (f32[4,64,128]{2,1,0:T(8,128)S(1)}, f32[4,64,128]{2,1,0:T(8,128)S(1)}, u32[]{:S(2)}, u32[]{:S(2)}) collective-permute-start(f32[4,64,128]{2,1,0:T(8,128)S(1)} %collective-permute-done._.refs_1_), channel_id=1, source_target_pairs={{0,16},{8,24},{16,0},{24,8},{1,17},{9,25},{17,1},{25,9},{2,18},{10... | collective-permute-start | bytes 393224 | tf_op jit(solution)/shard_map/ppermute | solution.py:193
  10.4 0.0 copy-start.1
  10.4 0.0 copy-start
  10.4 1.5 %collective-permute-start.1 = (f32[4,64,128]{2,1,0:T(8,128)S(1)}, f32[4,64,128]{2,1,0:T(8,128)S(1)}, u32[]{:S(2)}, u32[]{:S(2)}) collective-permute-start(f32[4,64,128]{2,1,0:T(8,128)S(1)} %hold.1), channel_id=1, source_target_pairs={{0,24},{8,16},{16,8},{24,0},{1,25},{9,17},{17,9},{25,1},{2,26},{10... | collective-permute-start | bytes 393224 | tf_op jit(solution)/shard_map/ppermute | solution.py:193
  11.9 0.0 copy-start.2
  11.9 0.9 %copy-done.2 = f32[2,2,2,64,128]{4,3,2,1,0:T(8,128)S(1)} copy-done((f32[2,2,2,64,128]{4,3,2,1,0:T(8,128)S(1)}, f32[2,2,2,64,128]{4,3,2,1,0:T(8,128)}, u32[]{:S(2)}) %copy-start.2) | copy-done | bytes 262168
  12.9 0.0 copy-start.4
  12.9 0.7 %copy-done.4 = s32[64,5]{0,1:T(8,128)S(1)} copy-done((s32[64,5]{0,1:T(8,128)S(1)}, s32[64,5]{0,1:T(8,128)}, u32[]{:S(2)}) %copy-start.4) | copy-done | bytes 1304
  13.6 0.0 copy-start.6
  13.6 0.7 %copy-done.6 = f32[5]{0:T(128)S(1)} copy-done((f32[5]{0:T(128)S(1)}, f32[5]{0:T(128)}, u32[]{:S(2)}) %copy-start.6) | copy-done | bytes 44
  14.2 0.0 copy-start.5
  14.2 0.0 copy-start.7
  14.2 0.0 copy-start.9
  14.2 0.0 copy-start.10
  14.2 1.1 %prepare.1 = (bf16[64,128]{1,0:T(8,128)(2,1)S(1)}, bf16[64,128]{1,0:T(8,128)(2,1)S(1)}, f32[8,64,128]{2,1,0:T(8,128)S(1)}) custom-call(f32[8,64,128]{2,1,0:T(8,128)S(1)} %bitcast.11, s32[5,64]{1,0:T(8,128)S(1)} %bitcast.16, f32[5]{0:T(128)S(1)} %copy-done.6), custom_call_target="tpu_custom_call" | custom-call | flops 25165824 | bytes 524288 | tf_op jit(solution)/shard_map/prepare/pallas_call | solution.py:71
  15.3 0.0 collective-permute-done.2.refs_0_
  15.3 0.2 add_side.2.refs_3_
  15.6 0.0 collective-permute-done.3.refs_0_
  15.6 0.2 add_side.3.refs_4_
  15.8 0.5 %collective-permute-done.1.refs_0_ = f32[4,64,128]{2,1,0:T(8,128)S(1)} collective-permute-done((f32[4,64,128]{2,1,0:T(8,128)S(1)}, f32[4,64,128]{2,1,0:T(8,128)S(1)}, u32[]{:S(2)}, u32[]{:S(2)}) %collective-permute-start.1) | collective-permute-done | bytes 131104 | tf_op jit(solution)/shard_map/ppermute | solution.py:193
  16.4 0.2 finish.1
  16.6 0.1 collective-permute-start.4
  16.7 1.3 %collective-permute-done.4.swapped.refs_1_ = f32[4,64,128]{2,1,0:T(8,128)S(1)} collective-permute-done((f32[4,64,128]{2,1,0:T(8,128)S(1)}, f32[4,64,128]{2,1,0:T(8,128)S(1)}, u32[]{:S(2)}, u32[]{:S(2)}) %collective-permute-start.4) | collective-permute-done | bytes 131104 | tf_op jit(solution)/shard_map/ppermute | solution.py:417
  18.0 1.6 %collective-permute-start.5 = (f32[2,64,128]{2,1,0:T(8,128)S(1)}, f32[2,64,128]{2,1,0:T(8,128)S(1)}, u32[]{:S(2)}, u32[]{:S(2)}) collective-permute-start(f32[2,64,128]{2,1,0:T(8,128)S(1)} %get-tuple-element.23), channel_id=1, source_target_pairs={{0,2},{1,3},{2,0},{3,1},{4,6},{5,7},{6,4},{7,5},{8,10},{9,11},{10,... | collective-permute-start | bytes 196616 | tf_op jit(solution)/shard_map/ppermute | solution.py:417
  19.7 2.6 %collective-permute-start.6 = (f32[2,64,128]{2,1,0:T(8,128)S(1)}, f32[2,64,128]{2,1,0:T(8,128)S(1)}, u32[]{:S(2)}, u32[]{:S(2)}) collective-permute-start(f32[2,64,128]{2,1,0:T(8,128)S(1)} %get-tuple-element.24), channel_id=1, source_target_pairs={{0,4},{1,5},{2,6},{3,7},{4,0},{5,1},{6,2},{7,3},{8,12},{9,13},{10,... | collective-permute-start | bytes 196616 | tf_op jit(solution)/shard_map/ppermute | solution.py:417
  22.3 0.2 collective-permute-start.7
  22.5 0.0 copy-done.1
  22.5 0.0 copy-done
  22.5 0.0 copy-done.5
  22.5 0.0 copy-done.7
  22.5 0.0 copy-done.8
  22.5 0.0 copy-done.9
  22.5 0.0 copy-done.10
  22.5 0.0 copy-start.3
  22.6 0.0 copy-start.11
  22.6 1.3 %history.1 = (f32[5,64,1024]{2,1,0:T(8,128)S(1)}, f32[1,128]{1,0:T(1,128)S(1)}, f32[5,8,128]{2,1,0:T(8,128)S(1)}) custom-call(f32[5,64,1024]{2,1,0:T(8,128)S(1)} %bitcast.10, f32[5,64,1024]{2,1,0:T(8,128)S(1)} %bitcast.8, s32[5]{0:T(128)S(1)} %copy-done.5, s32[64]{0:T(128)S(1)} %copy-done.7, f32[4]{0:T(128)S(1)} %copy-done.8, f32[2]{0:T(128)S(1)} %copy-done.9, ...), custom_call_target="tpu_custom_call" | custom-call | flops 2621440 | bytes 3932160 | tf_op jit(solution)/shard_map/history/pallas_call | solution.py:242
  23.9 0.0 collective-permute-done.5.refs_2_
  23.9 3.3 %collective-permute-done.6.refs_3_ = f32[2,64,128]{2,1,0:T(8,128)S(1)} collective-permute-done((f32[2,64,128]{2,1,0:T(8,128)S(1)}, f32[2,64,128]{2,1,0:T(8,128)S(1)}, u32[]{:S(2)}, u32[]{:S(2)}) %collective-permute-start.6) | collective-permute-done | bytes 65568 | tf_op jit(solution)/shard_map/ppermute | solution.py:417
  27.2 1.2 %collective-permute-done.7.refs_4_ = f32[2,64,128]{2,1,0:T(8,128)S(1)} collective-permute-done((f32[2,64,128]{2,1,0:T(8,128)S(1)}, f32[2,64,128]{2,1,0:T(8,128)S(1)}, u32[]{:S(2)}, u32[]{:S(2)}) %collective-permute-start.7) | collective-permute-done | bytes 65568 | tf_op jit(solution)/shard_map/ppermute | solution.py:417
  28.4 0.0 copy-done.3
  28.4 0.0 copy-done.11
  28.5 1.0 %residual.1 = (f32[64,1024]{1,0:T(8,128)S(1)}, f32[32,1,128]{2,1,0:T(1,128)S(1)}) custom-call(f32[4,64,128]{2,1,0:T(8,128)S(1)} %get-tuple-element.21.own.refs_0_, f32[4,64,128]{2,1,0:T(8,128)S(1)} %collective-permute-done.4.swapped.refs_1_, f32[2,64,128]{2,1,0:T(8,128)S(1)} %collective-permute-done.5.refs_2_, ...), custom_call_target="tpu_custom_call" | custom-call | tf_op jit(solution)/shard_map/residual/pallas_call | solution.py:302
  29.5 10.3 %all_to_all.5.refs_0_ = f32[32,1,128]{2,1,0:T(1,128)S(1)} all-to-all(f32[32,1,128]{2,1,0:T(1,128)S(1)} %get-tuple-element.28), channel_id=1, replica_groups=mesh['kgrp'=4,'energy'=8] {'kgrp','energy'}, dimensions={0} | all-to-all | bytes 32768 | tf_op jit(solution)/shard_map/all_to_all | solution.py:423
  39.7 1.0 %mix.1 = f32[64,1024]{1,0:T(8,128)} custom-call(f32[32,1,128]{2,1,0:T(1,128)S(1)} %all_to_all.5.refs_0_, f32[64,1024]{1,0:T(8,128)S(1)} %get-tuple-element.29.refs_1_, f32[64,1024]{1,0:T(8,128)S(1)} %bitcast.13, f32[5,64,1024]{2,1,0:T(8,128)S(1)} %get-tuple-element.30.refs_3_), custom_call_target="tpu_custom_call" | custom-call | tf_op jit(solution)/shard_map/mix/pallas_call | solution.py:374
  (3 shorter events, 0.0 us)
Async XLA Ops:
  1.0 7.3 %collective-permute-start = (f32[4,64,128]{2,1,0:T(8,128)S(1)}, f32[4,64,128]{2,1,0:T(8,128)S(1)}, u32[]{:S(2)}, u32[]{:S(2)}) collective-permute-start(f32[4,64,128]{2,1,0:T(8,128)S(1)} %bitcast.17), channel_id=1, source_target_pairs={{0,8},{8,0},{16,24},{24,16},{1,9},{9,1},{17,25},{25,17},{2,10},{10... | collective-permute-start | bytes 393224 | tf_op jit(solution)/shard_map/ppermute | solution.py:193
  4.0 11.3 %collective-permute-start.2 = (f32[4,64,128]{2,1,0:T(8,128)S(1)}, f32[4,64,128]{2,1,0:T(8,128)S(1)}, u32[]{:S(2)}, u32[]{:S(2)}) collective-permute-start(f32[4,64,128]{2,1,0:T(8,128)S(1)} %bitcast.14), channel_id=1, source_target_pairs={{0,8},{8,0},{16,24},{24,16},{1,9},{9,1},{17,25},{25,17},{2,10},{10... | collective-permute-start | bytes 393224 | tf_op jit(solution)/shard_map/ppermute | solution.py:193
  8.3 7.3 %collective-permute-start.3 = (f32[4,64,128]{2,1,0:T(8,128)S(1)}, f32[4,64,128]{2,1,0:T(8,128)S(1)}, u32[]{:S(2)}, u32[]{:S(2)}) collective-permute-start(f32[4,64,128]{2,1,0:T(8,128)S(1)} %collective-permute-done._.refs_1_), channel_id=1, source_target_pairs={{0,16},{8,24},{16,0},{24,8},{1,17},{9,25},{17,1},{25,9},{2,18},{10... | collective-permute-start | bytes 393224 | tf_op jit(solution)/shard_map/ppermute | solution.py:193
  10.4 12.1 %copy-start.1 = (f32[5,2,2,2,8,1024]{5,4,3,2,1,0:T(8,128)S(1)}, f32[5,2,2,2,8,1024]{5,4,3,2,1,0:T(8,128)}, u32[]{:S(2)}) copy-start(f32[5,2,2,2,8,1024]{5,4,3,2,1,0:T(8,128)} %param.14) | copy-start | bytes 3932164
  10.4 12.1 %copy-start = (f32[5,2,2,2,8,1024]{5,4,3,2,1,0:T(8,128)S(1)}, f32[5,2,2,2,8,1024]{5,4,3,2,1,0:T(8,128)}, u32[]{:S(2)}) copy-start(f32[5,2,2,2,8,1024]{5,4,3,2,1,0:T(8,128)} %param.15) | copy-start | bytes 3932164
  10.4 5.9 %collective-permute-start.1 = (f32[4,64,128]{2,1,0:T(8,128)S(1)}, f32[4,64,128]{2,1,0:T(8,128)S(1)}, u32[]{:S(2)}, u32[]{:S(2)}) collective-permute-start(f32[4,64,128]{2,1,0:T(8,128)S(1)} %hold.1), channel_id=1, source_target_pairs={{0,24},{8,16},{16,8},{24,0},{1,25},{9,17},{17,9},{25,1},{2,26},{10... | collective-permute-start | bytes 393224 | tf_op jit(solution)/shard_map/ppermute | solution.py:193
  11.9 0.9 %copy-start.2 = (f32[2,2,2,64,128]{4,3,2,1,0:T(8,128)S(1)}, f32[2,2,2,64,128]{4,3,2,1,0:T(8,128)}, u32[]{:S(2)}) copy-start(f32[2,2,2,64,128]{4,3,2,1,0:T(8,128)} %param.12) | copy-start | bytes 786436
  12.9 0.7 %copy-start.4 = (s32[64,5]{0,1:T(8,128)S(1)}, s32[64,5]{0,1:T(8,128)}, u32[]{:S(2)}) copy-start(s32[64,5]{0,1:T(8,128)} %param.17) | copy-start | bytes 3844
  13.6 0.7 %copy-start.6 = (f32[5]{0:T(128)S(1)}, f32[5]{0:T(128)}, u32[]{:S(2)}) copy-start(f32[5]{0:T(128)} %refs_2_.2) | copy-start | bytes 64
  14.2 8.3 %copy-start.5 = (s32[5]{0:T(128)S(1)}, s32[5]{0:T(128)}, u32[]{:S(2)}) copy-start(s32[5]{0:T(128)} %refs_9_.1) | copy-start | bytes 64
  14.2 8.3 %copy-start.7 = (s32[64]{0:T(128)S(1)}, s32[64]{0:T(128)}, u32[]{:S(2)}) copy-start(s32[64]{0:T(128)} %refs_3_.1) | copy-start | bytes 772
  14.2 8.3 %copy-start.8 = (f32[4]{0:T(128)S(1)}, f32[4]{0:T(128)}, u32[]{:S(2)}) copy-start(f32[4]{0:T(128)} %refs_4_.1) | copy-start | bytes 52
  14.2 8.3 %copy-start.9 = (f32[2]{0:T(128)S(1)}, f32[2]{0:T(128)}, u32[]{:S(2)}) copy-start(f32[2]{0:T(128)} %refs_5_.1) | copy-start | bytes 28
  14.2 8.3 %copy-start.10 = (f32[2]{0:T(128)S(1)}, f32[2]{0:T(128)}, u32[]{:S(2)}) copy-start(f32[2]{0:T(128)} %refs_6_.1) | copy-start | bytes 28
  16.6 1.4 %collective-permute-start.4 = (f32[4,64,128]{2,1,0:T(8,128)S(1)}, f32[4,64,128]{2,1,0:T(8,128)S(1)}, u32[]{:S(2)}, u32[]{:S(2)}) collective-permute-start(f32[4,64,128]{2,1,0:T(8,128)S(1)} %get-tuple-element.22), channel_id=1, source_target_pairs={{0,1},{1,0},{2,3},{3,2},{4,5},{5,4},{6,7},{7,6},{8,9},{9,8},{10,11... | collective-permute-start | bytes 393224 | tf_op jit(solution)/shard_map/ppermute | solution.py:417
  18.0 5.8 %collective-permute-start.5 = (f32[2,64,128]{2,1,0:T(8,128)S(1)}, f32[2,64,128]{2,1,0:T(8,128)S(1)}, u32[]{:S(2)}, u32[]{:S(2)}) collective-permute-start(f32[2,64,128]{2,1,0:T(8,128)S(1)} %get-tuple-element.23), channel_id=1, source_target_pairs={{0,2},{1,3},{2,0},{3,1},{4,6},{5,7},{6,4},{7,5},{8,10},{9,11},{10,... | collective-permute-start | bytes 196616 | tf_op jit(solution)/shard_map/ppermute | solution.py:417
  19.7 7.5 %collective-permute-start.6 = (f32[2,64,128]{2,1,0:T(8,128)S(1)}, f32[2,64,128]{2,1,0:T(8,128)S(1)}, u32[]{:S(2)}, u32[]{:S(2)}) collective-permute-start(f32[2,64,128]{2,1,0:T(8,128)S(1)} %get-tuple-element.24), channel_id=1, source_target_pairs={{0,4},{1,5},{2,6},{3,7},{4,0},{5,1},{6,2},{7,3},{8,12},{9,13},{10,... | collective-permute-start | bytes 196616 | tf_op jit(solution)/shard_map/ppermute | solution.py:417
  22.3 6.2 %collective-permute-start.7 = (f32[2,64,128]{2,1,0:T(8,128)S(1)}, f32[2,64,128]{2,1,0:T(8,128)S(1)}, u32[]{:S(2)}, u32[]{:S(2)}) collective-permute-start(f32[2,64,128]{2,1,0:T(8,128)S(1)} %get-tuple-element.25), channel_id=1, source_target_pairs={{0,6},{1,7},{2,4},{3,5},{4,2},{5,3},{6,0},{7,1},{8,14},{9,15},{10,... | collective-permute-start | bytes 196616 | tf_op jit(solution)/shard_map/ppermute | solution.py:417
  22.5 5.9 %copy-start.3 = (f32[2,2,2,8,1024]{4,3,2,1,0:T(8,128)S(1)}, f32[2,2,2,8,1024]{4,3,2,1,0:T(8,128)}, u32[]{:S(2)}) copy-start(f32[2,2,2,8,1024]{4,3,2,1,0:T(8,128)} %param.13) | copy-start | bytes 786436
  22.6 5.9 %copy-start.11 = (s32[2]{0:T(128)S(1)}, s32[2]{0:T(128)}, u32[]{:S(2)}) copy-start(s32[2]{0:T(128)} %refs_10_.1) | copy-start | bytes 28

commit v6 on v5

--- a/solution.py
+++ b/solution.py
@@ -33,11 +33,21 @@
     return dot(left[0], right[0]) + (dot(left[0], right[1]) + dot(left[1], right[0]))
 
 
-def prepare_kernel(total_k, own, neighbour, weight, stencil_hi, stencil_lo, part):
-    comps, group_len, slice_len = own.shape
+def prepare_kernel(total_k, *refs):
+    *blocks, neighbour_hbm, weight_hbm, stencil_hi, stencil_lo, part, late, neighbour, weight, done = refs
+    fetches = [
+        pltpu.make_async_copy(neighbour_hbm, neighbour, done.at[0]),
+        pltpu.make_async_copy(weight_hbm, weight, done.at[1]),
+    ]
+    for fetch in fetches:
+        fetch.start()
+    late[...] = blocks[0][...]
+    _, group_len, slice_len = blocks[0].shape
     group_id = lax.axis_index("kgrp")
     parts = lax.axis_size("energy")
     rows = group_len // parts
+    for fetch in fetches:
+        fetch.wait()
     slots, _ = neighbour.shape
     padded = jnp.concatenate([neighbour[...], jnp.zeros((8 - slots, group_len), jnp.int32)], axis=0)
     targets = jnp.transpose(padded)
@@ -45,11 +55,12 @@
     bit = 1
     while bit < parts:
         span = bit * rows
-        blocks = [targets[at : at + span] for at in range(0, group_len, span)]
-        flipped = [blocks[b ^ 1] for b in range(len(blocks))]
+        pieces = [targets[at : at + span] for at in range(0, group_len, span)]
+        flipped = [pieces[b ^ 1] for b in range(len(pieces))]
         targets = jnp.where(place & bit != 0, jnp.concatenate(flipped, axis=0), targets)
         bit *= 2
-    local = (targets - group_id * group_len + (group_len + total_k)) % total_k
+    local = targets - group_id * group_len + group_len
+    local = jnp.where(local < 0, local + total_k, jnp.where(local >= total_k, local - total_k, local))
     spot = lax.broadcasted_iota(jnp.int32, (group_len, 3 * group_len), 1)
     stencil = jnp.zeros(spot.shape, jnp.float32)
     for n in range(slots):
@@ -59,26 +70,41 @@
     near, far = jnp.where(swapped, before, after), jnp.where(swapped, after, before)
     stencil_hi[...], stencil_lo[...] = split(jnp.concatenate([near, far], axis=1))
     centre = split(stencil[:, group_len : 2 * group_len])
-    for c in range(0, comps, 2):
-        result = product(centre, split(jnp.concatenate([own[c], own[c + 1]], axis=1)))
-        part[c] = result[:, :slice_len]
-        part[c + 1] = result[:, slice_len:]
-
-
-def prepare(own, neighbour, weight, total_k):
-    group_len = own.shape[1]
+    first = 0
+    for own in blocks:
+        for c in range(0, own.shape[0], 2):
+            result = product(centre, split(jnp.concatenate([own[c], own[c + 1]], axis=1)))
+            part[first + c] = result[:, :slice_len]
+            part[first + c + 1] = result[:, slice_len:]
+        first += own.shape[0]
+
+
+def prepare(blocks, neighbour, weight, total_k):
+    comps = sum(block.shape[0] for block in blocks)
+    _, group_len, slice_len = blocks[0].shape
     sides = jax.ShapeDtypeStruct((group_len, 2 * group_len), jnp.bfloat16)
+    size = comps * group_len * slice_len
     return pl.pallas_call(
         lambda *refs: prepare_kernel(total_k, *refs),
-        out_shape=(sides, sides, jax.ShapeDtypeStruct(own.shape, jnp.float32)),
-        in_specs=[VMEM, VMEM, SMEM],
-        out_specs=(VMEM,) * 3,
+        out_shape=(
+            sides,
+            sides,
+            jax.ShapeDtypeStruct((comps, group_len, slice_len), jnp.float32),
+            jax.ShapeDtypeStruct(blocks[0].shape, jnp.float32),
+        ),
+        in_specs=[VMEM] * len(blocks) + [pl.BlockSpec(memory_space=pltpu.HBM)] * 2,
+        out_specs=(VMEM,) * 4,
+        scratch_shapes=[
+            pltpu.VMEM(neighbour.shape[::-1], jnp.int32),
+            pltpu.SMEM(weight.shape, jnp.float32),
+            pltpu.SemaphoreType.DMA((2,)),
+        ],
         compiler_params=PARAMS,
         cost_estimate=pl.CostEstimate(
-            flops=6 * own.size * group_len, bytes_accessed=8 * own.size, transcendentals=0
+            flops=6 * size * group_len, bytes_accessed=8 * size, transcendentals=0
         ),
         name="prepare",
-    )(own, jnp.transpose(neighbour), weight)
+    )(*blocks, jnp.transpose(neighbour), weight)
 
 
 def smeared_pairs(side, first, block, stencil_hi, stencil_lo, part):
@@ -185,15 +211,19 @@
     )(block, until)
 
 
-def exchange(own, groups):
+def exchange(own, neighbour, weight, groups):
+    total_k = groups * own.shape[1]
     if not paired(groups):
         forward = [(i, (i + 1) % groups) for i in range(groups)]
         backward = [(target, source) for source, target in forward]
-        return [lax.ppermute(own, "kgrp", backward)], [lax.ppermute(own, "kgrp", forward)]
+        near, far = lax.ppermute(own, "kgrp", backward), lax.ppermute(own, "kgrp", forward)
+        return [near], [far], prepare([own], neighbour, weight, total_k)[:3]
     across = lambda block, flip: lax.ppermute(block, "kgrp", [(i, i ^ flip) for i in range(groups)])
     half = own.shape[0] // 2
-    near = [across(own[:half], 1), across(own[half:], 1)]
-    return near, [across(hold(own[:half], near[1]), 3), across(near[1], 2)]
+    blocks = own[:half], own[half:]
+    head = across(blocks[1], 1)
+    *made, late = prepare(blocks, neighbour, weight, total_k)
+    return [across(late, 1), head], [across(hold(late, head), 3), across(head, 2)], made
 
 
 def spread(values, shape):
@@ -406,10 +436,9 @@
     flat = current.reshape(height, width)
     old_in = past_inputs.reshape(HIST, height, width)
     old_res = past_residuals.reshape(HIST, height, width)
-    near, far = exchange(own, groups)
-    stencil_hi, stencil_lo, smeared = prepare(own, neighbour, stencil_weight, groups * group_len)
     scalars = (slot_order, momentum_class, acoustic_coupling, optical_coupling, occupation)
     aged, old_line, gains = history(old_in, old_res, scalars, rows)
+    near, far, (stencil_hi, stencil_lo, smeared) = exchange(own, neighbour, stencil_weight, groups)
     smeared = add_side(NEAR, 0, near, stencil_hi, stencil_lo, smeared)
     direct, *forwarded = far
     ready = [add_side(FAR, direct.shape[0], forwarded, stencil_hi, stencil_lo, smeared)] if forwarded else []

time: 41 us -> 40.7 us (level)
  local copies, waits for them, and re-layouts: 3.32 us -> 2.38 us
    unnamed x24 -> x22, local copies, waits for them, and re-layouts: 2.33 us -> 1.4 us
  transfers between devices with their start and end apart: 8 -> 8, of which waited for: 5 -> 7; matrix products, arithmetic and copies ran while one was open for 0% -> 0% of each run, Pallas kernels for 7% -> 7%
where the time goes in v6:
time: 40.7 us; the launch traced here: 40.5 us
  starting transfers between devices  11.3 us (28%)
  waiting for transfers between devices  10.9 us (27%)
  blocking collectives  10.6 us (26%)
  Pallas kernels  5.18 us (13%)
  local copies, waits for them, and re-layouts  2.38 us (6%)
    all_to_all x1, blocking collectives, per_device(): lax.all_to_all(lines, ('kgrp', 'energy'), split_axis=0, concat_axis=0, ti...  10.6 us
    ppermute x4, starting transfers between devices, exchange(): lax.ppermute(block, 'kgrp', [(i, i ^ flip) for i in range(groups)])  6.5 us
    ppermute x4, waiting for transfers between devices, per_device(): lax.ppermute(block, 'energy', [(e, e ^ m) for e in range(parts)])  6.09 us
    ppermute x4, waiting for transfers between devices, exchange(): lax.ppermute(block, 'kgrp', [(i, i ^ flip) for i in range(groups)])  4.79 us
    ppermute x4, starting transfers between devices, per_device(): lax.ppermute(block, 'energy', [(e, e ^ m) for e in range(parts)])  4.77 us
    unnamed x22, local copies, waits for them, and re-layouts  1.4 us
    pallas_call x1, Pallas kernels, history(): pl.pallas_call(lambda *refs: history_kernel(rows, *refs), out_shape=(jax....  1.31 us
    pallas_call x1, Pallas kernels, prepare(): pl.pallas_call(lambda *refs: prepare_kernel(total_k, *refs), out_shape=(s...  1.08 us
  transfers between devices with their start and end apart: 8, of which 7 were waited for; matrix products, arithmetic and copies ran while one was open for 0% of the time, Pallas kernels for 7%

profile of v6, /device:TPU:0, one launch (start us, length us, event | category | flops | bytes accessed | tf_op | source)
XLA Modules:
  0.0 40.5 jit_solution(3704525223973051609)
XLA Ops:
  0.0 1.0 %fusion = (f32[1,2,2,64,128]{4,3,2,1,0:T(8,128)S(1)}, f32[1,2,2,64,128]{4,3,2,1,0:T(8,128)S(1)}) fusion(f32[2,2,2,64,128]{4,3,2,1,0:T(8,128)} %param.12), kind=kLoop, calls=%fused_computation | loop fusion | bytes 524288 | tf_op jit(solution)/shard_map/slice | solution.py:223
  1.0 3.0 %collective-permute-start = (f32[4,64,128]{2,1,0:T(8,128)S(1)}, f32[4,64,128]{2,1,0:T(8,128)S(1)}, u32[]{:S(2)}, u32[]{:S(2)}) collective-permute-start(f32[4,64,128]{2,1,0:T(8,128)S(1)} %bitcast.12), channel_id=1, source_target_pairs={{0,8},{8,0},{16,24},{24,16},{1,9},{9,1},{17,25},{25,17},{2,10},{10... | collective-permute-start | bytes 393224 | tf_op jit(solution)/shard_map/ppermute | solution.py:221
  4.0 0.0 copy-start.3
  4.0 0.7 %copy-done.3 = s32[64,5]{0,1:T(8,128)S(1)} copy-done((s32[64,5]{0,1:T(8,128)S(1)}, s32[64,5]{0,1:T(8,128)}, u32[]{:S(2)}) %copy-start.3) | copy-done | bytes 1304
  4.7 0.0 copy-start.5
  4.7 0.7 %copy-done.5 = f32[5]{0:T(128)S(1)} copy-done((f32[5]{0:T(128)S(1)}, f32[5]{0:T(128)}, u32[]{:S(2)}) %copy-start.5) | copy-done | bytes 44
  5.3 0.0 copy-start.1
  5.3 1.1 %prepare.1 = (bf16[64,128]{1,0:T(8,128)(2,1)S(1)}, bf16[64,128]{1,0:T(8,128)(2,1)S(1)}, f32[8,64,128]{2,1,0:T(8,128)S(1)}, f32[4,64,128]{2,1,0:T(8,128)S(1)}) custom-call(f32[4,64,128]{2,1,0:T(8,128)S(1)} %bitcast.14, f32[4,64,128]{2,1,0:T(8,128)S(1)} %bitcast.13, s32[5,64]{1,0:T(8,128)S(1)} %bitcast.15, f32[5]{0:T(128)S(1)} %copy-done.5), custom_call_target="tpu_custom_call" | custom-call | flops 25165824 | bytes 524288 | tf_op jit(solution)/shard_map/prepare/pallas_call | solution.py:87
  6.4 0.0 copy-start
  6.4 0.0 copy-start.4
  6.5 0.0 copy-start.6
  6.5 0.0 copy-start.7
  6.5 0.0 copy-start.8
  6.5 0.0 copy-start.9
  6.5 0.1 collective-permute-start.2
  6.6 0.9 %collective-permute-done._.refs_1_ = f32[4,64,128]{2,1,0:T(8,128)S(1)} collective-permute-done((f32[4,64,128]{2,1,0:T(8,128)S(1)}, f32[4,64,128]{2,1,0:T(8,128)S(1)}, u32[]{:S(2)}, u32[]{:S(2)}) %collective-permute-start) | collective-permute-done | bytes 131104 | tf_op jit(solution)/shard_map/ppermute | solution.py:221
  7.5 1.8 %collective-permute-start.3 = (f32[4,64,128]{2,1,0:T(8,128)S(1)}, f32[4,64,128]{2,1,0:T(8,128)S(1)}, u32[]{:S(2)}, u32[]{:S(2)}) collective-permute-start(f32[4,64,128]{2,1,0:T(8,128)S(1)} %collective-permute-done._.refs_1_), channel_id=1, source_target_pairs={{0,16},{8,24},{16,0},{24,8},{1,17},{9,25},{17,1},{25,9},{2,18},{10... | collective-permute-start | bytes 393224 | tf_op jit(solution)/shard_map/ppermute | solution.py:221
  9.3 1.6 %collective-permute-start.1 = (f32[4,64,128]{2,1,0:T(8,128)S(1)}, f32[4,64,128]{2,1,0:T(8,128)S(1)}, u32[]{:S(2)}, u32[]{:S(2)}) collective-permute-start(f32[4,64,128]{2,1,0:T(8,128)S(1)} %hold.1), channel_id=1, source_target_pairs={{0,24},{8,16},{16,8},{24,0},{1,25},{9,17},{17,9},{25,1},{2,26},{10... | collective-permute-start | bytes 393224 | tf_op jit(solution)/shard_map/ppermute | solution.py:221
  10.9 1.6 %collective-permute-done.2.refs_0_ = f32[4,64,128]{2,1,0:T(8,128)S(1)} collective-permute-done((f32[4,64,128]{2,1,0:T(8,128)S(1)}, f32[4,64,128]{2,1,0:T(8,128)S(1)}, u32[]{:S(2)}, u32[]{:S(2)}) %collective-permute-start.2) | collective-permute-done | bytes 131104 | tf_op jit(solution)/shard_map/ppermute | solution.py:221
  12.5 0.2 add_side.2.refs_3_
  12.8 1.4 %collective-permute-done.3.refs_0_ = f32[4,64,128]{2,1,0:T(8,128)S(1)} collective-permute-done((f32[4,64,128]{2,1,0:T(8,128)S(1)}, f32[4,64,128]{2,1,0:T(8,128)S(1)}, u32[]{:S(2)}, u32[]{:S(2)}) %collective-permute-start.3) | collective-permute-done | bytes 131104 | tf_op jit(solution)/shard_map/ppermute | solution.py:221
  14.2 0.2 add_side.3.refs_4_
  14.4 0.9 %collective-permute-done.1.refs_0_ = f32[4,64,128]{2,1,0:T(8,128)S(1)} collective-permute-done((f32[4,64,128]{2,1,0:T(8,128)S(1)}, f32[4,64,128]{2,1,0:T(8,128)S(1)}, u32[]{:S(2)}, u32[]{:S(2)}) %collective-permute-start.1) | collective-permute-done | bytes 131104 | tf_op jit(solution)/shard_map/ppermute | solution.py:221
  15.3 0.2 finish.1
  15.5 0.1 collective-permute-start.4
  15.6 1.3 %collective-permute-done.4.swapped.refs_1_ = f32[4,64,128]{2,1,0:T(8,128)S(1)} collective-permute-done((f32[4,64,128]{2,1,0:T(8,128)S(1)}, f32[4,64,128]{2,1,0:T(8,128)S(1)}, u32[]{:S(2)}, u32[]{:S(2)}) %collective-permute-start.4) | collective-permute-done | bytes 131104 | tf_op jit(solution)/shard_map/ppermute | solution.py:446
  17.0 2.1 %collective-permute-start.5 = (f32[2,64,128]{2,1,0:T(8,128)S(1)}, f32[2,64,128]{2,1,0:T(8,128)S(1)}, u32[]{:S(2)}, u32[]{:S(2)}) collective-permute-start(f32[2,64,128]{2,1,0:T(8,128)S(1)} %get-tuple-element.25), channel_id=1, source_target_pairs={{0,2},{1,3},{2,0},{3,1},{4,6},{5,7},{6,4},{7,5},{8,10},{9,11},{10,... | collective-permute-start | bytes 196616 | tf_op jit(solution)/shard_map/ppermute | solution.py:446
  19.1 2.6 %collective-permute-start.6 = (f32[2,64,128]{2,1,0:T(8,128)S(1)}, f32[2,64,128]{2,1,0:T(8,128)S(1)}, u32[]{:S(2)}, u32[]{:S(2)}) collective-permute-start(f32[2,64,128]{2,1,0:T(8,128)S(1)} %get-tuple-element.26), channel_id=1, source_target_pairs={{0,4},{1,5},{2,6},{3,7},{4,0},{5,1},{6,2},{7,3},{8,12},{9,13},{10,... | collective-permute-start | bytes 196616 | tf_op jit(solution)/shard_map/ppermute | solution.py:446
  21.7 0.0 collective-permute-start.7
  21.7 0.0 copy-done.1
  21.7 0.0 copy-done
  21.7 0.0 copy-done.4
  21.7 0.0 copy-done.6
  21.7 0.0 copy-done.7
  21.7 0.0 copy-done.8
  21.7 0.0 copy-done.9
  21.7 0.0 copy-start.2
  21.8 0.0 copy-start.10
  21.8 1.3 %history.1 = (f32[5,64,1024]{2,1,0:T(8,128)S(1)}, f32[1,128]{1,0:T(1,128)S(1)}, f32[5,8,128]{2,1,0:T(8,128)S(1)}) custom-call(f32[5,64,1024]{2,1,0:T(8,128)S(1)} %bitcast.9, f32[5,64,1024]{2,1,0:T(8,128)S(1)} %bitcast.7, s32[5]{0:T(128)S(1)} %copy-done.4, s32[64]{0:T(128)S(1)} %copy-done.6, f32[4]{0:T(128)S(1)} %copy-done.7, f32[2]{0:T(128)S(1)} %copy-done.8, ...), custom_call_target="tpu_custom_call" | custom-call | flops 2621440 | bytes 3932160 | tf_op jit(solution)/shard_map/history/pallas_call | solution.py:272
  23.1 0.0 collective-permute-done.5.refs_2_
  23.1 3.5 %collective-permute-done.6.refs_3_ = f32[2,64,128]{2,1,0:T(8,128)S(1)} collective-permute-done((f32[2,64,128]{2,1,0:T(8,128)S(1)}, f32[2,64,128]{2,1,0:T(8,128)S(1)}, u32[]{:S(2)}, u32[]{:S(2)}) %collective-permute-start.6) | collective-permute-done | bytes 65568 | tf_op jit(solution)/shard_map/ppermute | solution.py:446
  26.6 1.2 %collective-permute-done.7.refs_4_ = f32[2,64,128]{2,1,0:T(8,128)S(1)} collective-permute-done((f32[2,64,128]{2,1,0:T(8,128)S(1)}, f32[2,64,128]{2,1,0:T(8,128)S(1)}, u32[]{:S(2)}, u32[]{:S(2)}) %collective-permute-start.7) | collective-permute-done | bytes 65568 | tf_op jit(solution)/shard_map/ppermute | solution.py:446
  27.9 0.0 copy-done.2
  27.9 0.0 copy-done.10
  27.9 1.0 %residual.1 = (f32[64,1024]{1,0:T(8,128)S(1)}, f32[32,1,128]{2,1,0:T(1,128)S(1)}) custom-call(f32[4,64,128]{2,1,0:T(8,128)S(1)} %get-tuple-element.23.own.refs_0_, f32[4,64,128]{2,1,0:T(8,128)S(1)} %collective-permute-done.4.swapped.refs_1_, f32[2,64,128]{2,1,0:T(8,128)S(1)} %collective-permute-done.5.refs_2_, ...), custom_call_target="tpu_custom_call" | custom-call | tf_op jit(solution)/shard_map/residual/pallas_call | solution.py:332
  28.9 10.6 %all_to_all.5.refs_0_ = f32[32,1,128]{2,1,0:T(1,128)S(1)} all-to-all(f32[32,1,128]{2,1,0:T(1,128)S(1)} %get-tuple-element.30), channel_id=1, replica_groups=mesh['kgrp'=4,'energy'=8] {'kgrp','energy'}, dimensions={0} | all-to-all | bytes 32768 | tf_op jit(solution)/shard_map/all_to_all | solution.py:452
  39.5 1.0 %mix.1 = f32[64,1024]{1,0:T(8,128)} custom-call(f32[32,1,128]{2,1,0:T(1,128)S(1)} %all_to_all.5.refs_0_, f32[64,1024]{1,0:T(8,128)S(1)} %get-tuple-element.31.refs_1_, f32[64,1024]{1,0:T(8,128)S(1)} %bitcast.11, f32[5,64,1024]{2,1,0:T(8,128)S(1)} %get-tuple-element.32.refs_3_), custom_call_target="tpu_custom_call" | custom-call | tf_op jit(solution)/shard_map/mix/pallas_call | solution.py:404
  (2 shorter events, 0.0 us)
Async XLA Ops:
  1.0 6.5 %collective-permute-start = (f32[4,64,128]{2,1,0:T(8,128)S(1)}, f32[4,64,128]{2,1,0:T(8,128)S(1)}, u32[]{:S(2)}, u32[]{:S(2)}) collective-permute-start(f32[4,64,128]{2,1,0:T(8,128)S(1)} %bitcast.12), channel_id=1, source_target_pairs={{0,8},{8,0},{16,24},{24,16},{1,9},{9,1},{17,25},{25,17},{2,10},{10... | collective-permute-start | bytes 393224 | tf_op jit(solution)/shard_map/ppermute | solution.py:221
  4.0 0.7 %copy-start.3 = (s32[64,5]{0,1:T(8,128)S(1)}, s32[64,5]{0,1:T(8,128)}, u32[]{:S(2)}) copy-start(s32[64,5]{0,1:T(8,128)} %param.17) | copy-start | bytes 3844
  4.7 0.7 %copy-start.5 = (f32[5]{0:T(128)S(1)}, f32[5]{0:T(128)}, u32[]{:S(2)}) copy-start(f32[5]{0:T(128)} %refs_3_.2) | copy-start | bytes 64
  5.3 16.4 %copy-start.1 = (f32[5,2,2,2,8,1024]{5,4,3,2,1,0:T(8,128)S(1)}, f32[5,2,2,2,8,1024]{5,4,3,2,1,0:T(8,128)}, u32[]{:S(2)}) copy-start(f32[5,2,2,2,8,1024]{5,4,3,2,1,0:T(8,128)} %param.14) | copy-start | bytes 3932164
  6.4 15.3 %copy-start = (f32[5,2,2,2,8,1024]{5,4,3,2,1,0:T(8,128)S(1)}, f32[5,2,2,2,8,1024]{5,4,3,2,1,0:T(8,128)}, u32[]{:S(2)}) copy-start(f32[5,2,2,2,8,1024]{5,4,3,2,1,0:T(8,128)} %param.15) | copy-start | bytes 3932164
  6.4 15.3 %copy-start.4 = (s32[5]{0:T(128)S(1)}, s32[5]{0:T(128)}, u32[]{:S(2)}) copy-start(s32[5]{0:T(128)} %refs_9_.1) | copy-start | bytes 64
  6.5 15.2 %copy-start.6 = (s32[64]{0:T(128)S(1)}, s32[64]{0:T(128)}, u32[]{:S(2)}) copy-start(s32[64]{0:T(128)} %refs_3_.3) | copy-start | bytes 772
  6.5 15.2 %copy-start.7 = (f32[4]{0:T(128)S(1)}, f32[4]{0:T(128)}, u32[]{:S(2)}) copy-start(f32[4]{0:T(128)} %refs_4_.1) | copy-start | bytes 52
  6.5 15.2 %copy-start.8 = (f32[2]{0:T(128)S(1)}, f32[2]{0:T(128)}, u32[]{:S(2)}) copy-start(f32[2]{0:T(128)} %refs_5_.1) | copy-start | bytes 28
  6.5 15.2 %copy-start.9 = (f32[2]{0:T(128)S(1)}, f32[2]{0:T(128)}, u32[]{:S(2)}) copy-start(f32[2]{0:T(128)} %refs_6_.1) | copy-start | bytes 28
  6.5 6.0 %collective-permute-start.2 = (f32[4,64,128]{2,1,0:T(8,128)S(1)}, f32[4,64,128]{2,1,0:T(8,128)S(1)}, u32[]{:S(2)}, u32[]{:S(2)}) collective-permute-start(f32[4,64,128]{2,1,0:T(8,128)S(1)} %get-tuple-element.19.block), channel_id=1, source_target_pairs={{0,8},{8,0},{16,24},{24,16},{1,9},{9,1},{17,25},{25,17},{2,10},{10... | collective-permute-start | bytes 393224 | tf_op jit(solution)/shard_map/ppermute | solution.py:221
  7.5 6.7 %collective-permute-start.3 = (f32[4,64,128]{2,1,0:T(8,128)S(1)}, f32[4,64,128]{2,1,0:T(8,128)S(1)}, u32[]{:S(2)}, u32[]{:S(2)}) collective-permute-start(f32[4,64,128]{2,1,0:T(8,128)S(1)} %collective-permute-done._.refs_1_), channel_id=1, source_target_pairs={{0,16},{8,24},{16,0},{24,8},{1,17},{9,25},{17,1},{25,9},{2,18},{10... | collective-permute-start | bytes 393224 | tf_op jit(solution)/shard_map/ppermute | solution.py:221
  9.3 6.0 %collective-permute-start.1 = (f32[4,64,128]{2,1,0:T(8,128)S(1)}, f32[4,64,128]{2,1,0:T(8,128)S(1)}, u32[]{:S(2)}, u32[]{:S(2)}) collective-permute-start(f32[4,64,128]{2,1,0:T(8,128)S(1)} %hold.1), channel_id=1, source_target_pairs={{0,24},{8,16},{16,8},{24,0},{1,25},{9,17},{17,9},{25,1},{2,26},{10... | collective-permute-start | bytes 393224 | tf_op jit(solution)/shard_map/ppermute | solution.py:221
  15.5 1.4 %collective-permute-start.4 = (f32[4,64,128]{2,1,0:T(8,128)S(1)}, f32[4,64,128]{2,1,0:T(8,128)S(1)}, u32[]{:S(2)}, u32[]{:S(2)}) collective-permute-start(f32[4,64,128]{2,1,0:T(8,128)S(1)} %get-tuple-element.24), channel_id=1, source_target_pairs={{0,1},{1,0},{2,3},{3,2},{4,5},{5,4},{6,7},{7,6},{8,9},{9,8},{10,11... | collective-permute-start | bytes 393224 | tf_op jit(solution)/shard_map/ppermute | solution.py:446
  17.0 6.1 %collective-permute-start.5 = (f32[2,64,128]{2,1,0:T(8,128)S(1)}, f32[2,64,128]{2,1,0:T(8,128)S(1)}, u32[]{:S(2)}, u32[]{:S(2)}) collective-permute-start(f32[2,64,128]{2,1,0:T(8,128)S(1)} %get-tuple-element.25), channel_id=1, source_target_pairs={{0,2},{1,3},{2,0},{3,1},{4,6},{5,7},{6,4},{7,5},{8,10},{9,11},{10,... | collective-permute-start | bytes 196616 | tf_op jit(solution)/shard_map/ppermute | solution.py:446
  19.1 7.5 %collective-permute-start.6 = (f32[2,64,128]{2,1,0:T(8,128)S(1)}, f32[2,64,128]{2,1,0:T(8,128)S(1)}, u32[]{:S(2)}, u32[]{:S(2)}) collective-permute-start(f32[2,64,128]{2,1,0:T(8,128)S(1)} %get-tuple-element.26), channel_id=1, source_target_pairs={{0,4},{1,5},{2,6},{3,7},{4,0},{5,1},{6,2},{7,3},{8,12},{9,13},{10,... | collective-permute-start | bytes 196616 | tf_op jit(solution)/shard_map/ppermute | solution.py:446
  21.7 6.2 %collective-permute-start.7 = (f32[2,64,128]{2,1,0:T(8,128)S(1)}, f32[2,64,128]{2,1,0:T(8,128)S(1)}, u32[]{:S(2)}, u32[]{:S(2)}) collective-permute-start(f32[2,64,128]{2,1,0:T(8,128)S(1)} %get-tuple-element.27), channel_id=1, source_target_pairs={{0,6},{1,7},{2,4},{3,5},{4,2},{5,3},{6,0},{7,1},{8,14},{9,15},{10,... | collective-permute-start | bytes 196616 | tf_op jit(solution)/shard_map/ppermute | solution.py:446
  21.7 6.1 %copy-start.2 = (f32[2,2,2,8,1024]{4,3,2,1,0:T(8,128)S(1)}, f32[2,2,2,8,1024]{4,3,2,1,0:T(8,128)}, u32[]{:S(2)}) copy-start(f32[2,2,2,8,1024]{4,3,2,1,0:T(8,128)} %param.13) | copy-start | bytes 786436
  21.8 6.1 %copy-start.10 = (s32[2]{0:T(128)S(1)}, s32[2]{0:T(128)}, u32[]{:S(2)}) copy-start(s32[2]{0:T(128)} %refs_10_.1) | copy-start | bytes 28

commit v7 on v6

--- a/solution.py
+++ b/solution.py
@@ -15,8 +15,6 @@
 SMEM = pl.BlockSpec(memory_space=pltpu.SMEM)
 PARAMS = pltpu.CompilerParams(vmem_limit_bytes=16 * 1024 * 1024)
 
-NEAR, FAR = 0, 1
-
 PAIRS = [(i, j) for i in range(1, HIST + 1) for j in range(i, HIST + 1)]
 SPOTS = {pair: v for v, pair in enumerate(PAIRS)}
 for _j in range(HIST + 1):
@@ -34,14 +32,13 @@
 
 
 def prepare_kernel(total_k, *refs):
-    *blocks, neighbour_hbm, weight_hbm, stencil_hi, stencil_lo, part, late, neighbour, weight, done = refs
+    *blocks, neighbour_hbm, weight_hbm, stencil_hi, stencil_lo, part, neighbour, weight, done = refs
     fetches = [
         pltpu.make_async_copy(neighbour_hbm, neighbour, done.at[0]),
         pltpu.make_async_copy(weight_hbm, weight, done.at[1]),
     ]
     for fetch in fetches:
         fetch.start()
-    late[...] = blocks[0][...]
     _, group_len, slice_len = blocks[0].shape
     group_id = lax.axis_index("kgrp")
     parts = lax.axis_size("energy")
@@ -90,10 +87,9 @@
             sides,
             sides,
             jax.ShapeDtypeStruct((comps, group_len, slice_len), jnp.float32),
-            jax.ShapeDtypeStruct(blocks[0].shape, jnp.float32),
         ),
         in_specs=[VMEM] * len(blocks) + [pl.BlockSpec(memory_space=pltpu.HBM)] * 2,
-        out_specs=(VMEM,) * 4,
+        out_specs=(VMEM,) * 3,
         scratch_shapes=[
             pltpu.VMEM(neighbour.shape[::-1], jnp.int32),
             pltpu.SMEM(weight.shape, jnp.float32),
@@ -107,44 +103,55 @@
     )(*blocks, jnp.transpose(neighbour), weight)
 
 
-def smeared_pairs(side, first, block, stencil_hi, stencil_lo, part):
-    comps, group_len, slice_len = block.shape
-    at = slice(side * group_len, (side + 1) * group_len)
+def smeared_pairs(first, sides, stencil_hi, stencil_lo, part):
+    blocks = [block for block in sides if block is not None]
+    comps, group_len, slice_len = blocks[0].shape
+    start = 0 if sides[0] is not None else group_len
+    at = slice(start, start + len(blocks) * group_len)
     stencil = (stencil_hi[:, at], stencil_lo[:, at])
     for c in range(0, comps, 2):
-        result = product(stencil, split(jnp.concatenate([block[c], block[c + 1]], axis=1)))
+        stacked = [jnp.concatenate([block[c], block[c + 1]], axis=1) for block in blocks]
+        result = product(stencil, split(jnp.concatenate(stacked, axis=0)))
         for p in range(2):
             yield c + p, part[first + c + p] + result[:, p * slice_len : (p + 1) * slice_len]
 
 
-def add_side_kernel(side, first, *refs):
-    *blocks, stencil_hi, stencil_lo, part, out = refs
-    done = 0
-    for block in blocks:
-        for c, smeared in smeared_pairs(side, first + done, block, stencil_hi, stencil_lo, part):
-            out[done + c] = smeared
-        done += block.shape[0]
-
-
-def add_side(side, first, blocks, stencil_hi, stencil_lo, part):
-    shape = (sum(block.shape[0] for block in blocks),) + part.shape[1:]
-    return pl.pallas_call(
-        lambda *refs: add_side_kernel(side, first, *refs),
-        out_shape=jax.ShapeDtypeStruct(shape, jnp.float32),
-        in_specs=[VMEM] * (len(blocks) + 3),
+def with_sides(kernel, sides):
+    def body(*refs):
+        refs = list(refs)
+        kernel([None if side is None else refs.pop(0) for side in sides], *refs)
+
+    return body
+
+
+def smear_cost(blocks):
+    size = sum(block.size for block in blocks)
+    return pl.CostEstimate(
+        flops=6 * size * blocks[0].shape[1], bytes_accessed=12 * size, transcendentals=0
+    )
+
+
+def add_sides(first, sides, stencil_hi, stencil_lo, part, after):
+    def kernel(sides, stencil_hi, stencil_lo, part, *refs):
+        for c, smeared in smeared_pairs(first, sides, stencil_hi, stencil_lo, part):
+            refs[-1][c] = smeared
+
+    blocks = [block for block in sides if block is not None]
+    return pl.pallas_call(
+        with_sides(kernel, sides),
+        out_shape=jax.ShapeDtypeStruct(blocks[0].shape, jnp.float32),
+        in_specs=[VMEM] * (len(blocks) + 3) + [pl.BlockSpec(memory_space=pl.ANY)] * len(after),
         out_specs=VMEM,
         compiler_params=PARAMS,
-        cost_estimate=pl.CostEstimate(
-            flops=6 * part.size * part.shape[1], bytes_accessed=12 * part.size, transcendentals=0
-        ),
-        name="add_side",
-    )(*blocks, stencil_hi, stencil_lo, part)
-
-
-def finish_kernel(side, block, stencil_hi, stencil_lo, part, *refs):
+        cost_estimate=smear_cost(blocks),
+        name="add_sides",
+    )(*blocks, stencil_hi, stencil_lo, part, *after)
+
+
+def finish_kernel(sides, stencil_hi, stencil_lo, part, *refs):
     *ready, kept, given = refs
     chips, height, _ = kept.shape
-    comps = part.shape[0]
+    comps = part.shape[0] + sum(block.shape[0] for block in ready)
     rows = height // comps
 
     def place(c, smeared):
@@ -152,26 +159,26 @@
             out = given if m % 2 else kept
             out[m // 2, c * rows : (c + 1) * rows, :] = smeared[m * rows : (m + 1) * rows]
 
-    for c, smeared in smeared_pairs(side, 0, block, stencil_hi, stencil_lo, part):
+    for c, smeared in smeared_pairs(0, sides, stencil_hi, stencil_lo, part):
         place(c, smeared)
-    for c in range(block.shape[0], comps):
-        place(c, ready[0][c - block.shape[0]])
-
-
-def finish(side, block, stencil_hi, stencil_lo, part, ready, parts):
-    comps, group_len, slice_len = part.shape
+    for c in range(part.shape[0], comps):
+        place(c, ready[0][c - part.shape[0]])
+
+
+def finish(sides, stencil_hi, stencil_lo, part, ready, parts):
+    blocks = [block for block in sides if block is not None]
+    _, group_len, slice_len = part.shape
+    comps = part.shape[0] + sum(block.shape[0] for block in ready)
     shape = (parts // 2, comps * group_len // parts, slice_len)
     return pl.pallas_call(
-        lambda *refs: finish_kernel(side, *refs),
+        with_sides(finish_kernel, sides),
         out_shape=[jax.ShapeDtypeStruct(shape, jnp.float32)] * 2,
-        in_specs=[VMEM] * (len(ready) + 4),
+        in_specs=[VMEM] * (len(blocks) + len(ready) + 3),
         out_specs=[VMEM] * 2,
         compiler_params=PARAMS,
-        cost_estimate=pl.CostEstimate(
-            flops=6 * part.size * group_len, bytes_accessed=12 * part.size, transcendentals=0
-        ),
+        cost_estimate=smear_cost(blocks),
         name="finish",
-    )(block, stencil_hi, stencil_lo, part, *ready)
+    )(*blocks, stencil_hi, stencil_lo, part, *ready)
 
 
 def join_kernel(own, swapped, *out):
@@ -211,19 +218,22 @@
     )(block, until)
 
 
-def exchange(own, neighbour, weight, groups):
+def smear(own, neighbour, weight, groups, parts):
     total_k = groups * own.shape[1]
     if not paired(groups):
         forward = [(i, (i + 1) % groups) for i in range(groups)]
         backward = [(target, source) for source, target in forward]
         near, far = lax.ppermute(own, "kgrp", backward), lax.ppermute(own, "kgrp", forward)
-        return [near], [far], prepare([own], neighbour, weight, total_k)[:3]
+        return finish((near, far), *prepare([own], neighbour, weight, total_k), [], parts)
     across = lambda block, flip: lax.ppermute(block, "kgrp", [(i, i ^ flip) for i in range(groups)])
     half = own.shape[0] // 2
-    blocks = own[:half], own[half:]
-    head = across(blocks[1], 1)
-    *made, late = prepare(blocks, neighbour, weight, total_k)
-    return [across(late, 1), head], [across(hold(late, head), 3), across(head, 2)], made
+    tail, head = own[:half], own[half:]
+    near_head, far_tail = across(head, 1), across(tail, 3)
+    far_head, near_tail = across(near_head, 2), across(hold(tail, near_head), 1)
+    hi, lo, part = prepare([tail, head], neighbour, weight, total_k)
+    tail_part = add_sides(0, (None, far_tail), hi, lo, part, [])
+    head_part = add_sides(half, (near_head, far_head), hi, lo, part, [tail_part])
+    return finish((near_tail, None), hi, lo, tail_part, [head_part], parts)
 
 
 def spread(values, shape):
@@ -438,11 +448,7 @@
     old_res = past_residuals.reshape(HIST, height, width)
     scalars = (slot_order, momentum_class, acoustic_coupling, optical_coupling, occupation)
     aged, old_line, gains = history(old_in, old_res, scalars, rows)
-    near, far, (stencil_hi, stencil_lo, smeared) = exchange(own, neighbour, stencil_weight, groups)
-    smeared = add_side(NEAR, 0, near, stencil_hi, stencil_lo, smeared)
-    direct, *forwarded = far
-    ready = [add_side(FAR, direct.shape[0], forwarded, stencil_hi, stencil_lo, smeared)] if forwarded else []
-    kept, given = finish(FAR, direct, stencil_hi, stencil_lo, smeared, ready, parts)
+    kept, given = smear(own, neighbour, stencil_weight, groups, parts)
     meet = lambda block, m: lax.ppermute(block, "energy", [(e, e ^ m) for e in range(parts)])
     swapped = meet(given, 1)
     smeared = [meet(block, 2 * chip) for chip, block in enumerate(join(kept, swapped), 1)]

time: 40.7 us -> 40 us (0.983)
  waiting for transfers between devices: 10.9 us -> 8.75 us
  starting transfers between devices: 11.3 us -> 13.1 us
    ppermute x4, starting transfers between devices: 6.5 us -> 8.63 us  [smear(): lax.ppermute(block, 'kgrp', [(i, i ^ flip) for i in range(groups)])]
    ppermute x4, waiting for transfers between devices: 4.79 us -> 2.87 us  [smear(): lax.ppermute(block, 'kgrp', [(i, i ^ flip) for i in range(groups)])]
  transfers between devices with their start and end apart: 8 -> 8, of which waited for: 7 -> 5; matrix products, arithmetic and copies ran while one was open for 0% -> 0% of each run, Pallas kernels for 7% -> 7%
where the time goes in v7:
time: 40 us; the launch traced here: 39.8 us
  starting transfers between devices  13.1 us (33%)
  blocking collectives  10.2 us (25%)
  waiting for transfers between devices  8.75 us (22%)
  Pallas kernels  5.08 us (13%)
  local copies, waits for them, and re-layouts  2.37 us (6%)
    all_to_all x1, blocking collectives, per_device(): lax.all_to_all(lines, ('kgrp', 'energy'), split_axis=0, concat_axis=0, ti...  10.2 us
    ppermute x4, starting transfers between devices, smear(): lax.ppermute(block, 'kgrp', [(i, i ^ flip) for i in range(groups)])  8.63 us
    ppermute x4, waiting for transfers between devices, per_device(): lax.ppermute(block, 'energy', [(e, e ^ m) for e in range(parts)])  5.88 us
    ppermute x4, starting transfers between devices, per_device(): lax.ppermute(block, 'energy', [(e, e ^ m) for e in range(parts)])  4.52 us
    ppermute x4, waiting for transfers between devices, smear(): lax.ppermute(block, 'kgrp', [(i, i ^ flip) for i in range(groups)])  2.87 us
    unnamed x22, local copies, waits for them, and re-layouts  1.39 us
    pallas_call x1, Pallas kernels, history(): pl.pallas_call(lambda *refs: history_kernel(rows, *refs), out_shape=(jax....  1.31 us
    pallas_call x1, Pallas kernels, prepare(): pl.pallas_call(lambda *refs: prepare_kernel(total_k, *refs), out_shape=(s...  1.08 us
  transfers between devices with their start and end apart: 8, of which 5 were waited for; matrix products, arithmetic and copies ran while one was open for 0% of the time, Pallas kernels for 7%

profile of v7, /device:TPU:0, one launch (start us, length us, event | category | flops | bytes accessed | tf_op | source)
XLA Modules:
  0.0 39.8 jit_solution(13441269262020763726)
XLA Ops:
  0.0 1.0 %fusion = (f32[1,2,2,64,128]{4,3,2,1,0:T(8,128)S(1)}, f32[1,2,2,64,128]{4,3,2,1,0:T(8,128)S(1)}) fusion(f32[2,2,2,64,128]{4,3,2,1,0:T(8,128)} %param.12), kind=kLoop, calls=%fused_computation | loop fusion | bytes 524288 | tf_op jit(solution)/shard_map/slice | solution.py:230
  1.0 3.0 %collective-permute-start = (f32[4,64,128]{2,1,0:T(8,128)S(1)}, f32[4,64,128]{2,1,0:T(8,128)S(1)}, u32[]{:S(2)}, u32[]{:S(2)}) collective-permute-start(f32[4,64,128]{2,1,0:T(8,128)S(1)} %bitcast.15), channel_id=1, source_target_pairs={{0,8},{8,0},{16,24},{24,16},{1,9},{9,1},{17,25},{25,17},{2,10},{10... | collective-permute-start | bytes 393224 | tf_op jit(solution)/shard_map/ppermute | solution.py:228
  4.0 0.0 copy-start.8
  4.0 0.0 copy-start.9
  4.0 0.0 copy-start.4
  4.0 0.0 copy-start.6
  4.0 0.0 copy-start.7
  4.0 0.0 copy-start
  4.0 0.0 copy-start.1
  4.0 1.6 %collective-permute-start.2 = (f32[4,64,128]{2,1,0:T(8,128)S(1)}, f32[4,64,128]{2,1,0:T(8,128)S(1)}, u32[]{:S(2)}, u32[]{:S(2)}) collective-permute-start(f32[4,64,128]{2,1,0:T(8,128)S(1)} %bitcast.10), channel_id=1, source_target_pairs={{0,24},{8,16},{16,8},{24,0},{1,25},{9,17},{17,9},{25,1},{2,26},{10... | collective-permute-start | bytes 393224 | tf_op jit(solution)/shard_map/ppermute | solution.py:228
  5.6 2.3 %collective-permute-done._.refs_0_ = f32[4,64,128]{2,1,0:T(8,128)S(1)} collective-permute-done((f32[4,64,128]{2,1,0:T(8,128)S(1)}, f32[4,64,128]{2,1,0:T(8,128)S(1)}, u32[]{:S(2)}, u32[]{:S(2)}) %collective-permute-start) | collective-permute-done | bytes 131104 | tf_op jit(solution)/shard_map/ppermute | solution.py:228
  7.9 2.5 %collective-permute-start.3 = (f32[4,64,128]{2,1,0:T(8,128)S(1)}, f32[4,64,128]{2,1,0:T(8,128)S(1)}, u32[]{:S(2)}, u32[]{:S(2)}) collective-permute-start(f32[4,64,128]{2,1,0:T(8,128)S(1)} %collective-permute-done._.refs_0_), channel_id=1, source_target_pairs={{0,16},{8,24},{16,0},{24,8},{1,17},{9,25},{17,1},{25,9},{2,18},{10... | collective-permute-start | bytes 393224 | tf_op jit(solution)/shard_map/ppermute | solution.py:228
  10.4 1.6 %collective-permute-start.1 = (f32[4,64,128]{2,1,0:T(8,128)S(1)}, f32[4,64,128]{2,1,0:T(8,128)S(1)}, u32[]{:S(2)}, u32[]{:S(2)}) collective-permute-start(f32[4,64,128]{2,1,0:T(8,128)S(1)} %hold.1), channel_id=1, source_target_pairs={{0,8},{8,0},{16,24},{24,16},{1,9},{9,1},{17,25},{25,17},{2,10},{10... | collective-permute-start | bytes 393224 | tf_op jit(solution)/shard_map/ppermute | solution.py:228
  12.0 0.0 copy-start.3
  12.0 0.7 %copy-done.3 = s32[64,5]{0,1:T(8,128)S(1)} copy-done((s32[64,5]{0,1:T(8,128)S(1)}, s32[64,5]{0,1:T(8,128)}, u32[]{:S(2)}) %copy-start.3) | copy-done | bytes 1304
  12.7 0.0 copy-start.5
  12.7 0.7 %copy-done.5 = f32[5]{0:T(128)S(1)} copy-done((f32[5]{0:T(128)S(1)}, f32[5]{0:T(128)}, u32[]{:S(2)}) %copy-start.5) | copy-done | bytes 44
  13.3 1.1 %prepare.1 = (bf16[64,128]{1,0:T(8,128)(2,1)S(1)}, bf16[64,128]{1,0:T(8,128)(2,1)S(1)}, f32[8,64,128]{2,1,0:T(8,128)S(1)}) custom-call(f32[4,64,128]{2,1,0:T(8,128)S(1)} %bitcast.12, f32[4,64,128]{2,1,0:T(8,128)S(1)} %bitcast.16, s32[5,64]{1,0:T(8,128)S(1)} %bitcast.17, f32[5]{0:T(128)S(1)} %copy-done.5), custom_call_target="tpu_custom_call" | custom-call | flops 25165824 | bytes 524288 | tf_op jit(solution)/shard_map/prepare/pallas_call | solution.py:84
  14.4 0.0 collective-permute-done.2.refs_0_
  14.4 0.2 add_sides.2.refs_5_.refs_3_
  14.7 0.0 collective-permute-done.3.refs_1_
  14.7 0.2 add_sides.3.refs_4_
  14.9 0.6 %collective-permute-done.1.refs_0_ = f32[4,64,128]{2,1,0:T(8,128)S(1)} collective-permute-done((f32[4,64,128]{2,1,0:T(8,128)S(1)}, f32[4,64,128]{2,1,0:T(8,128)S(1)}, u32[]{:S(2)}, u32[]{:S(2)}) %collective-permute-start.1) | collective-permute-done | bytes 131104 | tf_op jit(solution)/shard_map/ppermute | solution.py:228
  15.5 0.2 finish.1
  15.6 0.1 collective-permute-start.4
  15.7 1.3 %collective-permute-done.4.swapped.refs_1_ = f32[4,64,128]{2,1,0:T(8,128)S(1)} collective-permute-done((f32[4,64,128]{2,1,0:T(8,128)S(1)}, f32[4,64,128]{2,1,0:T(8,128)S(1)}, u32[]{:S(2)}, u32[]{:S(2)}) %collective-permute-start.4) | collective-permute-done | bytes 131104 | tf_op jit(solution)/shard_map/ppermute | solution.py:452
  17.1 1.6 %collective-permute-start.5 = (f32[2,64,128]{2,1,0:T(8,128)S(1)}, f32[2,64,128]{2,1,0:T(8,128)S(1)}, u32[]{:S(2)}, u32[]{:S(2)}) collective-permute-start(f32[2,64,128]{2,1,0:T(8,128)S(1)} %get-tuple-element.23), channel_id=1, source_target_pairs={{0,2},{1,3},{2,0},{3,1},{4,6},{5,7},{6,4},{7,5},{8,10},{9,11},{10,... | collective-permute-start | bytes 196616 | tf_op jit(solution)/shard_map/ppermute | solution.py:452
  18.7 2.6 %collective-permute-start.6 = (f32[2,64,128]{2,1,0:T(8,128)S(1)}, f32[2,64,128]{2,1,0:T(8,128)S(1)}, u32[]{:S(2)}, u32[]{:S(2)}) collective-permute-start(f32[2,64,128]{2,1,0:T(8,128)S(1)} %get-tuple-element.24), channel_id=1, source_target_pairs={{0,4},{1,5},{2,6},{3,7},{4,0},{5,1},{6,2},{7,3},{8,12},{9,13},{10,... | collective-permute-start | bytes 196616 | tf_op jit(solution)/shard_map/ppermute | solution.py:452
  21.3 0.2 collective-permute-start.7
  21.5 0.0 copy-done.8
  21.5 0.0 copy-done.9
  21.5 0.0 copy-done.4
  21.5 0.0 copy-done.6
  21.5 0.0 copy-done.7
  21.6 0.0 copy-done
  21.6 0.0 copy-done.1
  21.6 0.0 copy-start.2
  21.6 0.0 copy-start.10
  21.6 1.3 %history.1 = (f32[5,64,1024]{2,1,0:T(8,128)S(1)}, f32[1,128]{1,0:T(1,128)S(1)}, f32[5,8,128]{2,1,0:T(8,128)S(1)}) custom-call(f32[5,64,1024]{2,1,0:T(8,128)S(1)} %bitcast.9, f32[5,64,1024]{2,1,0:T(8,128)S(1)} %bitcast.7, s32[5]{0:T(128)S(1)} %copy-done.4, s32[64]{0:T(128)S(1)} %copy-done.6, f32[4]{0:T(128)S(1)} %copy-done.7, f32[2]{0:T(128)S(1)} %copy-done.8, ...), custom_call_target="tpu_custom_call" | custom-call | flops 2621440 | bytes 3932160 | tf_op jit(solution)/shard_map/history/pallas_call | solution.py:282
  22.9 0.0 collective-permute-done.5.refs_2_
  22.9 3.3 %collective-permute-done.6.refs_3_ = f32[2,64,128]{2,1,0:T(8,128)S(1)} collective-permute-done((f32[2,64,128]{2,1,0:T(8,128)S(1)}, f32[2,64,128]{2,1,0:T(8,128)S(1)}, u32[]{:S(2)}, u32[]{:S(2)}) %collective-permute-start.6) | collective-permute-done | bytes 65568 | tf_op jit(solution)/shard_map/ppermute | solution.py:452
  26.3 1.2 %collective-permute-done.7.refs_4_ = f32[2,64,128]{2,1,0:T(8,128)S(1)} collective-permute-done((f32[2,64,128]{2,1,0:T(8,128)S(1)}, f32[2,64,128]{2,1,0:T(8,128)S(1)}, u32[]{:S(2)}, u32[]{:S(2)}) %collective-permute-start.7) | collective-permute-done | bytes 65568 | tf_op jit(solution)/shard_map/ppermute | solution.py:452
  27.5 0.0 copy-done.2
  27.5 0.0 copy-done.10
  27.5 1.0 %residual.1 = (f32[64,1024]{1,0:T(8,128)S(1)}, f32[32,1,128]{2,1,0:T(1,128)S(1)}) custom-call(f32[4,64,128]{2,1,0:T(8,128)S(1)} %get-tuple-element.21.own.refs_0_, f32[4,64,128]{2,1,0:T(8,128)S(1)} %collective-permute-done.4.swapped.refs_1_, f32[2,64,128]{2,1,0:T(8,128)S(1)} %collective-permute-done.5.refs_2_, ...), custom_call_target="tpu_custom_call" | custom-call | tf_op jit(solution)/shard_map/residual/pallas_call | solution.py:342
  28.5 10.2 %all_to_all.5.refs_0_ = f32[32,1,128]{2,1,0:T(1,128)S(1)} all-to-all(f32[32,1,128]{2,1,0:T(1,128)S(1)} %get-tuple-element.28), channel_id=1, replica_groups=mesh['kgrp'=4,'energy'=8] {'kgrp','energy'}, dimensions={0} | all-to-all | bytes 32768 | tf_op jit(solution)/shard_map/all_to_all | solution.py:458
  38.8 1.0 %mix.1 = f32[64,1024]{1,0:T(8,128)} custom-call(f32[32,1,128]{2,1,0:T(1,128)S(1)} %all_to_all.5.refs_0_, f32[64,1024]{1,0:T(8,128)S(1)} %get-tuple-element.29.refs_1_, f32[64,1024]{1,0:T(8,128)S(1)} %bitcast.14, f32[5,64,1024]{2,1,0:T(8,128)S(1)} %get-tuple-element.30.refs_3_), custom_call_target="tpu_custom_call" | custom-call | tf_op jit(solution)/shard_map/mix/pallas_call | solution.py:414
  (2 shorter events, 0.0 us)
Async XLA Ops:
  1.0 6.9 %collective-permute-start = (f32[4,64,128]{2,1,0:T(8,128)S(1)}, f32[4,64,128]{2,1,0:T(8,128)S(1)}, u32[]{:S(2)}, u32[]{:S(2)}) collective-permute-start(f32[4,64,128]{2,1,0:T(8,128)S(1)} %bitcast.15), channel_id=1, source_target_pairs={{0,8},{8,0},{16,24},{24,16},{1,9},{9,1},{17,25},{25,17},{2,10},{10... | collective-permute-start | bytes 393224 | tf_op jit(solution)/shard_map/ppermute | solution.py:228
  4.0 17.5 %copy-start.8 = (f32[2]{0:T(128)S(1)}, f32[2]{0:T(128)}, u32[]{:S(2)}) copy-start(f32[2]{0:T(128)} %refs_5_.1) | copy-start | bytes 28
  4.0 17.5 %copy-start.9 = (f32[2]{0:T(128)S(1)}, f32[2]{0:T(128)}, u32[]{:S(2)}) copy-start(f32[2]{0:T(128)} %refs_6_.1) | copy-start | bytes 28
  4.0 17.5 %copy-start.4 = (s32[5]{0:T(128)S(1)}, s32[5]{0:T(128)}, u32[]{:S(2)}) copy-start(s32[5]{0:T(128)} %refs_9_.1) | copy-start | bytes 64
  4.0 17.5 %copy-start.6 = (s32[64]{0:T(128)S(1)}, s32[64]{0:T(128)}, u32[]{:S(2)}) copy-start(s32[64]{0:T(128)} %refs_3_.3) | copy-start | bytes 772
  4.0 17.5 %copy-start.7 = (f32[4]{0:T(128)S(1)}, f32[4]{0:T(128)}, u32[]{:S(2)}) copy-start(f32[4]{0:T(128)} %refs_4_.1) | copy-start | bytes 52
  4.0 17.5 %copy-start = (f32[5,2,2,2,8,1024]{5,4,3,2,1,0:T(8,128)S(1)}, f32[5,2,2,2,8,1024]{5,4,3,2,1,0:T(8,128)}, u32[]{:S(2)}) copy-start(f32[5,2,2,2,8,1024]{5,4,3,2,1,0:T(8,128)} %param.15) | copy-start | bytes 3932164
  4.0 17.5 %copy-start.1 = (f32[5,2,2,2,8,1024]{5,4,3,2,1,0:T(8,128)S(1)}, f32[5,2,2,2,8,1024]{5,4,3,2,1,0:T(8,128)}, u32[]{:S(2)}) copy-start(f32[5,2,2,2,8,1024]{5,4,3,2,1,0:T(8,128)} %param.14) | copy-start | bytes 3932164
  4.0 10.4 %collective-permute-start.2 = (f32[4,64,128]{2,1,0:T(8,128)S(1)}, f32[4,64,128]{2,1,0:T(8,128)S(1)}, u32[]{:S(2)}, u32[]{:S(2)}) collective-permute-start(f32[4,64,128]{2,1,0:T(8,128)S(1)} %bitcast.10), channel_id=1, source_target_pairs={{0,24},{8,16},{16,8},{24,0},{1,25},{9,17},{17,9},{25,1},{2,26},{10... | collective-permute-start | bytes 393224 | tf_op jit(solution)/shard_map/ppermute | solution.py:228
  7.9 6.8 %collective-permute-start.3 = (f32[4,64,128]{2,1,0:T(8,128)S(1)}, f32[4,64,128]{2,1,0:T(8,128)S(1)}, u32[]{:S(2)}, u32[]{:S(2)}) collective-permute-start(f32[4,64,128]{2,1,0:T(8,128)S(1)} %collective-permute-done._.refs_0_), channel_id=1, source_target_pairs={{0,16},{8,24},{16,0},{24,8},{1,17},{9,25},{17,1},{25,9},{2,18},{10... | collective-permute-start | bytes 393224 | tf_op jit(solution)/shard_map/ppermute | solution.py:228
  10.4 5.0 %collective-permute-start.1 = (f32[4,64,128]{2,1,0:T(8,128)S(1)}, f32[4,64,128]{2,1,0:T(8,128)S(1)}, u32[]{:S(2)}, u32[]{:S(2)}) collective-permute-start(f32[4,64,128]{2,1,0:T(8,128)S(1)} %hold.1), channel_id=1, source_target_pairs={{0,8},{8,0},{16,24},{24,16},{1,9},{9,1},{17,25},{25,17},{2,10},{10... | collective-permute-start | bytes 393224 | tf_op jit(solution)/shard_map/ppermute | solution.py:228
  12.0 0.7 %copy-start.3 = (s32[64,5]{0,1:T(8,128)S(1)}, s32[64,5]{0,1:T(8,128)}, u32[]{:S(2)}) copy-start(s32[64,5]{0,1:T(8,128)} %param.17) | copy-start | bytes 3844
  12.7 0.7 %copy-start.5 = (f32[5]{0:T(128)S(1)}, f32[5]{0:T(128)}, u32[]{:S(2)}) copy-start(f32[5]{0:T(128)} %refs_3_.2) | copy-start | bytes 64
  15.6 1.4 %collective-permute-start.4 = (f32[4,64,128]{2,1,0:T(8,128)S(1)}, f32[4,64,128]{2,1,0:T(8,128)S(1)}, u32[]{:S(2)}, u32[]{:S(2)}) collective-permute-start(f32[4,64,128]{2,1,0:T(8,128)S(1)} %get-tuple-element.22), channel_id=1, source_target_pairs={{0,1},{1,0},{2,3},{3,2},{4,5},{5,4},{6,7},{7,6},{8,9},{9,8},{10,11... | collective-permute-start | bytes 393224 | tf_op jit(solution)/shard_map/ppermute | solution.py:452
  17.1 5.8 %collective-permute-start.5 = (f32[2,64,128]{2,1,0:T(8,128)S(1)}, f32[2,64,128]{2,1,0:T(8,128)S(1)}, u32[]{:S(2)}, u32[]{:S(2)}) collective-permute-start(f32[2,64,128]{2,1,0:T(8,128)S(1)} %get-tuple-element.23), channel_id=1, source_target_pairs={{0,2},{1,3},{2,0},{3,1},{4,6},{5,7},{6,4},{7,5},{8,10},{9,11},{10,... | collective-permute-start | bytes 196616 | tf_op jit(solution)/shard_map/ppermute | solution.py:452
  18.7 7.5 %collective-permute-start.6 = (f32[2,64,128]{2,1,0:T(8,128)S(1)}, f32[2,64,128]{2,1,0:T(8,128)S(1)}, u32[]{:S(2)}, u32[]{:S(2)}) collective-permute-start(f32[2,64,128]{2,1,0:T(8,128)S(1)} %get-tuple-element.24), channel_id=1, source_target_pairs={{0,4},{1,5},{2,6},{3,7},{4,0},{5,1},{6,2},{7,3},{8,12},{9,13},{10,... | collective-permute-start | bytes 196616 | tf_op jit(solution)/shard_map/ppermute | solution.py:452
  21.3 6.2 %collective-permute-start.7 = (f32[2,64,128]{2,1,0:T(8,128)S(1)}, f32[2,64,128]{2,1,0:T(8,128)S(1)}, u32[]{:S(2)}, u32[]{:S(2)}) collective-permute-start(f32[2,64,128]{2,1,0:T(8,128)S(1)} %get-tuple-element.25), channel_id=1, source_target_pairs={{0,6},{1,7},{2,4},{3,5},{4,2},{5,3},{6,0},{7,1},{8,14},{9,15},{10,... | collective-permute-start | bytes 196616 | tf_op jit(solution)/shard_map/ppermute | solution.py:452
  21.6 5.9 %copy-start.2 = (f32[2,2,2,8,1024]{4,3,2,1,0:T(8,128)S(1)}, f32[2,2,2,8,1024]{4,3,2,1,0:T(8,128)}, u32[]{:S(2)}) copy-start(f32[2,2,2,8,1024]{4,3,2,1,0:T(8,128)} %param.13) | copy-start | bytes 786436
  21.6 5.9 %copy-start.10 = (s32[2]{0:T(128)S(1)}, s32[2]{0:T(128)}, u32[]{:S(2)}) copy-start(s32[2]{0:T(128)} %refs_10_.1) | copy-start | bytes 28

commit v8 on v7

--- a/solution.py
+++ b/solution.py
@@ -32,13 +32,14 @@
 
 
 def prepare_kernel(total_k, *refs):
-    *blocks, neighbour_hbm, weight_hbm, stencil_hi, stencil_lo, part, neighbour, weight, done = refs
+    *blocks, neighbour_hbm, weight_hbm, stencil_hi, stencil_lo, part, late, neighbour, weight, done = refs
     fetches = [
         pltpu.make_async_copy(neighbour_hbm, neighbour, done.at[0]),
         pltpu.make_async_copy(weight_hbm, weight, done.at[1]),
     ]
     for fetch in fetches:
         fetch.start()
+    late[...] = blocks[-1][...]
     _, group_len, slice_len = blocks[0].shape
     group_id = lax.axis_index("kgrp")
     parts = lax.axis_size("energy")
@@ -87,9 +88,10 @@
             sides,
             sides,
             jax.ShapeDtypeStruct((comps, group_len, slice_len), jnp.float32),
+            jax.ShapeDtypeStruct(blocks[-1].shape, jnp.float32),
         ),
         in_specs=[VMEM] * len(blocks) + [pl.BlockSpec(memory_space=pltpu.HBM)] * 2,
-        out_specs=(VMEM,) * 3,
+        out_specs=(VMEM,) * 4,
         scratch_shapes=[
             pltpu.VMEM(neighbour.shape[::-1], jnp.int32),
             pltpu.SMEM(weight.shape, jnp.float32),
@@ -151,7 +153,7 @@
 def finish_kernel(sides, stencil_hi, stencil_lo, part, *refs):
     *ready, kept, given = refs
     chips, height, _ = kept.shape
-    comps = part.shape[0] + sum(block.shape[0] for block in ready)
+    comps = part.shape[0]
     rows = height // comps
 
     def place(c, smeared):
@@ -159,16 +161,18 @@
             out = given if m % 2 else kept
             out[m // 2, c * rows : (c + 1) * rows, :] = smeared[m * rows : (m + 1) * rows]
 
+    first = 0
     for c, smeared in smeared_pairs(0, sides, stencil_hi, stencil_lo, part):
         place(c, smeared)
-    for c in range(part.shape[0], comps):
-        place(c, ready[0][c - part.shape[0]])
+        first = c + 1
+    for block in ready:
+        for c in range(block.shape[0]):
+            place(first + c, block[c])
 
 
 def finish(sides, stencil_hi, stencil_lo, part, ready, parts):
     blocks = [block for block in sides if block is not None]
-    _, group_len, slice_len = part.shape
-    comps = part.shape[0] + sum(block.shape[0] for block in ready)
+    comps, group_len, slice_len = part.shape
     shape = (parts // 2, comps * group_len // parts, slice_len)
     return pl.pallas_call(
         with_sides(finish_kernel, sides),
@@ -224,16 +228,15 @@
         forward = [(i, (i + 1) % groups) for i in range(groups)]
         backward = [(target, source) for source, target in forward]
         near, far = lax.ppermute(own, "kgrp", backward), lax.ppermute(own, "kgrp", forward)
-        return finish((near, far), *prepare([own], neighbour, weight, total_k), [], parts)
+        return finish((near, far), *prepare([own], neighbour, weight, total_k)[:3], [], parts)
     across = lambda block, flip: lax.ppermute(block, "kgrp", [(i, i ^ flip) for i in range(groups)])
     half = own.shape[0] // 2
-    tail, head = own[:half], own[half:]
+    head, tail = own[:half], own[half:]
     near_head, far_tail = across(head, 1), across(tail, 3)
-    far_head, near_tail = across(near_head, 2), across(hold(tail, near_head), 1)
-    hi, lo, part = prepare([tail, head], neighbour, weight, total_k)
-    tail_part = add_sides(0, (None, far_tail), hi, lo, part, [])
-    head_part = add_sides(half, (near_head, far_head), hi, lo, part, [tail_part])
-    return finish((near_tail, None), hi, lo, tail_part, [head_part], parts)
+    hi, lo, part, late = prepare([head, tail], neighbour, weight, total_k)
+    near_tail, far_head = across(late, 1), across(hold(near_head, late), 2)
+    tail_part = add_sides(half, (near_tail, far_tail), hi, lo, part, [])
+    return finish((near_head, far_head), hi, lo, part, [tail_part], parts)
 
 
 def spread(values, shape):

time: 40 us -> 39.6 us (0.990)
  starting transfers between devices: 13.1 us -> 11.5 us
  waiting for transfers between devices: 8.75 us -> 9.92 us
    ppermute x4, starting transfers between devices: 8.63 us -> 7.02 us  [smear(): lax.ppermute(block, 'kgrp', [(i, i ^ flip) for i in range(groups)])]
    ppermute x4, waiting for transfers between devices: 2.87 us -> 4.03 us  [smear(): lax.ppermute(block, 'kgrp', [(i, i ^ flip) for i in range(groups)])]
  transfers between devices with their start and end apart: 8 -> 8, of which waited for: 5 -> 6; matrix products, arithmetic and copies ran while one was open for 0% -> 0% of each run, Pallas kernels for 7% -> 7%
where the time goes in v8:
time: 39.6 us; the launch traced here: 39.4 us
  starting transfers between devices  11.5 us (29%)
  blocking collectives  10.4 us (26%)
  waiting for transfers between devices  9.92 us (25%)
  Pallas kernels  4.86 us (12%)
  local copies, waits for them, and re-layouts  2.52 us (6%)
    all_to_all x1, blocking collectives, per_device(): lax.all_to_all(lines, ('kgrp', 'energy'), split_axis=0, concat_axis=0, ti...  10.4 us
    ppermute x4, starting transfers between devices, smear(): lax.ppermute(block, 'kgrp', [(i, i ^ flip) for i in range(groups)])  7.02 us
    ppermute x4, waiting for transfers between devices, per_device(): lax.ppermute(block, 'energy', [(e, e ^ m) for e in range(parts)])  5.88 us
    ppermute x4, starting transfers between devices, per_device(): lax.ppermute(block, 'energy', [(e, e ^ m) for e in range(parts)])  4.52 us
    ppermute x4, waiting for transfers between devices, smear(): lax.ppermute(block, 'kgrp', [(i, i ^ flip) for i in range(groups)])  4.03 us
    unnamed x22, local copies, waits for them, and re-layouts  1.38 us
    pallas_call x1, Pallas kernels, history(): pl.pallas_call(lambda *refs: history_kernel(rows, *refs), out_shape=(jax....  1.31 us
    slice x1, local copies, waits for them, and re-layouts, smear(): head, tail = (own[:half], own[half:])  1.14 us
  transfers between devices with their start and end apart: 8, of which 6 were waited for; matrix products, arithmetic and copies ran while one was open for 0% of the time, Pallas kernels for 7%

profile of v8, /device:TPU:0, one launch (start us, length us, event | category | flops | bytes accessed | tf_op | source)
XLA Modules:
  0.0 39.4 jit_solution(11772529414468420797)
XLA Ops:
  0.0 0.0 copy-start
  0.0 0.0 copy-start.1
  0.0 1.1 %fusion = (f32[1,2,2,64,128]{4,3,2,1,0:T(8,128)S(1)}, f32[1,2,2,64,128]{4,3,2,1,0:T(8,128)S(1)}) fusion(f32[2,2,2,64,128]{4,3,2,1,0:T(8,128)} %param.12), kind=kLoop, calls=%fused_computation | loop fusion | bytes 524288 | tf_op jit(solution)/shard_map/slice | solution.py:234
  1.1 3.0 %collective-permute-start = (f32[4,64,128]{2,1,0:T(8,128)S(1)}, f32[4,64,128]{2,1,0:T(8,128)S(1)}, u32[]{:S(2)}, u32[]{:S(2)}) collective-permute-start(f32[4,64,128]{2,1,0:T(8,128)S(1)} %bitcast.14), channel_id=1, source_target_pairs={{0,8},{8,0},{16,24},{24,16},{1,9},{9,1},{17,25},{25,17},{2,10},{10... | collective-permute-start | bytes 393224 | tf_op jit(solution)/shard_map/ppermute | solution.py:232
  4.1 1.5 %collective-permute-start.3 = (f32[4,64,128]{2,1,0:T(8,128)S(1)}, f32[4,64,128]{2,1,0:T(8,128)S(1)}, u32[]{:S(2)}, u32[]{:S(2)}) collective-permute-start(f32[4,64,128]{2,1,0:T(8,128)S(1)} %bitcast.12), channel_id=1, source_target_pairs={{0,24},{8,16},{16,8},{24,0},{1,25},{9,17},{17,9},{25,1},{2,26},{10... | collective-permute-start | bytes 393224 | tf_op jit(solution)/shard_map/ppermute | solution.py:232
  5.6 0.0 copy-start.3
  5.6 0.7 %copy-done.3 = s32[64,5]{0,1:T(8,128)S(1)} copy-done((s32[64,5]{0,1:T(8,128)S(1)}, s32[64,5]{0,1:T(8,128)}, u32[]{:S(2)}) %copy-start.3) | copy-done | bytes 1304
  6.3 0.0 copy-start.5
  6.3 0.7 %copy-done.5 = f32[5]{0:T(128)S(1)} copy-done((f32[5]{0:T(128)S(1)}, f32[5]{0:T(128)}, u32[]{:S(2)}) %copy-start.5) | copy-done | bytes 44
  7.0 0.0 copy-start.4
  7.0 0.0 copy-start.6
  7.0 0.0 copy-start.7
  7.0 0.0 copy-start.8
  7.0 0.0 copy-start.9
  7.0 1.1 %prepare.1 = (bf16[64,128]{1,0:T(8,128)(2,1)S(1)}, bf16[64,128]{1,0:T(8,128)(2,1)S(1)}, f32[8,64,128]{2,1,0:T(8,128)S(1)}, f32[4,64,128]{2,1,0:T(8,128)S(1)}) custom-call(f32[4,64,128]{2,1,0:T(8,128)S(1)} %bitcast.15, f32[4,64,128]{2,1,0:T(8,128)S(1)} %bitcast.13, s32[5,64]{1,0:T(8,128)S(1)} %bitcast.16, f32[5]{0:T(128)S(1)} %copy-done.5), custom_call_target="tpu_custom_call" | custom-call | flops 25165824 | bytes 524288 | tf_op jit(solution)/shard_map/prepare/pallas_call | solution.py:85
  8.1 1.6 %collective-permute-start.2 = (f32[4,64,128]{2,1,0:T(8,128)S(1)}, f32[4,64,128]{2,1,0:T(8,128)S(1)}, u32[]{:S(2)}, u32[]{:S(2)}) collective-permute-start(f32[4,64,128]{2,1,0:T(8,128)S(1)} %get-tuple-element.19._), channel_id=1, source_target_pairs={{0,8},{8,0},{16,24},{24,16},{1,9},{9,1},{17,25},{25,17},{2,10},{10... | collective-permute-start | bytes 393224 | tf_op jit(solution)/shard_map/ppermute | solution.py:232
  9.7 0.0 collective-permute-done.block.refs_0_
  9.7 1.0 %collective-permute-start.1 = (f32[4,64,128]{2,1,0:T(8,128)S(1)}, f32[4,64,128]{2,1,0:T(8,128)S(1)}, u32[]{:S(2)}, u32[]{:S(2)}) collective-permute-start(f32[4,64,128]{2,1,0:T(8,128)S(1)} %hold.1), channel_id=1, source_target_pairs={{0,16},{8,24},{16,0},{24,8},{1,17},{9,25},{17,1},{25,9},{2,18},{10... | collective-permute-start | bytes 393224 | tf_op jit(solution)/shard_map/ppermute | solution.py:232
  10.6 2.2 %collective-permute-done.3.refs_1_ = f32[4,64,128]{2,1,0:T(8,128)S(1)} collective-permute-done((f32[4,64,128]{2,1,0:T(8,128)S(1)}, f32[4,64,128]{2,1,0:T(8,128)S(1)}, u32[]{:S(2)}, u32[]{:S(2)}) %collective-permute-start.3) | collective-permute-done | bytes 131104 | tf_op jit(solution)/shard_map/ppermute | solution.py:232
  12.8 0.5 %collective-permute-done.2.refs_0_ = f32[4,64,128]{2,1,0:T(8,128)S(1)} collective-permute-done((f32[4,64,128]{2,1,0:T(8,128)S(1)}, f32[4,64,128]{2,1,0:T(8,128)S(1)}, u32[]{:S(2)}, u32[]{:S(2)}) %collective-permute-start.2) | collective-permute-done | bytes 131104 | tf_op jit(solution)/shard_map/ppermute | solution.py:232
  13.3 0.2 add_sides.1.refs_5_
  13.5 1.4 %collective-permute-done.1.refs_1_ = f32[4,64,128]{2,1,0:T(8,128)S(1)} collective-permute-done((f32[4,64,128]{2,1,0:T(8,128)S(1)}, f32[4,64,128]{2,1,0:T(8,128)S(1)}, u32[]{:S(2)}, u32[]{:S(2)}) %collective-permute-start.1) | collective-permute-done | bytes 131104 | tf_op jit(solution)/shard_map/ppermute | solution.py:232
  14.9 0.2 finish.1
  15.1 0.1 collective-permute-start.4
  15.2 1.3 %collective-permute-done.4.swapped.refs_1_ = f32[4,64,128]{2,1,0:T(8,128)S(1)} collective-permute-done((f32[4,64,128]{2,1,0:T(8,128)S(1)}, f32[4,64,128]{2,1,0:T(8,128)S(1)}, u32[]{:S(2)}, u32[]{:S(2)}) %collective-permute-start.4) | collective-permute-done | bytes 131104 | tf_op jit(solution)/shard_map/ppermute | solution.py:455
  16.5 1.6 %collective-permute-start.5 = (f32[2,64,128]{2,1,0:T(8,128)S(1)}, f32[2,64,128]{2,1,0:T(8,128)S(1)}, u32[]{:S(2)}, u32[]{:S(2)}) collective-permute-start(f32[2,64,128]{2,1,0:T(8,128)S(1)} %get-tuple-element.25), channel_id=1, source_target_pairs={{0,2},{1,3},{2,0},{3,1},{4,6},{5,7},{6,4},{7,5},{8,10},{9,11},{10,... | collective-permute-start | bytes 196616 | tf_op jit(solution)/shard_map/ppermute | solution.py:455
  18.2 2.6 %collective-permute-start.6 = (f32[2,64,128]{2,1,0:T(8,128)S(1)}, f32[2,64,128]{2,1,0:T(8,128)S(1)}, u32[]{:S(2)}, u32[]{:S(2)}) collective-permute-start(f32[2,64,128]{2,1,0:T(8,128)S(1)} %get-tuple-element.26), channel_id=1, source_target_pairs={{0,4},{1,5},{2,6},{3,7},{4,0},{5,1},{6,2},{7,3},{8,12},{9,13},{10,... | collective-permute-start | bytes 196616 | tf_op jit(solution)/shard_map/ppermute | solution.py:455
  20.7 0.2 collective-permute-start.7
  21.0 0.0 copy-done
  21.0 0.0 copy-done.1
  21.0 0.0 copy-done.4
  21.0 0.0 copy-done.6
  21.0 0.0 copy-done.7
  21.0 0.0 copy-done.8
  21.0 0.0 copy-done.9
  21.0 0.0 copy-start.2
  21.0 0.0 copy-start.10
  21.0 1.3 %history.1 = (f32[5,64,1024]{2,1,0:T(8,128)S(1)}, f32[1,128]{1,0:T(1,128)S(1)}, f32[5,8,128]{2,1,0:T(8,128)S(1)}) custom-call(f32[5,64,1024]{2,1,0:T(8,128)S(1)} %bitcast.9, f32[5,64,1024]{2,1,0:T(8,128)S(1)} %bitcast.7, s32[5]{0:T(128)S(1)} %copy-done.4, s32[64]{0:T(128)S(1)} %copy-done.6, f32[4]{0:T(128)S(1)} %copy-done.7, f32[2]{0:T(128)S(1)} %copy-done.8, ...), custom_call_target="tpu_custom_call" | custom-call | flops 2621440 | bytes 3932160 | tf_op jit(solution)/shard_map/history/pallas_call | solution.py:285
  22.4 0.0 collective-permute-done.5.refs_2_
  22.4 3.3 %collective-permute-done.6.refs_3_ = f32[2,64,128]{2,1,0:T(8,128)S(1)} collective-permute-done((f32[2,64,128]{2,1,0:T(8,128)S(1)}, f32[2,64,128]{2,1,0:T(8,128)S(1)}, u32[]{:S(2)}, u32[]{:S(2)}) %collective-permute-start.6) | collective-permute-done | bytes 65568 | tf_op jit(solution)/shard_map/ppermute | solution.py:455
  25.7 1.2 %collective-permute-done.7.refs_4_ = f32[2,64,128]{2,1,0:T(8,128)S(1)} collective-permute-done((f32[2,64,128]{2,1,0:T(8,128)S(1)}, f32[2,64,128]{2,1,0:T(8,128)S(1)}, u32[]{:S(2)}, u32[]{:S(2)}) %collective-permute-start.7) | collective-permute-done | bytes 65568 | tf_op jit(solution)/shard_map/ppermute | solution.py:455
  26.9 0.0 copy-done.2
  26.9 0.0 copy-done.10
  26.9 1.0 %residual.1 = (f32[64,1024]{1,0:T(8,128)S(1)}, f32[32,1,128]{2,1,0:T(1,128)S(1)}) custom-call(f32[4,64,128]{2,1,0:T(8,128)S(1)} %get-tuple-element.23.own.refs_0_, f32[4,64,128]{2,1,0:T(8,128)S(1)} %collective-permute-done.4.swapped.refs_1_, f32[2,64,128]{2,1,0:T(8,128)S(1)} %collective-permute-done.5.refs_2_, ...), custom_call_target="tpu_custom_call" | custom-call | tf_op jit(solution)/shard_map/residual/pallas_call | solution.py:345
  28.0 10.4 %all_to_all.5.refs_0_ = f32[32,1,128]{2,1,0:T(1,128)S(1)} all-to-all(f32[32,1,128]{2,1,0:T(1,128)S(1)} %get-tuple-element.30), channel_id=1, replica_groups=mesh['kgrp'=4,'energy'=8] {'kgrp','energy'}, dimensions={0} | all-to-all | bytes 32768 | tf_op jit(solution)/shard_map/all_to_all | solution.py:461
  38.4 1.0 %mix.1 = f32[64,1024]{1,0:T(8,128)} custom-call(f32[32,1,128]{2,1,0:T(1,128)S(1)} %all_to_all.5.refs_0_, f32[64,1024]{1,0:T(8,128)S(1)} %get-tuple-element.31.refs_1_, f32[64,1024]{1,0:T(8,128)S(1)} %bitcast.11, f32[5,64,1024]{2,1,0:T(8,128)S(1)} %get-tuple-element.32.refs_3_), custom_call_target="tpu_custom_call" | custom-call | tf_op jit(solution)/shard_map/mix/pallas_call | solution.py:417
  (2 shorter events, 0.0 us)
Async XLA Ops:
  0.0 21.0 %copy-start = (f32[5,2,2,2,8,1024]{5,4,3,2,1,0:T(8,128)S(1)}, f32[5,2,2,2,8,1024]{5,4,3,2,1,0:T(8,128)}, u32[]{:S(2)}) copy-start(f32[5,2,2,2,8,1024]{5,4,3,2,1,0:T(8,128)} %param.15) | copy-start | bytes 3932164
  0.0 21.0 %copy-start.1 = (f32[5,2,2,2,8,1024]{5,4,3,2,1,0:T(8,128)S(1)}, f32[5,2,2,2,8,1024]{5,4,3,2,1,0:T(8,128)}, u32[]{:S(2)}) copy-start(f32[5,2,2,2,8,1024]{5,4,3,2,1,0:T(8,128)} %param.14) | copy-start | bytes 3932164
  1.1 8.5 %collective-permute-start = (f32[4,64,128]{2,1,0:T(8,128)S(1)}, f32[4,64,128]{2,1,0:T(8,128)S(1)}, u32[]{:S(2)}, u32[]{:S(2)}) collective-permute-start(f32[4,64,128]{2,1,0:T(8,128)S(1)} %bitcast.14), channel_id=1, source_target_pairs={{0,8},{8,0},{16,24},{24,16},{1,9},{9,1},{17,25},{25,17},{2,10},{10... | collective-permute-start | bytes 393224 | tf_op jit(solution)/shard_map/ppermute | solution.py:232
  4.1 8.7 %collective-permute-start.3 = (f32[4,64,128]{2,1,0:T(8,128)S(1)}, f32[4,64,128]{2,1,0:T(8,128)S(1)}, u32[]{:S(2)}, u32[]{:S(2)}) collective-permute-start(f32[4,64,128]{2,1,0:T(8,128)S(1)} %bitcast.12), channel_id=1, source_target_pairs={{0,24},{8,16},{16,8},{24,0},{1,25},{9,17},{17,9},{25,1},{2,26},{10... | collective-permute-start | bytes 393224 | tf_op jit(solution)/shard_map/ppermute | solution.py:232
  5.6 0.7 %copy-start.3 = (s32[64,5]{0,1:T(8,128)S(1)}, s32[64,5]{0,1:T(8,128)}, u32[]{:S(2)}) copy-start(s32[64,5]{0,1:T(8,128)} %param.17) | copy-start | bytes 3844
  6.3 0.7 %copy-start.5 = (f32[5]{0:T(128)S(1)}, f32[5]{0:T(128)}, u32[]{:S(2)}) copy-start(f32[5]{0:T(128)} %refs_3_.2) | copy-start | bytes 64
  7.0 14.0 %copy-start.4 = (s32[5]{0:T(128)S(1)}, s32[5]{0:T(128)}, u32[]{:S(2)}) copy-start(s32[5]{0:T(128)} %refs_9_.1) | copy-start | bytes 64
  7.0 14.0 %copy-start.6 = (s32[64]{0:T(128)S(1)}, s32[64]{0:T(128)}, u32[]{:S(2)}) copy-start(s32[64]{0:T(128)} %refs_3_.3) | copy-start | bytes 772
  7.0 14.0 %copy-start.7 = (f32[4]{0:T(128)S(1)}, f32[4]{0:T(128)}, u32[]{:S(2)}) copy-start(f32[4]{0:T(128)} %refs_4_.1) | copy-start | bytes 52
  7.0 14.0 %copy-start.8 = (f32[2]{0:T(128)S(1)}, f32[2]{0:T(128)}, u32[]{:S(2)}) copy-start(f32[2]{0:T(128)} %refs_5_.1) | copy-start | bytes 28
  7.0 14.0 %copy-start.9 = (f32[2]{0:T(128)S(1)}, f32[2]{0:T(128)}, u32[]{:S(2)}) copy-start(f32[2]{0:T(128)} %refs_6_.1) | copy-start | bytes 28
  8.1 5.2 %collective-permute-start.2 = (f32[4,64,128]{2,1,0:T(8,128)S(1)}, f32[4,64,128]{2,1,0:T(8,128)S(1)}, u32[]{:S(2)}, u32[]{:S(2)}) collective-permute-start(f32[4,64,128]{2,1,0:T(8,128)S(1)} %get-tuple-element.19._), channel_id=1, source_target_pairs={{0,8},{8,0},{16,24},{24,16},{1,9},{9,1},{17,25},{25,17},{2,10},{10... | collective-permute-start | bytes 393224 | tf_op jit(solution)/shard_map/ppermute | solution.py:232
  9.7 5.2 %collective-permute-start.1 = (f32[4,64,128]{2,1,0:T(8,128)S(1)}, f32[4,64,128]{2,1,0:T(8,128)S(1)}, u32[]{:S(2)}, u32[]{:S(2)}) collective-permute-start(f32[4,64,128]{2,1,0:T(8,128)S(1)} %hold.1), channel_id=1, source_target_pairs={{0,16},{8,24},{16,0},{24,8},{1,17},{9,25},{17,1},{25,9},{2,18},{10... | collective-permute-start | bytes 393224 | tf_op jit(solution)/shard_map/ppermute | solution.py:232
  15.1 1.4 %collective-permute-start.4 = (f32[4,64,128]{2,1,0:T(8,128)S(1)}, f32[4,64,128]{2,1,0:T(8,128)S(1)}, u32[]{:S(2)}, u32[]{:S(2)}) collective-permute-start(f32[4,64,128]{2,1,0:T(8,128)S(1)} %get-tuple-element.24), channel_id=1, source_target_pairs={{0,1},{1,0},{2,3},{3,2},{4,5},{5,4},{6,7},{7,6},{8,9},{9,8},{10,11... | collective-permute-start | bytes 393224 | tf_op jit(solution)/shard_map/ppermute | solution.py:455
  16.5 5.8 %collective-permute-start.5 = (f32[2,64,128]{2,1,0:T(8,128)S(1)}, f32[2,64,128]{2,1,0:T(8,128)S(1)}, u32[]{:S(2)}, u32[]{:S(2)}) collective-permute-start(f32[2,64,128]{2,1,0:T(8,128)S(1)} %get-tuple-element.25), channel_id=1, source_target_pairs={{0,2},{1,3},{2,0},{3,1},{4,6},{5,7},{6,4},{7,5},{8,10},{9,11},{10,... | collective-permute-start | bytes 196616 | tf_op jit(solution)/shard_map/ppermute | solution.py:455
  18.2 7.5 %collective-permute-start.6 = (f32[2,64,128]{2,1,0:T(8,128)S(1)}, f32[2,64,128]{2,1,0:T(8,128)S(1)}, u32[]{:S(2)}, u32[]{:S(2)}) collective-permute-start(f32[2,64,128]{2,1,0:T(8,128)S(1)} %get-tuple-element.26), channel_id=1, source_target_pairs={{0,4},{1,5},{2,6},{3,7},{4,0},{5,1},{6,2},{7,3},{8,12},{9,13},{10,... | collective-permute-start | bytes 196616 | tf_op jit(solution)/shard_map/ppermute | solution.py:455
  20.7 6.2 %collective-permute-start.7 = (f32[2,64,128]{2,1,0:T(8,128)S(1)}, f32[2,64,128]{2,1,0:T(8,128)S(1)}, u32[]{:S(2)}, u32[]{:S(2)}) collective-permute-start(f32[2,64,128]{2,1,0:T(8,128)S(1)} %get-tuple-element.27), channel_id=1, source_target_pairs={{0,6},{1,7},{2,4},{3,5},{4,2},{5,3},{6,0},{7,1},{8,14},{9,15},{10,... | collective-permute-start | bytes 196616 | tf_op jit(solution)/shard_map/ppermute | solution.py:455
  21.0 5.9 %copy-start.2 = (f32[2,2,2,8,1024]{4,3,2,1,0:T(8,128)S(1)}, f32[2,2,2,8,1024]{4,3,2,1,0:T(8,128)}, u32[]{:S(2)}) copy-start(f32[2,2,2,8,1024]{4,3,2,1,0:T(8,128)} %param.13) | copy-start | bytes 786436
  21.0 5.9 %copy-start.10 = (s32[2]{0:T(128)S(1)}, s32[2]{0:T(128)}, u32[]{:S(2)}) copy-start(s32[2]{0:T(128)} %refs_10_.1) | copy-start | bytes 28

commit v9 on v8

--- a/solution.py
+++ b/solution.py
@@ -185,8 +185,13 @@
     )(*blocks, stencil_hi, stencil_lo, part, *ready)
 
 
+def chip_order(parts):
+    chips = parts // 2
+    return [*range(chips // 2, chips), *range(1, chips // 2)] if chips > 1 else []
+
+
 def join_kernel(own, swapped, *out):
-    for chip, block in enumerate(out, 1):
+    for chip, block in zip(chip_order(2 * own.shape[0]), out):
         block[0], block[1] = own[chip], swapped[chip]
 
 
@@ -252,7 +257,8 @@
 
 
 def history_kernel(
-    total_rows, past_inputs, past_residuals, slots, classes, acoustic, optical, number, aged, line, gains,
+    total_rows, past_inputs, past_residuals, slots, classes, acoustic, optical, number, shift,
+    aged, residuals, line, gains, shifts,
 ):
     first = lax.axis_index("energy") * total_rows
     row = lax.broadcasted_iota(jnp.int32, (8, LANES), 0) % total_rows
@@ -263,6 +269,7 @@
     for m in range(2):
         gains[2 * m + 1] = jnp.full((8, LANES), optical[m] * (number[m] + 1.0))
         gains[2 * m + 2] = jnp.full((8, LANES), optical[m] * number[m])
+        shifts[m] = jnp.full((8, LANES), shift[m], jnp.int32)
     _, rows, width = past_inputs.shape
     acc = [jnp.zeros((8, LANES), jnp.float32) for _ in PAIRS]
     for top in range(0, rows, 8):
@@ -274,6 +281,7 @@
                 aged[j, top : top + 8, at] = (
                     past_inputs[slots[j], top : top + 8, at] + mixing_share * res
                 )
+                residuals[j, top : top + 8, at] = res
                 old.append(res)
             return [a + old[i - 1] * old[j - 1] for a, (i, j) in zip(acc, PAIRS)]
         acc = lax.fori_loop(0, width // LANES, column, acc, unroll=4)
@@ -286,11 +294,13 @@
         lambda *refs: history_kernel(rows, *refs),
         out_shape=(
             jax.ShapeDtypeStruct(past_inputs.shape, jnp.float32),
+            jax.ShapeDtypeStruct(past_inputs.shape, jnp.float32),
             jax.ShapeDtypeStruct((1, LANES), jnp.float32),
             jax.ShapeDtypeStruct((5, 8, LANES), jnp.float32),
+            jax.ShapeDtypeStruct((2, 8, LANES), jnp.int32),
         ),
-        in_specs=[VMEM, VMEM] + [SMEM] * 5,
-        out_specs=(VMEM,) * 3,
+        in_specs=[VMEM, VMEM] + [SMEM] * 6,
+        out_specs=(VMEM,) * 5,
         compiler_params=PARAMS,
         cost_estimate=pl.CostEstimate(flops=8 * size, bytes_accessed=12 * size, transcendentals=0),
         name="history",
@@ -299,18 +309,19 @@
 
 def residual_kernel(count, own, swapped, *refs):
     received = refs[:count]
-    current, past_residuals, old_line, gains, slots, shift, fresh, lines, smeared = refs[count:]
+    current, residuals, old_line, gains, shifts, fresh, lines, smeared = refs[count:]
     parts, height, slice_len = smeared.shape
     place = lax.axis_index("energy")
     smeared[place], smeared[place ^ 1] = own[0], swapped[0]
-    for chip, block in enumerate(received, 1):
+    for chip, block in zip(chip_order(parts), received):
         smeared[place ^ (2 * chip)], smeared[place ^ (2 * chip + 1)] = block[0], block[1]
     lane = lax.broadcasted_iota(jnp.int32, (8, slice_len), 1)
     coupling = gains[0]
-    modes = [
-        (shift[m], lane < slice_len - shift[m], lane >= shift[m], gains[2 * m + 1], gains[2 * m + 2])
-        for m in range(2)
-    ]
+    modes = []
+    for m in range(2):
+        wide = shifts[m]
+        keeps = lane < slice_len - wide, lane >= wide
+        modes.append((jnp.max(wide), *keeps, gains[2 * m + 1], gains[2 * m + 2]))
     zero = jnp.zeros((8, slice_len), jnp.float32)
     acc = [zero] * (HIST + 1)
     for top in range(0, height, 8):
@@ -332,7 +343,7 @@
             fresh[where] = new
             acc[0] = acc[0] + new * new
             for j in range(HIST):
-                acc[j + 1] = acc[j + 1] + new * past_residuals[(slots[j],) + where]
+                acc[j + 1] = acc[j + 1] + new * residuals[(j,) + where]
     mine = jnp.concatenate([jnp.sum(a, axis=0, keepdims=True) for a in acc] + [zero[: 8 - HIST - 1]], axis=0)
     mine = jnp.sum(mine, axis=1, keepdims=True)
     spot = lax.broadcasted_iota(jnp.int32, (8, LANES), 0) + SPOTS[(0, 0)]
@@ -341,19 +352,19 @@
     lines[...] = jnp.broadcast_to(mine[None], lines.shape)
 
 
-def residual(kept, swapped, smeared, current, past_residuals, old_line, gains, slots, shift, copies):
+def residual(kept, swapped, smeared, current, residuals, old_line, gains, shifts, copies):
     return pl.pallas_call(
         lambda *refs: residual_kernel(len(smeared), *refs),
         out_shape=(
             jax.ShapeDtypeStruct(current.shape, jnp.float32),
             jax.ShapeDtypeStruct((copies, 1, LANES), jnp.float32),
         ),
-        in_specs=[VMEM] * (len(smeared) + 6) + [SMEM] * 2,
+        in_specs=[VMEM] * (len(smeared) + 7),
         out_specs=(VMEM, VMEM),
         scratch_shapes=[pltpu.VMEM((2 * kept.shape[0],) + kept.shape[1:], jnp.float32)],
         compiler_params=PARAMS,
         name="residual",
-    )(kept, swapped, *smeared, current, past_residuals, old_line, gains, slots, shift)
+    )(kept, swapped, *smeared, current, residuals, old_line, gains, shifts)
 
 
 def solve(products):
@@ -391,7 +402,7 @@
     return weights
 
 
-def mix_kernel(entries, lines, fresh, current, aged, out, wide):
+def mix_kernel(entries, lines, fresh, current, aged, out, wide, mixed_rows, done):
     summed = jnp.sum(lines[...], axis=0) / entries
     row = lax.broadcasted_iota(jnp.int32, (8, LANES), 0)
     lane = lax.broadcasted_iota(jnp.int32, (8, LANES), 1)
@@ -404,13 +415,21 @@
     }
     weights = solve(products)
     rows, width = fresh.shape
-    for top in range(0, rows, 8):
-        for left in range(0, width, LANES):
-            at = (slice(top, top + 8), slice(left, left + LANES))
-            mixed = weights[0] * (current[at] + mixing_share * fresh[at])
-            for j in range(HIST):
-                mixed = mixed + weights[j + 1] * aged[(j,) + at]
-            out[at] = mixed
+    span = rows // done.shape[0]
+    writes = []
+    for part in range(done.shape[0]):
+        for top in range(part * span, (part + 1) * span, 8):
+            for left in range(0, width, LANES):
+                at = (slice(top, top + 8), slice(left, left + LANES))
+                mixed = weights[0] * (current[at] + mixing_share * fresh[at])
+                for j in range(HIST):
+                    mixed = mixed + weights[j + 1] * aged[(j,) + at]
+                mixed_rows[at] = mixed
+        at = pl.ds(part * span, span)
+        writes.append(pltpu.make_async_copy(mixed_rows.at[at], out.at[at], done.at[part]))
+        writes[-1].start()
+    for write in writes:
+        write.wait()
 
 
 def mix(lines, fresh, current, aged, entries):
@@ -418,8 +437,12 @@
         lambda *refs: mix_kernel(entries, *refs),
         out_shape=jax.ShapeDtypeStruct(fresh.shape, jnp.float32),
         in_specs=[VMEM] * 4,
-        out_specs=VMEM,
-        scratch_shapes=[pltpu.VMEM((3, 8, LANES), jnp.float32)],
+        out_specs=pl.BlockSpec(memory_space=pltpu.HBM),
+        scratch_shapes=[
+            pltpu.VMEM((3, 8, LANES), jnp.float32),
+            pltpu.VMEM(fresh.shape, jnp.float32),
+            pltpu.SemaphoreType.DMA((2,)),
+        ],
         compiler_params=PARAMS,
         name="mix",
     )(lines, fresh, current, aged)
@@ -449,14 +472,16 @@
     flat = current.reshape(height, width)
     old_in = past_inputs.reshape(HIST, height, width)
     old_res = past_residuals.reshape(HIST, height, width)
-    scalars = (slot_order, momentum_class, acoustic_coupling, optical_coupling, occupation)
-    aged, old_line, gains = history(old_in, old_res, scalars, rows)
+    scalars = (
+        slot_order, momentum_class, acoustic_coupling, optical_coupling, occupation, phonon_shift
+    )
+    aged, residuals, old_line, gains, shifts = history(old_in, old_res, scalars, rows)
     kept, given = smear(own, neighbour, stencil_weight, groups, parts)
     meet = lambda block, m: lax.ppermute(block, "energy", [(e, e ^ m) for e in range(parts)])
     swapped = meet(given, 1)
-    smeared = [meet(block, 2 * chip) for chip, block in enumerate(join(kept, swapped), 1)]
+    smeared = [meet(block, 2 * chip) for chip, block in zip(chip_order(parts), join(kept, swapped))]
     fresh, lines = residual(
-        kept, swapped, smeared, flat, old_res, old_line, gains, slot_order, phonon_shift, groups * parts
+        kept, swapped, smeared, flat, residuals, old_line, gains, shifts, groups * parts
     )
     lines = lax.all_to_all(lines, ("kgrp", "energy"), split_axis=0, concat_axis=0, tiled=True)
     entries = float(flat.size * groups * parts)

time: 39.6 us -> 39.4 us (level)
  blocking collectives: 10.4 us -> 11.6 us
  waiting for transfers between devices: 9.92 us -> 9.04 us
    all_to_all x1, blocking collectives: 10.4 us -> 11.6 us  [per_device(): lax.all_to_all(lines, ('kgrp', 'energy'), split_axis=0, concat_axis=0, ti...]
    ppermute x4, waiting for transfers between devices: 5.88 us -> 5 us  [per_device(): lax.ppermute(block, 'energy', [(e, e ^ m) for e in range(parts)])]
  transfers between devices with their start and end apart: 8 -> 8, of which waited for: 6 -> 7; matrix products, arithmetic and copies ran while one was open for 0% -> 0% of each run, Pallas kernels for 7% -> 7%
where the time goes in v9:
time: 39.4 us; the launch traced here: 39.2 us
  blocking collectives  11.6 us (29%)
  starting transfers between devices  11.3 us (29%)
  waiting for transfers between devices  9.04 us (23%)
  Pallas kernels  4.61 us (12%)
  local copies, waits for them, and re-layouts  2.52 us (6%)
    all_to_all x1, blocking collectives, per_device(): lax.all_to_all(lines, ('kgrp', 'energy'), split_axis=0, concat_axis=0, ti...  11.6 us
    ppermute x4, starting transfers between devices, smear(): lax.ppermute(block, 'kgrp', [(i, i ^ flip) for i in range(groups)])  7 us
    ppermute x4, waiting for transfers between devices, per_device(): lax.ppermute(block, 'energy', [(e, e ^ m) for e in range(parts)])  5 us
    ppermute x4, starting transfers between devices, per_device(): lax.ppermute(block, 'energy', [(e, e ^ m) for e in range(parts)])  4.31 us
    ppermute x4, waiting for transfers between devices, smear(): lax.ppermute(block, 'kgrp', [(i, i ^ flip) for i in range(groups)])  4.04 us
    pallas_call x1, Pallas kernels, history(): pl.pallas_call(lambda *refs: history_kernel(rows, *refs), out_shape=(jax....  1.43 us
    unnamed x22, local copies, waits for them, and re-layouts  1.38 us
    slice x1, local copies, waits for them, and re-layouts, smear(): head, tail = (own[:half], own[half:])  1.14 us
  transfers between devices with their start and end apart: 8, of which 7 were waited for; matrix products, arithmetic and copies ran while one was open for 0% of the time, Pallas kernels for 7%

profile of v9, /device:TPU:0, one launch (start us, length us, event | category | flops | bytes accessed | tf_op | source)
XLA Modules:
  0.0 39.2 jit_solution(7061027751320495380)
XLA Ops:
  0.0 0.0 copy-start.1
  0.0 0.0 copy-start
  0.0 1.1 %fusion = (f32[1,2,2,64,128]{4,3,2,1,0:T(8,128)S(1)}, f32[1,2,2,64,128]{4,3,2,1,0:T(8,128)S(1)}) fusion(f32[2,2,2,64,128]{4,3,2,1,0:T(8,128)} %param.12), kind=kLoop, calls=%fused_computation | loop fusion | bytes 524288 | tf_op jit(solution)/shard_map/slice | solution.py:239
  1.1 3.0 %collective-permute-start = (f32[4,64,128]{2,1,0:T(8,128)S(1)}, f32[4,64,128]{2,1,0:T(8,128)S(1)}, u32[]{:S(2)}, u32[]{:S(2)}) collective-permute-start(f32[4,64,128]{2,1,0:T(8,128)S(1)} %bitcast.13), channel_id=1, source_target_pairs={{0,8},{8,0},{16,24},{24,16},{1,9},{9,1},{17,25},{25,17},{2,10},{10... | collective-permute-start | bytes 393224 | tf_op jit(solution)/shard_map/ppermute | solution.py:237
  4.1 1.5 %collective-permute-start.3 = (f32[4,64,128]{2,1,0:T(8,128)S(1)}, f32[4,64,128]{2,1,0:T(8,128)S(1)}, u32[]{:S(2)}, u32[]{:S(2)}) collective-permute-start(f32[4,64,128]{2,1,0:T(8,128)S(1)} %bitcast.11), channel_id=1, source_target_pairs={{0,24},{8,16},{16,8},{24,0},{1,25},{9,17},{17,9},{25,1},{2,26},{10... | collective-permute-start | bytes 393224 | tf_op jit(solution)/shard_map/ppermute | solution.py:237
  5.6 0.0 copy-start.3
  5.6 0.7 %copy-done.3 = s32[64,5]{0,1:T(8,128)S(1)} copy-done((s32[64,5]{0,1:T(8,128)S(1)}, s32[64,5]{0,1:T(8,128)}, u32[]{:S(2)}) %copy-start.3) | copy-done | bytes 1304
  6.3 0.0 copy-start.4
  6.3 0.7 %copy-done.4 = f32[5]{0:T(128)S(1)} copy-done((f32[5]{0:T(128)S(1)}, f32[5]{0:T(128)}, u32[]{:S(2)}) %copy-start.4) | copy-done | bytes 44
  7.0 0.0 copy-start.5
  7.0 0.0 copy-start.6
  7.0 0.0 copy-start.7
  7.0 0.0 copy-start.8
  7.0 0.0 copy-start.9
  7.0 0.0 copy-start.10
  7.0 1.1 %prepare.1 = (bf16[64,128]{1,0:T(8,128)(2,1)S(1)}, bf16[64,128]{1,0:T(8,128)(2,1)S(1)}, f32[8,64,128]{2,1,0:T(8,128)S(1)}, f32[4,64,128]{2,1,0:T(8,128)S(1)}) custom-call(f32[4,64,128]{2,1,0:T(8,128)S(1)} %bitcast.14, f32[4,64,128]{2,1,0:T(8,128)S(1)} %bitcast.12, s32[5,64]{1,0:T(8,128)S(1)} %bitcast.15, f32[5]{0:T(128)S(1)} %copy-done.4), custom_call_target="tpu_custom_call" | custom-call | flops 25165824 | bytes 524288 | tf_op jit(solution)/shard_map/prepare/pallas_call | solution.py:85
  8.1 1.6 %collective-permute-start.2 = (f32[4,64,128]{2,1,0:T(8,128)S(1)}, f32[4,64,128]{2,1,0:T(8,128)S(1)}, u32[]{:S(2)}, u32[]{:S(2)}) collective-permute-start(f32[4,64,128]{2,1,0:T(8,128)S(1)} %get-tuple-element.21._), channel_id=1, source_target_pairs={{0,8},{8,0},{16,24},{24,16},{1,9},{9,1},{17,25},{25,17},{2,10},{10... | collective-permute-start | bytes 393224 | tf_op jit(solution)/shard_map/ppermute | solution.py:237
  9.7 0.0 collective-permute-done.block.refs_0_
  9.7 0.9 %collective-permute-start.1 = (f32[4,64,128]{2,1,0:T(8,128)S(1)}, f32[4,64,128]{2,1,0:T(8,128)S(1)}, u32[]{:S(2)}, u32[]{:S(2)}) collective-permute-start(f32[4,64,128]{2,1,0:T(8,128)S(1)} %hold.1), channel_id=1, source_target_pairs={{0,16},{8,24},{16,0},{24,8},{1,17},{9,25},{17,1},{25,9},{2,18},{10... | collective-permute-start | bytes 393224 | tf_op jit(solution)/shard_map/ppermute | solution.py:237
  10.6 2.2 %collective-permute-done.3.refs_1_ = f32[4,64,128]{2,1,0:T(8,128)S(1)} collective-permute-done((f32[4,64,128]{2,1,0:T(8,128)S(1)}, f32[4,64,128]{2,1,0:T(8,128)S(1)}, u32[]{:S(2)}, u32[]{:S(2)}) %collective-permute-start.3) | collective-permute-done | bytes 131104 | tf_op jit(solution)/shard_map/ppermute | solution.py:237
  12.8 0.5 %collective-permute-done.2.refs_0_ = f32[4,64,128]{2,1,0:T(8,128)S(1)} collective-permute-done((f32[4,64,128]{2,1,0:T(8,128)S(1)}, f32[4,64,128]{2,1,0:T(8,128)S(1)}, u32[]{:S(2)}, u32[]{:S(2)}) %collective-permute-start.2) | collective-permute-done | bytes 131104 | tf_op jit(solution)/shard_map/ppermute | solution.py:237
  13.3 0.2 add_sides.1.refs_5_
  13.5 1.4 %collective-permute-done.1.refs_1_ = f32[4,64,128]{2,1,0:T(8,128)S(1)} collective-permute-done((f32[4,64,128]{2,1,0:T(8,128)S(1)}, f32[4,64,128]{2,1,0:T(8,128)S(1)}, u32[]{:S(2)}, u32[]{:S(2)}) %collective-permute-start.1) | collective-permute-done | bytes 131104 | tf_op jit(solution)/shard_map/ppermute | solution.py:237
  14.9 0.2 finish.1
  15.1 0.1 collective-permute-start.4
  15.2 1.3 %collective-permute-done.4.swapped.refs_1_ = f32[4,64,128]{2,1,0:T(8,128)S(1)} collective-permute-done((f32[4,64,128]{2,1,0:T(8,128)S(1)}, f32[4,64,128]{2,1,0:T(8,128)S(1)}, u32[]{:S(2)}, u32[]{:S(2)}) %collective-permute-start.4) | collective-permute-done | bytes 131104 | tf_op jit(solution)/shard_map/ppermute | solution.py:480
  16.5 2.7 %collective-permute-start.5 = (f32[2,64,128]{2,1,0:T(8,128)S(1)}, f32[2,64,128]{2,1,0:T(8,128)S(1)}, u32[]{:S(2)}, u32[]{:S(2)}) collective-permute-start(f32[2,64,128]{2,1,0:T(8,128)S(1)} %get-tuple-element.27), channel_id=1, source_target_pairs={{0,4},{1,5},{2,6},{3,7},{4,0},{5,1},{6,2},{7,3},{8,12},{9,13},{10,... | collective-permute-start | bytes 196616 | tf_op jit(solution)/shard_map/ppermute | solution.py:480
  19.2 1.3 %collective-permute-start.6 = (f32[2,64,128]{2,1,0:T(8,128)S(1)}, f32[2,64,128]{2,1,0:T(8,128)S(1)}, u32[]{:S(2)}, u32[]{:S(2)}) collective-permute-start(f32[2,64,128]{2,1,0:T(8,128)S(1)} %get-tuple-element.28), channel_id=1, source_target_pairs={{0,6},{1,7},{2,4},{3,5},{4,2},{5,3},{6,0},{7,1},{8,14},{9,15},{10,... | collective-permute-start | bytes 196616 | tf_op jit(solution)/shard_map/ppermute | solution.py:480
  20.5 0.2 collective-permute-start.7
  20.8 0.0 copy-done.1
  20.8 0.0 copy-done
  20.8 0.0 copy-done.5
  20.8 0.0 copy-done.6
  20.8 0.0 copy-done.7
  20.8 0.0 copy-done.8
  20.8 0.0 copy-done.9
  20.8 0.0 copy-done.10
  20.8 0.0 copy-start.2
  20.8 1.4 %history.1 = (f32[5,64,1024]{2,1,0:T(8,128)S(1)}, f32[5,64,1024]{2,1,0:T(8,128)S(1)}, f32[1,128]{1,0:T(1,128)S(1)}, f32[5,8,128]{2,1,0:T(8,128)S(1)}, s32[2,8,128]{2,1,0:T(8,128)S(1)}) custom-call(f32[5,64,1024]{2,1,0:T(8,128)S(1)} %bitcast.7, f32[5,64,1024]{2,1,0:T(8,128)S(1)} %bitcast.8, s32[5]{0:T(128)S(1)} %copy-done.5, s32[64]{0:T(128)S(1)} %copy-done.6, ...), custom_call_target="tpu_custom_call" | custom-call | flops 2621440 | bytes 3932160 | tf_op jit(solution)/shard_map/history/pallas_call | solution.py:293
  22.3 2.0 %collective-permute-done.5.refs_2_ = f32[2,64,128]{2,1,0:T(8,128)S(1)} collective-permute-done((f32[2,64,128]{2,1,0:T(8,128)S(1)}, f32[2,64,128]{2,1,0:T(8,128)S(1)}, u32[]{:S(2)}, u32[]{:S(2)}) %collective-permute-start.5) | collective-permute-done | bytes 65568 | tf_op jit(solution)/shard_map/ppermute | solution.py:480
  24.3 1.3 %collective-permute-done.6.refs_3_ = f32[2,64,128]{2,1,0:T(8,128)S(1)} collective-permute-done((f32[2,64,128]{2,1,0:T(8,128)S(1)}, f32[2,64,128]{2,1,0:T(8,128)S(1)}, u32[]{:S(2)}, u32[]{:S(2)}) %collective-permute-start.6) | collective-permute-done | bytes 65568 | tf_op jit(solution)/shard_map/ppermute | solution.py:480
  25.6 0.3 collective-permute-done.7.refs_4_
  25.9 0.0 copy-done.2
  25.9 0.7 %residual.1 = (f32[64,1024]{1,0:T(8,128)S(1)}, f32[32,1,128]{2,1,0:T(1,128)S(1)}) custom-call(f32[4,64,128]{2,1,0:T(8,128)S(1)} %get-tuple-element.25.own.refs_0_, f32[4,64,128]{2,1,0:T(8,128)S(1)} %collective-permute-done.4.swapped.refs_1_, f32[2,64,128]{2,1,0:T(8,128)S(1)} %collective-permute-done.5.refs_2_, ...), custom_call_target="tpu_custom_call" | custom-call | tf_op jit(solution)/shard_map/residual/pallas_call | solution.py:356
  26.6 11.6 %all_to_all.5.refs_0_ = f32[32,1,128]{2,1,0:T(1,128)S(1)} all-to-all(f32[32,1,128]{2,1,0:T(1,128)S(1)} %get-tuple-element.34), channel_id=1, replica_groups=mesh['kgrp'=4,'energy'=8] {'kgrp','energy'}, dimensions={0} | all-to-all | bytes 32768 | tf_op jit(solution)/shard_map/all_to_all | solution.py:486
  38.2 1.0 %mix.1 = f32[64,1024]{1,0:T(8,128)} custom-call(f32[32,1,128]{2,1,0:T(1,128)S(1)} %all_to_all.5.refs_0_, f32[64,1024]{1,0:T(8,128)S(1)} %get-tuple-element.35.refs_1_, f32[64,1024]{1,0:T(8,128)S(1)} %bitcast.10, f32[5,64,1024]{2,1,0:T(8,128)S(1)} %get-tuple-element.36.refs_3_), custom_call_target="tpu_custom_call" | custom-call | tf_op jit(solution)/shard_map/mix/pallas_call | solution.py:436
  (2 shorter events, 0.0 us)
Async XLA Ops:
  0.0 20.8 %copy-start.1 = (f32[5,2,2,2,8,1024]{5,4,3,2,1,0:T(8,128)S(1)}, f32[5,2,2,2,8,1024]{5,4,3,2,1,0:T(8,128)}, u32[]{:S(2)}) copy-start(f32[5,2,2,2,8,1024]{5,4,3,2,1,0:T(8,128)} %param.15) | copy-start | bytes 3932164
  0.0 20.8 %copy-start = (f32[5,2,2,2,8,1024]{5,4,3,2,1,0:T(8,128)S(1)}, f32[5,2,2,2,8,1024]{5,4,3,2,1,0:T(8,128)}, u32[]{:S(2)}) copy-start(f32[5,2,2,2,8,1024]{5,4,3,2,1,0:T(8,128)} %param.14) | copy-start | bytes 3932164
  1.1 8.5 %collective-permute-start = (f32[4,64,128]{2,1,0:T(8,128)S(1)}, f32[4,64,128]{2,1,0:T(8,128)S(1)}, u32[]{:S(2)}, u32[]{:S(2)}) collective-permute-start(f32[4,64,128]{2,1,0:T(8,128)S(1)} %bitcast.13), channel_id=1, source_target_pairs={{0,8},{8,0},{16,24},{24,16},{1,9},{9,1},{17,25},{25,17},{2,10},{10... | collective-permute-start | bytes 393224 | tf_op jit(solution)/shard_map/ppermute | solution.py:237
  4.1 8.7 %collective-permute-start.3 = (f32[4,64,128]{2,1,0:T(8,128)S(1)}, f32[4,64,128]{2,1,0:T(8,128)S(1)}, u32[]{:S(2)}, u32[]{:S(2)}) collective-permute-start(f32[4,64,128]{2,1,0:T(8,128)S(1)} %bitcast.11), channel_id=1, source_target_pairs={{0,24},{8,16},{16,8},{24,0},{1,25},{9,17},{17,9},{25,1},{2,26},{10... | collective-permute-start | bytes 393224 | tf_op jit(solution)/shard_map/ppermute | solution.py:237
  5.6 0.7 %copy-start.3 = (s32[64,5]{0,1:T(8,128)S(1)}, s32[64,5]{0,1:T(8,128)}, u32[]{:S(2)}) copy-start(s32[64,5]{0,1:T(8,128)} %param.17) | copy-start | bytes 3844
  6.3 0.7 %copy-start.4 = (f32[5]{0:T(128)S(1)}, f32[5]{0:T(128)}, u32[]{:S(2)}) copy-start(f32[5]{0:T(128)} %refs_3_.2) | copy-start | bytes 64
  7.0 13.8 %copy-start.5 = (s32[5]{0:T(128)S(1)}, s32[5]{0:T(128)}, u32[]{:S(2)}) copy-start(s32[5]{0:T(128)} %refs_2_.1) | copy-start | bytes 64
  7.0 13.8 %copy-start.6 = (s32[64]{0:T(128)S(1)}, s32[64]{0:T(128)}, u32[]{:S(2)}) copy-start(s32[64]{0:T(128)} %refs_3_.3) | copy-start | bytes 772
  7.0 13.8 %copy-start.7 = (f32[4]{0:T(128)S(1)}, f32[4]{0:T(128)}, u32[]{:S(2)}) copy-start(f32[4]{0:T(128)} %refs_4_.1) | copy-start | bytes 52
  7.0 13.8 %copy-start.8 = (f32[2]{0:T(128)S(1)}, f32[2]{0:T(128)}, u32[]{:S(2)}) copy-start(f32[2]{0:T(128)} %refs_5_.1) | copy-start | bytes 28
  7.0 13.8 %copy-start.9 = (f32[2]{0:T(128)S(1)}, f32[2]{0:T(128)}, u32[]{:S(2)}) copy-start(f32[2]{0:T(128)} %refs_6_.1) | copy-start | bytes 28
  7.0 13.8 %copy-start.10 = (s32[2]{0:T(128)S(1)}, s32[2]{0:T(128)}, u32[]{:S(2)}) copy-start(s32[2]{0:T(128)} %refs_7_.1) | copy-start | bytes 28
  8.1 5.1 %collective-permute-start.2 = (f32[4,64,128]{2,1,0:T(8,128)S(1)}, f32[4,64,128]{2,1,0:T(8,128)S(1)}, u32[]{:S(2)}, u32[]{:S(2)}) collective-permute-start(f32[4,64,128]{2,1,0:T(8,128)S(1)} %get-tuple-element.21._), channel_id=1, source_target_pairs={{0,8},{8,0},{16,24},{24,16},{1,9},{9,1},{17,25},{25,17},{2,10},{10... | collective-permute-start | bytes 393224 | tf_op jit(solution)/shard_map/ppermute | solution.py:237
  9.7 5.2 %collective-permute-start.1 = (f32[4,64,128]{2,1,0:T(8,128)S(1)}, f32[4,64,128]{2,1,0:T(8,128)S(1)}, u32[]{:S(2)}, u32[]{:S(2)}) collective-permute-start(f32[4,64,128]{2,1,0:T(8,128)S(1)} %hold.1), channel_id=1, source_target_pairs={{0,16},{8,24},{16,0},{24,8},{1,17},{9,25},{17,1},{25,9},{2,18},{10... | collective-permute-start | bytes 393224 | tf_op jit(solution)/shard_map/ppermute | solution.py:237
  15.1 1.4 %collective-permute-start.4 = (f32[4,64,128]{2,1,0:T(8,128)S(1)}, f32[4,64,128]{2,1,0:T(8,128)S(1)}, u32[]{:S(2)}, u32[]{:S(2)}) collective-permute-start(f32[4,64,128]{2,1,0:T(8,128)S(1)} %get-tuple-element.26), channel_id=1, source_target_pairs={{0,1},{1,0},{2,3},{3,2},{4,5},{5,4},{6,7},{7,6},{8,9},{9,8},{10,11... | collective-permute-start | bytes 393224 | tf_op jit(solution)/shard_map/ppermute | solution.py:480
  16.5 7.8 %collective-permute-start.5 = (f32[2,64,128]{2,1,0:T(8,128)S(1)}, f32[2,64,128]{2,1,0:T(8,128)S(1)}, u32[]{:S(2)}, u32[]{:S(2)}) collective-permute-start(f32[2,64,128]{2,1,0:T(8,128)S(1)} %get-tuple-element.27), channel_id=1, source_target_pairs={{0,4},{1,5},{2,6},{3,7},{4,0},{5,1},{6,2},{7,3},{8,12},{9,13},{10,... | collective-permute-start | bytes 196616 | tf_op jit(solution)/shard_map/ppermute | solution.py:480
  19.2 6.4 %collective-permute-start.6 = (f32[2,64,128]{2,1,0:T(8,128)S(1)}, f32[2,64,128]{2,1,0:T(8,128)S(1)}, u32[]{:S(2)}, u32[]{:S(2)}) collective-permute-start(f32[2,64,128]{2,1,0:T(8,128)S(1)} %get-tuple-element.28), channel_id=1, source_target_pairs={{0,6},{1,7},{2,4},{3,5},{4,2},{5,3},{6,0},{7,1},{8,14},{9,15},{10,... | collective-permute-start | bytes 196616 | tf_op jit(solution)/shard_map/ppermute | solution.py:480
  20.5 5.4 %collective-permute-start.7 = (f32[2,64,128]{2,1,0:T(8,128)S(1)}, f32[2,64,128]{2,1,0:T(8,128)S(1)}, u32[]{:S(2)}, u32[]{:S(2)}) collective-permute-start(f32[2,64,128]{2,1,0:T(8,128)S(1)} %get-tuple-element.29), channel_id=1, source_target_pairs={{0,2},{1,3},{2,0},{3,1},{4,6},{5,7},{6,4},{7,5},{8,10},{9,11},{10,... | collective-permute-start | bytes 196616 | tf_op jit(solution)/shard_map/ppermute | solution.py:480
  20.8 5.1 %copy-start.2 = (f32[2,2,2,8,1024]{4,3,2,1,0:T(8,128)S(1)}, f32[2,2,2,8,1024]{4,3,2,1,0:T(8,128)}, u32[]{:S(2)}) copy-start(f32[2,2,2,8,1024]{4,3,2,1,0:T(8,128)} %param.13) | copy-start | bytes 786436

commit v10 on v9

--- a/solution.py
+++ b/solution.py
@@ -309,7 +309,7 @@
 
 def residual_kernel(count, own, swapped, *refs):
     received = refs[:count]
-    current, residuals, old_line, gains, shifts, fresh, lines, smeared = refs[count:]
+    current, residuals, old_line, gains, shifts, fresh, line, smeared = refs[count:]
     parts, height, slice_len = smeared.shape
     place = lax.axis_index("energy")
     smeared[place], smeared[place ^ 1] = own[0], swapped[0]
@@ -349,15 +349,15 @@
     spot = lax.broadcasted_iota(jnp.int32, (8, LANES), 0) + SPOTS[(0, 0)]
     mine = jnp.where(lax.broadcasted_iota(jnp.int32, (8, LANES), 1) == spot, mine, 0.0)
     mine = old_line[...] + jnp.sum(mine, axis=0, keepdims=True)
-    lines[...] = jnp.broadcast_to(mine[None], lines.shape)
-
-
-def residual(kept, swapped, smeared, current, residuals, old_line, gains, shifts, copies):
+    line[...] = mine
+
+
+def residual(kept, swapped, smeared, current, residuals, old_line, gains, shifts):
     return pl.pallas_call(
         lambda *refs: residual_kernel(len(smeared), *refs),
         out_shape=(
             jax.ShapeDtypeStruct(current.shape, jnp.float32),
-            jax.ShapeDtypeStruct((copies, 1, LANES), jnp.float32),
+            jax.ShapeDtypeStruct((1, LANES), jnp.float32),
         ),
         in_specs=[VMEM] * (len(smeared) + 7),
         out_specs=(VMEM, VMEM),
@@ -402,8 +402,12 @@
     return weights
 
 
-def mix_kernel(entries, lines, fresh, current, aged, out, wide, mixed_rows, done):
-    summed = jnp.sum(lines[...], axis=0) / entries
+def mix_kernel(entries, count, *refs):
+    lines, (fresh, current, aged, out, wide, mixed_rows, done) = refs[:count], refs[count:]
+    summed = lines[0][...]
+    for line in lines[1:]:
+        summed = summed + line[...]
+    summed = summed / entries
     row = lax.broadcasted_iota(jnp.int32, (8, LANES), 0)
     lane = lax.broadcasted_iota(jnp.int32, (8, LANES), 1)
     for part in range(wide.shape[0]):
@@ -434,9 +438,9 @@
 
 def mix(lines, fresh, current, aged, entries):
     return pl.pallas_call(
-        lambda *refs: mix_kernel(entries, *refs),
+        lambda *refs: mix_kernel(entries, len(lines), *refs),
         out_shape=jax.ShapeDtypeStruct(fresh.shape, jnp.float32),
-        in_specs=[VMEM] * 4,
+        in_specs=[VMEM] * (len(lines) + 3),
         out_specs=pl.BlockSpec(memory_space=pltpu.HBM),
         scratch_shapes=[
             pltpu.VMEM((3, 8, LANES), jnp.float32),
@@ -445,7 +449,7 @@
         ],
         compiler_params=PARAMS,
         name="mix",
-    )(lines, fresh, current, aged)
+    )(*lines, fresh, current, aged)
 
 
 def per_device(
@@ -480,10 +484,14 @@
     meet = lambda block, m: lax.ppermute(block, "energy", [(e, e ^ m) for e in range(parts)])
     swapped = meet(given, 1)
     smeared = [meet(block, 2 * chip) for chip, block in zip(chip_order(parts), join(kept, swapped))]
-    fresh, lines = residual(
-        kept, swapped, smeared, flat, residuals, old_line, gains, shifts, groups * parts
+    fresh, line = residual(
+        kept, swapped, smeared, flat, residuals, old_line, gains, shifts
     )
-    lines = lax.all_to_all(lines, ("kgrp", "energy"), split_axis=0, concat_axis=0, tiled=True)
+    line = line + meet(line, 1)
+    line = sum((meet(line, 2 * chip) for chip in chip_order(parts)), line)
+    lines = [line] + [
+        lax.ppermute(line, "kgrp", [(g, g ^ m) for g in range(groups)]) for m in range(1, groups)
+    ]
     entries = float(flat.size * groups * parts)
     return mix(lines, fresh, flat, aged, entries).reshape(current.shape)
 

time: 39.4 us -> 43.4 us (1.10)
  blocking collectives: 11.6 us -> 0 us
  waiting for transfers between devices: 9.04 us -> 17.2 us
  starting transfers between devices: 11.3 us -> 18.8 us
    all_to_all x1 -> x0, blocking collectives: 11.6 us -> none  [per_device(): lax.all_to_all(lines, ('kgrp', 'energy'), split_axis=0, concat_axis=0, ti...]
    ppermute x4 -> x8, waiting for transfers between devices: 5 us -> 10.6 us  [per_device(): lax.ppermute(block, 'energy', [(e, e ^ m) for e in range(parts)])]
    ppermute x4 -> x8, starting transfers between devices: 4.31 us -> 8.33 us  [per_device(): lax.ppermute(block, 'energy', [(e, e ^ m) for e in range(parts)])]
    ppermute x0 -> x3, starting transfers between devices: none -> 3.49 us  [per_device(): lax.ppermute(line, 'kgrp', [(g, g ^ m) for g in range(groups)])]
    ppermute x0 -> x3, waiting for transfers between devices: none -> 2.59 us  [per_device(): lax.ppermute(line, 'kgrp', [(g, g ^ m) for g in range(groups)])]
  transfers between devices with their start and end apart: 8 -> 15, of which waited for: 7 -> 13; matrix products, arithmetic and copies ran while one was open for 0% -> 0% of each run, Pallas kernels for 7% -> 6%
where the time goes in v10:
time: 43.4 us; the launch traced here: 43.2 us
  starting transfers between devices  18.8 us (43%)
  waiting for transfers between devices  17.2 us (40%)
  Pallas kernels  4.58 us (11%)
  local copies, waits for them, and re-layouts  2.52 us (6%)
    ppermute x8, waiting for transfers between devices, per_device(): lax.ppermute(block, 'energy', [(e, e ^ m) for e in range(parts)])  10.6 us
    ppermute x8, starting transfers between devices, per_device(): lax.ppermute(block, 'energy', [(e, e ^ m) for e in range(parts)])  8.33 us
    ppermute x4, starting transfers between devices, smear(): lax.ppermute(block, 'kgrp', [(i, i ^ flip) for i in range(groups)])  7 us
    ppermute x4, waiting for transfers between devices, smear(): lax.ppermute(block, 'kgrp', [(i, i ^ flip) for i in range(groups)])  4.04 us
    ppermute x3, starting transfers between devices, per_device(): lax.ppermute(line, 'kgrp', [(g, g ^ m) for g in range(groups)])  3.49 us
    ppermute x3, waiting for transfers between devices, per_device(): lax.ppermute(line, 'kgrp', [(g, g ^ m) for g in range(groups)])  2.59 us
    pallas_call x1, Pallas kernels, history(): pl.pallas_call(lambda *refs: history_kernel(rows, *refs), out_shape=(jax....  1.43 us
    unnamed x22, local copies, waits for them, and re-layouts  1.38 us
  transfers between devices with their start and end apart: 15, of which 13 were waited for; matrix products, arithmetic and copies ran while one was open for 0% of the time, Pallas kernels for 6%

profile of v10, /device:TPU:0, one launch (start us, length us, event | category | flops | bytes accessed | tf_op | source)
XLA Modules:
  0.0 43.2 jit_solution(7832788873523599638)
XLA Ops:
  0.0 1.1 %fusion = (f32[1,2,2,64,128]{4,3,2,1,0:T(8,128)S(1)}, f32[1,2,2,64,128]{4,3,2,1,0:T(8,128)S(1)}) fusion(f32[2,2,2,64,128]{4,3,2,1,0:T(8,128)} %param.12), kind=kLoop, calls=%fused_computation.1 | loop fusion | bytes 524288 | tf_op jit(solution)/shard_map/slice | solution.py:239
  1.1 3.0 %collective-permute-start = (f32[4,64,128]{2,1,0:T(8,128)S(1)}, f32[4,64,128]{2,1,0:T(8,128)S(1)}, u32[]{:S(2)}, u32[]{:S(2)}) collective-permute-start(f32[4,64,128]{2,1,0:T(8,128)S(1)} %bitcast.13), channel_id=1, source_target_pairs={{0,8},{8,0},{16,24},{24,16},{1,9},{9,1},{17,25},{25,17},{2,10},{10... | collective-permute-start | bytes 393224 | tf_op jit(solution)/shard_map/ppermute | solution.py:237
  4.1 1.5 %collective-permute-start.3 = (f32[4,64,128]{2,1,0:T(8,128)S(1)}, f32[4,64,128]{2,1,0:T(8,128)S(1)}, u32[]{:S(2)}, u32[]{:S(2)}) collective-permute-start(f32[4,64,128]{2,1,0:T(8,128)S(1)} %bitcast.11), channel_id=1, source_target_pairs={{0,24},{8,16},{16,8},{24,0},{1,25},{9,17},{17,9},{25,1},{2,26},{10... | collective-permute-start | bytes 393224 | tf_op jit(solution)/shard_map/ppermute | solution.py:237
  5.6 0.7 %copy-done.3 = s32[64,5]{0,1:T(8,128)S(1)} copy-done((s32[64,5]{0,1:T(8,128)S(1)}, s32[64,5]{0,1:T(8,128)}, u32[]{:S(2)}) %copy-start.3) | copy-done | bytes 1304
  6.3 0.7 %copy-done.4 = f32[5]{0:T(128)S(1)} copy-done((f32[5]{0:T(128)S(1)}, f32[5]{0:T(128)}, u32[]{:S(2)}) %copy-start.4) | copy-done | bytes 44
  7.0 0.0 copy-start.9
  7.0 0.0 copy-start.10
  7.0 1.1 %prepare.1 = (bf16[64,128]{1,0:T(8,128)(2,1)S(1)}, bf16[64,128]{1,0:T(8,128)(2,1)S(1)}, f32[8,64,128]{2,1,0:T(8,128)S(1)}, f32[4,64,128]{2,1,0:T(8,128)S(1)}) custom-call(f32[4,64,128]{2,1,0:T(8,128)S(1)} %bitcast.14, f32[4,64,128]{2,1,0:T(8,128)S(1)} %bitcast.12, s32[5,64]{1,0:T(8,128)S(1)} %bitcast.15, f32[5]{0:T(128)S(1)} %copy-done.4), custom_call_target="tpu_custom_call" | custom-call | flops 25165824 | bytes 524288 | tf_op jit(solution)/shard_map/prepare/pallas_call | solution.py:85
  8.1 1.6 %collective-permute-start.2 = (f32[4,64,128]{2,1,0:T(8,128)S(1)}, f32[4,64,128]{2,1,0:T(8,128)S(1)}, u32[]{:S(2)}, u32[]{:S(2)}) collective-permute-start(f32[4,64,128]{2,1,0:T(8,128)S(1)} %get-tuple-element.21._), channel_id=1, source_target_pairs={{0,8},{8,0},{16,24},{24,16},{1,9},{9,1},{17,25},{25,17},{2,10},{10... | collective-permute-start | bytes 393224 | tf_op jit(solution)/shard_map/ppermute | solution.py:237
  9.7 0.0 collective-permute-done.block.refs_0_
  9.7 0.9 %collective-permute-start.1 = (f32[4,64,128]{2,1,0:T(8,128)S(1)}, f32[4,64,128]{2,1,0:T(8,128)S(1)}, u32[]{:S(2)}, u32[]{:S(2)}) collective-permute-start(f32[4,64,128]{2,1,0:T(8,128)S(1)} %hold.1), channel_id=1, source_target_pairs={{0,16},{8,24},{16,0},{24,8},{1,17},{9,25},{17,1},{25,9},{2,18},{10... | collective-permute-start | bytes 393224 | tf_op jit(solution)/shard_map/ppermute | solution.py:237
  10.6 2.2 %collective-permute-done.3.refs_1_ = f32[4,64,128]{2,1,0:T(8,128)S(1)} collective-permute-done((f32[4,64,128]{2,1,0:T(8,128)S(1)}, f32[4,64,128]{2,1,0:T(8,128)S(1)}, u32[]{:S(2)}, u32[]{:S(2)}) %collective-permute-start.3) | collective-permute-done | bytes 131104 | tf_op jit(solution)/shard_map/ppermute | solution.py:237
  12.8 0.5 %collective-permute-done.2.refs_0_ = f32[4,64,128]{2,1,0:T(8,128)S(1)} collective-permute-done((f32[4,64,128]{2,1,0:T(8,128)S(1)}, f32[4,64,128]{2,1,0:T(8,128)S(1)}, u32[]{:S(2)}, u32[]{:S(2)}) %collective-permute-start.2) | collective-permute-done | bytes 131104 | tf_op jit(solution)/shard_map/ppermute | solution.py:237
  13.3 0.2 add_sides.1.refs_5_
  13.5 1.4 %collective-permute-done.1.refs_1_ = f32[4,64,128]{2,1,0:T(8,128)S(1)} collective-permute-done((f32[4,64,128]{2,1,0:T(8,128)S(1)}, f32[4,64,128]{2,1,0:T(8,128)S(1)}, u32[]{:S(2)}, u32[]{:S(2)}) %collective-permute-start.1) | collective-permute-done | bytes 131104 | tf_op jit(solution)/shard_map/ppermute | solution.py:237
  14.9 0.2 finish.1
  15.1 0.1 collective-permute-start.4
  15.2 1.3 %collective-permute-done.4.swapped.refs_1_ = f32[4,64,128]{2,1,0:T(8,128)S(1)} collective-permute-done((f32[4,64,128]{2,1,0:T(8,128)S(1)}, f32[4,64,128]{2,1,0:T(8,128)S(1)}, u32[]{:S(2)}, u32[]{:S(2)}) %collective-permute-start.4) | collective-permute-done | bytes 131104 | tf_op jit(solution)/shard_map/ppermute | solution.py:484
  16.5 2.7 %collective-permute-start.5 = (f32[2,64,128]{2,1,0:T(8,128)S(1)}, f32[2,64,128]{2,1,0:T(8,128)S(1)}, u32[]{:S(2)}, u32[]{:S(2)}) collective-permute-start(f32[2,64,128]{2,1,0:T(8,128)S(1)} %get-tuple-element.27), channel_id=1, source_target_pairs={{0,4},{1,5},{2,6},{3,7},{4,0},{5,1},{6,2},{7,3},{8,12},{9,13},{10,... | collective-permute-start | bytes 196616 | tf_op jit(solution)/shard_map/ppermute | solution.py:484
  19.2 1.3 %collective-permute-start.6 = (f32[2,64,128]{2,1,0:T(8,128)S(1)}, f32[2,64,128]{2,1,0:T(8,128)S(1)}, u32[]{:S(2)}, u32[]{:S(2)}) collective-permute-start(f32[2,64,128]{2,1,0:T(8,128)S(1)} %get-tuple-element.28), channel_id=1, source_target_pairs={{0,6},{1,7},{2,4},{3,5},{4,2},{5,3},{6,0},{7,1},{8,14},{9,15},{10,... | collective-permute-start | bytes 196616 | tf_op jit(solution)/shard_map/ppermute | solution.py:484
  20.5 0.2 collective-permute-start.7
  20.8 0.0 copy-done.1
  20.8 0.0 copy-done
  20.8 0.0 copy-done.5
  20.8 0.0 copy-done.6
  20.8 0.0 copy-done.7
  20.8 0.0 copy-done.8
  20.8 0.0 copy-start.2
  20.8 1.4 %history.1 = (f32[5,64,1024]{2,1,0:T(8,128)S(1)}, f32[5,64,1024]{2,1,0:T(8,128)S(1)}, f32[1,128]{1,0:T(1,128)S(1)}, f32[5,8,128]{2,1,0:T(8,128)S(1)}, s32[2,8,128]{2,1,0:T(8,128)S(1)}) custom-call(f32[5,64,1024]{2,1,0:T(8,128)S(1)} %bitcast.7, f32[5,64,1024]{2,1,0:T(8,128)S(1)} %bitcast.8, s32[5]{0:T(128)S(1)} %copy-done.5, s32[64]{0:T(128)S(1)} %copy-done.6, ...), custom_call_target="tpu_custom_call" | custom-call | flops 2621440 | bytes 3932160 | tf_op jit(solution)/shard_map/history/pallas_call | solution.py:293
  22.3 2.0 %collective-permute-done.5.refs_2_ = f32[2,64,128]{2,1,0:T(8,128)S(1)} collective-permute-done((f32[2,64,128]{2,1,0:T(8,128)S(1)}, f32[2,64,128]{2,1,0:T(8,128)S(1)}, u32[]{:S(2)}, u32[]{:S(2)}) %collective-permute-start.5) | collective-permute-done | bytes 65568 | tf_op jit(solution)/shard_map/ppermute | solution.py:484
  24.3 1.3 %collective-permute-done.6.refs_3_ = f32[2,64,128]{2,1,0:T(8,128)S(1)} collective-permute-done((f32[2,64,128]{2,1,0:T(8,128)S(1)}, f32[2,64,128]{2,1,0:T(8,128)S(1)}, u32[]{:S(2)}, u32[]{:S(2)}) %collective-permute-start.6) | collective-permute-done | bytes 65568 | tf_op jit(solution)/shard_map/ppermute | solution.py:484
  25.6 0.3 collective-permute-done.7.refs_4_
  25.9 0.7 %residual.1 = (f32[64,1024]{1,0:T(8,128)S(1)}, f32[1,128]{1,0:T(1,128)S(1)}) custom-call(f32[4,64,128]{2,1,0:T(8,128)S(1)} %get-tuple-element.25.own.refs_0_, f32[4,64,128]{2,1,0:T(8,128)S(1)} %collective-permute-done.4.swapped.refs_1_, f32[2,64,128]{2,1,0:T(8,128)S(1)} %collective-permute-done.5.refs_2_, f32[2,64,128]{2,1,0:T(8,128)S(1)} %collective-permute-done.6.refs_3_, ...), custom_call_target="tpu_custom_call" | custom-call | tf_op jit(solution)/shard_map/residual/pallas_call | solution.py:356
  26.6 0.0 collective-permute-start.8
  26.6 1.1 %collective-permute-done.8 = f32[1,128]{1,0:T(1,128)S(1)} collective-permute-done((f32[1,128]{1,0:T(1,128)S(1)}, f32[1,128]{1,0:T(1,128)S(1)}, u32[]{:S(2)}, u32[]{:S(2)}) %collective-permute-start.8) | collective-permute-done | bytes 544 | tf_op jit(solution)/shard_map/ppermute | solution.py:484
  27.8 0.6 %collective-permute-start.11 = (f32[1,128]{1,0:T(1,128)S(1)}, f32[1,128]{1,0:T(1,128)S(1)}, u32[]{:S(2)}, u32[]{:S(2)}) collective-permute-start(f32[1,128]{1,0:T(1,128)S(1)} %add.12), channel_id=1, source_target_pairs={{0,2},{1,3},{2,0},{3,1},{4,6},{5,7},{6,4},{7,5},{8,10},{9,11},{10,... | collective-permute-start | bytes 1544 | tf_op jit(solution)/shard_map/ppermute | solution.py:484
  28.4 3.4 %collective-permute-start.10 = (f32[1,128]{1,0:T(1,128)S(1)}, f32[1,128]{1,0:T(1,128)S(1)}, u32[]{:S(2)}, u32[]{:S(2)}) collective-permute-start(f32[1,128]{1,0:T(1,128)S(1)} %add.12), channel_id=1, source_target_pairs={{0,6},{1,7},{2,4},{3,5},{4,2},{5,3},{6,0},{7,1},{8,14},{9,15},{10,... | collective-permute-start | bytes 1544 | tf_op jit(solution)/shard_map/ppermute | solution.py:484
  31.8 0.0 collective-permute-start.9
  31.8 0.0 collective-permute-done.11
  31.8 2.0 %collective-permute-done.10 = f32[1,128]{1,0:T(1,128)S(1)} collective-permute-done((f32[1,128]{1,0:T(1,128)S(1)}, f32[1,128]{1,0:T(1,128)S(1)}, u32[]{:S(2)}, u32[]{:S(2)}) %collective-permute-start.10) | collective-permute-done | bytes 544 | tf_op jit(solution)/shard_map/ppermute | solution.py:484
  33.7 2.5 %collective-permute-done.9 = f32[1,128]{1,0:T(1,128)S(1)} collective-permute-done((f32[1,128]{1,0:T(1,128)S(1)}, f32[1,128]{1,0:T(1,128)S(1)}, u32[]{:S(2)}, u32[]{:S(2)}) %collective-permute-start.9) | collective-permute-done | bytes 544 | tf_op jit(solution)/shard_map/ppermute | solution.py:484
  36.2 1.7 %collective-permute-start.14 = (f32[1,128]{1,0:T(1,128)S(1)}, f32[1,128]{1,0:T(1,128)S(1)}, u32[]{:S(2)}, u32[]{:S(2)}) collective-permute-start(f32[1,128]{1,0:T(1,128)S(1)} %add_add_fusion.refs_0_), channel_id=1, source_target_pairs={{0,24},{8,16},{16,8},{24,0},{1,25},{9,17},{17,9},{25,1},{2,26},{10... | collective-permute-start | bytes 1544 | tf_op jit(solution)/shard_map/ppermute | solution.py:493
  37.9 0.9 %collective-permute-start.13 = (f32[1,128]{1,0:T(1,128)S(1)}, f32[1,128]{1,0:T(1,128)S(1)}, u32[]{:S(2)}, u32[]{:S(2)}) collective-permute-start(f32[1,128]{1,0:T(1,128)S(1)} %add_add_fusion.refs_0_), channel_id=1, source_target_pairs={{0,16},{8,24},{16,0},{24,8},{1,17},{9,25},{17,1},{25,9},{2,18},{10... | collective-permute-start | bytes 1544 | tf_op jit(solution)/shard_map/ppermute | solution.py:493
  38.7 1.0 %collective-permute-start.12 = (f32[1,128]{1,0:T(1,128)S(1)}, f32[1,128]{1,0:T(1,128)S(1)}, u32[]{:S(2)}, u32[]{:S(2)}) collective-permute-start(f32[1,128]{1,0:T(1,128)S(1)} %add_add_fusion.refs_0_), channel_id=1, source_target_pairs={{0,8},{8,0},{16,24},{24,16},{1,9},{9,1},{17,25},{25,17},{2,10},{10... | collective-permute-start | bytes 1544 | tf_op jit(solution)/shard_map/ppermute | solution.py:493
  39.7 0.9 %collective-permute-done.14.refs_3_ = f32[1,128]{1,0:T(1,128)S(1)} collective-permute-done((f32[1,128]{1,0:T(1,128)S(1)}, f32[1,128]{1,0:T(1,128)S(1)}, u32[]{:S(2)}, u32[]{:S(2)}) %collective-permute-start.14) | collective-permute-done | bytes 544 | tf_op jit(solution)/shard_map/ppermute | solution.py:493
  40.7 0.8 %collective-permute-done.13.refs_2_ = f32[1,128]{1,0:T(1,128)S(1)} collective-permute-done((f32[1,128]{1,0:T(1,128)S(1)}, f32[1,128]{1,0:T(1,128)S(1)}, u32[]{:S(2)}, u32[]{:S(2)}) %collective-permute-start.13) | collective-permute-done | bytes 544 | tf_op jit(solution)/shard_map/ppermute | solution.py:493
  41.4 0.9 %collective-permute-done.12.refs_1_ = f32[1,128]{1,0:T(1,128)S(1)} collective-permute-done((f32[1,128]{1,0:T(1,128)S(1)}, f32[1,128]{1,0:T(1,128)S(1)}, u32[]{:S(2)}, u32[]{:S(2)}) %collective-permute-start.12) | collective-permute-done | bytes 544 | tf_op jit(solution)/shard_map/ppermute | solution.py:493
  42.3 1.0 %mix.1 = f32[64,1024]{1,0:T(8,128)} custom-call(f32[1,128]{1,0:T(1,128)S(1)} %add_add_fusion.refs_0_, f32[1,128]{1,0:T(1,128)S(1)} %collective-permute-done.12.refs_1_, f32[1,128]{1,0:T(1,128)S(1)} %collective-permute-done.13.refs_2_, f32[1,128]{1,0:T(1,128)S(1)} %collective-permute-done.14.refs_3_, f32[64,1024]{1,0:T(8,128)S(1)} %get-tuple-element.35.refs_4_, ...), custom_call_target="tpu_custom_call" | custom-call | tf_op jit(solution)/shard_map/mix/pallas_call | solution.py:440
  (15 shorter events, 0.1 us)
Async XLA Ops:
  0.0 20.8 %copy-start.1 = (f32[5,2,2,2,8,1024]{5,4,3,2,1,0:T(8,128)S(1)}, f32[5,2,2,2,8,1024]{5,4,3,2,1,0:T(8,128)}, u32[]{:S(2)}) copy-start(f32[5,2,2,2,8,1024]{5,4,3,2,1,0:T(8,128)} %param.15) | copy-start | bytes 3932164
  0.0 20.8 %copy-start = (f32[5,2,2,2,8,1024]{5,4,3,2,1,0:T(8,128)S(1)}, f32[5,2,2,2,8,1024]{5,4,3,2,1,0:T(8,128)}, u32[]{:S(2)}) copy-start(f32[5,2,2,2,8,1024]{5,4,3,2,1,0:T(8,128)} %param.14) | copy-start | bytes 3932164
  1.1 8.5 %collective-permute-start = (f32[4,64,128]{2,1,0:T(8,128)S(1)}, f32[4,64,128]{2,1,0:T(8,128)S(1)}, u32[]{:S(2)}, u32[]{:S(2)}) collective-permute-start(f32[4,64,128]{2,1,0:T(8,128)S(1)} %bitcast.13), channel_id=1, source_target_pairs={{0,8},{8,0},{16,24},{24,16},{1,9},{9,1},{17,25},{25,17},{2,10},{10... | collective-permute-start | bytes 393224 | tf_op jit(solution)/shard_map/ppermute | solution.py:237
  4.1 8.7 %collective-permute-start.3 = (f32[4,64,128]{2,1,0:T(8,128)S(1)}, f32[4,64,128]{2,1,0:T(8,128)S(1)}, u32[]{:S(2)}, u32[]{:S(2)}) collective-permute-start(f32[4,64,128]{2,1,0:T(8,128)S(1)} %bitcast.11), channel_id=1, source_target_pairs={{0,24},{8,16},{16,8},{24,0},{1,25},{9,17},{17,9},{25,1},{2,26},{10... | collective-permute-start | bytes 393224 | tf_op jit(solution)/shard_map/ppermute | solution.py:237
  5.6 0.7 %copy-start.3 = (s32[64,5]{0,1:T(8,128)S(1)}, s32[64,5]{0,1:T(8,128)}, u32[]{:S(2)}) copy-start(s32[64,5]{0,1:T(8,128)} %param.17) | copy-start | bytes 3844
  6.3 0.7 %copy-start.4 = (f32[5]{0:T(128)S(1)}, f32[5]{0:T(128)}, u32[]{:S(2)}) copy-start(f32[5]{0:T(128)} %refs_3_.2) | copy-start | bytes 64
  7.0 13.8 %copy-start.5 = (s32[5]{0:T(128)S(1)}, s32[5]{0:T(128)}, u32[]{:S(2)}) copy-start(s32[5]{0:T(128)} %refs_2_.1) | copy-start | bytes 64
  7.0 13.8 %copy-start.6 = (s32[64]{0:T(128)S(1)}, s32[64]{0:T(128)}, u32[]{:S(2)}) copy-start(s32[64]{0:T(128)} %refs_3_.3) | copy-start | bytes 772
  7.0 13.8 %copy-start.7 = (f32[4]{0:T(128)S(1)}, f32[4]{0:T(128)}, u32[]{:S(2)}) copy-start(f32[4]{0:T(128)} %refs_4_.1) | copy-start | bytes 52
  7.0 13.8 %copy-start.8 = (f32[2]{0:T(128)S(1)}, f32[2]{0:T(128)}, u32[]{:S(2)}) copy-start(f32[2]{0:T(128)} %refs_5_.1) | copy-start | bytes 28
  7.0 13.8 %copy-start.9 = (f32[2]{0:T(128)S(1)}, f32[2]{0:T(128)}, u32[]{:S(2)}) copy-start(f32[2]{0:T(128)} %refs_6_.1) | copy-start | bytes 28
  7.0 13.8 %copy-start.10 = (s32[2]{0:T(128)S(1)}, s32[2]{0:T(128)}, u32[]{:S(2)}) copy-start(s32[2]{0:T(128)} %refs_7_.1) | copy-start | bytes 28
  8.1 5.1 %collective-permute-start.2 = (f32[4,64,128]{2,1,0:T(8,128)S(1)}, f32[4,64,128]{2,1,0:T(8,128)S(1)}, u32[]{:S(2)}, u32[]{:S(2)}) collective-permute-start(f32[4,64,128]{2,1,0:T(8,128)S(1)} %get-tuple-element.21._), channel_id=1, source_target_pairs={{0,8},{8,0},{16,24},{24,16},{1,9},{9,1},{17,25},{25,17},{2,10},{10... | collective-permute-start | bytes 393224 | tf_op jit(solution)/shard_map/ppermute | solution.py:237
  9.7 5.2 %collective-permute-start.1 = (f32[4,64,128]{2,1,0:T(8,128)S(1)}, f32[4,64,128]{2,1,0:T(8,128)S(1)}, u32[]{:S(2)}, u32[]{:S(2)}) collective-permute-start(f32[4,64,128]{2,1,0:T(8,128)S(1)} %hold.1), channel_id=1, source_target_pairs={{0,16},{8,24},{16,0},{24,8},{1,17},{9,25},{17,1},{25,9},{2,18},{10... | collective-permute-start | bytes 393224 | tf_op jit(solution)/shard_map/ppermute | solution.py:237
  15.1 1.4 %collective-permute-start.4 = (f32[4,64,128]{2,1,0:T(8,128)S(1)}, f32[4,64,128]{2,1,0:T(8,128)S(1)}, u32[]{:S(2)}, u32[]{:S(2)}) collective-permute-start(f32[4,64,128]{2,1,0:T(8,128)S(1)} %get-tuple-element.26), channel_id=1, source_target_pairs={{0,1},{1,0},{2,3},{3,2},{4,5},{5,4},{6,7},{7,6},{8,9},{9,8},{10,11... | collective-permute-start | bytes 393224 | tf_op jit(solution)/shard_map/ppermute | solution.py:484
  16.5 7.8 %collective-permute-start.5 = (f32[2,64,128]{2,1,0:T(8,128)S(1)}, f32[2,64,128]{2,1,0:T(8,128)S(1)}, u32[]{:S(2)}, u32[]{:S(2)}) collective-permute-start(f32[2,64,128]{2,1,0:T(8,128)S(1)} %get-tuple-element.27), channel_id=1, source_target_pairs={{0,4},{1,5},{2,6},{3,7},{4,0},{5,1},{6,2},{7,3},{8,12},{9,13},{10,... | collective-permute-start | bytes 196616 | tf_op jit(solution)/shard_map/ppermute | solution.py:484
  19.2 6.4 %collective-permute-start.6 = (f32[2,64,128]{2,1,0:T(8,128)S(1)}, f32[2,64,128]{2,1,0:T(8,128)S(1)}, u32[]{:S(2)}, u32[]{:S(2)}) collective-permute-start(f32[2,64,128]{2,1,0:T(8,128)S(1)} %get-tuple-element.28), channel_id=1, source_target_pairs={{0,6},{1,7},{2,4},{3,5},{4,2},{5,3},{6,0},{7,1},{8,14},{9,15},{10,... | collective-permute-start | bytes 196616 | tf_op jit(solution)/shard_map/ppermute | solution.py:484
  20.5 5.4 %collective-permute-start.7 = (f32[2,64,128]{2,1,0:T(8,128)S(1)}, f32[2,64,128]{2,1,0:T(8,128)S(1)}, u32[]{:S(2)}, u32[]{:S(2)}) collective-permute-start(f32[2,64,128]{2,1,0:T(8,128)S(1)} %get-tuple-element.29), channel_id=1, source_target_pairs={{0,2},{1,3},{2,0},{3,1},{4,6},{5,7},{6,4},{7,5},{8,10},{9,11},{10,... | collective-permute-start | bytes 196616 | tf_op jit(solution)/shard_map/ppermute | solution.py:484
  20.8 5.1 %copy-start.2 = (f32[2,2,2,8,1024]{4,3,2,1,0:T(8,128)S(1)}, f32[2,2,2,8,1024]{4,3,2,1,0:T(8,128)}, u32[]{:S(2)}) copy-start(f32[2,2,2,8,1024]{4,3,2,1,0:T(8,128)} %param.13) | copy-start | bytes 786436
  26.6 1.1 %collective-permute-start.8 = (f32[1,128]{1,0:T(1,128)S(1)}, f32[1,128]{1,0:T(1,128)S(1)}, u32[]{:S(2)}, u32[]{:S(2)}) collective-permute-start(f32[1,128]{1,0:T(1,128)S(1)} %get-tuple-element.34), channel_id=1, source_target_pairs={{0,1},{1,0},{2,3},{3,2},{4,5},{5,4},{6,7},{7,6},{8,9},{9,8},{10,11... | collective-permute-start | bytes 1544 | tf_op jit(solution)/shard_map/ppermute | solution.py:484
  27.8 4.0 %collective-permute-start.11 = (f32[1,128]{1,0:T(1,128)S(1)}, f32[1,128]{1,0:T(1,128)S(1)}, u32[]{:S(2)}, u32[]{:S(2)}) collective-permute-start(f32[1,128]{1,0:T(1,128)S(1)} %add.12), channel_id=1, source_target_pairs={{0,2},{1,3},{2,0},{3,1},{4,6},{5,7},{6,4},{7,5},{8,10},{9,11},{10,... | collective-permute-start | bytes 1544 | tf_op jit(solution)/shard_map/ppermute | solution.py:484
  28.4 5.3 %collective-permute-start.10 = (f32[1,128]{1,0:T(1,128)S(1)}, f32[1,128]{1,0:T(1,128)S(1)}, u32[]{:S(2)}, u32[]{:S(2)}) collective-permute-start(f32[1,128]{1,0:T(1,128)S(1)} %add.12), channel_id=1, source_target_pairs={{0,6},{1,7},{2,4},{3,5},{4,2},{5,3},{6,0},{7,1},{8,14},{9,15},{10,... | collective-permute-start | bytes 1544 | tf_op jit(solution)/shard_map/ppermute | solution.py:484
  31.8 4.4 %collective-permute-start.9 = (f32[1,128]{1,0:T(1,128)S(1)}, f32[1,128]{1,0:T(1,128)S(1)}, u32[]{:S(2)}, u32[]{:S(2)}) collective-permute-start(f32[1,128]{1,0:T(1,128)S(1)} %add.12), channel_id=1, source_target_pairs={{0,4},{1,5},{2,6},{3,7},{4,0},{5,1},{6,2},{7,3},{8,12},{9,13},{10,... | collective-permute-start | bytes 1544 | tf_op jit(solution)/shard_map/ppermute | solution.py:484
  36.2 4.4 %collective-permute-start.14 = (f32[1,128]{1,0:T(1,128)S(1)}, f32[1,128]{1,0:T(1,128)S(1)}, u32[]{:S(2)}, u32[]{:S(2)}) collective-permute-start(f32[1,128]{1,0:T(1,128)S(1)} %add_add_fusion.refs_0_), channel_id=1, source_target_pairs={{0,24},{8,16},{16,8},{24,0},{1,25},{9,17},{17,9},{25,1},{2,26},{10... | collective-permute-start | bytes 1544 | tf_op jit(solution)/shard_map/ppermute | solution.py:493
  37.9 3.5 %collective-permute-start.13 = (f32[1,128]{1,0:T(1,128)S(1)}, f32[1,128]{1,0:T(1,128)S(1)}, u32[]{:S(2)}, u32[]{:S(2)}) collective-permute-start(f32[1,128]{1,0:T(1,128)S(1)} %add_add_fusion.refs_0_), channel_id=1, source_target_pairs={{0,16},{8,24},{16,0},{24,8},{1,17},{9,25},{17,1},{25,9},{2,18},{10... | collective-permute-start | bytes 1544 | tf_op jit(solution)/shard_map/ppermute | solution.py:493
  38.7 3.5 %collective-permute-start.12 = (f32[1,128]{1,0:T(1,128)S(1)}, f32[1,128]{1,0:T(1,128)S(1)}, u32[]{:S(2)}, u32[]{:S(2)}) collective-permute-start(f32[1,128]{1,0:T(1,128)S(1)} %add_add_fusion.refs_0_), channel_id=1, source_target_pairs={{0,8},{8,0},{16,24},{24,16},{1,9},{9,1},{17,25},{25,17},{2,10},{10... | collective-permute-start | bytes 1544 | tf_op jit(solution)/shard_map/ppermute | solution.py:493

commit v11 on v9

--- a/solution.py
+++ b/solution.py
@@ -483,7 +483,7 @@
     fresh, lines = residual(
         kept, swapped, smeared, flat, residuals, old_line, gains, shifts, groups * parts
     )
-    lines = lax.all_to_all(lines, ("kgrp", "energy"), split_axis=0, concat_axis=0, tiled=True)
+    lines = lax.all_to_all(lines, ("energy", "kgrp"), split_axis=0, concat_axis=0, tiled=True)
     entries = float(flat.size * groups * parts)
     return mix(lines, fresh, flat, aged, entries).reshape(current.shape)
 

time: 39.4 us -> 39.4 us (level)
  no operation moved by 1% of the time
where the time goes in v11:
time: 39.4 us; the launch traced here: 39.2 us
  blocking collectives  11.6 us (29%)
  starting transfers between devices  11.3 us (29%)
  waiting for transfers between devices  9.04 us (23%)
  Pallas kernels  4.61 us (12%)
  local copies, waits for them, and re-layouts  2.52 us (6%)
    all_to_all x1, blocking collectives, per_device(): lax.all_to_all(lines, ('energy', 'kgrp'), split_axis=0, concat_axis=0, ti...  11.6 us
    ppermute x4, starting transfers between devices, smear(): lax.ppermute(block, 'kgrp', [(i, i ^ flip) for i in range(groups)])  7 us
    ppermute x4, waiting for transfers between devices, per_device(): lax.ppermute(block, 'energy', [(e, e ^ m) for e in range(parts)])  5 us
    ppermute x4, starting transfers between devices, per_device(): lax.ppermute(block, 'energy', [(e, e ^ m) for e in range(parts)])  4.31 us
    ppermute x4, waiting for transfers between devices, smear(): lax.ppermute(block, 'kgrp', [(i, i ^ flip) for i in range(groups)])  4.04 us
    pallas_call x1, Pallas kernels, history(): pl.pallas_call(lambda *refs: history_kernel(rows, *refs), out_shape=(jax....  1.43 us
    unnamed x22, local copies, waits for them, and re-layouts  1.38 us
    slice x1, local copies, waits for them, and re-layouts, smear(): head, tail = (own[:half], own[half:])  1.14 us
  transfers between devices with their start and end apart: 8, of which 7 were waited for; matrix products, arithmetic and copies ran while one was open for 0% of the time, Pallas kernels for 7%

profile of v11, /device:TPU:0, one launch (start us, length us, event | category | flops | bytes accessed | tf_op | source)
XLA Modules:
  0.0 39.2 jit_solution(306078043968109510)
XLA Ops:
  0.0 0.0 copy-start.1
  0.0 0.0 copy-start
  0.0 1.1 %fusion = (f32[1,2,2,64,128]{4,3,2,1,0:T(8,128)S(1)}, f32[1,2,2,64,128]{4,3,2,1,0:T(8,128)S(1)}) fusion(f32[2,2,2,64,128]{4,3,2,1,0:T(8,128)} %param.12), kind=kLoop, calls=%fused_computation | loop fusion | bytes 524288 | tf_op jit(solution)/shard_map/slice | solution.py:239
  1.1 3.0 %collective-permute-start = (f32[4,64,128]{2,1,0:T(8,128)S(1)}, f32[4,64,128]{2,1,0:T(8,128)S(1)}, u32[]{:S(2)}, u32[]{:S(2)}) collective-permute-start(f32[4,64,128]{2,1,0:T(8,128)S(1)} %bitcast.13), channel_id=1, source_target_pairs={{0,8},{8,0},{16,24},{24,16},{1,9},{9,1},{17,25},{25,17},{2,10},{10... | collective-permute-start | bytes 393224 | tf_op jit(solution)/shard_map/ppermute | solution.py:237
  4.1 1.5 %collective-permute-start.3 = (f32[4,64,128]{2,1,0:T(8,128)S(1)}, f32[4,64,128]{2,1,0:T(8,128)S(1)}, u32[]{:S(2)}, u32[]{:S(2)}) collective-permute-start(f32[4,64,128]{2,1,0:T(8,128)S(1)} %bitcast.11), channel_id=1, source_target_pairs={{0,24},{8,16},{16,8},{24,0},{1,25},{9,17},{17,9},{25,1},{2,26},{10... | collective-permute-start | bytes 393224 | tf_op jit(solution)/shard_map/ppermute | solution.py:237
  5.6 0.0 copy-start.3
  5.6 0.7 %copy-done.3 = s32[64,5]{0,1:T(8,128)S(1)} copy-done((s32[64,5]{0,1:T(8,128)S(1)}, s32[64,5]{0,1:T(8,128)}, u32[]{:S(2)}) %copy-start.3) | copy-done | bytes 1304
  6.3 0.0 copy-start.4
  6.3 0.7 %copy-done.4 = f32[5]{0:T(128)S(1)} copy-done((f32[5]{0:T(128)S(1)}, f32[5]{0:T(128)}, u32[]{:S(2)}) %copy-start.4) | copy-done | bytes 44
  7.0 0.0 copy-start.5
  7.0 0.0 copy-start.6
  7.0 0.0 copy-start.7
  7.0 0.0 copy-start.8
  7.0 0.0 copy-start.9
  7.0 0.0 copy-start.10
  7.0 1.1 %prepare.1 = (bf16[64,128]{1,0:T(8,128)(2,1)S(1)}, bf16[64,128]{1,0:T(8,128)(2,1)S(1)}, f32[8,64,128]{2,1,0:T(8,128)S(1)}, f32[4,64,128]{2,1,0:T(8,128)S(1)}) custom-call(f32[4,64,128]{2,1,0:T(8,128)S(1)} %bitcast.14, f32[4,64,128]{2,1,0:T(8,128)S(1)} %bitcast.12, s32[5,64]{1,0:T(8,128)S(1)} %bitcast.15, f32[5]{0:T(128)S(1)} %copy-done.4), custom_call_target="tpu_custom_call" | custom-call | flops 25165824 | bytes 524288 | tf_op jit(solution)/shard_map/prepare/pallas_call | solution.py:85
  8.1 1.6 %collective-permute-start.2 = (f32[4,64,128]{2,1,0:T(8,128)S(1)}, f32[4,64,128]{2,1,0:T(8,128)S(1)}, u32[]{:S(2)}, u32[]{:S(2)}) collective-permute-start(f32[4,64,128]{2,1,0:T(8,128)S(1)} %get-tuple-element.21._), channel_id=1, source_target_pairs={{0,8},{8,0},{16,24},{24,16},{1,9},{9,1},{17,25},{25,17},{2,10},{10... | collective-permute-start | bytes 393224 | tf_op jit(solution)/shard_map/ppermute | solution.py:237
  9.7 0.0 collective-permute-done.block.refs_0_
  9.7 0.9 %collective-permute-start.1 = (f32[4,64,128]{2,1,0:T(8,128)S(1)}, f32[4,64,128]{2,1,0:T(8,128)S(1)}, u32[]{:S(2)}, u32[]{:S(2)}) collective-permute-start(f32[4,64,128]{2,1,0:T(8,128)S(1)} %hold.1), channel_id=1, source_target_pairs={{0,16},{8,24},{16,0},{24,8},{1,17},{9,25},{17,1},{25,9},{2,18},{10... | collective-permute-start | bytes 393224 | tf_op jit(solution)/shard_map/ppermute | solution.py:237
  10.6 2.2 %collective-permute-done.3.refs_1_ = f32[4,64,128]{2,1,0:T(8,128)S(1)} collective-permute-done((f32[4,64,128]{2,1,0:T(8,128)S(1)}, f32[4,64,128]{2,1,0:T(8,128)S(1)}, u32[]{:S(2)}, u32[]{:S(2)}) %collective-permute-start.3) | collective-permute-done | bytes 131104 | tf_op jit(solution)/shard_map/ppermute | solution.py:237
  12.8 0.5 %collective-permute-done.2.refs_0_ = f32[4,64,128]{2,1,0:T(8,128)S(1)} collective-permute-done((f32[4,64,128]{2,1,0:T(8,128)S(1)}, f32[4,64,128]{2,1,0:T(8,128)S(1)}, u32[]{:S(2)}, u32[]{:S(2)}) %collective-permute-start.2) | collective-permute-done | bytes 131104 | tf_op jit(solution)/shard_map/ppermute | solution.py:237
  13.3 0.2 add_sides.1.refs_5_
  13.5 1.4 %collective-permute-done.1.refs_1_ = f32[4,64,128]{2,1,0:T(8,128)S(1)} collective-permute-done((f32[4,64,128]{2,1,0:T(8,128)S(1)}, f32[4,64,128]{2,1,0:T(8,128)S(1)}, u32[]{:S(2)}, u32[]{:S(2)}) %collective-permute-start.1) | collective-permute-done | bytes 131104 | tf_op jit(solution)/shard_map/ppermute | solution.py:237
  14.9 0.2 finish.1
  15.1 0.1 collective-permute-start.4
  15.2 1.3 %collective-permute-done.4.swapped.refs_1_ = f32[4,64,128]{2,1,0:T(8,128)S(1)} collective-permute-done((f32[4,64,128]{2,1,0:T(8,128)S(1)}, f32[4,64,128]{2,1,0:T(8,128)S(1)}, u32[]{:S(2)}, u32[]{:S(2)}) %collective-permute-start.4) | collective-permute-done | bytes 131104 | tf_op jit(solution)/shard_map/ppermute | solution.py:480
  16.5 2.7 %collective-permute-start.5 = (f32[2,64,128]{2,1,0:T(8,128)S(1)}, f32[2,64,128]{2,1,0:T(8,128)S(1)}, u32[]{:S(2)}, u32[]{:S(2)}) collective-permute-start(f32[2,64,128]{2,1,0:T(8,128)S(1)} %get-tuple-element.27), channel_id=1, source_target_pairs={{0,4},{1,5},{2,6},{3,7},{4,0},{5,1},{6,2},{7,3},{8,12},{9,13},{10,... | collective-permute-start | bytes 196616 | tf_op jit(solution)/shard_map/ppermute | solution.py:480
  19.2 1.3 %collective-permute-start.6 = (f32[2,64,128]{2,1,0:T(8,128)S(1)}, f32[2,64,128]{2,1,0:T(8,128)S(1)}, u32[]{:S(2)}, u32[]{:S(2)}) collective-permute-start(f32[2,64,128]{2,1,0:T(8,128)S(1)} %get-tuple-element.28), channel_id=1, source_target_pairs={{0,6},{1,7},{2,4},{3,5},{4,2},{5,3},{6,0},{7,1},{8,14},{9,15},{10,... | collective-permute-start | bytes 196616 | tf_op jit(solution)/shard_map/ppermute | solution.py:480
  20.5 0.2 collective-permute-start.7
  20.8 0.0 copy-done.1
  20.8 0.0 copy-done
  20.8 0.0 copy-done.5
  20.8 0.0 copy-done.6
  20.8 0.0 copy-done.7
  20.8 0.0 copy-done.8
  20.8 0.0 copy-done.9
  20.8 0.0 copy-done.10
  20.8 0.0 copy-start.2
  20.8 1.4 %history.1 = (f32[5,64,1024]{2,1,0:T(8,128)S(1)}, f32[5,64,1024]{2,1,0:T(8,128)S(1)}, f32[1,128]{1,0:T(1,128)S(1)}, f32[5,8,128]{2,1,0:T(8,128)S(1)}, s32[2,8,128]{2,1,0:T(8,128)S(1)}) custom-call(f32[5,64,1024]{2,1,0:T(8,128)S(1)} %bitcast.7, f32[5,64,1024]{2,1,0:T(8,128)S(1)} %bitcast.8, s32[5]{0:T(128)S(1)} %copy-done.5, s32[64]{0:T(128)S(1)} %copy-done.6, ...), custom_call_target="tpu_custom_call" | custom-call | flops 2621440 | bytes 3932160 | tf_op jit(solution)/shard_map/history/pallas_call | solution.py:293
  22.3 2.0 %collective-permute-done.5.refs_2_ = f32[2,64,128]{2,1,0:T(8,128)S(1)} collective-permute-done((f32[2,64,128]{2,1,0:T(8,128)S(1)}, f32[2,64,128]{2,1,0:T(8,128)S(1)}, u32[]{:S(2)}, u32[]{:S(2)}) %collective-permute-start.5) | collective-permute-done | bytes 65568 | tf_op jit(solution)/shard_map/ppermute | solution.py:480
  24.3 1.3 %collective-permute-done.6.refs_3_ = f32[2,64,128]{2,1,0:T(8,128)S(1)} collective-permute-done((f32[2,64,128]{2,1,0:T(8,128)S(1)}, f32[2,64,128]{2,1,0:T(8,128)S(1)}, u32[]{:S(2)}, u32[]{:S(2)}) %collective-permute-start.6) | collective-permute-done | bytes 65568 | tf_op jit(solution)/shard_map/ppermute | solution.py:480
  25.6 0.3 collective-permute-done.7.refs_4_
  25.9 0.0 copy-done.2
  25.9 0.7 %residual.1 = (f32[64,1024]{1,0:T(8,128)S(1)}, f32[32,1,128]{2,1,0:T(1,128)S(1)}) custom-call(f32[4,64,128]{2,1,0:T(8,128)S(1)} %get-tuple-element.25.own.refs_0_, f32[4,64,128]{2,1,0:T(8,128)S(1)} %collective-permute-done.4.swapped.refs_1_, f32[2,64,128]{2,1,0:T(8,128)S(1)} %collective-permute-done.5.refs_2_, ...), custom_call_target="tpu_custom_call" | custom-call | tf_op jit(solution)/shard_map/residual/pallas_call | solution.py:356
  26.6 11.6 %all_to_all.5.refs_0_ = f32[32,1,128]{2,1,0:T(1,128)S(1)} all-to-all(f32[32,1,128]{2,1,0:T(1,128)S(1)} %get-tuple-element.34), channel_id=1, replica_groups=mesh['kgrp'=4,'energy'=8] {'energy','kgrp'}, dimensions={0} | all-to-all | bytes 32768 | tf_op jit(solution)/shard_map/all_to_all | solution.py:486
  38.2 1.0 %mix.1 = f32[64,1024]{1,0:T(8,128)} custom-call(f32[32,1,128]{2,1,0:T(1,128)S(1)} %all_to_all.5.refs_0_, f32[64,1024]{1,0:T(8,128)S(1)} %get-tuple-element.35.refs_1_, f32[64,1024]{1,0:T(8,128)S(1)} %bitcast.10, f32[5,64,1024]{2,1,0:T(8,128)S(1)} %get-tuple-element.36.refs_3_), custom_call_target="tpu_custom_call" | custom-call | tf_op jit(solution)/shard_map/mix/pallas_call | solution.py:436
  (2 shorter events, 0.0 us)
Async XLA Ops:
  0.0 20.8 %copy-start.1 = (f32[5,2,2,2,8,1024]{5,4,3,2,1,0:T(8,128)S(1)}, f32[5,2,2,2,8,1024]{5,4,3,2,1,0:T(8,128)}, u32[]{:S(2)}) copy-start(f32[5,2,2,2,8,1024]{5,4,3,2,1,0:T(8,128)} %param.15) | copy-start | bytes 3932164
  0.0 20.8 %copy-start = (f32[5,2,2,2,8,1024]{5,4,3,2,1,0:T(8,128)S(1)}, f32[5,2,2,2,8,1024]{5,4,3,2,1,0:T(8,128)}, u32[]{:S(2)}) copy-start(f32[5,2,2,2,8,1024]{5,4,3,2,1,0:T(8,128)} %param.14) | copy-start | bytes 3932164
  1.1 8.5 %collective-permute-start = (f32[4,64,128]{2,1,0:T(8,128)S(1)}, f32[4,64,128]{2,1,0:T(8,128)S(1)}, u32[]{:S(2)}, u32[]{:S(2)}) collective-permute-start(f32[4,64,128]{2,1,0:T(8,128)S(1)} %bitcast.13), channel_id=1, source_target_pairs={{0,8},{8,0},{16,24},{24,16},{1,9},{9,1},{17,25},{25,17},{2,10},{10... | collective-permute-start | bytes 393224 | tf_op jit(solution)/shard_map/ppermute | solution.py:237
  4.1 8.7 %collective-permute-start.3 = (f32[4,64,128]{2,1,0:T(8,128)S(1)}, f32[4,64,128]{2,1,0:T(8,128)S(1)}, u32[]{:S(2)}, u32[]{:S(2)}) collective-permute-start(f32[4,64,128]{2,1,0:T(8,128)S(1)} %bitcast.11), channel_id=1, source_target_pairs={{0,24},{8,16},{16,8},{24,0},{1,25},{9,17},{17,9},{25,1},{2,26},{10... | collective-permute-start | bytes 393224 | tf_op jit(solution)/shard_map/ppermute | solution.py:237
  5.6 0.7 %copy-start.3 = (s32[64,5]{0,1:T(8,128)S(1)}, s32[64,5]{0,1:T(8,128)}, u32[]{:S(2)}) copy-start(s32[64,5]{0,1:T(8,128)} %param.17) | copy-start | bytes 3844
  6.3 0.7 %copy-start.4 = (f32[5]{0:T(128)S(1)}, f32[5]{0:T(128)}, u32[]{:S(2)}) copy-start(f32[5]{0:T(128)} %refs_3_.2) | copy-start | bytes 64
  7.0 13.8 %copy-start.5 = (s32[5]{0:T(128)S(1)}, s32[5]{0:T(128)}, u32[]{:S(2)}) copy-start(s32[5]{0:T(128)} %refs_2_.1) | copy-start | bytes 64
  7.0 13.8 %copy-start.6 = (s32[64]{0:T(128)S(1)}, s32[64]{0:T(128)}, u32[]{:S(2)}) copy-start(s32[64]{0:T(128)} %refs_3_.3) | copy-start | bytes 772
  7.0 13.8 %copy-start.7 = (f32[4]{0:T(128)S(1)}, f32[4]{0:T(128)}, u32[]{:S(2)}) copy-start(f32[4]{0:T(128)} %refs_4_.1) | copy-start | bytes 52
  7.0 13.8 %copy-start.8 = (f32[2]{0:T(128)S(1)}, f32[2]{0:T(128)}, u32[]{:S(2)}) copy-start(f32[2]{0:T(128)} %refs_5_.1) | copy-start | bytes 28
  7.0 13.8 %copy-start.9 = (f32[2]{0:T(128)S(1)}, f32[2]{0:T(128)}, u32[]{:S(2)}) copy-start(f32[2]{0:T(128)} %refs_6_.1) | copy-start | bytes 28
  7.0 13.8 %copy-start.10 = (s32[2]{0:T(128)S(1)}, s32[2]{0:T(128)}, u32[]{:S(2)}) copy-start(s32[2]{0:T(128)} %refs_7_.1) | copy-start | bytes 28
  8.1 5.1 %collective-permute-start.2 = (f32[4,64,128]{2,1,0:T(8,128)S(1)}, f32[4,64,128]{2,1,0:T(8,128)S(1)}, u32[]{:S(2)}, u32[]{:S(2)}) collective-permute-start(f32[4,64,128]{2,1,0:T(8,128)S(1)} %get-tuple-element.21._), channel_id=1, source_target_pairs={{0,8},{8,0},{16,24},{24,16},{1,9},{9,1},{17,25},{25,17},{2,10},{10... | collective-permute-start | bytes 393224 | tf_op jit(solution)/shard_map/ppermute | solution.py:237
  9.7 5.2 %collective-permute-start.1 = (f32[4,64,128]{2,1,0:T(8,128)S(1)}, f32[4,64,128]{2,1,0:T(8,128)S(1)}, u32[]{:S(2)}, u32[]{:S(2)}) collective-permute-start(f32[4,64,128]{2,1,0:T(8,128)S(1)} %hold.1), channel_id=1, source_target_pairs={{0,16},{8,24},{16,0},{24,8},{1,17},{9,25},{17,1},{25,9},{2,18},{10... | collective-permute-start | bytes 393224 | tf_op jit(solution)/shard_map/ppermute | solution.py:237
  15.1 1.4 %collective-permute-start.4 = (f32[4,64,128]{2,1,0:T(8,128)S(1)}, f32[4,64,128]{2,1,0:T(8,128)S(1)}, u32[]{:S(2)}, u32[]{:S(2)}) collective-permute-start(f32[4,64,128]{2,1,0:T(8,128)S(1)} %get-tuple-element.26), channel_id=1, source_target_pairs={{0,1},{1,0},{2,3},{3,2},{4,5},{5,4},{6,7},{7,6},{8,9},{9,8},{10,11... | collective-permute-start | bytes 393224 | tf_op jit(solution)/shard_map/ppermute | solution.py:480
  16.5 7.8 %collective-permute-start.5 = (f32[2,64,128]{2,1,0:T(8,128)S(1)}, f32[2,64,128]{2,1,0:T(8,128)S(1)}, u32[]{:S(2)}, u32[]{:S(2)}) collective-permute-start(f32[2,64,128]{2,1,0:T(8,128)S(1)} %get-tuple-element.27), channel_id=1, source_target_pairs={{0,4},{1,5},{2,6},{3,7},{4,0},{5,1},{6,2},{7,3},{8,12},{9,13},{10,... | collective-permute-start | bytes 196616 | tf_op jit(solution)/shard_map/ppermute | solution.py:480
  19.2 6.4 %collective-permute-start.6 = (f32[2,64,128]{2,1,0:T(8,128)S(1)}, f32[2,64,128]{2,1,0:T(8,128)S(1)}, u32[]{:S(2)}, u32[]{:S(2)}) collective-permute-start(f32[2,64,128]{2,1,0:T(8,128)S(1)} %get-tuple-element.28), channel_id=1, source_target_pairs={{0,6},{1,7},{2,4},{3,5},{4,2},{5,3},{6,0},{7,1},{8,14},{9,15},{10,... | collective-permute-start | bytes 196616 | tf_op jit(solution)/shard_map/ppermute | solution.py:480
  20.5 5.4 %collective-permute-start.7 = (f32[2,64,128]{2,1,0:T(8,128)S(1)}, f32[2,64,128]{2,1,0:T(8,128)S(1)}, u32[]{:S(2)}, u32[]{:S(2)}) collective-permute-start(f32[2,64,128]{2,1,0:T(8,128)S(1)} %get-tuple-element.29), channel_id=1, source_target_pairs={{0,2},{1,3},{2,0},{3,1},{4,6},{5,7},{6,4},{7,5},{8,10},{9,11},{10,... | collective-permute-start | bytes 196616 | tf_op jit(solution)/shard_map/ppermute | solution.py:480
  20.8 5.1 %copy-start.2 = (f32[2,2,2,8,1024]{4,3,2,1,0:T(8,128)S(1)}, f32[2,2,2,8,1024]{4,3,2,1,0:T(8,128)}, u32[]{:S(2)}) copy-start(f32[2,2,2,8,1024]{4,3,2,1,0:T(8,128)} %param.13) | copy-start | bytes 786436

commit v12 on v11

--- a/solution.py
+++ b/solution.py
@@ -187,7 +187,8 @@
 
 def chip_order(parts):
     chips = parts // 2
-    return [*range(chips // 2, chips), *range(1, chips // 2)] if chips > 1 else []
+    half = chips // 2
+    return [half, *range(1, half), *range(half + 1, chips)] if chips > 1 else []
 
 
 def join_kernel(own, swapped, *out):

time: 39.4 us -> 38.7 us (0.982)
  blocking collectives: 11.6 us -> 10 us
  waiting for transfers between devices: 9.04 us -> 9.71 us
    all_to_all x1, blocking collectives: 11.6 us -> 10 us  [per_device(): lax.all_to_all(lines, ('energy', 'kgrp'), split_axis=0, concat_axis=0, ti...]
    ppermute x4, waiting for transfers between devices: 5 us -> 5.68 us  [per_device(): lax.ppermute(block, 'energy', [(e, e ^ m) for e in range(parts)])]
where the time goes in v12:
time: 38.7 us; the launch traced here: 38.5 us
  starting transfers between devices  11.5 us (30%)
  blocking collectives  10 us (26%)
  waiting for transfers between devices  9.71 us (25%)
  Pallas kernels  4.61 us (12%)
  local copies, waits for them, and re-layouts  2.52 us (7%)
    all_to_all x1, blocking collectives, per_device(): lax.all_to_all(lines, ('energy', 'kgrp'), split_axis=0, concat_axis=0, ti...  10 us
    ppermute x4, starting transfers between devices, smear(): lax.ppermute(block, 'kgrp', [(i, i ^ flip) for i in range(groups)])  7 us
    ppermute x4, waiting for transfers between devices, per_device(): lax.ppermute(block, 'energy', [(e, e ^ m) for e in range(parts)])  5.68 us
    ppermute x4, starting transfers between devices, per_device(): lax.ppermute(block, 'energy', [(e, e ^ m) for e in range(parts)])  4.52 us
    ppermute x4, waiting for transfers between devices, smear(): lax.ppermute(block, 'kgrp', [(i, i ^ flip) for i in range(groups)])  4.04 us
    pallas_call x1, Pallas kernels, history(): pl.pallas_call(lambda *refs: history_kernel(rows, *refs), out_shape=(jax....  1.43 us
    unnamed x22, local copies, waits for them, and re-layouts  1.38 us
    slice x1, local copies, waits for them, and re-layouts, smear(): head, tail = (own[:half], own[half:])  1.14 us
  transfers between devices with their start and end apart: 8, of which 7 were waited for; matrix products, arithmetic and copies ran while one was open for 0% of the time, Pallas kernels for 7%

profile of v12, /device:TPU:0, one launch (start us, length us, event | category | flops | bytes accessed | tf_op | source)
XLA Modules:
  0.0 38.5 jit_solution(1465085879463817991)
XLA Ops:
  0.0 0.0 copy-start.1
  0.0 0.0 copy-start
  0.0 1.1 %fusion = (f32[1,2,2,64,128]{4,3,2,1,0:T(8,128)S(1)}, f32[1,2,2,64,128]{4,3,2,1,0:T(8,128)S(1)}) fusion(f32[2,2,2,64,128]{4,3,2,1,0:T(8,128)} %param.12), kind=kLoop, calls=%fused_computation | loop fusion | bytes 524288 | tf_op jit(solution)/shard_map/slice | solution.py:240
  1.1 3.0 %collective-permute-start = (f32[4,64,128]{2,1,0:T(8,128)S(1)}, f32[4,64,128]{2,1,0:T(8,128)S(1)}, u32[]{:S(2)}, u32[]{:S(2)}) collective-permute-start(f32[4,64,128]{2,1,0:T(8,128)S(1)} %bitcast.13), channel_id=1, source_target_pairs={{0,8},{8,0},{16,24},{24,16},{1,9},{9,1},{17,25},{25,17},{2,10},{10... | collective-permute-start | bytes 393224 | tf_op jit(solution)/shard_map/ppermute | solution.py:238
  4.1 1.5 %collective-permute-start.3 = (f32[4,64,128]{2,1,0:T(8,128)S(1)}, f32[4,64,128]{2,1,0:T(8,128)S(1)}, u32[]{:S(2)}, u32[]{:S(2)}) collective-permute-start(f32[4,64,128]{2,1,0:T(8,128)S(1)} %bitcast.11), channel_id=1, source_target_pairs={{0,24},{8,16},{16,8},{24,0},{1,25},{9,17},{17,9},{25,1},{2,26},{10... | collective-permute-start | bytes 393224 | tf_op jit(solution)/shard_map/ppermute | solution.py:238
  5.6 0.0 copy-start.3
  5.6 0.7 %copy-done.3 = s32[64,5]{0,1:T(8,128)S(1)} copy-done((s32[64,5]{0,1:T(8,128)S(1)}, s32[64,5]{0,1:T(8,128)}, u32[]{:S(2)}) %copy-start.3) | copy-done | bytes 1304
  6.3 0.0 copy-start.4
  6.3 0.7 %copy-done.4 = f32[5]{0:T(128)S(1)} copy-done((f32[5]{0:T(128)S(1)}, f32[5]{0:T(128)}, u32[]{:S(2)}) %copy-start.4) | copy-done | bytes 44
  7.0 0.0 copy-start.5
  7.0 0.0 copy-start.6
  7.0 0.0 copy-start.7
  7.0 0.0 copy-start.8
  7.0 0.0 copy-start.9
  7.0 0.0 copy-start.10
  7.0 1.1 %prepare.1 = (bf16[64,128]{1,0:T(8,128)(2,1)S(1)}, bf16[64,128]{1,0:T(8,128)(2,1)S(1)}, f32[8,64,128]{2,1,0:T(8,128)S(1)}, f32[4,64,128]{2,1,0:T(8,128)S(1)}) custom-call(f32[4,64,128]{2,1,0:T(8,128)S(1)} %bitcast.14, f32[4,64,128]{2,1,0:T(8,128)S(1)} %bitcast.12, s32[5,64]{1,0:T(8,128)S(1)} %bitcast.15, f32[5]{0:T(128)S(1)} %copy-done.4), custom_call_target="tpu_custom_call" | custom-call | flops 25165824 | bytes 524288 | tf_op jit(solution)/shard_map/prepare/pallas_call | solution.py:85
  8.1 1.6 %collective-permute-start.2 = (f32[4,64,128]{2,1,0:T(8,128)S(1)}, f32[4,64,128]{2,1,0:T(8,128)S(1)}, u32[]{:S(2)}, u32[]{:S(2)}) collective-permute-start(f32[4,64,128]{2,1,0:T(8,128)S(1)} %get-tuple-element.21._), channel_id=1, source_target_pairs={{0,8},{8,0},{16,24},{24,16},{1,9},{9,1},{17,25},{25,17},{2,10},{10... | collective-permute-start | bytes 393224 | tf_op jit(solution)/shard_map/ppermute | solution.py:238
  9.7 0.0 collective-permute-done.block.refs_0_
  9.7 0.9 %collective-permute-start.1 = (f32[4,64,128]{2,1,0:T(8,128)S(1)}, f32[4,64,128]{2,1,0:T(8,128)S(1)}, u32[]{:S(2)}, u32[]{:S(2)}) collective-permute-start(f32[4,64,128]{2,1,0:T(8,128)S(1)} %hold.1), channel_id=1, source_target_pairs={{0,16},{8,24},{16,0},{24,8},{1,17},{9,25},{17,1},{25,9},{2,18},{10... | collective-permute-start | bytes 393224 | tf_op jit(solution)/shard_map/ppermute | solution.py:238
  10.6 2.2 %collective-permute-done.3.refs_1_ = f32[4,64,128]{2,1,0:T(8,128)S(1)} collective-permute-done((f32[4,64,128]{2,1,0:T(8,128)S(1)}, f32[4,64,128]{2,1,0:T(8,128)S(1)}, u32[]{:S(2)}, u32[]{:S(2)}) %collective-permute-start.3) | collective-permute-done | bytes 131104 | tf_op jit(solution)/shard_map/ppermute | solution.py:238
  12.8 0.5 %collective-permute-done.2.refs_0_ = f32[4,64,128]{2,1,0:T(8,128)S(1)} collective-permute-done((f32[4,64,128]{2,1,0:T(8,128)S(1)}, f32[4,64,128]{2,1,0:T(8,128)S(1)}, u32[]{:S(2)}, u32[]{:S(2)}) %collective-permute-start.2) | collective-permute-done | bytes 131104 | tf_op jit(solution)/shard_map/ppermute | solution.py:238
  13.3 0.2 add_sides.1.refs_5_
  13.5 1.4 %collective-permute-done.1.refs_1_ = f32[4,64,128]{2,1,0:T(8,128)S(1)} collective-permute-done((f32[4,64,128]{2,1,0:T(8,128)S(1)}, f32[4,64,128]{2,1,0:T(8,128)S(1)}, u32[]{:S(2)}, u32[]{:S(2)}) %collective-permute-start.1) | collective-permute-done | bytes 131104 | tf_op jit(solution)/shard_map/ppermute | solution.py:238
  14.9 0.2 finish.1
  15.1 0.1 collective-permute-start.4
  15.2 1.3 %collective-permute-done.4.swapped.refs_1_ = f32[4,64,128]{2,1,0:T(8,128)S(1)} collective-permute-done((f32[4,64,128]{2,1,0:T(8,128)S(1)}, f32[4,64,128]{2,1,0:T(8,128)S(1)}, u32[]{:S(2)}, u32[]{:S(2)}) %collective-permute-start.4) | collective-permute-done | bytes 131104 | tf_op jit(solution)/shard_map/ppermute | solution.py:481
  16.5 2.7 %collective-permute-start.5 = (f32[2,64,128]{2,1,0:T(8,128)S(1)}, f32[2,64,128]{2,1,0:T(8,128)S(1)}, u32[]{:S(2)}, u32[]{:S(2)}) collective-permute-start(f32[2,64,128]{2,1,0:T(8,128)S(1)} %get-tuple-element.27), channel_id=1, source_target_pairs={{0,4},{1,5},{2,6},{3,7},{4,0},{5,1},{6,2},{7,3},{8,12},{9,13},{10,... | collective-permute-start | bytes 196616 | tf_op jit(solution)/shard_map/ppermute | solution.py:481
  19.2 1.6 %collective-permute-start.6 = (f32[2,64,128]{2,1,0:T(8,128)S(1)}, f32[2,64,128]{2,1,0:T(8,128)S(1)}, u32[]{:S(2)}, u32[]{:S(2)}) collective-permute-start(f32[2,64,128]{2,1,0:T(8,128)S(1)} %get-tuple-element.28), channel_id=1, source_target_pairs={{0,2},{1,3},{2,0},{3,1},{4,6},{5,7},{6,4},{7,5},{8,10},{9,11},{10,... | collective-permute-start | bytes 196616 | tf_op jit(solution)/shard_map/ppermute | solution.py:481
  20.8 0.2 collective-permute-start.7
  21.0 0.0 copy-done.1
  21.0 0.0 copy-done
  21.0 0.0 copy-done.5
  21.0 0.0 copy-done.6
  21.0 0.0 copy-done.7
  21.0 0.0 copy-done.8
  21.0 0.0 copy-done.9
  21.0 0.0 copy-done.10
  21.0 0.0 copy-start.2
  21.0 1.4 %history.1 = (f32[5,64,1024]{2,1,0:T(8,128)S(1)}, f32[5,64,1024]{2,1,0:T(8,128)S(1)}, f32[1,128]{1,0:T(1,128)S(1)}, f32[5,8,128]{2,1,0:T(8,128)S(1)}, s32[2,8,128]{2,1,0:T(8,128)S(1)}) custom-call(f32[5,64,1024]{2,1,0:T(8,128)S(1)} %bitcast.7, f32[5,64,1024]{2,1,0:T(8,128)S(1)} %bitcast.8, s32[5]{0:T(128)S(1)} %copy-done.5, s32[64]{0:T(128)S(1)} %copy-done.6, ...), custom_call_target="tpu_custom_call" | custom-call | flops 2621440 | bytes 3932160 | tf_op jit(solution)/shard_map/history/pallas_call | solution.py:294
  22.5 0.4 %collective-permute-done.5.refs_2_ = f32[2,64,128]{2,1,0:T(8,128)S(1)} collective-permute-done((f32[2,64,128]{2,1,0:T(8,128)S(1)}, f32[2,64,128]{2,1,0:T(8,128)S(1)}, u32[]{:S(2)}, u32[]{:S(2)}) %collective-permute-start.5) | collective-permute-done | bytes 65568 | tf_op jit(solution)/shard_map/ppermute | solution.py:481
  22.9 0.6 %collective-permute-done.6.refs_3_ = f32[2,64,128]{2,1,0:T(8,128)S(1)} collective-permute-done((f32[2,64,128]{2,1,0:T(8,128)S(1)}, f32[2,64,128]{2,1,0:T(8,128)S(1)}, u32[]{:S(2)}, u32[]{:S(2)}) %collective-permute-start.6) | collective-permute-done | bytes 65568 | tf_op jit(solution)/shard_map/ppermute | solution.py:481
  23.5 3.3 %collective-permute-done.7.refs_4_ = f32[2,64,128]{2,1,0:T(8,128)S(1)} collective-permute-done((f32[2,64,128]{2,1,0:T(8,128)S(1)}, f32[2,64,128]{2,1,0:T(8,128)S(1)}, u32[]{:S(2)}, u32[]{:S(2)}) %collective-permute-start.7) | collective-permute-done | bytes 65568 | tf_op jit(solution)/shard_map/ppermute | solution.py:481
  26.8 0.0 copy-done.2
  26.8 0.7 %residual.1 = (f32[64,1024]{1,0:T(8,128)S(1)}, f32[32,1,128]{2,1,0:T(1,128)S(1)}) custom-call(f32[4,64,128]{2,1,0:T(8,128)S(1)} %get-tuple-element.25.own.refs_0_, f32[4,64,128]{2,1,0:T(8,128)S(1)} %collective-permute-done.4.swapped.refs_1_, f32[2,64,128]{2,1,0:T(8,128)S(1)} %collective-permute-done.5.refs_2_, ...), custom_call_target="tpu_custom_call" | custom-call | tf_op jit(solution)/shard_map/residual/pallas_call | solution.py:357
  27.5 10.0 %all_to_all.5.refs_0_ = f32[32,1,128]{2,1,0:T(1,128)S(1)} all-to-all(f32[32,1,128]{2,1,0:T(1,128)S(1)} %get-tuple-element.34), channel_id=1, replica_groups=mesh['kgrp'=4,'energy'=8] {'energy','kgrp'}, dimensions={0} | all-to-all | bytes 32768 | tf_op jit(solution)/shard_map/all_to_all | solution.py:487
  37.6 1.0 %mix.1 = f32[64,1024]{1,0:T(8,128)} custom-call(f32[32,1,128]{2,1,0:T(1,128)S(1)} %all_to_all.5.refs_0_, f32[64,1024]{1,0:T(8,128)S(1)} %get-tuple-element.35.refs_1_, f32[64,1024]{1,0:T(8,128)S(1)} %bitcast.10, f32[5,64,1024]{2,1,0:T(8,128)S(1)} %get-tuple-element.36.refs_3_), custom_call_target="tpu_custom_call" | custom-call | tf_op jit(solution)/shard_map/mix/pallas_call | solution.py:437
  (2 shorter events, 0.0 us)
Async XLA Ops:
  0.0 21.0 %copy-start.1 = (f32[5,2,2,2,8,1024]{5,4,3,2,1,0:T(8,128)S(1)}, f32[5,2,2,2,8,1024]{5,4,3,2,1,0:T(8,128)}, u32[]{:S(2)}) copy-start(f32[5,2,2,2,8,1024]{5,4,3,2,1,0:T(8,128)} %param.15) | copy-start | bytes 3932164
  0.0 21.0 %copy-start = (f32[5,2,2,2,8,1024]{5,4,3,2,1,0:T(8,128)S(1)}, f32[5,2,2,2,8,1024]{5,4,3,2,1,0:T(8,128)}, u32[]{:S(2)}) copy-start(f32[5,2,2,2,8,1024]{5,4,3,2,1,0:T(8,128)} %param.14) | copy-start | bytes 3932164
  1.1 8.5 %collective-permute-start = (f32[4,64,128]{2,1,0:T(8,128)S(1)}, f32[4,64,128]{2,1,0:T(8,128)S(1)}, u32[]{:S(2)}, u32[]{:S(2)}) collective-permute-start(f32[4,64,128]{2,1,0:T(8,128)S(1)} %bitcast.13), channel_id=1, source_target_pairs={{0,8},{8,0},{16,24},{24,16},{1,9},{9,1},{17,25},{25,17},{2,10},{10... | collective-permute-start | bytes 393224 | tf_op jit(solution)/shard_map/ppermute | solution.py:238
  4.1 8.7 %collective-permute-start.3 = (f32[4,64,128]{2,1,0:T(8,128)S(1)}, f32[4,64,128]{2,1,0:T(8,128)S(1)}, u32[]{:S(2)}, u32[]{:S(2)}) collective-permute-start(f32[4,64,128]{2,1,0:T(8,128)S(1)} %bitcast.11), channel_id=1, source_target_pairs={{0,24},{8,16},{16,8},{24,0},{1,25},{9,17},{17,9},{25,1},{2,26},{10... | collective-permute-start | bytes 393224 | tf_op jit(solution)/shard_map/ppermute | solution.py:238
  5.6 0.7 %copy-start.3 = (s32[64,5]{0,1:T(8,128)S(1)}, s32[64,5]{0,1:T(8,128)}, u32[]{:S(2)}) copy-start(s32[64,5]{0,1:T(8,128)} %param.17) | copy-start | bytes 3844
  6.3 0.7 %copy-start.4 = (f32[5]{0:T(128)S(1)}, f32[5]{0:T(128)}, u32[]{:S(2)}) copy-start(f32[5]{0:T(128)} %refs_3_.2) | copy-start | bytes 64
  7.0 14.0 %copy-start.5 = (s32[5]{0:T(128)S(1)}, s32[5]{0:T(128)}, u32[]{:S(2)}) copy-start(s32[5]{0:T(128)} %refs_2_.1) | copy-start | bytes 64
  7.0 14.0 %copy-start.6 = (s32[64]{0:T(128)S(1)}, s32[64]{0:T(128)}, u32[]{:S(2)}) copy-start(s32[64]{0:T(128)} %refs_3_.3) | copy-start | bytes 772
  7.0 14.0 %copy-start.7 = (f32[4]{0:T(128)S(1)}, f32[4]{0:T(128)}, u32[]{:S(2)}) copy-start(f32[4]{0:T(128)} %refs_4_.1) | copy-start | bytes 52
  7.0 14.0 %copy-start.8 = (f32[2]{0:T(128)S(1)}, f32[2]{0:T(128)}, u32[]{:S(2)}) copy-start(f32[2]{0:T(128)} %refs_5_.1) | copy-start | bytes 28
  7.0 14.0 %copy-start.9 = (f32[2]{0:T(128)S(1)}, f32[2]{0:T(128)}, u32[]{:S(2)}) copy-start(f32[2]{0:T(128)} %refs_6_.1) | copy-start | bytes 28
  7.0 14.0 %copy-start.10 = (s32[2]{0:T(128)S(1)}, s32[2]{0:T(128)}, u32[]{:S(2)}) copy-start(s32[2]{0:T(128)} %refs_7_.1) | copy-start | bytes 28
  8.1 5.1 %collective-permute-start.2 = (f32[4,64,128]{2,1,0:T(8,128)S(1)}, f32[4,64,128]{2,1,0:T(8,128)S(1)}, u32[]{:S(2)}, u32[]{:S(2)}) collective-permute-start(f32[4,64,128]{2,1,0:T(8,128)S(1)} %get-tuple-element.21._), channel_id=1, source_target_pairs={{0,8},{8,0},{16,24},{24,16},{1,9},{9,1},{17,25},{25,17},{2,10},{10... | collective-permute-start | bytes 393224 | tf_op jit(solution)/shard_map/ppermute | solution.py:238
  9.7 5.2 %collective-permute-start.1 = (f32[4,64,128]{2,1,0:T(8,128)S(1)}, f32[4,64,128]{2,1,0:T(8,128)S(1)}, u32[]{:S(2)}, u32[]{:S(2)}) collective-permute-start(f32[4,64,128]{2,1,0:T(8,128)S(1)} %hold.1), channel_id=1, source_target_pairs={{0,16},{8,24},{16,0},{24,8},{1,17},{9,25},{17,1},{25,9},{2,18},{10... | collective-permute-start | bytes 393224 | tf_op jit(solution)/shard_map/ppermute | solution.py:238
  15.1 1.4 %collective-permute-start.4 = (f32[4,64,128]{2,1,0:T(8,128)S(1)}, f32[4,64,128]{2,1,0:T(8,128)S(1)}, u32[]{:S(2)}, u32[]{:S(2)}) collective-permute-start(f32[4,64,128]{2,1,0:T(8,128)S(1)} %get-tuple-element.26), channel_id=1, source_target_pairs={{0,1},{1,0},{2,3},{3,2},{4,5},{5,4},{6,7},{7,6},{8,9},{9,8},{10,11... | collective-permute-start | bytes 393224 | tf_op jit(solution)/shard_map/ppermute | solution.py:481
  16.5 6.3 %collective-permute-start.5 = (f32[2,64,128]{2,1,0:T(8,128)S(1)}, f32[2,64,128]{2,1,0:T(8,128)S(1)}, u32[]{:S(2)}, u32[]{:S(2)}) collective-permute-start(f32[2,64,128]{2,1,0:T(8,128)S(1)} %get-tuple-element.27), channel_id=1, source_target_pairs={{0,4},{1,5},{2,6},{3,7},{4,0},{5,1},{6,2},{7,3},{8,12},{9,13},{10,... | collective-permute-start | bytes 196616 | tf_op jit(solution)/shard_map/ppermute | solution.py:481
  19.2 4.3 %collective-permute-start.6 = (f32[2,64,128]{2,1,0:T(8,128)S(1)}, f32[2,64,128]{2,1,0:T(8,128)S(1)}, u32[]{:S(2)}, u32[]{:S(2)}) collective-permute-start(f32[2,64,128]{2,1,0:T(8,128)S(1)} %get-tuple-element.28), channel_id=1, source_target_pairs={{0,2},{1,3},{2,0},{3,1},{4,6},{5,7},{6,4},{7,5},{8,10},{9,11},{10,... | collective-permute-start | bytes 196616 | tf_op jit(solution)/shard_map/ppermute | solution.py:481
  20.8 6.1 %collective-permute-start.7 = (f32[2,64,128]{2,1,0:T(8,128)S(1)}, f32[2,64,128]{2,1,0:T(8,128)S(1)}, u32[]{:S(2)}, u32[]{:S(2)}) collective-permute-start(f32[2,64,128]{2,1,0:T(8,128)S(1)} %get-tuple-element.29), channel_id=1, source_target_pairs={{0,6},{1,7},{2,4},{3,5},{4,2},{5,3},{6,0},{7,1},{8,14},{9,15},{10,... | collective-permute-start | bytes 196616 | tf_op jit(solution)/shard_map/ppermute | solution.py:481
  21.0 5.8 %copy-start.2 = (f32[2,2,2,8,1024]{4,3,2,1,0:T(8,128)S(1)}, f32[2,2,2,8,1024]{4,3,2,1,0:T(8,128)}, u32[]{:S(2)}) copy-start(f32[2,2,2,8,1024]{4,3,2,1,0:T(8,128)} %param.13) | copy-start | bytes 786436

commit v13 on v12

--- a/solution.py
+++ b/solution.py
@@ -238,9 +238,9 @@
     across = lambda block, flip: lax.ppermute(block, "kgrp", [(i, i ^ flip) for i in range(groups)])
     half = own.shape[0] // 2
     head, tail = own[:half], own[half:]
-    near_head, far_tail = across(head, 1), across(tail, 3)
+    near_head = across(head, 1)
     hi, lo, part, late = prepare([head, tail], neighbour, weight, total_k)
-    near_tail, far_head = across(late, 1), across(hold(near_head, late), 2)
+    far_tail, near_tail, far_head = across(late, 3), across(late, 1), across(hold(near_head, late), 2)
     tail_part = add_sides(half, (near_tail, far_tail), hi, lo, part, [])
     return finish((near_head, far_head), hi, lo, part, [tail_part], parts)
 

time: 38.7 us -> 39.1 us (1.010)
  waiting for transfers between devices: 9.71 us -> 10.8 us
  starting transfers between devices: 11.5 us -> 11.1 us
    ppermute x4, waiting for transfers between devices: 4.04 us -> 5.15 us  [smear(): lax.ppermute(block, 'kgrp', [(i, i ^ flip) for i in range(groups)])]
    all_to_all x1, blocking collectives: 10 us -> 9.63 us  [per_device(): lax.all_to_all(lines, ('energy', 'kgrp'), split_axis=0, concat_axis=0, ti...]
  transfers between devices with their start and end apart: 8 -> 8, of which waited for: 7 -> 6; matrix products, arithmetic and copies ran while one was open for 0% -> 0% of each run, Pallas kernels for 7% -> 7%
where the time goes in v13:
time: 39.1 us; the launch traced here: 38.9 us
  starting transfers between devices  11.1 us (28%)
  waiting for transfers between devices  10.8 us (28%)
  blocking collectives  9.63 us (25%)
  Pallas kernels  4.61 us (12%)
  local copies, waits for them, and re-layouts  2.52 us (6%)
    all_to_all x1, blocking collectives, per_device(): lax.all_to_all(lines, ('energy', 'kgrp'), split_axis=0, concat_axis=0, ti...  9.63 us
    ppermute x4, starting transfers between devices, smear(): lax.ppermute(block, 'kgrp', [(i, i ^ flip) for i in range(groups)])  6.62 us
    ppermute x4, waiting for transfers between devices, per_device(): lax.ppermute(block, 'energy', [(e, e ^ m) for e in range(parts)])  5.68 us
    ppermute x4, waiting for transfers between devices, smear(): lax.ppermute(block, 'kgrp', [(i, i ^ flip) for i in range(groups)])  5.15 us
    ppermute x4, starting transfers between devices, per_device(): lax.ppermute(block, 'energy', [(e, e ^ m) for e in range(parts)])  4.52 us
    pallas_call x1, Pallas kernels, history(): pl.pallas_call(lambda *refs: history_kernel(rows, *refs), out_shape=(jax....  1.43 us
    unnamed x22, local copies, waits for them, and re-layouts  1.38 us
    slice x1, local copies, waits for them, and re-layouts, smear(): head, tail = (own[:half], own[half:])  1.14 us
  transfers between devices with their start and end apart: 8, of which 6 were waited for; matrix products, arithmetic and copies ran while one was open for 0% of the time, Pallas kernels for 7%

profile of v13, /device:TPU:0, one launch (start us, length us, event | category | flops | bytes accessed | tf_op | source)
XLA Modules:
  0.0 38.9 jit_solution(7589893148088328619)
XLA Ops:
  0.0 0.0 copy-start.1
  0.0 0.0 copy-start
  0.0 1.1 %fusion = (f32[1,2,2,64,128]{4,3,2,1,0:T(8,128)S(1)}, f32[1,2,2,64,128]{4,3,2,1,0:T(8,128)S(1)}) fusion(f32[2,2,2,64,128]{4,3,2,1,0:T(8,128)} %param.12), kind=kLoop, calls=%fused_computation | loop fusion | bytes 524288 | tf_op jit(solution)/shard_map/slice | solution.py:240
  1.1 3.0 %collective-permute-start = (f32[4,64,128]{2,1,0:T(8,128)S(1)}, f32[4,64,128]{2,1,0:T(8,128)S(1)}, u32[]{:S(2)}, u32[]{:S(2)}) collective-permute-start(f32[4,64,128]{2,1,0:T(8,128)S(1)} %bitcast.11), channel_id=1, source_target_pairs={{0,8},{8,0},{16,24},{24,16},{1,9},{9,1},{17,25},{25,17},{2,10},{10... | collective-permute-start | bytes 393224 | tf_op jit(solution)/shard_map/ppermute | solution.py:238
  4.1 0.0 copy-start.3
  4.1 0.7 %copy-done.3 = s32[64,5]{0,1:T(8,128)S(1)} copy-done((s32[64,5]{0,1:T(8,128)S(1)}, s32[64,5]{0,1:T(8,128)}, u32[]{:S(2)}) %copy-start.3) | copy-done | bytes 1304
  4.8 0.0 copy-start.4
  4.8 0.7 %copy-done.4 = f32[5]{0:T(128)S(1)} copy-done((f32[5]{0:T(128)S(1)}, f32[5]{0:T(128)}, u32[]{:S(2)}) %copy-start.4) | copy-done | bytes 44
  5.5 0.0 copy-start.5
  5.5 0.0 copy-start.6
  5.5 0.0 copy-start.7
  5.5 0.0 copy-start.8
  5.5 0.0 copy-start.9
  5.5 0.0 copy-start.10
  5.5 1.1 %prepare.1 = (bf16[64,128]{1,0:T(8,128)(2,1)S(1)}, bf16[64,128]{1,0:T(8,128)(2,1)S(1)}, f32[8,64,128]{2,1,0:T(8,128)S(1)}, f32[4,64,128]{2,1,0:T(8,128)S(1)}) custom-call(f32[4,64,128]{2,1,0:T(8,128)S(1)} %bitcast.12, f32[4,64,128]{2,1,0:T(8,128)S(1)} %bitcast.13, s32[5,64]{1,0:T(8,128)S(1)} %bitcast.14, f32[5]{0:T(128)S(1)} %copy-done.4), custom_call_target="tpu_custom_call" | custom-call | flops 25165824 | bytes 524288 | tf_op jit(solution)/shard_map/prepare/pallas_call | solution.py:85
  6.6 1.6 %collective-permute-start.3 = (f32[4,64,128]{2,1,0:T(8,128)S(1)}, f32[4,64,128]{2,1,0:T(8,128)S(1)}, u32[]{:S(2)}, u32[]{:S(2)}) collective-permute-start(f32[4,64,128]{2,1,0:T(8,128)S(1)} %get-tuple-element.21._), channel_id=1, source_target_pairs={{0,24},{8,16},{16,8},{24,0},{1,25},{9,17},{17,9},{25,1},{2,26},{10... | collective-permute-start | bytes 393224 | tf_op jit(solution)/shard_map/ppermute | solution.py:238
  8.2 1.5 %collective-permute-start.2 = (f32[4,64,128]{2,1,0:T(8,128)S(1)}, f32[4,64,128]{2,1,0:T(8,128)S(1)}, u32[]{:S(2)}, u32[]{:S(2)}) collective-permute-start(f32[4,64,128]{2,1,0:T(8,128)S(1)} %get-tuple-element.21._), channel_id=1, source_target_pairs={{0,8},{8,0},{16,24},{24,16},{1,9},{9,1},{17,25},{25,17},{2,10},{10... | collective-permute-start | bytes 393224 | tf_op jit(solution)/shard_map/ppermute | solution.py:238
  9.7 0.0 collective-permute-done.block.refs_0_
  9.7 0.6 %collective-permute-start.1 = (f32[4,64,128]{2,1,0:T(8,128)S(1)}, f32[4,64,128]{2,1,0:T(8,128)S(1)}, u32[]{:S(2)}, u32[]{:S(2)}) collective-permute-start(f32[4,64,128]{2,1,0:T(8,128)S(1)} %hold.1), channel_id=1, source_target_pairs={{0,16},{8,24},{16,0},{24,8},{1,17},{9,25},{17,1},{25,9},{2,18},{10... | collective-permute-start | bytes 393224 | tf_op jit(solution)/shard_map/ppermute | solution.py:238
  10.3 3.8 %collective-permute-done.3.refs_1_ = f32[4,64,128]{2,1,0:T(8,128)S(1)} collective-permute-done((f32[4,64,128]{2,1,0:T(8,128)S(1)}, f32[4,64,128]{2,1,0:T(8,128)S(1)}, u32[]{:S(2)}, u32[]{:S(2)}) %collective-permute-start.3) | collective-permute-done | bytes 131104 | tf_op jit(solution)/shard_map/ppermute | solution.py:238
  14.1 1.4 %collective-permute-done.2.refs_0_ = f32[4,64,128]{2,1,0:T(8,128)S(1)} collective-permute-done((f32[4,64,128]{2,1,0:T(8,128)S(1)}, f32[4,64,128]{2,1,0:T(8,128)S(1)}, u32[]{:S(2)}, u32[]{:S(2)}) %collective-permute-start.2) | collective-permute-done | bytes 131104 | tf_op jit(solution)/shard_map/ppermute | solution.py:238
  15.4 0.2 add_sides.1.refs_5_
  15.6 0.0 collective-permute-done.1.refs_1_
  15.6 0.2 finish.1
  15.8 0.1 collective-permute-start.4
  15.9 1.3 %collective-permute-done.4.swapped.refs_1_ = f32[4,64,128]{2,1,0:T(8,128)S(1)} collective-permute-done((f32[4,64,128]{2,1,0:T(8,128)S(1)}, f32[4,64,128]{2,1,0:T(8,128)S(1)}, u32[]{:S(2)}, u32[]{:S(2)}) %collective-permute-start.4) | collective-permute-done | bytes 131104 | tf_op jit(solution)/shard_map/ppermute | solution.py:481
  17.3 2.7 %collective-permute-start.5 = (f32[2,64,128]{2,1,0:T(8,128)S(1)}, f32[2,64,128]{2,1,0:T(8,128)S(1)}, u32[]{:S(2)}, u32[]{:S(2)}) collective-permute-start(f32[2,64,128]{2,1,0:T(8,128)S(1)} %get-tuple-element.27), channel_id=1, source_target_pairs={{0,4},{1,5},{2,6},{3,7},{4,0},{5,1},{6,2},{7,3},{8,12},{9,13},{10,... | collective-permute-start | bytes 196616 | tf_op jit(solution)/shard_map/ppermute | solution.py:481
  19.9 1.6 %collective-permute-start.6 = (f32[2,64,128]{2,1,0:T(8,128)S(1)}, f32[2,64,128]{2,1,0:T(8,128)S(1)}, u32[]{:S(2)}, u32[]{:S(2)}) collective-permute-start(f32[2,64,128]{2,1,0:T(8,128)S(1)} %get-tuple-element.28), channel_id=1, source_target_pairs={{0,2},{1,3},{2,0},{3,1},{4,6},{5,7},{6,4},{7,5},{8,10},{9,11},{10,... | collective-permute-start | bytes 196616 | tf_op jit(solution)/shard_map/ppermute | solution.py:481
  21.5 0.2 collective-permute-start.7
  21.7 0.0 copy-done.1
  21.7 0.0 copy-done
  21.7 0.0 copy-done.5
  21.7 0.0 copy-done.6
  21.7 0.0 copy-done.7
  21.7 0.0 copy-done.8
  21.8 0.0 copy-done.9
  21.8 0.0 copy-done.10
  21.8 0.0 copy-start.2
  21.8 1.4 %history.1 = (f32[5,64,1024]{2,1,0:T(8,128)S(1)}, f32[5,64,1024]{2,1,0:T(8,128)S(1)}, f32[1,128]{1,0:T(1,128)S(1)}, f32[5,8,128]{2,1,0:T(8,128)S(1)}, s32[2,8,128]{2,1,0:T(8,128)S(1)}) custom-call(f32[5,64,1024]{2,1,0:T(8,128)S(1)} %bitcast.7, f32[5,64,1024]{2,1,0:T(8,128)S(1)} %bitcast.8, s32[5]{0:T(128)S(1)} %copy-done.5, s32[64]{0:T(128)S(1)} %copy-done.6, ...), custom_call_target="tpu_custom_call" | custom-call | flops 2621440 | bytes 3932160 | tf_op jit(solution)/shard_map/history/pallas_call | solution.py:294
  23.2 0.4 collective-permute-done.5.refs_2_
  23.6 0.6 %collective-permute-done.6.refs_3_ = f32[2,64,128]{2,1,0:T(8,128)S(1)} collective-permute-done((f32[2,64,128]{2,1,0:T(8,128)S(1)}, f32[2,64,128]{2,1,0:T(8,128)S(1)}, u32[]{:S(2)}, u32[]{:S(2)}) %collective-permute-start.6) | collective-permute-done | bytes 65568 | tf_op jit(solution)/shard_map/ppermute | solution.py:481
  24.3 3.3 %collective-permute-done.7.refs_4_ = f32[2,64,128]{2,1,0:T(8,128)S(1)} collective-permute-done((f32[2,64,128]{2,1,0:T(8,128)S(1)}, f32[2,64,128]{2,1,0:T(8,128)S(1)}, u32[]{:S(2)}, u32[]{:S(2)}) %collective-permute-start.7) | collective-permute-done | bytes 65568 | tf_op jit(solution)/shard_map/ppermute | solution.py:481
  27.6 0.0 copy-done.2
  27.6 0.7 %residual.1 = (f32[64,1024]{1,0:T(8,128)S(1)}, f32[32,1,128]{2,1,0:T(1,128)S(1)}) custom-call(f32[4,64,128]{2,1,0:T(8,128)S(1)} %get-tuple-element.25.own.refs_0_, f32[4,64,128]{2,1,0:T(8,128)S(1)} %collective-permute-done.4.swapped.refs_1_, f32[2,64,128]{2,1,0:T(8,128)S(1)} %collective-permute-done.5.refs_2_, ...), custom_call_target="tpu_custom_call" | custom-call | tf_op jit(solution)/shard_map/residual/pallas_call | solution.py:357
  28.3 9.6 %all_to_all.5.refs_0_ = f32[32,1,128]{2,1,0:T(1,128)S(1)} all-to-all(f32[32,1,128]{2,1,0:T(1,128)S(1)} %get-tuple-element.34), channel_id=1, replica_groups=mesh['kgrp'=4,'energy'=8] {'energy','kgrp'}, dimensions={0} | all-to-all | bytes 32768 | tf_op jit(solution)/shard_map/all_to_all | solution.py:487
  37.9 1.0 %mix.1 = f32[64,1024]{1,0:T(8,128)} custom-call(f32[32,1,128]{2,1,0:T(1,128)S(1)} %all_to_all.5.refs_0_, f32[64,1024]{1,0:T(8,128)S(1)} %get-tuple-element.35.refs_1_, f32[64,1024]{1,0:T(8,128)S(1)} %bitcast.10, f32[5,64,1024]{2,1,0:T(8,128)S(1)} %get-tuple-element.36.refs_3_), custom_call_target="tpu_custom_call" | custom-call | tf_op jit(solution)/shard_map/mix/pallas_call | solution.py:437
  (2 shorter events, 0.0 us)
Async XLA Ops:
  0.0 21.7 %copy-start.1 = (f32[5,2,2,2,8,1024]{5,4,3,2,1,0:T(8,128)S(1)}, f32[5,2,2,2,8,1024]{5,4,3,2,1,0:T(8,128)}, u32[]{:S(2)}) copy-start(f32[5,2,2,2,8,1024]{5,4,3,2,1,0:T(8,128)} %param.15) | copy-start | bytes 3932164
  0.0 21.7 %copy-start = (f32[5,2,2,2,8,1024]{5,4,3,2,1,0:T(8,128)S(1)}, f32[5,2,2,2,8,1024]{5,4,3,2,1,0:T(8,128)}, u32[]{:S(2)}) copy-start(f32[5,2,2,2,8,1024]{5,4,3,2,1,0:T(8,128)} %param.14) | copy-start | bytes 3932164
  1.1 8.5 %collective-permute-start = (f32[4,64,128]{2,1,0:T(8,128)S(1)}, f32[4,64,128]{2,1,0:T(8,128)S(1)}, u32[]{:S(2)}, u32[]{:S(2)}) collective-permute-start(f32[4,64,128]{2,1,0:T(8,128)S(1)} %bitcast.11), channel_id=1, source_target_pairs={{0,8},{8,0},{16,24},{24,16},{1,9},{9,1},{17,25},{25,17},{2,10},{10... | collective-permute-start | bytes 393224 | tf_op jit(solution)/shard_map/ppermute | solution.py:238
  4.1 0.7 %copy-start.3 = (s32[64,5]{0,1:T(8,128)S(1)}, s32[64,5]{0,1:T(8,128)}, u32[]{:S(2)}) copy-start(s32[64,5]{0,1:T(8,128)} %param.17) | copy-start | bytes 3844
  4.8 0.7 %copy-start.4 = (f32[5]{0:T(128)S(1)}, f32[5]{0:T(128)}, u32[]{:S(2)}) copy-start(f32[5]{0:T(128)} %refs_3_.2) | copy-start | bytes 64
  5.5 16.2 %copy-start.5 = (s32[5]{0:T(128)S(1)}, s32[5]{0:T(128)}, u32[]{:S(2)}) copy-start(s32[5]{0:T(128)} %refs_2_.1) | copy-start | bytes 64
  5.5 16.2 %copy-start.6 = (s32[64]{0:T(128)S(1)}, s32[64]{0:T(128)}, u32[]{:S(2)}) copy-start(s32[64]{0:T(128)} %refs_3_.3) | copy-start | bytes 772
  5.5 16.2 %copy-start.7 = (f32[4]{0:T(128)S(1)}, f32[4]{0:T(128)}, u32[]{:S(2)}) copy-start(f32[4]{0:T(128)} %refs_4_.1) | copy-start | bytes 52
  5.5 16.2 %copy-start.8 = (f32[2]{0:T(128)S(1)}, f32[2]{0:T(128)}, u32[]{:S(2)}) copy-start(f32[2]{0:T(128)} %refs_5_.1) | copy-start | bytes 28
  5.5 16.3 %copy-start.9 = (f32[2]{0:T(128)S(1)}, f32[2]{0:T(128)}, u32[]{:S(2)}) copy-start(f32[2]{0:T(128)} %refs_6_.1) | copy-start | bytes 28
  5.5 16.3 %copy-start.10 = (s32[2]{0:T(128)S(1)}, s32[2]{0:T(128)}, u32[]{:S(2)}) copy-start(s32[2]{0:T(128)} %refs_7_.1) | copy-start | bytes 28
  6.6 7.4 %collective-permute-start.3 = (f32[4,64,128]{2,1,0:T(8,128)S(1)}, f32[4,64,128]{2,1,0:T(8,128)S(1)}, u32[]{:S(2)}, u32[]{:S(2)}) collective-permute-start(f32[4,64,128]{2,1,0:T(8,128)S(1)} %get-tuple-element.21._), channel_id=1, source_target_pairs={{0,24},{8,16},{16,8},{24,0},{1,25},{9,17},{17,9},{25,1},{2,26},{10... | collective-permute-start | bytes 393224 | tf_op jit(solution)/shard_map/ppermute | solution.py:238
  8.2 7.2 %collective-permute-start.2 = (f32[4,64,128]{2,1,0:T(8,128)S(1)}, f32[4,64,128]{2,1,0:T(8,128)S(1)}, u32[]{:S(2)}, u32[]{:S(2)}) collective-permute-start(f32[4,64,128]{2,1,0:T(8,128)S(1)} %get-tuple-element.21._), channel_id=1, source_target_pairs={{0,8},{8,0},{16,24},{24,16},{1,9},{9,1},{17,25},{25,17},{2,10},{10... | collective-permute-start | bytes 393224 | tf_op jit(solution)/shard_map/ppermute | solution.py:238
  9.7 5.9 %collective-permute-start.1 = (f32[4,64,128]{2,1,0:T(8,128)S(1)}, f32[4,64,128]{2,1,0:T(8,128)S(1)}, u32[]{:S(2)}, u32[]{:S(2)}) collective-permute-start(f32[4,64,128]{2,1,0:T(8,128)S(1)} %hold.1), channel_id=1, source_target_pairs={{0,16},{8,24},{16,0},{24,8},{1,17},{9,25},{17,1},{25,9},{2,18},{10... | collective-permute-start | bytes 393224 | tf_op jit(solution)/shard_map/ppermute | solution.py:238
  15.8 1.4 %collective-permute-start.4 = (f32[4,64,128]{2,1,0:T(8,128)S(1)}, f32[4,64,128]{2,1,0:T(8,128)S(1)}, u32[]{:S(2)}, u32[]{:S(2)}) collective-permute-start(f32[4,64,128]{2,1,0:T(8,128)S(1)} %get-tuple-element.26), channel_id=1, source_target_pairs={{0,1},{1,0},{2,3},{3,2},{4,5},{5,4},{6,7},{7,6},{8,9},{9,8},{10,11... | collective-permute-start | bytes 393224 | tf_op jit(solution)/shard_map/ppermute | solution.py:481
  17.3 6.3 %collective-permute-start.5 = (f32[2,64,128]{2,1,0:T(8,128)S(1)}, f32[2,64,128]{2,1,0:T(8,128)S(1)}, u32[]{:S(2)}, u32[]{:S(2)}) collective-permute-start(f32[2,64,128]{2,1,0:T(8,128)S(1)} %get-tuple-element.27), channel_id=1, source_target_pairs={{0,4},{1,5},{2,6},{3,7},{4,0},{5,1},{6,2},{7,3},{8,12},{9,13},{10,... | collective-permute-start | bytes 196616 | tf_op jit(solution)/shard_map/ppermute | solution.py:481
  19.9 4.3 %collective-permute-start.6 = (f32[2,64,128]{2,1,0:T(8,128)S(1)}, f32[2,64,128]{2,1,0:T(8,128)S(1)}, u32[]{:S(2)}, u32[]{:S(2)}) collective-permute-start(f32[2,64,128]{2,1,0:T(8,128)S(1)} %get-tuple-element.28), channel_id=1, source_target_pairs={{0,2},{1,3},{2,0},{3,1},{4,6},{5,7},{6,4},{7,5},{8,10},{9,11},{10,... | collective-permute-start | bytes 196616 | tf_op jit(solution)/shard_map/ppermute | solution.py:481
  21.5 6.1 %collective-permute-start.7 = (f32[2,64,128]{2,1,0:T(8,128)S(1)}, f32[2,64,128]{2,1,0:T(8,128)S(1)}, u32[]{:S(2)}, u32[]{:S(2)}) collective-permute-start(f32[2,64,128]{2,1,0:T(8,128)S(1)} %get-tuple-element.29), channel_id=1, source_target_pairs={{0,6},{1,7},{2,4},{3,5},{4,2},{5,3},{6,0},{7,1},{8,14},{9,15},{10,... | collective-permute-start | bytes 196616 | tf_op jit(solution)/shard_map/ppermute | solution.py:481
  21.8 5.8 %copy-start.2 = (f32[2,2,2,8,1024]{4,3,2,1,0:T(8,128)S(1)}, f32[2,2,2,8,1024]{4,3,2,1,0:T(8,128)}, u32[]{:S(2)}) copy-start(f32[2,2,2,8,1024]{4,3,2,1,0:T(8,128)} %param.13) | copy-start | bytes 786436

commit v14 on v12

--- a/solution.py
+++ b/solution.py
@@ -213,6 +213,29 @@
     return groups == 4
 
 
+def halves_kernel(source, head, tail, done):
+    fetches = []
+    for n, half in enumerate((head, tail)):
+        rows = pl.ds(n * head.shape[0], half.shape[0])
+        fetches.append(pltpu.make_async_copy(source.at[rows], half, done.at[n]))
+        fetches[-1].start()
+    for fetch in fetches:
+        fetch.wait()
+
+
+def halves(source):
+    shape = jax.ShapeDtypeStruct((source.shape[0] // 2,) + source.shape[1:], source.dtype)
+    return pl.pallas_call(
+        halves_kernel,
+        out_shape=(shape, shape),
+        in_specs=[pl.BlockSpec(memory_space=pltpu.HBM)],
+        out_specs=(VMEM, VMEM),
+        scratch_shapes=[pltpu.SemaphoreType.DMA((2,))],
+        compiler_params=PARAMS,
+        name="halves",
+    )(source)
+
+
 def hold_kernel(block, _, out):
     out[...] = block[...]
 
@@ -237,7 +260,7 @@
         return finish((near, far), *prepare([own], neighbour, weight, total_k)[:3], [], parts)
     across = lambda block, flip: lax.ppermute(block, "kgrp", [(i, i ^ flip) for i in range(groups)])
     half = own.shape[0] // 2
-    head, tail = own[:half], own[half:]
+    head, tail = halves(pltpu.with_memory_space_constraint(own, pltpu.HBM))
     near_head, far_tail = across(head, 1), across(tail, 3)
     hi, lo, part, late = prepare([head, tail], neighbour, weight, total_k)
     near_tail, far_head = across(late, 1), across(hold(near_head, late), 2)

time: 38.7 us -> 38.7 us (level)
  waiting for transfers between devices: 9.71 us -> 8.4 us
  Pallas kernels: 4.61 us -> 5.69 us
    ppermute x4, waiting for transfers between devices: 5.68 us -> 4.36 us  [per_device(): lax.ppermute(block, 'energy', [(e, e ^ m) for e in range(parts)])]
    unnamed x22, local copies, waits for them, and re-layouts: 1.38 us -> 2.69 us
    slice x1 -> x0, local copies, waits for them, and re-layouts: 1.14 us -> none  [smear(): head, tail = (own[:half], own[half:])]
    pallas_call x0 -> x1, Pallas kernels: none -> 1.09 us  [halves(): pl.pallas_call(halves_kernel, out_shape=(shape, shape), in_specs=[pl.Bloc...]
  transfers between devices with their start and end apart: 8 -> 8, of which waited for: 7 -> 5; matrix products, arithmetic and copies ran while one was open for 0% -> 0% of each run, Pallas kernels for 7% -> 7%
where the time goes in v14:
time: 38.7 us; the launch traced here: 38.5 us
  starting transfers between devices  11.5 us (30%)
  blocking collectives  10 us (26%)
  waiting for transfers between devices  8.4 us (22%)
  Pallas kernels  5.69 us (15%)
  local copies, waits for them, and re-layouts  2.69 us (7%)
    all_to_all x1, blocking collectives, per_device(): lax.all_to_all(lines, ('energy', 'kgrp'), split_axis=0, concat_axis=0, ti...  10 us
    ppermute x4, starting transfers between devices, smear(): lax.ppermute(block, 'kgrp', [(i, i ^ flip) for i in range(groups)])  7.01 us
    ppermute x4, starting transfers between devices, per_device(): lax.ppermute(block, 'energy', [(e, e ^ m) for e in range(parts)])  4.52 us
    ppermute x4, waiting for transfers between devices, per_device(): lax.ppermute(block, 'energy', [(e, e ^ m) for e in range(parts)])  4.36 us
    ppermute x4, waiting for transfers between devices, smear(): lax.ppermute(block, 'kgrp', [(i, i ^ flip) for i in range(groups)])  4.04 us
    unnamed x22, local copies, waits for them, and re-layouts  2.69 us
    pallas_call x1, Pallas kernels, history(): pl.pallas_call(lambda *refs: history_kernel(rows, *refs), out_shape=(jax....  1.43 us
    pallas_call x1, Pallas kernels, halves(): pl.pallas_call(halves_kernel, out_shape=(shape, shape), in_specs=[pl.Bloc...  1.09 us
  transfers between devices with their start and end apart: 8, of which 5 were waited for; matrix products, arithmetic and copies ran while one was open for 0% of the time, Pallas kernels for 7%

profile of v14, /device:TPU:0, one launch (start us, length us, event | category | flops | bytes accessed | tf_op | source)
XLA Modules:
  0.0 38.5 jit_solution(16785988604944824297)
XLA Ops:
  0.0 0.0 copy-start
  0.0 1.1 %halves.1 = (f32[4,64,128]{2,1,0:T(8,128)S(1)}, f32[4,64,128]{2,1,0:T(8,128)S(1)}) custom-call(f32[8,64,128]{2,1,0:T(8,128)} %bitcast.11), custom_call_target="tpu_custom_call" | custom-call | tf_op jit(solution)/shard_map/halves/pallas_call | solution.py:228
  1.1 3.0 %collective-permute-start = (f32[4,64,128]{2,1,0:T(8,128)S(1)}, f32[4,64,128]{2,1,0:T(8,128)S(1)}, u32[]{:S(2)}, u32[]{:S(2)}) collective-permute-start(f32[4,64,128]{2,1,0:T(8,128)S(1)} %get-tuple-element.23.refs_0_), channel_id=1, source_target_pairs={{0,8},{8,0},{16,24},{24,16},{1,9},{9,1},{17,25},{25,17},{2,10},{10... | collective-permute-start | bytes 393224 | tf_op jit(solution)/shard_map/ppermute | solution.py:261
  4.1 1.5 %collective-permute-start.3 = (f32[4,64,128]{2,1,0:T(8,128)S(1)}, f32[4,64,128]{2,1,0:T(8,128)S(1)}, u32[]{:S(2)}, u32[]{:S(2)}) collective-permute-start(f32[4,64,128]{2,1,0:T(8,128)S(1)} %get-tuple-element.24.refs_1_), channel_id=1, source_target_pairs={{0,24},{8,16},{16,8},{24,0},{1,25},{9,17},{17,9},{25,1},{2,26},{10... | collective-permute-start | bytes 393224 | tf_op jit(solution)/shard_map/ppermute | solution.py:261
  5.6 0.0 copy-start.3
  5.6 0.7 %copy-done.3 = s32[64,5]{0,1:T(8,128)S(1)} copy-done((s32[64,5]{0,1:T(8,128)S(1)}, s32[64,5]{0,1:T(8,128)}, u32[]{:S(2)}) %copy-start.3) | copy-done | bytes 1304
  6.3 0.0 copy-start.4
  6.3 0.7 %copy-done.4 = f32[5]{0:T(128)S(1)} copy-done((f32[5]{0:T(128)S(1)}, f32[5]{0:T(128)}, u32[]{:S(2)}) %copy-start.4) | copy-done | bytes 44
  6.9 0.0 copy-start.5
  6.9 0.0 copy-start.6
  6.9 0.0 copy-start.7
  6.9 0.0 copy-start.8
  6.9 0.0 copy-start.9
  7.0 0.0 copy-start.10
  7.0 1.1 %prepare.1 = (bf16[64,128]{1,0:T(8,128)(2,1)S(1)}, bf16[64,128]{1,0:T(8,128)(2,1)S(1)}, f32[8,64,128]{2,1,0:T(8,128)S(1)}, f32[4,64,128]{2,1,0:T(8,128)S(1)}) custom-call(f32[4,64,128]{2,1,0:T(8,128)S(1)} %get-tuple-element.23.refs_0_, f32[4,64,128]{2,1,0:T(8,128)S(1)} %get-tuple-element.24.refs_1_, s32[5,64]{1,0:T(8,128)S(1)} %bitcast.10, f32[5]{0:T(128)S(1)} %copy-done.4), custom_call_target="tpu_custom_call" | custom-call | flops 25165824 | bytes 524288 | tf_op jit(solution)/shard_map/prepare/pallas_call | solution.py:85
  8.1 1.6 %collective-permute-start.2 = (f32[4,64,128]{2,1,0:T(8,128)S(1)}, f32[4,64,128]{2,1,0:T(8,128)S(1)}, u32[]{:S(2)}, u32[]{:S(2)}) collective-permute-start(f32[4,64,128]{2,1,0:T(8,128)S(1)} %get-tuple-element.25._), channel_id=1, source_target_pairs={{0,8},{8,0},{16,24},{24,16},{1,9},{9,1},{17,25},{25,17},{2,10},{10... | collective-permute-start | bytes 393224 | tf_op jit(solution)/shard_map/ppermute | solution.py:261
  9.6 0.0 collective-permute-done.block.refs_0_
  9.6 1.0 %collective-permute-start.1 = (f32[4,64,128]{2,1,0:T(8,128)S(1)}, f32[4,64,128]{2,1,0:T(8,128)S(1)}, u32[]{:S(2)}, u32[]{:S(2)}) collective-permute-start(f32[4,64,128]{2,1,0:T(8,128)S(1)} %hold.1), channel_id=1, source_target_pairs={{0,16},{8,24},{16,0},{24,8},{1,17},{9,25},{17,1},{25,9},{2,18},{10... | collective-permute-start | bytes 393224 | tf_op jit(solution)/shard_map/ppermute | solution.py:261
  10.6 2.2 %collective-permute-done.3.refs_1_ = f32[4,64,128]{2,1,0:T(8,128)S(1)} collective-permute-done((f32[4,64,128]{2,1,0:T(8,128)S(1)}, f32[4,64,128]{2,1,0:T(8,128)S(1)}, u32[]{:S(2)}, u32[]{:S(2)}) %collective-permute-start.3) | collective-permute-done | bytes 131104 | tf_op jit(solution)/shard_map/ppermute | solution.py:261
  12.8 0.5 %collective-permute-done.2.refs_0_ = f32[4,64,128]{2,1,0:T(8,128)S(1)} collective-permute-done((f32[4,64,128]{2,1,0:T(8,128)S(1)}, f32[4,64,128]{2,1,0:T(8,128)S(1)}, u32[]{:S(2)}, u32[]{:S(2)}) %collective-permute-start.2) | collective-permute-done | bytes 131104 | tf_op jit(solution)/shard_map/ppermute | solution.py:261
  13.2 0.2 add_sides.1.refs_5_
  13.4 1.4 %collective-permute-done.1.refs_1_ = f32[4,64,128]{2,1,0:T(8,128)S(1)} collective-permute-done((f32[4,64,128]{2,1,0:T(8,128)S(1)}, f32[4,64,128]{2,1,0:T(8,128)S(1)}, u32[]{:S(2)}, u32[]{:S(2)}) %collective-permute-start.1) | collective-permute-done | bytes 131104 | tf_op jit(solution)/shard_map/ppermute | solution.py:261
  14.8 0.2 finish.1
  15.1 0.1 collective-permute-start.4
  15.1 1.3 %collective-permute-done.4.swapped.refs_1_ = f32[4,64,128]{2,1,0:T(8,128)S(1)} collective-permute-done((f32[4,64,128]{2,1,0:T(8,128)S(1)}, f32[4,64,128]{2,1,0:T(8,128)S(1)}, u32[]{:S(2)}, u32[]{:S(2)}) %collective-permute-start.4) | collective-permute-done | bytes 131104 | tf_op jit(solution)/shard_map/ppermute | solution.py:504
  16.5 2.6 %collective-permute-start.5 = (f32[2,64,128]{2,1,0:T(8,128)S(1)}, f32[2,64,128]{2,1,0:T(8,128)S(1)}, u32[]{:S(2)}, u32[]{:S(2)}) collective-permute-start(f32[2,64,128]{2,1,0:T(8,128)S(1)} %get-tuple-element.31), channel_id=1, source_target_pairs={{0,4},{1,5},{2,6},{3,7},{4,0},{5,1},{6,2},{7,3},{8,12},{9,13},{10,... | collective-permute-start | bytes 196616 | tf_op jit(solution)/shard_map/ppermute | solution.py:504
  19.1 1.6 %collective-permute-start.6 = (f32[2,64,128]{2,1,0:T(8,128)S(1)}, f32[2,64,128]{2,1,0:T(8,128)S(1)}, u32[]{:S(2)}, u32[]{:S(2)}) collective-permute-start(f32[2,64,128]{2,1,0:T(8,128)S(1)} %get-tuple-element.32), channel_id=1, source_target_pairs={{0,2},{1,3},{2,0},{3,1},{4,6},{5,7},{6,4},{7,5},{8,10},{9,11},{10,... | collective-permute-start | bytes 196616 | tf_op jit(solution)/shard_map/ppermute | solution.py:504
  20.7 0.2 collective-permute-start.7
  20.9 0.0 copy-done
  20.9 0.0 copy-done.5
  20.9 0.0 copy-done.6
  20.9 0.0 copy-done.7
  20.9 0.0 copy-done.8
  21.0 0.0 copy-done.9
  21.0 0.0 copy-done.10
  21.0 0.0 copy-start.1
  21.0 1.3 %copy-done.1 = f32[5,2,2,2,8,1024]{5,4,3,2,1,0:T(8,128)S(1)} copy-done((f32[5,2,2,2,8,1024]{5,4,3,2,1,0:T(8,128)S(1)}, f32[5,2,2,2,8,1024]{5,4,3,2,1,0:T(8,128)}, u32[]{:S(2)}) %copy-start.1) | copy-done | bytes 1310744
  22.3 0.0 copy-start.2
  22.3 1.4 %history.1 = (f32[5,64,1024]{2,1,0:T(8,128)S(1)}, f32[5,64,1024]{2,1,0:T(8,128)S(1)}, f32[1,128]{1,0:T(1,128)S(1)}, f32[5,8,128]{2,1,0:T(8,128)S(1)}, s32[2,8,128]{2,1,0:T(8,128)S(1)}) custom-call(f32[5,64,1024]{2,1,0:T(8,128)S(1)} %bitcast.6, f32[5,64,1024]{2,1,0:T(8,128)S(1)} %bitcast.7, s32[5]{0:T(128)S(1)} %copy-done.5, s32[64]{0:T(128)S(1)} %copy-done.6, ...), custom_call_target="tpu_custom_call" | custom-call | flops 2621440 | bytes 3932160 | tf_op jit(solution)/shard_map/history/pallas_call | solution.py:317
  23.7 0.0 collective-permute-done.5.refs_2_
  23.7 0.0 collective-permute-done.6.refs_3_
  23.8 3.0 %collective-permute-done.7.refs_4_ = f32[2,64,128]{2,1,0:T(8,128)S(1)} collective-permute-done((f32[2,64,128]{2,1,0:T(8,128)S(1)}, f32[2,64,128]{2,1,0:T(8,128)S(1)}, u32[]{:S(2)}, u32[]{:S(2)}) %collective-permute-start.7) | collective-permute-done | bytes 65568 | tf_op jit(solution)/shard_map/ppermute | solution.py:504
  26.8 0.0 copy-done.2
  26.8 0.7 %residual.1 = (f32[64,1024]{1,0:T(8,128)S(1)}, f32[32,1,128]{2,1,0:T(1,128)S(1)}) custom-call(f32[4,64,128]{2,1,0:T(8,128)S(1)} %get-tuple-element.29.own.refs_0_, f32[4,64,128]{2,1,0:T(8,128)S(1)} %collective-permute-done.4.swapped.refs_1_, f32[2,64,128]{2,1,0:T(8,128)S(1)} %collective-permute-done.5.refs_2_, ...), custom_call_target="tpu_custom_call" | custom-call | tf_op jit(solution)/shard_map/residual/pallas_call | solution.py:380
  27.5 10.0 %all_to_all.5.refs_0_ = f32[32,1,128]{2,1,0:T(1,128)S(1)} all-to-all(f32[32,1,128]{2,1,0:T(1,128)S(1)} %get-tuple-element.38), channel_id=1, replica_groups=mesh['kgrp'=4,'energy'=8] {'energy','kgrp'}, dimensions={0} | all-to-all | bytes 32768 | tf_op jit(solution)/shard_map/all_to_all | solution.py:510
  37.5 1.0 %mix.1 = f32[64,1024]{1,0:T(8,128)} custom-call(f32[32,1,128]{2,1,0:T(1,128)S(1)} %all_to_all.5.refs_0_, f32[64,1024]{1,0:T(8,128)S(1)} %get-tuple-element.39.refs_1_, f32[64,1024]{1,0:T(8,128)S(1)} %bitcast.9, f32[5,64,1024]{2,1,0:T(8,128)S(1)} %get-tuple-element.40.refs_3_), custom_call_target="tpu_custom_call" | custom-call | tf_op jit(solution)/shard_map/mix/pallas_call | solution.py:460
  (2 shorter events, 0.0 us)
Async XLA Ops:
  0.0 20.9 %copy-start = (f32[5,2,2,2,8,1024]{5,4,3,2,1,0:T(8,128)S(1)}, f32[5,2,2,2,8,1024]{5,4,3,2,1,0:T(8,128)}, u32[]{:S(2)}) copy-start(f32[5,2,2,2,8,1024]{5,4,3,2,1,0:T(8,128)} %param.14) | copy-start | bytes 3932164
  1.1 8.5 %collective-permute-start = (f32[4,64,128]{2,1,0:T(8,128)S(1)}, f32[4,64,128]{2,1,0:T(8,128)S(1)}, u32[]{:S(2)}, u32[]{:S(2)}) collective-permute-start(f32[4,64,128]{2,1,0:T(8,128)S(1)} %get-tuple-element.23.refs_0_), channel_id=1, source_target_pairs={{0,8},{8,0},{16,24},{24,16},{1,9},{9,1},{17,25},{25,17},{2,10},{10... | collective-permute-start | bytes 393224 | tf_op jit(solution)/shard_map/ppermute | solution.py:261
  4.1 8.7 %collective-permute-start.3 = (f32[4,64,128]{2,1,0:T(8,128)S(1)}, f32[4,64,128]{2,1,0:T(8,128)S(1)}, u32[]{:S(2)}, u32[]{:S(2)}) collective-permute-start(f32[4,64,128]{2,1,0:T(8,128)S(1)} %get-tuple-element.24.refs_1_), channel_id=1, source_target_pairs={{0,24},{8,16},{16,8},{24,0},{1,25},{9,17},{17,9},{25,1},{2,26},{10... | collective-permute-start | bytes 393224 | tf_op jit(solution)/shard_map/ppermute | solution.py:261
  5.6 0.7 %copy-start.3 = (s32[64,5]{0,1:T(8,128)S(1)}, s32[64,5]{0,1:T(8,128)}, u32[]{:S(2)}) copy-start(s32[64,5]{0,1:T(8,128)} %param.17) | copy-start | bytes 3844
  6.3 0.7 %copy-start.4 = (f32[5]{0:T(128)S(1)}, f32[5]{0:T(128)}, u32[]{:S(2)}) copy-start(f32[5]{0:T(128)} %refs_3_.2) | copy-start | bytes 64
  6.9 14.0 %copy-start.5 = (s32[5]{0:T(128)S(1)}, s32[5]{0:T(128)}, u32[]{:S(2)}) copy-start(s32[5]{0:T(128)} %refs_2_.1) | copy-start | bytes 64
  6.9 14.0 %copy-start.6 = (s32[64]{0:T(128)S(1)}, s32[64]{0:T(128)}, u32[]{:S(2)}) copy-start(s32[64]{0:T(128)} %refs_3_.3) | copy-start | bytes 772
  6.9 14.0 %copy-start.7 = (f32[4]{0:T(128)S(1)}, f32[4]{0:T(128)}, u32[]{:S(2)}) copy-start(f32[4]{0:T(128)} %refs_4_.1) | copy-start | bytes 52
  6.9 14.0 %copy-start.8 = (f32[2]{0:T(128)S(1)}, f32[2]{0:T(128)}, u32[]{:S(2)}) copy-start(f32[2]{0:T(128)} %refs_5_.1) | copy-start | bytes 28
  6.9 14.0 %copy-start.9 = (f32[2]{0:T(128)S(1)}, f32[2]{0:T(128)}, u32[]{:S(2)}) copy-start(f32[2]{0:T(128)} %refs_6_.1) | copy-start | bytes 28
  7.0 14.0 %copy-start.10 = (s32[2]{0:T(128)S(1)}, s32[2]{0:T(128)}, u32[]{:S(2)}) copy-start(s32[2]{0:T(128)} %refs_7_.1) | copy-start | bytes 28
  8.1 5.2 %collective-permute-start.2 = (f32[4,64,128]{2,1,0:T(8,128)S(1)}, f32[4,64,128]{2,1,0:T(8,128)S(1)}, u32[]{:S(2)}, u32[]{:S(2)}) collective-permute-start(f32[4,64,128]{2,1,0:T(8,128)S(1)} %get-tuple-element.25._), channel_id=1, source_target_pairs={{0,8},{8,0},{16,24},{24,16},{1,9},{9,1},{17,25},{25,17},{2,10},{10... | collective-permute-start | bytes 393224 | tf_op jit(solution)/shard_map/ppermute | solution.py:261
  9.6 5.2 %collective-permute-start.1 = (f32[4,64,128]{2,1,0:T(8,128)S(1)}, f32[4,64,128]{2,1,0:T(8,128)S(1)}, u32[]{:S(2)}, u32[]{:S(2)}) collective-permute-start(f32[4,64,128]{2,1,0:T(8,128)S(1)} %hold.1), channel_id=1, source_target_pairs={{0,16},{8,24},{16,0},{24,8},{1,17},{9,25},{17,1},{25,9},{2,18},{10... | collective-permute-start | bytes 393224 | tf_op jit(solution)/shard_map/ppermute | solution.py:261
  15.1 1.4 %collective-permute-start.4 = (f32[4,64,128]{2,1,0:T(8,128)S(1)}, f32[4,64,128]{2,1,0:T(8,128)S(1)}, u32[]{:S(2)}, u32[]{:S(2)}) collective-permute-start(f32[4,64,128]{2,1,0:T(8,128)S(1)} %get-tuple-element.30), channel_id=1, source_target_pairs={{0,1},{1,0},{2,3},{3,2},{4,5},{5,4},{6,7},{7,6},{8,9},{9,8},{10,11... | collective-permute-start | bytes 393224 | tf_op jit(solution)/shard_map/ppermute | solution.py:504
  16.5 7.3 %collective-permute-start.5 = (f32[2,64,128]{2,1,0:T(8,128)S(1)}, f32[2,64,128]{2,1,0:T(8,128)S(1)}, u32[]{:S(2)}, u32[]{:S(2)}) collective-permute-start(f32[2,64,128]{2,1,0:T(8,128)S(1)} %get-tuple-element.31), channel_id=1, source_target_pairs={{0,4},{1,5},{2,6},{3,7},{4,0},{5,1},{6,2},{7,3},{8,12},{9,13},{10,... | collective-permute-start | bytes 196616 | tf_op jit(solution)/shard_map/ppermute | solution.py:504
  19.1 4.6 %collective-permute-start.6 = (f32[2,64,128]{2,1,0:T(8,128)S(1)}, f32[2,64,128]{2,1,0:T(8,128)S(1)}, u32[]{:S(2)}, u32[]{:S(2)}) collective-permute-start(f32[2,64,128]{2,1,0:T(8,128)S(1)} %get-tuple-element.32), channel_id=1, source_target_pairs={{0,2},{1,3},{2,0},{3,1},{4,6},{5,7},{6,4},{7,5},{8,10},{9,11},{10,... | collective-permute-start | bytes 196616 | tf_op jit(solution)/shard_map/ppermute | solution.py:504
  20.7 6.1 %collective-permute-start.7 = (f32[2,64,128]{2,1,0:T(8,128)S(1)}, f32[2,64,128]{2,1,0:T(8,128)S(1)}, u32[]{:S(2)}, u32[]{:S(2)}) collective-permute-start(f32[2,64,128]{2,1,0:T(8,128)S(1)} %get-tuple-element.33), channel_id=1, source_target_pairs={{0,6},{1,7},{2,4},{3,5},{4,2},{5,3},{6,0},{7,1},{8,14},{9,15},{10,... | collective-permute-start | bytes 196616 | tf_op jit(solution)/shard_map/ppermute | solution.py:504
  21.0 1.3 %copy-start.1 = (f32[5,2,2,2,8,1024]{5,4,3,2,1,0:T(8,128)S(1)}, f32[5,2,2,2,8,1024]{5,4,3,2,1,0:T(8,128)}, u32[]{:S(2)}) copy-start(f32[5,2,2,2,8,1024]{5,4,3,2,1,0:T(8,128)} %param.15) | copy-start | bytes 3932164
  22.3 4.5 %copy-start.2 = (f32[2,2,2,8,1024]{4,3,2,1,0:T(8,128)S(1)}, f32[2,2,2,8,1024]{4,3,2,1,0:T(8,128)}, u32[]{:S(2)}) copy-start(f32[2,2,2,8,1024]{4,3,2,1,0:T(8,128)} %param.13) | copy-start | bytes 786436

commit v15 on v12

--- a/solution.py
+++ b/solution.py
@@ -341,7 +341,7 @@
         for e in range(parts):
             where = (at, slice(e * slice_len, (e + 1) * slice_len))
             new = sigma[e] - current[where]
-            fresh[where] = new
+            fresh[where] = current[where] + mixing_share * new
             acc[0] = acc[0] + new * new
             for j in range(HIST):
                 acc[j + 1] = acc[j + 1] + new * residuals[(j,) + where]
@@ -379,23 +379,22 @@
     trace = system[0][0]
     for i in range(1, n):
         trace = trace + system[i][i]
-    ridge = ridge_share * trace / n + 1e-06
+    ridge = (ridge_share / n) * trace + 1e-06
     for i in range(n):
         system[i][i] = system[i][i] + ridge
-    inverse = [None] * n
     for k in range(n):
-        inverse[k] = 1.0 / system[k][k]
-        for i in range(k + 1, n):
-            factor = system[k][i] * inverse[k]
-            for j in range(i, n):
-                system[i][j] = system[i][j] - factor * system[k][j]
-            target[i] = target[i] - factor * target[k]
-    gamma = [None] * n
-    for k in range(n - 1, -1, -1):
-        value = target[k]
-        for j in range(k + 1, n):
-            value = value - system[k][j] * gamma[j]
-        gamma[k] = value * inverse[k]
+        inverse = 1.0 / system[k][k]
+        row = [system[k][j] * inverse if j > k else None for j in range(n)]
+        value = target[k] * inverse
+        for i in range(n):
+            if i == k:
+                continue
+            for j in range(k + 1, n):
+                system[i][j] = system[i][j] - system[i][k] * row[j]
+            target[i] = target[i] - system[i][k] * value
+        system[k] = row
+        target[k] = value
+    gamma = target
     weights = [1.0 - gamma[0]]
     for j in range(1, n):
         weights.append(gamma[j - 1] - gamma[j])
@@ -403,8 +402,8 @@
     return weights
 
 
-def mix_kernel(entries, lines, fresh, current, aged, out, wide, mixed_rows, done):
-    summed = jnp.sum(lines[...], axis=0) / entries
+def mix_kernel(entries, lines, fresh, aged, out, wide, mixed_rows, done):
+    summed = jnp.sum(lines[...], axis=0) * (1.0 / entries)
     row = lax.broadcasted_iota(jnp.int32, (8, LANES), 0)
     lane = lax.broadcasted_iota(jnp.int32, (8, LANES), 1)
     for part in range(wide.shape[0]):
@@ -422,7 +421,7 @@
         for top in range(part * span, (part + 1) * span, 8):
             for left in range(0, width, LANES):
                 at = (slice(top, top + 8), slice(left, left + LANES))
-                mixed = weights[0] * (current[at] + mixing_share * fresh[at])
+                mixed = weights[0] * fresh[at]
                 for j in range(HIST):
                     mixed = mixed + weights[j + 1] * aged[(j,) + at]
                 mixed_rows[at] = mixed
@@ -433,20 +432,20 @@
         write.wait()
 
 
-def mix(lines, fresh, current, aged, entries):
+def mix(lines, fresh, aged, entries):
     return pl.pallas_call(
         lambda *refs: mix_kernel(entries, *refs),
         out_shape=jax.ShapeDtypeStruct(fresh.shape, jnp.float32),
-        in_specs=[VMEM] * 4,
+        in_specs=[VMEM] * 3,
         out_specs=pl.BlockSpec(memory_space=pltpu.HBM),
         scratch_shapes=[
             pltpu.VMEM((3, 8, LANES), jnp.float32),
             pltpu.VMEM(fresh.shape, jnp.float32),
-            pltpu.SemaphoreType.DMA((2,)),
+            pltpu.SemaphoreType.DMA((min(4, fresh.shape[0] // 8),)),
         ],
         compiler_params=PARAMS,
         name="mix",
-    )(lines, fresh, current, aged)
+    )(lines, fresh, aged)
 
 
 def per_device(
@@ -486,7 +485,7 @@
     )
     lines = lax.all_to_all(lines, ("energy", "kgrp"), split_axis=0, concat_axis=0, tiled=True)
     entries = float(flat.size * groups * parts)
-    return mix(lines, fresh, flat, aged, entries).reshape(current.shape)
+    return mix(lines, fresh, aged, entries).reshape(current.shape)
 
 
 def solution(mesh):

time: 38.7 us -> 38.7 us (level)
  no operation moved by 1% of the time
where the time goes in v15:
time: 38.7 us; the launch traced here: 38.5 us
  starting transfers between devices  11.5 us (30%)
  blocking collectives  10 us (26%)
  waiting for transfers between devices  9.71 us (25%)
  Pallas kernels  4.6 us (12%)
  local copies, waits for them, and re-layouts  2.52 us (7%)
    all_to_all x1, blocking collectives, per_device(): lax.all_to_all(lines, ('energy', 'kgrp'), split_axis=0, concat_axis=0, ti...  10 us
    ppermute x4, starting transfers between devices, smear(): lax.ppermute(block, 'kgrp', [(i, i ^ flip) for i in range(groups)])  7 us
    ppermute x4, waiting for transfers between devices, per_device(): lax.ppermute(block, 'energy', [(e, e ^ m) for e in range(parts)])  5.68 us
    ppermute x4, starting transfers between devices, per_device(): lax.ppermute(block, 'energy', [(e, e ^ m) for e in range(parts)])  4.52 us
    ppermute x4, waiting for transfers between devices, smear(): lax.ppermute(block, 'kgrp', [(i, i ^ flip) for i in range(groups)])  4.04 us
    pallas_call x1, Pallas kernels, history(): pl.pallas_call(lambda *refs: history_kernel(rows, *refs), out_shape=(jax....  1.43 us
    unnamed x22, local copies, waits for them, and re-layouts  1.38 us
    slice x1, local copies, waits for them, and re-layouts, smear(): head, tail = (own[:half], own[half:])  1.14 us
  transfers between devices with their start and end apart: 8, of which 7 were waited for; matrix products, arithmetic and copies ran while one was open for 0% of the time, Pallas kernels for 7%

profile of v15, /device:TPU:0, one launch (start us, length us, event | category | flops | bytes accessed | tf_op | source)
XLA Modules:
  0.0 38.5 jit_solution(17409644153759995498)
XLA Ops:
  0.0 0.0 copy-start.1
  0.0 0.0 copy-start
  0.0 1.1 %fusion = (f32[1,2,2,64,128]{4,3,2,1,0:T(8,128)S(1)}, f32[1,2,2,64,128]{4,3,2,1,0:T(8,128)S(1)}) fusion(f32[2,2,2,64,128]{4,3,2,1,0:T(8,128)} %param.12), kind=kLoop, calls=%fused_computation | loop fusion | bytes 524288 | tf_op jit(solution)/shard_map/slice | solution.py:240
  1.1 3.0 %collective-permute-start = (f32[4,64,128]{2,1,0:T(8,128)S(1)}, f32[4,64,128]{2,1,0:T(8,128)S(1)}, u32[]{:S(2)}, u32[]{:S(2)}) collective-permute-start(f32[4,64,128]{2,1,0:T(8,128)S(1)} %bitcast.11), channel_id=1, source_target_pairs={{0,8},{8,0},{16,24},{24,16},{1,9},{9,1},{17,25},{25,17},{2,10},{10... | collective-permute-start | bytes 393224 | tf_op jit(solution)/shard_map/ppermute | solution.py:238
  4.1 1.5 %collective-permute-start.3 = (f32[4,64,128]{2,1,0:T(8,128)S(1)}, f32[4,64,128]{2,1,0:T(8,128)S(1)}, u32[]{:S(2)}, u32[]{:S(2)}) collective-permute-start(f32[4,64,128]{2,1,0:T(8,128)S(1)} %bitcast.9), channel_id=1, source_target_pairs={{0,24},{8,16},{16,8},{24,0},{1,25},{9,17},{17,9},{25,1},{2,26},{10... | collective-permute-start | bytes 393224 | tf_op jit(solution)/shard_map/ppermute | solution.py:238
  5.6 0.0 copy-start.3
  5.6 0.7 %copy-done.3 = s32[64,5]{0,1:T(8,128)S(1)} copy-done((s32[64,5]{0,1:T(8,128)S(1)}, s32[64,5]{0,1:T(8,128)}, u32[]{:S(2)}) %copy-start.3) | copy-done | bytes 1304
  6.3 0.0 copy-start.4
  6.3 0.7 %copy-done.4 = f32[5]{0:T(128)S(1)} copy-done((f32[5]{0:T(128)S(1)}, f32[5]{0:T(128)}, u32[]{:S(2)}) %copy-start.4) | copy-done | bytes 44
  7.0 0.0 copy-start.5
  7.0 0.0 copy-start.6
  7.0 0.0 copy-start.7
  7.0 0.0 copy-start.8
  7.0 0.0 copy-start.9
  7.0 0.0 copy-start.10
  7.0 1.1 %prepare.1 = (bf16[64,128]{1,0:T(8,128)(2,1)S(1)}, bf16[64,128]{1,0:T(8,128)(2,1)S(1)}, f32[8,64,128]{2,1,0:T(8,128)S(1)}, f32[4,64,128]{2,1,0:T(8,128)S(1)}) custom-call(f32[4,64,128]{2,1,0:T(8,128)S(1)} %bitcast.12, f32[4,64,128]{2,1,0:T(8,128)S(1)} %bitcast.10, s32[5,64]{1,0:T(8,128)S(1)} %bitcast.14, f32[5]{0:T(128)S(1)} %copy-done.4), custom_call_target="tpu_custom_call" | custom-call | flops 25165824 | bytes 524288 | tf_op jit(solution)/shard_map/prepare/pallas_call | solution.py:85
  8.1 1.6 %collective-permute-start.2 = (f32[4,64,128]{2,1,0:T(8,128)S(1)}, f32[4,64,128]{2,1,0:T(8,128)S(1)}, u32[]{:S(2)}, u32[]{:S(2)}) collective-permute-start(f32[4,64,128]{2,1,0:T(8,128)S(1)} %get-tuple-element.21._), channel_id=1, source_target_pairs={{0,8},{8,0},{16,24},{24,16},{1,9},{9,1},{17,25},{25,17},{2,10},{10... | collective-permute-start | bytes 393224 | tf_op jit(solution)/shard_map/ppermute | solution.py:238
  9.7 0.0 collective-permute-done.block.refs_0_
  9.7 0.9 %collective-permute-start.1 = (f32[4,64,128]{2,1,0:T(8,128)S(1)}, f32[4,64,128]{2,1,0:T(8,128)S(1)}, u32[]{:S(2)}, u32[]{:S(2)}) collective-permute-start(f32[4,64,128]{2,1,0:T(8,128)S(1)} %hold.1), channel_id=1, source_target_pairs={{0,16},{8,24},{16,0},{24,8},{1,17},{9,25},{17,1},{25,9},{2,18},{10... | collective-permute-start | bytes 393224 | tf_op jit(solution)/shard_map/ppermute | solution.py:238
  10.6 2.2 %collective-permute-done.3.refs_1_ = f32[4,64,128]{2,1,0:T(8,128)S(1)} collective-permute-done((f32[4,64,128]{2,1,0:T(8,128)S(1)}, f32[4,64,128]{2,1,0:T(8,128)S(1)}, u32[]{:S(2)}, u32[]{:S(2)}) %collective-permute-start.3) | collective-permute-done | bytes 131104 | tf_op jit(solution)/shard_map/ppermute | solution.py:238
  12.8 0.5 %collective-permute-done.2.refs_0_ = f32[4,64,128]{2,1,0:T(8,128)S(1)} collective-permute-done((f32[4,64,128]{2,1,0:T(8,128)S(1)}, f32[4,64,128]{2,1,0:T(8,128)S(1)}, u32[]{:S(2)}, u32[]{:S(2)}) %collective-permute-start.2) | collective-permute-done | bytes 131104 | tf_op jit(solution)/shard_map/ppermute | solution.py:238
  13.3 0.2 add_sides.1.refs_5_
  13.5 1.4 %collective-permute-done.1.refs_1_ = f32[4,64,128]{2,1,0:T(8,128)S(1)} collective-permute-done((f32[4,64,128]{2,1,0:T(8,128)S(1)}, f32[4,64,128]{2,1,0:T(8,128)S(1)}, u32[]{:S(2)}, u32[]{:S(2)}) %collective-permute-start.1) | collective-permute-done | bytes 131104 | tf_op jit(solution)/shard_map/ppermute | solution.py:238
  14.9 0.2 finish.1
  15.1 0.1 collective-permute-start.4
  15.2 1.3 %collective-permute-done.4.swapped.refs_1_ = f32[4,64,128]{2,1,0:T(8,128)S(1)} collective-permute-done((f32[4,64,128]{2,1,0:T(8,128)S(1)}, f32[4,64,128]{2,1,0:T(8,128)S(1)}, u32[]{:S(2)}, u32[]{:S(2)}) %collective-permute-start.4) | collective-permute-done | bytes 131104 | tf_op jit(solution)/shard_map/ppermute | solution.py:480
  16.5 2.7 %collective-permute-start.5 = (f32[2,64,128]{2,1,0:T(8,128)S(1)}, f32[2,64,128]{2,1,0:T(8,128)S(1)}, u32[]{:S(2)}, u32[]{:S(2)}) collective-permute-start(f32[2,64,128]{2,1,0:T(8,128)S(1)} %get-tuple-element.27), channel_id=1, source_target_pairs={{0,4},{1,5},{2,6},{3,7},{4,0},{5,1},{6,2},{7,3},{8,12},{9,13},{10,... | collective-permute-start | bytes 196616 | tf_op jit(solution)/shard_map/ppermute | solution.py:480
  19.2 1.6 %collective-permute-start.6 = (f32[2,64,128]{2,1,0:T(8,128)S(1)}, f32[2,64,128]{2,1,0:T(8,128)S(1)}, u32[]{:S(2)}, u32[]{:S(2)}) collective-permute-start(f32[2,64,128]{2,1,0:T(8,128)S(1)} %get-tuple-element.28), channel_id=1, source_target_pairs={{0,2},{1,3},{2,0},{3,1},{4,6},{5,7},{6,4},{7,5},{8,10},{9,11},{10,... | collective-permute-start | bytes 196616 | tf_op jit(solution)/shard_map/ppermute | solution.py:480
  20.8 0.2 collective-permute-start.7
  21.0 0.0 copy-done.1
  21.0 0.0 copy-done
  21.0 0.0 copy-done.5
  21.0 0.0 copy-done.6
  21.0 0.0 copy-done.7
  21.0 0.0 copy-done.8
  21.0 0.0 copy-done.9
  21.0 0.0 copy-done.10
  21.0 0.0 copy-start.2
  21.0 1.4 %history.1 = (f32[5,64,1024]{2,1,0:T(8,128)S(1)}, f32[5,64,1024]{2,1,0:T(8,128)S(1)}, f32[1,128]{1,0:T(1,128)S(1)}, f32[5,8,128]{2,1,0:T(8,128)S(1)}, s32[2,8,128]{2,1,0:T(8,128)S(1)}) custom-call(f32[5,64,1024]{2,1,0:T(8,128)S(1)} %bitcast.7, f32[5,64,1024]{2,1,0:T(8,128)S(1)} %bitcast.8, s32[5]{0:T(128)S(1)} %copy-done.5, s32[64]{0:T(128)S(1)} %copy-done.6, ...), custom_call_target="tpu_custom_call" | custom-call | flops 2621440 | bytes 3932160 | tf_op jit(solution)/shard_map/history/pallas_call | solution.py:294
  22.5 0.4 %collective-permute-done.5.refs_2_ = f32[2,64,128]{2,1,0:T(8,128)S(1)} collective-permute-done((f32[2,64,128]{2,1,0:T(8,128)S(1)}, f32[2,64,128]{2,1,0:T(8,128)S(1)}, u32[]{:S(2)}, u32[]{:S(2)}) %collective-permute-start.5) | collective-permute-done | bytes 65568 | tf_op jit(solution)/shard_map/ppermute | solution.py:480
  22.9 0.6 %collective-permute-done.6.refs_3_ = f32[2,64,128]{2,1,0:T(8,128)S(1)} collective-permute-done((f32[2,64,128]{2,1,0:T(8,128)S(1)}, f32[2,64,128]{2,1,0:T(8,128)S(1)}, u32[]{:S(2)}, u32[]{:S(2)}) %collective-permute-start.6) | collective-permute-done | bytes 65568 | tf_op jit(solution)/shard_map/ppermute | solution.py:480
  23.5 3.3 %collective-permute-done.7.refs_4_ = f32[2,64,128]{2,1,0:T(8,128)S(1)} collective-permute-done((f32[2,64,128]{2,1,0:T(8,128)S(1)}, f32[2,64,128]{2,1,0:T(8,128)S(1)}, u32[]{:S(2)}, u32[]{:S(2)}) %collective-permute-start.7) | collective-permute-done | bytes 65568 | tf_op jit(solution)/shard_map/ppermute | solution.py:480
  26.8 0.0 copy-done.2
  26.8 0.7 %residual.1 = (f32[64,1024]{1,0:T(8,128)S(1)}, f32[32,1,128]{2,1,0:T(1,128)S(1)}) custom-call(f32[4,64,128]{2,1,0:T(8,128)S(1)} %get-tuple-element.25.own.refs_0_, f32[4,64,128]{2,1,0:T(8,128)S(1)} %collective-permute-done.4.swapped.refs_1_, f32[2,64,128]{2,1,0:T(8,128)S(1)} %collective-permute-done.5.refs_2_, ...), custom_call_target="tpu_custom_call" | custom-call | tf_op jit(solution)/shard_map/residual/pallas_call | solution.py:357
  27.5 10.0 %all_to_all.5.refs_0_ = f32[32,1,128]{2,1,0:T(1,128)S(1)} all-to-all(f32[32,1,128]{2,1,0:T(1,128)S(1)} %get-tuple-element.34), channel_id=1, replica_groups=mesh['kgrp'=4,'energy'=8] {'energy','kgrp'}, dimensions={0} | all-to-all | bytes 32768 | tf_op jit(solution)/shard_map/all_to_all | solution.py:486
  37.6 1.0 %mix.1 = f32[64,1024]{1,0:T(8,128)} custom-call(f32[32,1,128]{2,1,0:T(1,128)S(1)} %all_to_all.5.refs_0_, f32[64,1024]{1,0:T(8,128)S(1)} %get-tuple-element.35.refs_1_, f32[5,64,1024]{2,1,0:T(8,128)S(1)} %get-tuple-element.36.refs_2_), custom_call_target="tpu_custom_call" | custom-call | tf_op jit(solution)/shard_map/mix/pallas_call | solution.py:436
  (2 shorter events, 0.0 us)
Async XLA Ops:
  0.0 21.0 %copy-start.1 = (f32[5,2,2,2,8,1024]{5,4,3,2,1,0:T(8,128)S(1)}, f32[5,2,2,2,8,1024]{5,4,3,2,1,0:T(8,128)}, u32[]{:S(2)}) copy-start(f32[5,2,2,2,8,1024]{5,4,3,2,1,0:T(8,128)} %param.15) | copy-start | bytes 3932164
  0.0 21.0 %copy-start = (f32[5,2,2,2,8,1024]{5,4,3,2,1,0:T(8,128)S(1)}, f32[5,2,2,2,8,1024]{5,4,3,2,1,0:T(8,128)}, u32[]{:S(2)}) copy-start(f32[5,2,2,2,8,1024]{5,4,3,2,1,0:T(8,128)} %param.14) | copy-start | bytes 3932164
  1.1 8.5 %collective-permute-start = (f32[4,64,128]{2,1,0:T(8,128)S(1)}, f32[4,64,128]{2,1,0:T(8,128)S(1)}, u32[]{:S(2)}, u32[]{:S(2)}) collective-permute-start(f32[4,64,128]{2,1,0:T(8,128)S(1)} %bitcast.11), channel_id=1, source_target_pairs={{0,8},{8,0},{16,24},{24,16},{1,9},{9,1},{17,25},{25,17},{2,10},{10... | collective-permute-start | bytes 393224 | tf_op jit(solution)/shard_map/ppermute | solution.py:238
  4.1 8.7 %collective-permute-start.3 = (f32[4,64,128]{2,1,0:T(8,128)S(1)}, f32[4,64,128]{2,1,0:T(8,128)S(1)}, u32[]{:S(2)}, u32[]{:S(2)}) collective-permute-start(f32[4,64,128]{2,1,0:T(8,128)S(1)} %bitcast.9), channel_id=1, source_target_pairs={{0,24},{8,16},{16,8},{24,0},{1,25},{9,17},{17,9},{25,1},{2,26},{10... | collective-permute-start | bytes 393224 | tf_op jit(solution)/shard_map/ppermute | solution.py:238
  5.6 0.7 %copy-start.3 = (s32[64,5]{0,1:T(8,128)S(1)}, s32[64,5]{0,1:T(8,128)}, u32[]{:S(2)}) copy-start(s32[64,5]{0,1:T(8,128)} %param.17) | copy-start | bytes 3844
  6.3 0.7 %copy-start.4 = (f32[5]{0:T(128)S(1)}, f32[5]{0:T(128)}, u32[]{:S(2)}) copy-start(f32[5]{0:T(128)} %refs_3_.2) | copy-start | bytes 64
  7.0 14.0 %copy-start.5 = (s32[5]{0:T(128)S(1)}, s32[5]{0:T(128)}, u32[]{:S(2)}) copy-start(s32[5]{0:T(128)} %refs_2_.1) | copy-start | bytes 64
  7.0 14.0 %copy-start.6 = (s32[64]{0:T(128)S(1)}, s32[64]{0:T(128)}, u32[]{:S(2)}) copy-start(s32[64]{0:T(128)} %refs_3_.3) | copy-start | bytes 772
  7.0 14.0 %copy-start.7 = (f32[4]{0:T(128)S(1)}, f32[4]{0:T(128)}, u32[]{:S(2)}) copy-start(f32[4]{0:T(128)} %refs_4_.1) | copy-start | bytes 52
  7.0 14.0 %copy-start.8 = (f32[2]{0:T(128)S(1)}, f32[2]{0:T(128)}, u32[]{:S(2)}) copy-start(f32[2]{0:T(128)} %refs_5_.1) | copy-start | bytes 28
  7.0 14.0 %copy-start.9 = (f32[2]{0:T(128)S(1)}, f32[2]{0:T(128)}, u32[]{:S(2)}) copy-start(f32[2]{0:T(128)} %refs_6_.1) | copy-start | bytes 28
  7.0 14.0 %copy-start.10 = (s32[2]{0:T(128)S(1)}, s32[2]{0:T(128)}, u32[]{:S(2)}) copy-start(s32[2]{0:T(128)} %refs_7_.1) | copy-start | bytes 28
  8.1 5.1 %collective-permute-start.2 = (f32[4,64,128]{2,1,0:T(8,128)S(1)}, f32[4,64,128]{2,1,0:T(8,128)S(1)}, u32[]{:S(2)}, u32[]{:S(2)}) collective-permute-start(f32[4,64,128]{2,1,0:T(8,128)S(1)} %get-tuple-element.21._), channel_id=1, source_target_pairs={{0,8},{8,0},{16,24},{24,16},{1,9},{9,1},{17,25},{25,17},{2,10},{10... | collective-permute-start | bytes 393224 | tf_op jit(solution)/shard_map/ppermute | solution.py:238
  9.7 5.2 %collective-permute-start.1 = (f32[4,64,128]{2,1,0:T(8,128)S(1)}, f32[4,64,128]{2,1,0:T(8,128)S(1)}, u32[]{:S(2)}, u32[]{:S(2)}) collective-permute-start(f32[4,64,128]{2,1,0:T(8,128)S(1)} %hold.1), channel_id=1, source_target_pairs={{0,16},{8,24},{16,0},{24,8},{1,17},{9,25},{17,1},{25,9},{2,18},{10... | collective-permute-start | bytes 393224 | tf_op jit(solution)/shard_map/ppermute | solution.py:238
  15.1 1.4 %collective-permute-start.4 = (f32[4,64,128]{2,1,0:T(8,128)S(1)}, f32[4,64,128]{2,1,0:T(8,128)S(1)}, u32[]{:S(2)}, u32[]{:S(2)}) collective-permute-start(f32[4,64,128]{2,1,0:T(8,128)S(1)} %get-tuple-element.26), channel_id=1, source_target_pairs={{0,1},{1,0},{2,3},{3,2},{4,5},{5,4},{6,7},{7,6},{8,9},{9,8},{10,11... | collective-permute-start | bytes 393224 | tf_op jit(solution)/shard_map/ppermute | solution.py:480
  16.5 6.3 %collective-permute-start.5 = (f32[2,64,128]{2,1,0:T(8,128)S(1)}, f32[2,64,128]{2,1,0:T(8,128)S(1)}, u32[]{:S(2)}, u32[]{:S(2)}) collective-permute-start(f32[2,64,128]{2,1,0:T(8,128)S(1)} %get-tuple-element.27), channel_id=1, source_target_pairs={{0,4},{1,5},{2,6},{3,7},{4,0},{5,1},{6,2},{7,3},{8,12},{9,13},{10,... | collective-permute-start | bytes 196616 | tf_op jit(solution)/shard_map/ppermute | solution.py:480
  19.2 4.3 %collective-permute-start.6 = (f32[2,64,128]{2,1,0:T(8,128)S(1)}, f32[2,64,128]{2,1,0:T(8,128)S(1)}, u32[]{:S(2)}, u32[]{:S(2)}) collective-permute-start(f32[2,64,128]{2,1,0:T(8,128)S(1)} %get-tuple-element.28), channel_id=1, source_target_pairs={{0,2},{1,3},{2,0},{3,1},{4,6},{5,7},{6,4},{7,5},{8,10},{9,11},{10,... | collective-permute-start | bytes 196616 | tf_op jit(solution)/shard_map/ppermute | solution.py:480
  20.8 6.1 %collective-permute-start.7 = (f32[2,64,128]{2,1,0:T(8,128)S(1)}, f32[2,64,128]{2,1,0:T(8,128)S(1)}, u32[]{:S(2)}, u32[]{:S(2)}) collective-permute-start(f32[2,64,128]{2,1,0:T(8,128)S(1)} %get-tuple-element.29), channel_id=1, source_target_pairs={{0,6},{1,7},{2,4},{3,5},{4,2},{5,3},{6,0},{7,1},{8,14},{9,15},{10,... | collective-permute-start | bytes 196616 | tf_op jit(solution)/shard_map/ppermute | solution.py:480
  21.0 5.8 %copy-start.2 = (f32[2,2,2,8,1024]{4,3,2,1,0:T(8,128)S(1)}, f32[2,2,2,8,1024]{4,3,2,1,0:T(8,128)}, u32[]{:S(2)}) copy-start(f32[2,2,2,8,1024]{4,3,2,1,0:T(8,128)} %param.13) | copy-start | bytes 786436

commit v16 on v15

--- a/solution.py
+++ b/solution.py
@@ -188,7 +188,7 @@
 def chip_order(parts):
     chips = parts // 2
     half = chips // 2
-    return [half, *range(1, half), *range(half + 1, chips)] if chips > 1 else []
+    return [*range(half + 1, chips), *range(1, half), half] if chips > 1 else []
 
 
 def join_kernel(own, swapped, *out):

time: 38.7 us -> 38.5 us (level)
  waiting for transfers between devices: 9.71 us -> 8.96 us
  blocking collectives: 10 us -> 10.6 us
    ppermute x4, waiting for transfers between devices: 5.68 us -> 4.92 us  [per_device(): lax.ppermute(block, 'energy', [(e, e ^ m) for e in range(parts)])]
    all_to_all x1, blocking collectives: 10 us -> 10.6 us  [per_device(): lax.all_to_all(lines, ('energy', 'kgrp'), split_axis=0, concat_axis=0, ti...]
where the time goes in v16:
time: 38.5 us; the launch traced here: 38.3 us
  starting transfers between devices  11.5 us (30%)
  blocking collectives  10.6 us (28%)
  waiting for transfers between devices  8.96 us (23%)
  Pallas kernels  4.6 us (12%)
  local copies, waits for them, and re-layouts  2.52 us (7%)
    all_to_all x1, blocking collectives, per_device(): lax.all_to_all(lines, ('energy', 'kgrp'), split_axis=0, concat_axis=0, ti...  10.6 us
    ppermute x4, starting transfers between devices, smear(): lax.ppermute(block, 'kgrp', [(i, i ^ flip) for i in range(groups)])  7 us
    ppermute x4, waiting for transfers between devices, per_device(): lax.ppermute(block, 'energy', [(e, e ^ m) for e in range(parts)])  4.92 us
    ppermute x4, starting transfers between devices, per_device(): lax.ppermute(block, 'energy', [(e, e ^ m) for e in range(parts)])  4.52 us
    ppermute x4, waiting for transfers between devices, smear(): lax.ppermute(block, 'kgrp', [(i, i ^ flip) for i in range(groups)])  4.04 us
    pallas_call x1, Pallas kernels, history(): pl.pallas_call(lambda *refs: history_kernel(rows, *refs), out_shape=(jax....  1.43 us
    unnamed x22, local copies, waits for them, and re-layouts  1.38 us
    slice x1, local copies, waits for them, and re-layouts, smear(): head, tail = (own[:half], own[half:])  1.14 us
  transfers between devices with their start and end apart: 8, of which 7 were waited for; matrix products, arithmetic and copies ran while one was open for 0% of the time, Pallas kernels for 7%

profile of v16, /device:TPU:0, one launch (start us, length us, event | category | flops | bytes accessed | tf_op | source)
XLA Modules:
  0.0 38.3 jit_solution(10413011885010984364)
XLA Ops:
  0.0 0.0 copy-start.1
  0.0 0.0 copy-start
  0.0 1.1 %fusion = (f32[1,2,2,64,128]{4,3,2,1,0:T(8,128)S(1)}, f32[1,2,2,64,128]{4,3,2,1,0:T(8,128)S(1)}) fusion(f32[2,2,2,64,128]{4,3,2,1,0:T(8,128)} %param.12), kind=kLoop, calls=%fused_computation | loop fusion | bytes 524288 | tf_op jit(solution)/shard_map/slice | solution.py:240
  1.1 3.0 %collective-permute-start = (f32[4,64,128]{2,1,0:T(8,128)S(1)}, f32[4,64,128]{2,1,0:T(8,128)S(1)}, u32[]{:S(2)}, u32[]{:S(2)}) collective-permute-start(f32[4,64,128]{2,1,0:T(8,128)S(1)} %bitcast.11), channel_id=1, source_target_pairs={{0,8},{8,0},{16,24},{24,16},{1,9},{9,1},{17,25},{25,17},{2,10},{10... | collective-permute-start | bytes 393224 | tf_op jit(solution)/shard_map/ppermute | solution.py:238
  4.1 1.5 %collective-permute-start.3 = (f32[4,64,128]{2,1,0:T(8,128)S(1)}, f32[4,64,128]{2,1,0:T(8,128)S(1)}, u32[]{:S(2)}, u32[]{:S(2)}) collective-permute-start(f32[4,64,128]{2,1,0:T(8,128)S(1)} %bitcast.9), channel_id=1, source_target_pairs={{0,24},{8,16},{16,8},{24,0},{1,25},{9,17},{17,9},{25,1},{2,26},{10... | collective-permute-start | bytes 393224 | tf_op jit(solution)/shard_map/ppermute | solution.py:238
  5.6 0.0 copy-start.3
  5.6 0.7 %copy-done.3 = s32[64,5]{0,1:T(8,128)S(1)} copy-done((s32[64,5]{0,1:T(8,128)S(1)}, s32[64,5]{0,1:T(8,128)}, u32[]{:S(2)}) %copy-start.3) | copy-done | bytes 1304
  6.3 0.0 copy-start.4
  6.3 0.7 %copy-done.4 = f32[5]{0:T(128)S(1)} copy-done((f32[5]{0:T(128)S(1)}, f32[5]{0:T(128)}, u32[]{:S(2)}) %copy-start.4) | copy-done | bytes 44
  7.0 0.0 copy-start.5
  7.0 0.0 copy-start.6
  7.0 0.0 copy-start.7
  7.0 0.0 copy-start.8
  7.0 0.0 copy-start.9
  7.0 0.0 copy-start.10
  7.0 1.1 %prepare.1 = (bf16[64,128]{1,0:T(8,128)(2,1)S(1)}, bf16[64,128]{1,0:T(8,128)(2,1)S(1)}, f32[8,64,128]{2,1,0:T(8,128)S(1)}, f32[4,64,128]{2,1,0:T(8,128)S(1)}) custom-call(f32[4,64,128]{2,1,0:T(8,128)S(1)} %bitcast.12, f32[4,64,128]{2,1,0:T(8,128)S(1)} %bitcast.10, s32[5,64]{1,0:T(8,128)S(1)} %bitcast.14, f32[5]{0:T(128)S(1)} %copy-done.4), custom_call_target="tpu_custom_call" | custom-call | flops 25165824 | bytes 524288 | tf_op jit(solution)/shard_map/prepare/pallas_call | solution.py:85
  8.1 1.6 %collective-permute-start.2 = (f32[4,64,128]{2,1,0:T(8,128)S(1)}, f32[4,64,128]{2,1,0:T(8,128)S(1)}, u32[]{:S(2)}, u32[]{:S(2)}) collective-permute-start(f32[4,64,128]{2,1,0:T(8,128)S(1)} %get-tuple-element.21._), channel_id=1, source_target_pairs={{0,8},{8,0},{16,24},{24,16},{1,9},{9,1},{17,25},{25,17},{2,10},{10... | collective-permute-start | bytes 393224 | tf_op jit(solution)/shard_map/ppermute | solution.py:238
  9.7 0.0 collective-permute-done.block.refs_0_
  9.7 0.9 %collective-permute-start.1 = (f32[4,64,128]{2,1,0:T(8,128)S(1)}, f32[4,64,128]{2,1,0:T(8,128)S(1)}, u32[]{:S(2)}, u32[]{:S(2)}) collective-permute-start(f32[4,64,128]{2,1,0:T(8,128)S(1)} %hold.1), channel_id=1, source_target_pairs={{0,16},{8,24},{16,0},{24,8},{1,17},{9,25},{17,1},{25,9},{2,18},{10... | collective-permute-start | bytes 393224 | tf_op jit(solution)/shard_map/ppermute | solution.py:238
  10.6 2.2 %collective-permute-done.3.refs_1_ = f32[4,64,128]{2,1,0:T(8,128)S(1)} collective-permute-done((f32[4,64,128]{2,1,0:T(8,128)S(1)}, f32[4,64,128]{2,1,0:T(8,128)S(1)}, u32[]{:S(2)}, u32[]{:S(2)}) %collective-permute-start.3) | collective-permute-done | bytes 131104 | tf_op jit(solution)/shard_map/ppermute | solution.py:238
  12.8 0.5 %collective-permute-done.2.refs_0_ = f32[4,64,128]{2,1,0:T(8,128)S(1)} collective-permute-done((f32[4,64,128]{2,1,0:T(8,128)S(1)}, f32[4,64,128]{2,1,0:T(8,128)S(1)}, u32[]{:S(2)}, u32[]{:S(2)}) %collective-permute-start.2) | collective-permute-done | bytes 131104 | tf_op jit(solution)/shard_map/ppermute | solution.py:238
  13.3 0.2 add_sides.1.refs_5_
  13.5 1.4 %collective-permute-done.1.refs_1_ = f32[4,64,128]{2,1,0:T(8,128)S(1)} collective-permute-done((f32[4,64,128]{2,1,0:T(8,128)S(1)}, f32[4,64,128]{2,1,0:T(8,128)S(1)}, u32[]{:S(2)}, u32[]{:S(2)}) %collective-permute-start.1) | collective-permute-done | bytes 131104 | tf_op jit(solution)/shard_map/ppermute | solution.py:238
  14.9 0.2 finish.1
  15.1 0.1 collective-permute-start.4
  15.2 1.3 %collective-permute-done.4.swapped.refs_1_ = f32[4,64,128]{2,1,0:T(8,128)S(1)} collective-permute-done((f32[4,64,128]{2,1,0:T(8,128)S(1)}, f32[4,64,128]{2,1,0:T(8,128)S(1)}, u32[]{:S(2)}, u32[]{:S(2)}) %collective-permute-start.4) | collective-permute-done | bytes 131104 | tf_op jit(solution)/shard_map/ppermute | solution.py:480
  16.5 3.7 %collective-permute-start.5 = (f32[2,64,128]{2,1,0:T(8,128)S(1)}, f32[2,64,128]{2,1,0:T(8,128)S(1)}, u32[]{:S(2)}, u32[]{:S(2)}) collective-permute-start(f32[2,64,128]{2,1,0:T(8,128)S(1)} %get-tuple-element.27), channel_id=1, source_target_pairs={{0,6},{1,7},{2,4},{3,5},{4,2},{5,3},{6,0},{7,1},{8,14},{9,15},{10,... | collective-permute-start | bytes 196616 | tf_op jit(solution)/shard_map/ppermute | solution.py:480
  20.2 0.0 collective-permute-start.6
  20.2 0.8 %collective-permute-start.7 = (f32[2,64,128]{2,1,0:T(8,128)S(1)}, f32[2,64,128]{2,1,0:T(8,128)S(1)}, u32[]{:S(2)}, u32[]{:S(2)}) collective-permute-start(f32[2,64,128]{2,1,0:T(8,128)S(1)} %get-tuple-element.29), channel_id=1, source_target_pairs={{0,4},{1,5},{2,6},{3,7},{4,0},{5,1},{6,2},{7,3},{8,12},{9,13},{10,... | collective-permute-start | bytes 196616 | tf_op jit(solution)/shard_map/ppermute | solution.py:480
  21.0 0.0 copy-done.1
  21.0 0.0 copy-done
  21.0 0.0 copy-done.5
  21.0 0.0 copy-done.6
  21.0 0.0 copy-done.7
  21.0 0.0 copy-done.8
  21.0 0.0 copy-done.9
  21.0 0.0 copy-done.10
  21.0 0.0 copy-start.2
  21.0 1.4 %history.1 = (f32[5,64,1024]{2,1,0:T(8,128)S(1)}, f32[5,64,1024]{2,1,0:T(8,128)S(1)}, f32[1,128]{1,0:T(1,128)S(1)}, f32[5,8,128]{2,1,0:T(8,128)S(1)}, s32[2,8,128]{2,1,0:T(8,128)S(1)}) custom-call(f32[5,64,1024]{2,1,0:T(8,128)S(1)} %bitcast.7, f32[5,64,1024]{2,1,0:T(8,128)S(1)} %bitcast.8, s32[5]{0:T(128)S(1)} %copy-done.5, s32[64]{0:T(128)S(1)} %copy-done.6, ...), custom_call_target="tpu_custom_call" | custom-call | flops 2621440 | bytes 3932160 | tf_op jit(solution)/shard_map/history/pallas_call | solution.py:294
  22.5 0.9 %collective-permute-done.5.refs_2_ = f32[2,64,128]{2,1,0:T(8,128)S(1)} collective-permute-done((f32[2,64,128]{2,1,0:T(8,128)S(1)}, f32[2,64,128]{2,1,0:T(8,128)S(1)}, u32[]{:S(2)}, u32[]{:S(2)}) %collective-permute-start.5) | collective-permute-done | bytes 65568 | tf_op jit(solution)/shard_map/ppermute | solution.py:480
  23.4 1.9 %collective-permute-done.6.refs_3_ = f32[2,64,128]{2,1,0:T(8,128)S(1)} collective-permute-done((f32[2,64,128]{2,1,0:T(8,128)S(1)}, f32[2,64,128]{2,1,0:T(8,128)S(1)}, u32[]{:S(2)}, u32[]{:S(2)}) %collective-permute-start.6) | collective-permute-done | bytes 65568 | tf_op jit(solution)/shard_map/ppermute | solution.py:480
  25.3 0.8 %collective-permute-done.7.refs_4_ = f32[2,64,128]{2,1,0:T(8,128)S(1)} collective-permute-done((f32[2,64,128]{2,1,0:T(8,128)S(1)}, f32[2,64,128]{2,1,0:T(8,128)S(1)}, u32[]{:S(2)}, u32[]{:S(2)}) %collective-permute-start.7) | collective-permute-done | bytes 65568 | tf_op jit(solution)/shard_map/ppermute | solution.py:480
  26.1 0.0 copy-done.2
  26.1 0.7 %residual.1 = (f32[64,1024]{1,0:T(8,128)S(1)}, f32[32,1,128]{2,1,0:T(1,128)S(1)}) custom-call(f32[4,64,128]{2,1,0:T(8,128)S(1)} %get-tuple-element.25.own.refs_0_, f32[4,64,128]{2,1,0:T(8,128)S(1)} %collective-permute-done.4.swapped.refs_1_, f32[2,64,128]{2,1,0:T(8,128)S(1)} %collective-permute-done.5.refs_2_, ...), custom_call_target="tpu_custom_call" | custom-call | tf_op jit(solution)/shard_map/residual/pallas_call | solution.py:357
  26.8 10.6 %all_to_all.5.refs_0_ = f32[32,1,128]{2,1,0:T(1,128)S(1)} all-to-all(f32[32,1,128]{2,1,0:T(1,128)S(1)} %get-tuple-element.34), channel_id=1, replica_groups=mesh['kgrp'=4,'energy'=8] {'energy','kgrp'}, dimensions={0} | all-to-all | bytes 32768 | tf_op jit(solution)/shard_map/all_to_all | solution.py:486
  37.4 1.0 %mix.1 = f32[64,1024]{1,0:T(8,128)} custom-call(f32[32,1,128]{2,1,0:T(1,128)S(1)} %all_to_all.5.refs_0_, f32[64,1024]{1,0:T(8,128)S(1)} %get-tuple-element.35.refs_1_, f32[5,64,1024]{2,1,0:T(8,128)S(1)} %get-tuple-element.36.refs_2_), custom_call_target="tpu_custom_call" | custom-call | tf_op jit(solution)/shard_map/mix/pallas_call | solution.py:436
  (2 shorter events, 0.0 us)
Async XLA Ops:
  0.0 21.0 %copy-start.1 = (f32[5,2,2,2,8,1024]{5,4,3,2,1,0:T(8,128)S(1)}, f32[5,2,2,2,8,1024]{5,4,3,2,1,0:T(8,128)}, u32[]{:S(2)}) copy-start(f32[5,2,2,2,8,1024]{5,4,3,2,1,0:T(8,128)} %param.15) | copy-start | bytes 3932164
  0.0 21.0 %copy-start = (f32[5,2,2,2,8,1024]{5,4,3,2,1,0:T(8,128)S(1)}, f32[5,2,2,2,8,1024]{5,4,3,2,1,0:T(8,128)}, u32[]{:S(2)}) copy-start(f32[5,2,2,2,8,1024]{5,4,3,2,1,0:T(8,128)} %param.14) | copy-start | bytes 3932164
  1.1 8.5 %collective-permute-start = (f32[4,64,128]{2,1,0:T(8,128)S(1)}, f32[4,64,128]{2,1,0:T(8,128)S(1)}, u32[]{:S(2)}, u32[]{:S(2)}) collective-permute-start(f32[4,64,128]{2,1,0:T(8,128)S(1)} %bitcast.11), channel_id=1, source_target_pairs={{0,8},{8,0},{16,24},{24,16},{1,9},{9,1},{17,25},{25,17},{2,10},{10... | collective-permute-start | bytes 393224 | tf_op jit(solution)/shard_map/ppermute | solution.py:238
  4.1 8.7 %collective-permute-start.3 = (f32[4,64,128]{2,1,0:T(8,128)S(1)}, f32[4,64,128]{2,1,0:T(8,128)S(1)}, u32[]{:S(2)}, u32[]{:S(2)}) collective-permute-start(f32[4,64,128]{2,1,0:T(8,128)S(1)} %bitcast.9), channel_id=1, source_target_pairs={{0,24},{8,16},{16,8},{24,0},{1,25},{9,17},{17,9},{25,1},{2,26},{10... | collective-permute-start | bytes 393224 | tf_op jit(solution)/shard_map/ppermute | solution.py:238
  5.6 0.7 %copy-start.3 = (s32[64,5]{0,1:T(8,128)S(1)}, s32[64,5]{0,1:T(8,128)}, u32[]{:S(2)}) copy-start(s32[64,5]{0,1:T(8,128)} %param.17) | copy-start | bytes 3844
  6.3 0.7 %copy-start.4 = (f32[5]{0:T(128)S(1)}, f32[5]{0:T(128)}, u32[]{:S(2)}) copy-start(f32[5]{0:T(128)} %refs_3_.2) | copy-start | bytes 64
  7.0 14.0 %copy-start.5 = (s32[5]{0:T(128)S(1)}, s32[5]{0:T(128)}, u32[]{:S(2)}) copy-start(s32[5]{0:T(128)} %refs_2_.1) | copy-start | bytes 64
  7.0 14.0 %copy-start.6 = (s32[64]{0:T(128)S(1)}, s32[64]{0:T(128)}, u32[]{:S(2)}) copy-start(s32[64]{0:T(128)} %refs_3_.3) | copy-start | bytes 772
  7.0 14.0 %copy-start.7 = (f32[4]{0:T(128)S(1)}, f32[4]{0:T(128)}, u32[]{:S(2)}) copy-start(f32[4]{0:T(128)} %refs_4_.1) | copy-start | bytes 52
  7.0 14.0 %copy-start.8 = (f32[2]{0:T(128)S(1)}, f32[2]{0:T(128)}, u32[]{:S(2)}) copy-start(f32[2]{0:T(128)} %refs_5_.1) | copy-start | bytes 28
  7.0 14.0 %copy-start.9 = (f32[2]{0:T(128)S(1)}, f32[2]{0:T(128)}, u32[]{:S(2)}) copy-start(f32[2]{0:T(128)} %refs_6_.1) | copy-start | bytes 28
  7.0 14.0 %copy-start.10 = (s32[2]{0:T(128)S(1)}, s32[2]{0:T(128)}, u32[]{:S(2)}) copy-start(s32[2]{0:T(128)} %refs_7_.1) | copy-start | bytes 28
  8.1 5.1 %collective-permute-start.2 = (f32[4,64,128]{2,1,0:T(8,128)S(1)}, f32[4,64,128]{2,1,0:T(8,128)S(1)}, u32[]{:S(2)}, u32[]{:S(2)}) collective-permute-start(f32[4,64,128]{2,1,0:T(8,128)S(1)} %get-tuple-element.21._), channel_id=1, source_target_pairs={{0,8},{8,0},{16,24},{24,16},{1,9},{9,1},{17,25},{25,17},{2,10},{10... | collective-permute-start | bytes 393224 | tf_op jit(solution)/shard_map/ppermute | solution.py:238
  9.7 5.2 %collective-permute-start.1 = (f32[4,64,128]{2,1,0:T(8,128)S(1)}, f32[4,64,128]{2,1,0:T(8,128)S(1)}, u32[]{:S(2)}, u32[]{:S(2)}) collective-permute-start(f32[4,64,128]{2,1,0:T(8,128)S(1)} %hold.1), channel_id=1, source_target_pairs={{0,16},{8,24},{16,0},{24,8},{1,17},{9,25},{17,1},{25,9},{2,18},{10... | collective-permute-start | bytes 393224 | tf_op jit(solution)/shard_map/ppermute | solution.py:238
  15.1 1.4 %collective-permute-start.4 = (f32[4,64,128]{2,1,0:T(8,128)S(1)}, f32[4,64,128]{2,1,0:T(8,128)S(1)}, u32[]{:S(2)}, u32[]{:S(2)}) collective-permute-start(f32[4,64,128]{2,1,0:T(8,128)S(1)} %get-tuple-element.26), channel_id=1, source_target_pairs={{0,1},{1,0},{2,3},{3,2},{4,5},{5,4},{6,7},{7,6},{8,9},{9,8},{10,11... | collective-permute-start | bytes 393224 | tf_op jit(solution)/shard_map/ppermute | solution.py:480
  16.5 6.9 %collective-permute-start.5 = (f32[2,64,128]{2,1,0:T(8,128)S(1)}, f32[2,64,128]{2,1,0:T(8,128)S(1)}, u32[]{:S(2)}, u32[]{:S(2)}) collective-permute-start(f32[2,64,128]{2,1,0:T(8,128)S(1)} %get-tuple-element.27), channel_id=1, source_target_pairs={{0,6},{1,7},{2,4},{3,5},{4,2},{5,3},{6,0},{7,1},{8,14},{9,15},{10,... | collective-permute-start | bytes 196616 | tf_op jit(solution)/shard_map/ppermute | solution.py:480
  20.2 5.1 %collective-permute-start.6 = (f32[2,64,128]{2,1,0:T(8,128)S(1)}, f32[2,64,128]{2,1,0:T(8,128)S(1)}, u32[]{:S(2)}, u32[]{:S(2)}) collective-permute-start(f32[2,64,128]{2,1,0:T(8,128)S(1)} %get-tuple-element.28), channel_id=1, source_target_pairs={{0,2},{1,3},{2,0},{3,1},{4,6},{5,7},{6,4},{7,5},{8,10},{9,11},{10,... | collective-permute-start | bytes 196616 | tf_op jit(solution)/shard_map/ppermute | solution.py:480
  20.2 5.9 %collective-permute-start.7 = (f32[2,64,128]{2,1,0:T(8,128)S(1)}, f32[2,64,128]{2,1,0:T(8,128)S(1)}, u32[]{:S(2)}, u32[]{:S(2)}) collective-permute-start(f32[2,64,128]{2,1,0:T(8,128)S(1)} %get-tuple-element.29), channel_id=1, source_target_pairs={{0,4},{1,5},{2,6},{3,7},{4,0},{5,1},{6,2},{7,3},{8,12},{9,13},{10,... | collective-permute-start | bytes 196616 | tf_op jit(solution)/shard_map/ppermute | solution.py:480
  21.0 5.0 %copy-start.2 = (f32[2,2,2,8,1024]{4,3,2,1,0:T(8,128)S(1)}, f32[2,2,2,8,1024]{4,3,2,1,0:T(8,128)}, u32[]{:S(2)}) copy-start(f32[2,2,2,8,1024]{4,3,2,1,0:T(8,128)} %param.13) | copy-start | bytes 786436

commit v17 on v16

--- a/solution.py
+++ b/solution.py
@@ -188,7 +188,7 @@
 def chip_order(parts):
     chips = parts // 2
     half = chips // 2
-    return [*range(half + 1, chips), *range(1, half), half] if chips > 1 else []
+    return [*range(1, half), *range(half + 1, chips), half] if chips > 1 else []
 
 
 def join_kernel(own, swapped, *out):

time: 38.5 us -> 40.1 us (1.042)
  waiting for transfers between devices: 8.96 us -> 10.3 us
  blocking collectives: 10.6 us -> 11.1 us
    ppermute x4, waiting for transfers between devices: 4.92 us -> 6.24 us  [per_device(): lax.ppermute(block, 'energy', [(e, e ^ m) for e in range(parts)])]
    all_to_all x1, blocking collectives: 10.6 us -> 11.1 us  [per_device(): lax.all_to_all(lines, ('energy', 'kgrp'), split_axis=0, concat_axis=0, ti...]
  transfers between devices with their start and end apart: 8 -> 8, of which waited for: 7 -> 6; matrix products, arithmetic and copies ran while one was open for 0% -> 0% of each run, Pallas kernels for 7% -> 7%
where the time goes in v17:
time: 40.1 us; the launch traced here: 39.9 us
  starting transfers between devices  11.3 us (28%)
  blocking collectives  11.1 us (28%)
  waiting for transfers between devices  10.3 us (26%)
  Pallas kernels  4.6 us (11%)
  local copies, waits for them, and re-layouts  2.52 us (6%)
    all_to_all x1, blocking collectives, per_device(): lax.all_to_all(lines, ('energy', 'kgrp'), split_axis=0, concat_axis=0, ti...  11.1 us
    ppermute x4, starting transfers between devices, smear(): lax.ppermute(block, 'kgrp', [(i, i ^ flip) for i in range(groups)])  7 us
    ppermute x4, waiting for transfers between devices, per_device(): lax.ppermute(block, 'energy', [(e, e ^ m) for e in range(parts)])  6.24 us
    ppermute x4, starting transfers between devices, per_device(): lax.ppermute(block, 'energy', [(e, e ^ m) for e in range(parts)])  4.31 us
    ppermute x4, waiting for transfers between devices, smear(): lax.ppermute(block, 'kgrp', [(i, i ^ flip) for i in range(groups)])  4.04 us
    pallas_call x1, Pallas kernels, history(): pl.pallas_call(lambda *refs: history_kernel(rows, *refs), out_shape=(jax....  1.43 us
    unnamed x22, local copies, waits for them, and re-layouts  1.38 us
    slice x1, local copies, waits for them, and re-layouts, smear(): head, tail = (own[:half], own[half:])  1.14 us
  transfers between devices with their start and end apart: 8, of which 6 were waited for; matrix products, arithmetic and copies ran while one was open for 0% of the time, Pallas kernels for 7%

profile of v17, /device:TPU:0, one launch (start us, length us, event | category | flops | bytes accessed | tf_op | source)
XLA Modules:
  0.0 39.9 jit_solution(2950652995670501393)
XLA Ops:
  0.0 0.0 copy-start.1
  0.0 0.0 copy-start
  0.0 1.1 %fusion = (f32[1,2,2,64,128]{4,3,2,1,0:T(8,128)S(1)}, f32[1,2,2,64,128]{4,3,2,1,0:T(8,128)S(1)}) fusion(f32[2,2,2,64,128]{4,3,2,1,0:T(8,128)} %param.12), kind=kLoop, calls=%fused_computation | loop fusion | bytes 524288 | tf_op jit(solution)/shard_map/slice | solution.py:240
  1.1 3.0 %collective-permute-start = (f32[4,64,128]{2,1,0:T(8,128)S(1)}, f32[4,64,128]{2,1,0:T(8,128)S(1)}, u32[]{:S(2)}, u32[]{:S(2)}) collective-permute-start(f32[4,64,128]{2,1,0:T(8,128)S(1)} %bitcast.11), channel_id=1, source_target_pairs={{0,8},{8,0},{16,24},{24,16},{1,9},{9,1},{17,25},{25,17},{2,10},{10... | collective-permute-start | bytes 393224 | tf_op jit(solution)/shard_map/ppermute | solution.py:238
  4.1 1.5 %collective-permute-start.3 = (f32[4,64,128]{2,1,0:T(8,128)S(1)}, f32[4,64,128]{2,1,0:T(8,128)S(1)}, u32[]{:S(2)}, u32[]{:S(2)}) collective-permute-start(f32[4,64,128]{2,1,0:T(8,128)S(1)} %bitcast.9), channel_id=1, source_target_pairs={{0,24},{8,16},{16,8},{24,0},{1,25},{9,17},{17,9},{25,1},{2,26},{10... | collective-permute-start | bytes 393224 | tf_op jit(solution)/shard_map/ppermute | solution.py:238
  5.6 0.0 copy-start.3
  5.6 0.7 %copy-done.3 = s32[64,5]{0,1:T(8,128)S(1)} copy-done((s32[64,5]{0,1:T(8,128)S(1)}, s32[64,5]{0,1:T(8,128)}, u32[]{:S(2)}) %copy-start.3) | copy-done | bytes 1304
  6.3 0.0 copy-start.4
  6.3 0.7 %copy-done.4 = f32[5]{0:T(128)S(1)} copy-done((f32[5]{0:T(128)S(1)}, f32[5]{0:T(128)}, u32[]{:S(2)}) %copy-start.4) | copy-done | bytes 44
  7.0 0.0 copy-start.5
  7.0 0.0 copy-start.6
  7.0 0.0 copy-start.7
  7.0 0.0 copy-start.8
  7.0 0.0 copy-start.9
  7.0 0.0 copy-start.10
  7.0 1.1 %prepare.1 = (bf16[64,128]{1,0:T(8,128)(2,1)S(1)}, bf16[64,128]{1,0:T(8,128)(2,1)S(1)}, f32[8,64,128]{2,1,0:T(8,128)S(1)}, f32[4,64,128]{2,1,0:T(8,128)S(1)}) custom-call(f32[4,64,128]{2,1,0:T(8,128)S(1)} %bitcast.12, f32[4,64,128]{2,1,0:T(8,128)S(1)} %bitcast.10, s32[5,64]{1,0:T(8,128)S(1)} %bitcast.14, f32[5]{0:T(128)S(1)} %copy-done.4), custom_call_target="tpu_custom_call" | custom-call | flops 25165824 | bytes 524288 | tf_op jit(solution)/shard_map/prepare/pallas_call | solution.py:85
  8.1 1.6 %collective-permute-start.2 = (f32[4,64,128]{2,1,0:T(8,128)S(1)}, f32[4,64,128]{2,1,0:T(8,128)S(1)}, u32[]{:S(2)}, u32[]{:S(2)}) collective-permute-start(f32[4,64,128]{2,1,0:T(8,128)S(1)} %get-tuple-element.21._), channel_id=1, source_target_pairs={{0,8},{8,0},{16,24},{24,16},{1,9},{9,1},{17,25},{25,17},{2,10},{10... | collective-permute-start | bytes 393224 | tf_op jit(solution)/shard_map/ppermute | solution.py:238
  9.7 0.0 collective-permute-done.block.refs_0_
  9.7 0.9 %collective-permute-start.1 = (f32[4,64,128]{2,1,0:T(8,128)S(1)}, f32[4,64,128]{2,1,0:T(8,128)S(1)}, u32[]{:S(2)}, u32[]{:S(2)}) collective-permute-start(f32[4,64,128]{2,1,0:T(8,128)S(1)} %hold.1), channel_id=1, source_target_pairs={{0,16},{8,24},{16,0},{24,8},{1,17},{9,25},{17,1},{25,9},{2,18},{10... | collective-permute-start | bytes 393224 | tf_op jit(solution)/shard_map/ppermute | solution.py:238
  10.6 2.2 %collective-permute-done.3.refs_1_ = f32[4,64,128]{2,1,0:T(8,128)S(1)} collective-permute-done((f32[4,64,128]{2,1,0:T(8,128)S(1)}, f32[4,64,128]{2,1,0:T(8,128)S(1)}, u32[]{:S(2)}, u32[]{:S(2)}) %collective-permute-start.3) | collective-permute-done | bytes 131104 | tf_op jit(solution)/shard_map/ppermute | solution.py:238
  12.8 0.5 %collective-permute-done.2.refs_0_ = f32[4,64,128]{2,1,0:T(8,128)S(1)} collective-permute-done((f32[4,64,128]{2,1,0:T(8,128)S(1)}, f32[4,64,128]{2,1,0:T(8,128)S(1)}, u32[]{:S(2)}, u32[]{:S(2)}) %collective-permute-start.2) | collective-permute-done | bytes 131104 | tf_op jit(solution)/shard_map/ppermute | solution.py:238
  13.3 0.2 add_sides.1.refs_5_
  13.5 1.4 %collective-permute-done.1.refs_1_ = f32[4,64,128]{2,1,0:T(8,128)S(1)} collective-permute-done((f32[4,64,128]{2,1,0:T(8,128)S(1)}, f32[4,64,128]{2,1,0:T(8,128)S(1)}, u32[]{:S(2)}, u32[]{:S(2)}) %collective-permute-start.1) | collective-permute-done | bytes 131104 | tf_op jit(solution)/shard_map/ppermute | solution.py:238
  14.9 0.2 finish.1
  15.1 0.1 collective-permute-start.4
  15.2 1.3 %collective-permute-done.4.swapped.refs_1_ = f32[4,64,128]{2,1,0:T(8,128)S(1)} collective-permute-done((f32[4,64,128]{2,1,0:T(8,128)S(1)}, f32[4,64,128]{2,1,0:T(8,128)S(1)}, u32[]{:S(2)}, u32[]{:S(2)}) %collective-permute-start.4) | collective-permute-done | bytes 131104 | tf_op jit(solution)/shard_map/ppermute | solution.py:480
  16.5 1.6 %collective-permute-start.5 = (f32[2,64,128]{2,1,0:T(8,128)S(1)}, f32[2,64,128]{2,1,0:T(8,128)S(1)}, u32[]{:S(2)}, u32[]{:S(2)}) collective-permute-start(f32[2,64,128]{2,1,0:T(8,128)S(1)} %get-tuple-element.27), channel_id=1, source_target_pairs={{0,2},{1,3},{2,0},{3,1},{4,6},{5,7},{6,4},{7,5},{8,10},{9,11},{10,... | collective-permute-start | bytes 196616 | tf_op jit(solution)/shard_map/ppermute | solution.py:480
  18.2 2.5 %collective-permute-start.6 = (f32[2,64,128]{2,1,0:T(8,128)S(1)}, f32[2,64,128]{2,1,0:T(8,128)S(1)}, u32[]{:S(2)}, u32[]{:S(2)}) collective-permute-start(f32[2,64,128]{2,1,0:T(8,128)S(1)} %get-tuple-element.28), channel_id=1, source_target_pairs={{0,6},{1,7},{2,4},{3,5},{4,2},{5,3},{6,0},{7,1},{8,14},{9,15},{10,... | collective-permute-start | bytes 196616 | tf_op jit(solution)/shard_map/ppermute | solution.py:480
  20.6 0.1 collective-permute-start.7
  20.8 0.0 copy-done.1
  20.8 0.0 copy-done
  20.8 0.0 copy-done.5
  20.8 0.0 copy-done.6
  20.8 0.0 copy-done.7
  20.8 0.0 copy-done.8
  20.8 0.0 copy-done.9
  20.8 0.0 copy-done.10
  20.8 0.0 copy-start.2
  20.8 1.4 %history.1 = (f32[5,64,1024]{2,1,0:T(8,128)S(1)}, f32[5,64,1024]{2,1,0:T(8,128)S(1)}, f32[1,128]{1,0:T(1,128)S(1)}, f32[5,8,128]{2,1,0:T(8,128)S(1)}, s32[2,8,128]{2,1,0:T(8,128)S(1)}) custom-call(f32[5,64,1024]{2,1,0:T(8,128)S(1)} %bitcast.7, f32[5,64,1024]{2,1,0:T(8,128)S(1)} %bitcast.8, s32[5]{0:T(128)S(1)} %copy-done.5, s32[64]{0:T(128)S(1)} %copy-done.6, ...), custom_call_target="tpu_custom_call" | custom-call | flops 2621440 | bytes 3932160 | tf_op jit(solution)/shard_map/history/pallas_call | solution.py:294
  22.3 0.0 collective-permute-done.5.refs_2_
  22.3 2.5 %collective-permute-done.6.refs_3_ = f32[2,64,128]{2,1,0:T(8,128)S(1)} collective-permute-done((f32[2,64,128]{2,1,0:T(8,128)S(1)}, f32[2,64,128]{2,1,0:T(8,128)S(1)}, u32[]{:S(2)}, u32[]{:S(2)}) %collective-permute-start.6) | collective-permute-done | bytes 65568 | tf_op jit(solution)/shard_map/ppermute | solution.py:480
  24.8 2.4 %collective-permute-done.7.refs_4_ = f32[2,64,128]{2,1,0:T(8,128)S(1)} collective-permute-done((f32[2,64,128]{2,1,0:T(8,128)S(1)}, f32[2,64,128]{2,1,0:T(8,128)S(1)}, u32[]{:S(2)}, u32[]{:S(2)}) %collective-permute-start.7) | collective-permute-done | bytes 65568 | tf_op jit(solution)/shard_map/ppermute | solution.py:480
  27.2 0.0 copy-done.2
  27.2 0.7 %residual.1 = (f32[64,1024]{1,0:T(8,128)S(1)}, f32[32,1,128]{2,1,0:T(1,128)S(1)}) custom-call(f32[4,64,128]{2,1,0:T(8,128)S(1)} %get-tuple-element.25.own.refs_0_, f32[4,64,128]{2,1,0:T(8,128)S(1)} %collective-permute-done.4.swapped.refs_1_, f32[2,64,128]{2,1,0:T(8,128)S(1)} %collective-permute-done.5.refs_2_, ...), custom_call_target="tpu_custom_call" | custom-call | tf_op jit(solution)/shard_map/residual/pallas_call | solution.py:357
  27.9 11.1 %all_to_all.5.refs_0_ = f32[32,1,128]{2,1,0:T(1,128)S(1)} all-to-all(f32[32,1,128]{2,1,0:T(1,128)S(1)} %get-tuple-element.34), channel_id=1, replica_groups=mesh['kgrp'=4,'energy'=8] {'energy','kgrp'}, dimensions={0} | all-to-all | bytes 32768 | tf_op jit(solution)/shard_map/all_to_all | solution.py:486
  39.0 1.0 %mix.1 = f32[64,1024]{1,0:T(8,128)} custom-call(f32[32,1,128]{2,1,0:T(1,128)S(1)} %all_to_all.5.refs_0_, f32[64,1024]{1,0:T(8,128)S(1)} %get-tuple-element.35.refs_1_, f32[5,64,1024]{2,1,0:T(8,128)S(1)} %get-tuple-element.36.refs_2_), custom_call_target="tpu_custom_call" | custom-call | tf_op jit(solution)/shard_map/mix/pallas_call | solution.py:436
  (2 shorter events, 0.0 us)
Async XLA Ops:
  0.0 20.8 %copy-start.1 = (f32[5,2,2,2,8,1024]{5,4,3,2,1,0:T(8,128)S(1)}, f32[5,2,2,2,8,1024]{5,4,3,2,1,0:T(8,128)}, u32[]{:S(2)}) copy-start(f32[5,2,2,2,8,1024]{5,4,3,2,1,0:T(8,128)} %param.15) | copy-start | bytes 3932164
  0.0 20.8 %copy-start = (f32[5,2,2,2,8,1024]{5,4,3,2,1,0:T(8,128)S(1)}, f32[5,2,2,2,8,1024]{5,4,3,2,1,0:T(8,128)}, u32[]{:S(2)}) copy-start(f32[5,2,2,2,8,1024]{5,4,3,2,1,0:T(8,128)} %param.14) | copy-start | bytes 3932164
  1.1 8.5 %collective-permute-start = (f32[4,64,128]{2,1,0:T(8,128)S(1)}, f32[4,64,128]{2,1,0:T(8,128)S(1)}, u32[]{:S(2)}, u32[]{:S(2)}) collective-permute-start(f32[4,64,128]{2,1,0:T(8,128)S(1)} %bitcast.11), channel_id=1, source_target_pairs={{0,8},{8,0},{16,24},{24,16},{1,9},{9,1},{17,25},{25,17},{2,10},{10... | collective-permute-start | bytes 393224 | tf_op jit(solution)/shard_map/ppermute | solution.py:238
  4.1 8.7 %collective-permute-start.3 = (f32[4,64,128]{2,1,0:T(8,128)S(1)}, f32[4,64,128]{2,1,0:T(8,128)S(1)}, u32[]{:S(2)}, u32[]{:S(2)}) collective-permute-start(f32[4,64,128]{2,1,0:T(8,128)S(1)} %bitcast.9), channel_id=1, source_target_pairs={{0,24},{8,16},{16,8},{24,0},{1,25},{9,17},{17,9},{25,1},{2,26},{10... | collective-permute-start | bytes 393224 | tf_op jit(solution)/shard_map/ppermute | solution.py:238
  5.6 0.7 %copy-start.3 = (s32[64,5]{0,1:T(8,128)S(1)}, s32[64,5]{0,1:T(8,128)}, u32[]{:S(2)}) copy-start(s32[64,5]{0,1:T(8,128)} %param.17) | copy-start | bytes 3844
  6.3 0.7 %copy-start.4 = (f32[5]{0:T(128)S(1)}, f32[5]{0:T(128)}, u32[]{:S(2)}) copy-start(f32[5]{0:T(128)} %refs_3_.2) | copy-start | bytes 64
  7.0 13.8 %copy-start.5 = (s32[5]{0:T(128)S(1)}, s32[5]{0:T(128)}, u32[]{:S(2)}) copy-start(s32[5]{0:T(128)} %refs_2_.1) | copy-start | bytes 64
  7.0 13.8 %copy-start.6 = (s32[64]{0:T(128)S(1)}, s32[64]{0:T(128)}, u32[]{:S(2)}) copy-start(s32[64]{0:T(128)} %refs_3_.3) | copy-start | bytes 772
  7.0 13.8 %copy-start.7 = (f32[4]{0:T(128)S(1)}, f32[4]{0:T(128)}, u32[]{:S(2)}) copy-start(f32[4]{0:T(128)} %refs_4_.1) | copy-start | bytes 52
  7.0 13.8 %copy-start.8 = (f32[2]{0:T(128)S(1)}, f32[2]{0:T(128)}, u32[]{:S(2)}) copy-start(f32[2]{0:T(128)} %refs_5_.1) | copy-start | bytes 28
  7.0 13.8 %copy-start.9 = (f32[2]{0:T(128)S(1)}, f32[2]{0:T(128)}, u32[]{:S(2)}) copy-start(f32[2]{0:T(128)} %refs_6_.1) | copy-start | bytes 28
  7.0 13.8 %copy-start.10 = (s32[2]{0:T(128)S(1)}, s32[2]{0:T(128)}, u32[]{:S(2)}) copy-start(s32[2]{0:T(128)} %refs_7_.1) | copy-start | bytes 28
  8.1 5.1 %collective-permute-start.2 = (f32[4,64,128]{2,1,0:T(8,128)S(1)}, f32[4,64,128]{2,1,0:T(8,128)S(1)}, u32[]{:S(2)}, u32[]{:S(2)}) collective-permute-start(f32[4,64,128]{2,1,0:T(8,128)S(1)} %get-tuple-element.21._), channel_id=1, source_target_pairs={{0,8},{8,0},{16,24},{24,16},{1,9},{9,1},{17,25},{25,17},{2,10},{10... | collective-permute-start | bytes 393224 | tf_op jit(solution)/shard_map/ppermute | solution.py:238
  9.7 5.2 %collective-permute-start.1 = (f32[4,64,128]{2,1,0:T(8,128)S(1)}, f32[4,64,128]{2,1,0:T(8,128)S(1)}, u32[]{:S(2)}, u32[]{:S(2)}) collective-permute-start(f32[4,64,128]{2,1,0:T(8,128)S(1)} %hold.1), channel_id=1, source_target_pairs={{0,16},{8,24},{16,0},{24,8},{1,17},{9,25},{17,1},{25,9},{2,18},{10... | collective-permute-start | bytes 393224 | tf_op jit(solution)/shard_map/ppermute | solution.py:238
  15.1 1.4 %collective-permute-start.4 = (f32[4,64,128]{2,1,0:T(8,128)S(1)}, f32[4,64,128]{2,1,0:T(8,128)S(1)}, u32[]{:S(2)}, u32[]{:S(2)}) collective-permute-start(f32[4,64,128]{2,1,0:T(8,128)S(1)} %get-tuple-element.26), channel_id=1, source_target_pairs={{0,1},{1,0},{2,3},{3,2},{4,5},{5,4},{6,7},{7,6},{8,9},{9,8},{10,11... | collective-permute-start | bytes 393224 | tf_op jit(solution)/shard_map/ppermute | solution.py:480
  16.5 5.7 %collective-permute-start.5 = (f32[2,64,128]{2,1,0:T(8,128)S(1)}, f32[2,64,128]{2,1,0:T(8,128)S(1)}, u32[]{:S(2)}, u32[]{:S(2)}) collective-permute-start(f32[2,64,128]{2,1,0:T(8,128)S(1)} %get-tuple-element.27), channel_id=1, source_target_pairs={{0,2},{1,3},{2,0},{3,1},{4,6},{5,7},{6,4},{7,5},{8,10},{9,11},{10,... | collective-permute-start | bytes 196616 | tf_op jit(solution)/shard_map/ppermute | solution.py:480
  18.2 6.7 %collective-permute-start.6 = (f32[2,64,128]{2,1,0:T(8,128)S(1)}, f32[2,64,128]{2,1,0:T(8,128)S(1)}, u32[]{:S(2)}, u32[]{:S(2)}) collective-permute-start(f32[2,64,128]{2,1,0:T(8,128)S(1)} %get-tuple-element.28), channel_id=1, source_target_pairs={{0,6},{1,7},{2,4},{3,5},{4,2},{5,3},{6,0},{7,1},{8,14},{9,15},{10,... | collective-permute-start | bytes 196616 | tf_op jit(solution)/shard_map/ppermute | solution.py:480
  20.6 6.5 %collective-permute-start.7 = (f32[2,64,128]{2,1,0:T(8,128)S(1)}, f32[2,64,128]{2,1,0:T(8,128)S(1)}, u32[]{:S(2)}, u32[]{:S(2)}) collective-permute-start(f32[2,64,128]{2,1,0:T(8,128)S(1)} %get-tuple-element.29), channel_id=1, source_target_pairs={{0,4},{1,5},{2,6},{3,7},{4,0},{5,1},{6,2},{7,3},{8,12},{9,13},{10,... | collective-permute-start | bytes 196616 | tf_op jit(solution)/shard_map/ppermute | solution.py:480
  20.8 6.4 %copy-start.2 = (f32[2,2,2,8,1024]{4,3,2,1,0:T(8,128)S(1)}, f32[2,2,2,8,1024]{4,3,2,1,0:T(8,128)}, u32[]{:S(2)}) copy-start(f32[2,2,2,8,1024]{4,3,2,1,0:T(8,128)} %param.13) | copy-start | bytes 786436

commit v18 on v16

--- a/solution.py
+++ b/solution.py
@@ -102,7 +102,7 @@
             flops=6 * size * group_len, bytes_accessed=8 * size, transcendentals=0
         ),
         name="prepare",
-    )(*blocks, jnp.transpose(neighbour), weight)
+    )(*blocks, *(pltpu.with_memory_space_constraint(x, pltpu.HBM) for x in (neighbour.T, weight)))
 
 
 def smeared_pairs(first, sides, stencil_hi, stencil_lo, part):

time: 38.5 us -> 38.6 us (level)
  local copies, waits for them, and re-layouts: 2.52 us -> 1.17 us
  starting transfers between devices: 11.5 us -> 12.7 us
  waiting for transfers between devices: 8.96 us -> 8.53 us
  blocking collectives: 10.6 us -> 11 us
    unnamed x22 -> x18, local copies, waits for them, and re-layouts: 1.38 us -> 0.04 us
    ppermute x4, starting transfers between devices: 7 us -> 8.15 us  [smear(): lax.ppermute(block, 'kgrp', [(i, i ^ flip) for i in range(groups)])]
    all_to_all x1, blocking collectives: 10.6 us -> 11 us  [per_device(): lax.all_to_all(lines, ('energy', 'kgrp'), split_axis=0, concat_axis=0, ti...]
    ppermute x4, waiting for transfers between devices: 4.04 us -> 3.62 us  [smear(): lax.ppermute(block, 'kgrp', [(i, i ^ flip) for i in range(groups)])]
  transfers between devices with their start and end apart: 8 -> 8, of which waited for: 7 -> 7; matrix products, arithmetic and copies ran while one was open for 0% -> 0% of each run, Pallas kernels for 7% -> 8%
where the time goes in v18:
time: 38.6 us; the launch traced here: 38.4 us
  starting transfers between devices  12.7 us (33%)
  blocking collectives  11 us (28%)
  waiting for transfers between devices  8.53 us (22%)
  Pallas kernels  4.84 us (13%)
  local copies, waits for them, and re-layouts  1.17 us (3%)
    all_to_all x1, blocking collectives, per_device(): lax.all_to_all(lines, ('energy', 'kgrp'), split_axis=0, concat_axis=0, ti...  11 us
    ppermute x4, starting transfers between devices, smear(): lax.ppermute(block, 'kgrp', [(i, i ^ flip) for i in range(groups)])  8.15 us
    ppermute x4, waiting for transfers between devices, per_device(): lax.ppermute(block, 'energy', [(e, e ^ m) for e in range(parts)])  4.91 us
    ppermute x4, starting transfers between devices, per_device(): lax.ppermute(block, 'energy', [(e, e ^ m) for e in range(parts)])  4.52 us
    ppermute x4, waiting for transfers between devices, smear(): lax.ppermute(block, 'kgrp', [(i, i ^ flip) for i in range(groups)])  3.62 us
    pallas_call x1, Pallas kernels, history(): pl.pallas_call(lambda *refs: history_kernel(rows, *refs), out_shape=(jax....  1.43 us
    pallas_call x1, Pallas kernels, prepare(): pl.pallas_call(lambda *refs: prepare_kernel(total_k, *refs), out_shape=(s...  1.33 us
    slice x1, local copies, waits for them, and re-layouts, smear(): head, tail = (own[:half], own[half:])  1.14 us
  transfers between devices with their start and end apart: 8, of which 7 were waited for; matrix products, arithmetic and copies ran while one was open for 0% of the time, Pallas kernels for 8%

profile of v18, /device:TPU:0, one launch (start us, length us, event | category | flops | bytes accessed | tf_op | source)
XLA Modules:
  0.0 38.4 jit_solution(9822997749445538841)
XLA Ops:
  0.0 0.0 copy-start.8
  0.0 0.0 copy-start.7
  0.0 0.0 copy-start.6
  0.0 0.0 copy-start.5
  0.0 0.0 copy-start.4
  0.0 0.0 copy-start.3
  0.0 0.0 copy-start.1
  0.0 0.0 copy-start
  0.0 1.1 %fusion = (f32[1,2,2,64,128]{4,3,2,1,0:T(8,128)S(1)}, f32[1,2,2,64,128]{4,3,2,1,0:T(8,128)S(1)}) fusion(f32[2,2,2,64,128]{4,3,2,1,0:T(8,128)} %param.12), kind=kLoop, calls=%fused_computation | loop fusion | bytes 524288 | tf_op jit(solution)/shard_map/slice | solution.py:240
  1.2 3.0 %collective-permute-start = (f32[4,64,128]{2,1,0:T(8,128)S(1)}, f32[4,64,128]{2,1,0:T(8,128)S(1)}, u32[]{:S(2)}, u32[]{:S(2)}) collective-permute-start(f32[4,64,128]{2,1,0:T(8,128)S(1)} %bitcast.11), channel_id=1, source_target_pairs={{0,8},{8,0},{16,24},{24,16},{1,9},{9,1},{17,25},{25,17},{2,10},{10... | collective-permute-start | bytes 393224 | tf_op jit(solution)/shard_map/ppermute | solution.py:238
  4.2 1.5 %collective-permute-start.3 = (f32[4,64,128]{2,1,0:T(8,128)S(1)}, f32[4,64,128]{2,1,0:T(8,128)S(1)}, u32[]{:S(2)}, u32[]{:S(2)}) collective-permute-start(f32[4,64,128]{2,1,0:T(8,128)S(1)} %bitcast.9), channel_id=1, source_target_pairs={{0,24},{8,16},{16,8},{24,0},{1,25},{9,17},{17,9},{25,1},{2,26},{10... | collective-permute-start | bytes 393224 | tf_op jit(solution)/shard_map/ppermute | solution.py:238
  5.7 1.3 %prepare.1 = (bf16[64,128]{1,0:T(8,128)(2,1)S(1)}, bf16[64,128]{1,0:T(8,128)(2,1)S(1)}, f32[8,64,128]{2,1,0:T(8,128)S(1)}, f32[4,64,128]{2,1,0:T(8,128)S(1)}) custom-call(f32[4,64,128]{2,1,0:T(8,128)S(1)} %bitcast.12, f32[4,64,128]{2,1,0:T(8,128)S(1)} %bitcast.10, s32[5,64]{1,0:T(8,128)} %bitcast.14, f32[5]{0:T(128)} %refs_3_.2), custom_call_target="tpu_custom_call" | custom-call | flops 25165824 | bytes 524288 | tf_op jit(solution)/shard_map/prepare/pallas_call | solution.py:85
  7.0 1.6 %collective-permute-start.2 = (f32[4,64,128]{2,1,0:T(8,128)S(1)}, f32[4,64,128]{2,1,0:T(8,128)S(1)}, u32[]{:S(2)}, u32[]{:S(2)}) collective-permute-start(f32[4,64,128]{2,1,0:T(8,128)S(1)} %get-tuple-element.21._), channel_id=1, source_target_pairs={{0,8},{8,0},{16,24},{24,16},{1,9},{9,1},{17,25},{25,17},{2,10},{10... | collective-permute-start | bytes 393224 | tf_op jit(solution)/shard_map/ppermute | solution.py:238
  8.6 0.0 collective-permute-done.block.refs_0_
  8.6 2.1 %collective-permute-start.1 = (f32[4,64,128]{2,1,0:T(8,128)S(1)}, f32[4,64,128]{2,1,0:T(8,128)S(1)}, u32[]{:S(2)}, u32[]{:S(2)}) collective-permute-start(f32[4,64,128]{2,1,0:T(8,128)S(1)} %hold.1), channel_id=1, source_target_pairs={{0,16},{8,24},{16,0},{24,8},{1,17},{9,25},{17,1},{25,9},{2,18},{10... | collective-permute-start | bytes 393224 | tf_op jit(solution)/shard_map/ppermute | solution.py:238
  10.7 2.2 %collective-permute-done.3.refs_1_ = f32[4,64,128]{2,1,0:T(8,128)S(1)} collective-permute-done((f32[4,64,128]{2,1,0:T(8,128)S(1)}, f32[4,64,128]{2,1,0:T(8,128)S(1)}, u32[]{:S(2)}, u32[]{:S(2)}) %collective-permute-start.3) | collective-permute-done | bytes 131104 | tf_op jit(solution)/shard_map/ppermute | solution.py:238
  12.9 0.5 %collective-permute-done.2.refs_0_ = f32[4,64,128]{2,1,0:T(8,128)S(1)} collective-permute-done((f32[4,64,128]{2,1,0:T(8,128)S(1)}, f32[4,64,128]{2,1,0:T(8,128)S(1)}, u32[]{:S(2)}, u32[]{:S(2)}) %collective-permute-start.2) | collective-permute-done | bytes 131104 | tf_op jit(solution)/shard_map/ppermute | solution.py:238
  13.3 0.2 add_sides.1.refs_5_
  13.5 1.0 %collective-permute-done.1.refs_1_ = f32[4,64,128]{2,1,0:T(8,128)S(1)} collective-permute-done((f32[4,64,128]{2,1,0:T(8,128)S(1)}, f32[4,64,128]{2,1,0:T(8,128)S(1)}, u32[]{:S(2)}, u32[]{:S(2)}) %collective-permute-start.1) | collective-permute-done | bytes 131104 | tf_op jit(solution)/shard_map/ppermute | solution.py:238
  14.5 0.2 finish.1
  14.7 0.1 collective-permute-start.4
  14.8 1.3 %collective-permute-done.4.swapped.refs_1_ = f32[4,64,128]{2,1,0:T(8,128)S(1)} collective-permute-done((f32[4,64,128]{2,1,0:T(8,128)S(1)}, f32[4,64,128]{2,1,0:T(8,128)S(1)}, u32[]{:S(2)}, u32[]{:S(2)}) %collective-permute-start.4) | collective-permute-done | bytes 131104 | tf_op jit(solution)/shard_map/ppermute | solution.py:480
  16.2 3.7 %collective-permute-start.5 = (f32[2,64,128]{2,1,0:T(8,128)S(1)}, f32[2,64,128]{2,1,0:T(8,128)S(1)}, u32[]{:S(2)}, u32[]{:S(2)}) collective-permute-start(f32[2,64,128]{2,1,0:T(8,128)S(1)} %get-tuple-element.27), channel_id=1, source_target_pairs={{0,6},{1,7},{2,4},{3,5},{4,2},{5,3},{6,0},{7,1},{8,14},{9,15},{10,... | collective-permute-start | bytes 196616 | tf_op jit(solution)/shard_map/ppermute | solution.py:480
  19.8 0.0 collective-permute-start.6
  19.8 0.8 %collective-permute-start.7 = (f32[2,64,128]{2,1,0:T(8,128)S(1)}, f32[2,64,128]{2,1,0:T(8,128)S(1)}, u32[]{:S(2)}, u32[]{:S(2)}) collective-permute-start(f32[2,64,128]{2,1,0:T(8,128)S(1)} %get-tuple-element.29), channel_id=1, source_target_pairs={{0,4},{1,5},{2,6},{3,7},{4,0},{5,1},{6,2},{7,3},{8,12},{9,13},{10,... | collective-permute-start | bytes 196616 | tf_op jit(solution)/shard_map/ppermute | solution.py:480
  20.6 0.0 copy-done.8
  20.6 0.0 copy-done.7
  20.6 0.0 copy-done.6
  20.6 0.0 copy-done.5
  20.6 0.0 copy-done.4
  20.6 0.0 copy-done.3
  20.7 0.0 copy-done.1
  20.7 0.0 copy-done
  20.7 0.0 copy-start.2
  20.7 1.4 %history.1 = (f32[5,64,1024]{2,1,0:T(8,128)S(1)}, f32[5,64,1024]{2,1,0:T(8,128)S(1)}, f32[1,128]{1,0:T(1,128)S(1)}, f32[5,8,128]{2,1,0:T(8,128)S(1)}, s32[2,8,128]{2,1,0:T(8,128)S(1)}) custom-call(f32[5,64,1024]{2,1,0:T(8,128)S(1)} %bitcast.7, f32[5,64,1024]{2,1,0:T(8,128)S(1)} %bitcast.8, s32[5]{0:T(128)S(1)} %copy-done.3, s32[64]{0:T(128)S(1)} %copy-done.4, ...), custom_call_target="tpu_custom_call" | custom-call | flops 2621440 | bytes 3932160 | tf_op jit(solution)/shard_map/history/pallas_call | solution.py:294
  22.1 0.9 %collective-permute-done.5.refs_2_ = f32[2,64,128]{2,1,0:T(8,128)S(1)} collective-permute-done((f32[2,64,128]{2,1,0:T(8,128)S(1)}, f32[2,64,128]{2,1,0:T(8,128)S(1)}, u32[]{:S(2)}, u32[]{:S(2)}) %collective-permute-start.5) | collective-permute-done | bytes 65568 | tf_op jit(solution)/shard_map/ppermute | solution.py:480
  23.0 1.9 %collective-permute-done.6.refs_3_ = f32[2,64,128]{2,1,0:T(8,128)S(1)} collective-permute-done((f32[2,64,128]{2,1,0:T(8,128)S(1)}, f32[2,64,128]{2,1,0:T(8,128)S(1)}, u32[]{:S(2)}, u32[]{:S(2)}) %collective-permute-start.6) | collective-permute-done | bytes 65568 | tf_op jit(solution)/shard_map/ppermute | solution.py:480
  24.9 0.8 %collective-permute-done.7.refs_4_ = f32[2,64,128]{2,1,0:T(8,128)S(1)} collective-permute-done((f32[2,64,128]{2,1,0:T(8,128)S(1)}, f32[2,64,128]{2,1,0:T(8,128)S(1)}, u32[]{:S(2)}, u32[]{:S(2)}) %collective-permute-start.7) | collective-permute-done | bytes 65568 | tf_op jit(solution)/shard_map/ppermute | solution.py:480
  25.7 0.0 copy-done.2
  25.7 0.7 %residual.1 = (f32[64,1024]{1,0:T(8,128)S(1)}, f32[32,1,128]{2,1,0:T(1,128)S(1)}) custom-call(f32[4,64,128]{2,1,0:T(8,128)S(1)} %get-tuple-element.25.own.refs_0_, f32[4,64,128]{2,1,0:T(8,128)S(1)} %collective-permute-done.4.swapped.refs_1_, f32[2,64,128]{2,1,0:T(8,128)S(1)} %collective-permute-done.5.refs_2_, ...), custom_call_target="tpu_custom_call" | custom-call | tf_op jit(solution)/shard_map/residual/pallas_call | solution.py:357
  26.4 11.0 %all_to_all.5.refs_0_ = f32[32,1,128]{2,1,0:T(1,128)S(1)} all-to-all(f32[32,1,128]{2,1,0:T(1,128)S(1)} %get-tuple-element.34), channel_id=1, replica_groups=mesh['kgrp'=4,'energy'=8] {'energy','kgrp'}, dimensions={0} | all-to-all | bytes 32768 | tf_op jit(solution)/shard_map/all_to_all | solution.py:486
  37.4 1.0 %mix.1 = f32[64,1024]{1,0:T(8,128)} custom-call(f32[32,1,128]{2,1,0:T(1,128)S(1)} %all_to_all.5.refs_0_, f32[64,1024]{1,0:T(8,128)S(1)} %get-tuple-element.35.refs_1_, f32[5,64,1024]{2,1,0:T(8,128)S(1)} %get-tuple-element.36.refs_2_), custom_call_target="tpu_custom_call" | custom-call | tf_op jit(solution)/shard_map/mix/pallas_call | solution.py:436
  (2 shorter events, 0.0 us)
Async XLA Ops:
  0.0 20.6 %copy-start.8 = (s32[2]{0:T(128)S(1)}, s32[2]{0:T(128)}, u32[]{:S(2)}) copy-start(s32[2]{0:T(128)} %refs_7_.1) | copy-start | bytes 28
  0.0 20.6 %copy-start.7 = (f32[2]{0:T(128)S(1)}, f32[2]{0:T(128)}, u32[]{:S(2)}) copy-start(f32[2]{0:T(128)} %refs_6_.1) | copy-start | bytes 28
  0.0 20.6 %copy-start.6 = (f32[2]{0:T(128)S(1)}, f32[2]{0:T(128)}, u32[]{:S(2)}) copy-start(f32[2]{0:T(128)} %refs_5_.1) | copy-start | bytes 28
  0.0 20.6 %copy-start.5 = (f32[4]{0:T(128)S(1)}, f32[4]{0:T(128)}, u32[]{:S(2)}) copy-start(f32[4]{0:T(128)} %refs_4_.1) | copy-start | bytes 52
  0.0 20.6 %copy-start.4 = (s32[64]{0:T(128)S(1)}, s32[64]{0:T(128)}, u32[]{:S(2)}) copy-start(s32[64]{0:T(128)} %refs_3_.3) | copy-start | bytes 772
  0.0 20.6 %copy-start.3 = (s32[5]{0:T(128)S(1)}, s32[5]{0:T(128)}, u32[]{:S(2)}) copy-start(s32[5]{0:T(128)} %refs_2_.1) | copy-start | bytes 64
  0.0 20.6 %copy-start.1 = (f32[5,2,2,2,8,1024]{5,4,3,2,1,0:T(8,128)S(1)}, f32[5,2,2,2,8,1024]{5,4,3,2,1,0:T(8,128)}, u32[]{:S(2)}) copy-start(f32[5,2,2,2,8,1024]{5,4,3,2,1,0:T(8,128)} %param.15) | copy-start | bytes 3932164
  0.0 20.6 %copy-start = (f32[5,2,2,2,8,1024]{5,4,3,2,1,0:T(8,128)S(1)}, f32[5,2,2,2,8,1024]{5,4,3,2,1,0:T(8,128)}, u32[]{:S(2)}) copy-start(f32[5,2,2,2,8,1024]{5,4,3,2,1,0:T(8,128)} %param.14) | copy-start | bytes 3932164
  1.2 7.4 %collective-permute-start = (f32[4,64,128]{2,1,0:T(8,128)S(1)}, f32[4,64,128]{2,1,0:T(8,128)S(1)}, u32[]{:S(2)}, u32[]{:S(2)}) collective-permute-start(f32[4,64,128]{2,1,0:T(8,128)S(1)} %bitcast.11), channel_id=1, source_target_pairs={{0,8},{8,0},{16,24},{24,16},{1,9},{9,1},{17,25},{25,17},{2,10},{10... | collective-permute-start | bytes 393224 | tf_op jit(solution)/shard_map/ppermute | solution.py:238
  4.2 8.7 %collective-permute-start.3 = (f32[4,64,128]{2,1,0:T(8,128)S(1)}, f32[4,64,128]{2,1,0:T(8,128)S(1)}, u32[]{:S(2)}, u32[]{:S(2)}) collective-permute-start(f32[4,64,128]{2,1,0:T(8,128)S(1)} %bitcast.9), channel_id=1, source_target_pairs={{0,24},{8,16},{16,8},{24,0},{1,25},{9,17},{17,9},{25,1},{2,26},{10... | collective-permute-start | bytes 393224 | tf_op jit(solution)/shard_map/ppermute | solution.py:238
  7.0 6.3 %collective-permute-start.2 = (f32[4,64,128]{2,1,0:T(8,128)S(1)}, f32[4,64,128]{2,1,0:T(8,128)S(1)}, u32[]{:S(2)}, u32[]{:S(2)}) collective-permute-start(f32[4,64,128]{2,1,0:T(8,128)S(1)} %get-tuple-element.21._), channel_id=1, source_target_pairs={{0,8},{8,0},{16,24},{24,16},{1,9},{9,1},{17,25},{25,17},{2,10},{10... | collective-permute-start | bytes 393224 | tf_op jit(solution)/shard_map/ppermute | solution.py:238
  8.6 5.9 %collective-permute-start.1 = (f32[4,64,128]{2,1,0:T(8,128)S(1)}, f32[4,64,128]{2,1,0:T(8,128)S(1)}, u32[]{:S(2)}, u32[]{:S(2)}) collective-permute-start(f32[4,64,128]{2,1,0:T(8,128)S(1)} %hold.1), channel_id=1, source_target_pairs={{0,16},{8,24},{16,0},{24,8},{1,17},{9,25},{17,1},{25,9},{2,18},{10... | collective-permute-start | bytes 393224 | tf_op jit(solution)/shard_map/ppermute | solution.py:238
  14.7 1.4 %collective-permute-start.4 = (f32[4,64,128]{2,1,0:T(8,128)S(1)}, f32[4,64,128]{2,1,0:T(8,128)S(1)}, u32[]{:S(2)}, u32[]{:S(2)}) collective-permute-start(f32[4,64,128]{2,1,0:T(8,128)S(1)} %get-tuple-element.26), channel_id=1, source_target_pairs={{0,1},{1,0},{2,3},{3,2},{4,5},{5,4},{6,7},{7,6},{8,9},{9,8},{10,11... | collective-permute-start | bytes 393224 | tf_op jit(solution)/shard_map/ppermute | solution.py:480
  16.2 6.9 %collective-permute-start.5 = (f32[2,64,128]{2,1,0:T(8,128)S(1)}, f32[2,64,128]{2,1,0:T(8,128)S(1)}, u32[]{:S(2)}, u32[]{:S(2)}) collective-permute-start(f32[2,64,128]{2,1,0:T(8,128)S(1)} %get-tuple-element.27), channel_id=1, source_target_pairs={{0,6},{1,7},{2,4},{3,5},{4,2},{5,3},{6,0},{7,1},{8,14},{9,15},{10,... | collective-permute-start | bytes 196616 | tf_op jit(solution)/shard_map/ppermute | solution.py:480
  19.8 5.1 %collective-permute-start.6 = (f32[2,64,128]{2,1,0:T(8,128)S(1)}, f32[2,64,128]{2,1,0:T(8,128)S(1)}, u32[]{:S(2)}, u32[]{:S(2)}) collective-permute-start(f32[2,64,128]{2,1,0:T(8,128)S(1)} %get-tuple-element.28), channel_id=1, source_target_pairs={{0,2},{1,3},{2,0},{3,1},{4,6},{5,7},{6,4},{7,5},{8,10},{9,11},{10,... | collective-permute-start | bytes 196616 | tf_op jit(solution)/shard_map/ppermute | solution.py:480
  19.8 5.9 %collective-permute-start.7 = (f32[2,64,128]{2,1,0:T(8,128)S(1)}, f32[2,64,128]{2,1,0:T(8,128)S(1)}, u32[]{:S(2)}, u32[]{:S(2)}) collective-permute-start(f32[2,64,128]{2,1,0:T(8,128)S(1)} %get-tuple-element.29), channel_id=1, source_target_pairs={{0,4},{1,5},{2,6},{3,7},{4,0},{5,1},{6,2},{7,3},{8,12},{9,13},{10,... | collective-permute-start | bytes 196616 | tf_op jit(solution)/shard_map/ppermute | solution.py:480
  20.7 5.0 %copy-start.2 = (f32[2,2,2,8,1024]{4,3,2,1,0:T(8,128)S(1)}, f32[2,2,2,8,1024]{4,3,2,1,0:T(8,128)}, u32[]{:S(2)}) copy-start(f32[2,2,2,8,1024]{4,3,2,1,0:T(8,128)} %param.13) | copy-start | bytes 786436

commit v19 on v18

--- a/solution.py
+++ b/solution.py
@@ -238,9 +238,9 @@
     across = lambda block, flip: lax.ppermute(block, "kgrp", [(i, i ^ flip) for i in range(groups)])
     half = own.shape[0] // 2
     head, tail = own[:half], own[half:]
-    near_head, far_tail = across(head, 1), across(tail, 3)
+    near_head = across(head, 1)
     hi, lo, part, late = prepare([head, tail], neighbour, weight, total_k)
-    near_tail, far_head = across(late, 1), across(hold(near_head, late), 2)
+    far_tail, near_tail, far_head = across(late, 3), across(late, 1), across(hold(near_head, late), 2)
     tail_part = add_sides(half, (near_tail, far_tail), hi, lo, part, [])
     return finish((near_head, far_head), hi, lo, part, [tail_part], parts)
 

time: 38.6 us -> 38.6 us (level)
  starting transfers between devices: 12.7 us -> 11.7 us
  waiting for transfers between devices: 8.53 us -> 9.53 us
    ppermute x4, waiting for transfers between devices: 3.62 us -> 4.62 us  [smear(): lax.ppermute(block, 'kgrp', [(i, i ^ flip) for i in range(groups)])]
    ppermute x4, starting transfers between devices: 8.15 us -> 7.17 us  [smear(): lax.ppermute(block, 'kgrp', [(i, i ^ flip) for i in range(groups)])]
  transfers between devices with their start and end apart: 8 -> 8, of which waited for: 7 -> 6; matrix products, arithmetic and copies ran while one was open for 0% -> 0% of each run, Pallas kernels for 8% -> 8%
where the time goes in v19:
time: 38.6 us; the launch traced here: 38.4 us
  starting transfers between devices  11.7 us (30%)
  blocking collectives  11 us (28%)
  waiting for transfers between devices  9.53 us (25%)
  Pallas kernels  4.85 us (13%)
  local copies, waits for them, and re-layouts  1.17 us (3%)
    all_to_all x1, blocking collectives, per_device(): lax.all_to_all(lines, ('energy', 'kgrp'), split_axis=0, concat_axis=0, ti...  11 us
    ppermute x4, starting transfers between devices, smear(): lax.ppermute(block, 'kgrp', [(i, i ^ flip) for i in range(groups)])  7.17 us
    ppermute x4, waiting for transfers between devices, per_device(): lax.ppermute(block, 'energy', [(e, e ^ m) for e in range(parts)])  4.91 us
    ppermute x4, waiting for transfers between devices, smear(): lax.ppermute(block, 'kgrp', [(i, i ^ flip) for i in range(groups)])  4.62 us
    ppermute x4, starting transfers between devices, per_device(): lax.ppermute(block, 'energy', [(e, e ^ m) for e in range(parts)])  4.52 us
    pallas_call x1, Pallas kernels, history(): pl.pallas_call(lambda *refs: history_kernel(rows, *refs), out_shape=(jax....  1.43 us
    pallas_call x1, Pallas kernels, prepare(): pl.pallas_call(lambda *refs: prepare_kernel(total_k, *refs), out_shape=(s...  1.33 us
    slice x1, local copies, waits for them, and re-layouts, smear(): head, tail = (own[:half], own[half:])  1.14 us
  transfers between devices with their start and end apart: 8, of which 6 were waited for; matrix products, arithmetic and copies ran while one was open for 0% of the time, Pallas kernels for 8%

profile of v19, /device:TPU:0, one launch (start us, length us, event | category | flops | bytes accessed | tf_op | source)
XLA Modules:
  0.0 38.4 jit_solution(18262360717758913719)
XLA Ops:
  0.0 0.0 copy-start.8
  0.0 0.0 copy-start.7
  0.0 0.0 copy-start.6
  0.0 0.0 copy-start.5
  0.0 0.0 copy-start.4
  0.0 0.0 copy-start.3
  0.0 0.0 copy-start.1
  0.0 0.0 copy-start
  0.0 1.1 %fusion = (f32[1,2,2,64,128]{4,3,2,1,0:T(8,128)S(1)}, f32[1,2,2,64,128]{4,3,2,1,0:T(8,128)S(1)}) fusion(f32[2,2,2,64,128]{4,3,2,1,0:T(8,128)} %param.12), kind=kLoop, calls=%fused_computation | loop fusion | bytes 524288 | tf_op jit(solution)/shard_map/slice | solution.py:240
  1.2 3.0 %collective-permute-start = (f32[4,64,128]{2,1,0:T(8,128)S(1)}, f32[4,64,128]{2,1,0:T(8,128)S(1)}, u32[]{:S(2)}, u32[]{:S(2)}) collective-permute-start(f32[4,64,128]{2,1,0:T(8,128)S(1)} %bitcast.9), channel_id=1, source_target_pairs={{0,8},{8,0},{16,24},{24,16},{1,9},{9,1},{17,25},{25,17},{2,10},{10... | collective-permute-start | bytes 393224 | tf_op jit(solution)/shard_map/ppermute | solution.py:238
  4.2 1.3 %prepare.1 = (bf16[64,128]{1,0:T(8,128)(2,1)S(1)}, bf16[64,128]{1,0:T(8,128)(2,1)S(1)}, f32[8,64,128]{2,1,0:T(8,128)S(1)}, f32[4,64,128]{2,1,0:T(8,128)S(1)}) custom-call(f32[4,64,128]{2,1,0:T(8,128)S(1)} %bitcast.10, f32[4,64,128]{2,1,0:T(8,128)S(1)} %bitcast.11, s32[5,64]{1,0:T(8,128)} %bitcast.13, f32[5]{0:T(128)} %refs_3_.2), custom_call_target="tpu_custom_call" | custom-call | flops 25165824 | bytes 524288 | tf_op jit(solution)/shard_map/prepare/pallas_call | solution.py:85
  5.5 1.6 %collective-permute-start.3 = (f32[4,64,128]{2,1,0:T(8,128)S(1)}, f32[4,64,128]{2,1,0:T(8,128)S(1)}, u32[]{:S(2)}, u32[]{:S(2)}) collective-permute-start(f32[4,64,128]{2,1,0:T(8,128)S(1)} %get-tuple-element.21._), channel_id=1, source_target_pairs={{0,24},{8,16},{16,8},{24,0},{1,25},{9,17},{17,9},{25,1},{2,26},{10... | collective-permute-start | bytes 393224 | tf_op jit(solution)/shard_map/ppermute | solution.py:238
  7.1 1.5 %collective-permute-start.2 = (f32[4,64,128]{2,1,0:T(8,128)S(1)}, f32[4,64,128]{2,1,0:T(8,128)S(1)}, u32[]{:S(2)}, u32[]{:S(2)}) collective-permute-start(f32[4,64,128]{2,1,0:T(8,128)S(1)} %get-tuple-element.21._), channel_id=1, source_target_pairs={{0,8},{8,0},{16,24},{24,16},{1,9},{9,1},{17,25},{25,17},{2,10},{10... | collective-permute-start | bytes 393224 | tf_op jit(solution)/shard_map/ppermute | solution.py:238
  8.6 0.0 collective-permute-done.block.refs_0_
  8.6 1.1 %collective-permute-start.1 = (f32[4,64,128]{2,1,0:T(8,128)S(1)}, f32[4,64,128]{2,1,0:T(8,128)S(1)}, u32[]{:S(2)}, u32[]{:S(2)}) collective-permute-start(f32[4,64,128]{2,1,0:T(8,128)S(1)} %hold.1), channel_id=1, source_target_pairs={{0,16},{8,24},{16,0},{24,8},{1,17},{9,25},{17,1},{25,9},{2,18},{10... | collective-permute-start | bytes 393224 | tf_op jit(solution)/shard_map/ppermute | solution.py:238
  9.7 3.2 %collective-permute-done.3.refs_1_ = f32[4,64,128]{2,1,0:T(8,128)S(1)} collective-permute-done((f32[4,64,128]{2,1,0:T(8,128)S(1)}, f32[4,64,128]{2,1,0:T(8,128)S(1)}, u32[]{:S(2)}, u32[]{:S(2)}) %collective-permute-start.3) | collective-permute-done | bytes 131104 | tf_op jit(solution)/shard_map/ppermute | solution.py:238
  12.9 1.4 %collective-permute-done.2.refs_0_ = f32[4,64,128]{2,1,0:T(8,128)S(1)} collective-permute-done((f32[4,64,128]{2,1,0:T(8,128)S(1)}, f32[4,64,128]{2,1,0:T(8,128)S(1)}, u32[]{:S(2)}, u32[]{:S(2)}) %collective-permute-start.2) | collective-permute-done | bytes 131104 | tf_op jit(solution)/shard_map/ppermute | solution.py:238
  14.3 0.2 add_sides.1.refs_5_
  14.5 0.0 collective-permute-done.1.refs_1_
  14.6 0.2 finish.1
  14.8 0.1 collective-permute-start.4
  14.8 1.3 %collective-permute-done.4.swapped.refs_1_ = f32[4,64,128]{2,1,0:T(8,128)S(1)} collective-permute-done((f32[4,64,128]{2,1,0:T(8,128)S(1)}, f32[4,64,128]{2,1,0:T(8,128)S(1)}, u32[]{:S(2)}, u32[]{:S(2)}) %collective-permute-start.4) | collective-permute-done | bytes 131104 | tf_op jit(solution)/shard_map/ppermute | solution.py:480
  16.2 3.7 %collective-permute-start.5 = (f32[2,64,128]{2,1,0:T(8,128)S(1)}, f32[2,64,128]{2,1,0:T(8,128)S(1)}, u32[]{:S(2)}, u32[]{:S(2)}) collective-permute-start(f32[2,64,128]{2,1,0:T(8,128)S(1)} %get-tuple-element.27), channel_id=1, source_target_pairs={{0,6},{1,7},{2,4},{3,5},{4,2},{5,3},{6,0},{7,1},{8,14},{9,15},{10,... | collective-permute-start | bytes 196616 | tf_op jit(solution)/shard_map/ppermute | solution.py:480
  19.9 0.0 collective-permute-start.6
  19.9 0.8 %collective-permute-start.7 = (f32[2,64,128]{2,1,0:T(8,128)S(1)}, f32[2,64,128]{2,1,0:T(8,128)S(1)}, u32[]{:S(2)}, u32[]{:S(2)}) collective-permute-start(f32[2,64,128]{2,1,0:T(8,128)S(1)} %get-tuple-element.29), channel_id=1, source_target_pairs={{0,4},{1,5},{2,6},{3,7},{4,0},{5,1},{6,2},{7,3},{8,12},{9,13},{10,... | collective-permute-start | bytes 196616 | tf_op jit(solution)/shard_map/ppermute | solution.py:480
  20.7 0.0 copy-done.8
  20.7 0.0 copy-done.7
  20.7 0.0 copy-done.6
  20.7 0.0 copy-done.5
  20.7 0.0 copy-done.4
  20.7 0.0 copy-done.3
  20.7 0.0 copy-done.1
  20.7 0.0 copy-done
  20.7 0.0 copy-start.2
  20.7 1.4 %history.1 = (f32[5,64,1024]{2,1,0:T(8,128)S(1)}, f32[5,64,1024]{2,1,0:T(8,128)S(1)}, f32[1,128]{1,0:T(1,128)S(1)}, f32[5,8,128]{2,1,0:T(8,128)S(1)}, s32[2,8,128]{2,1,0:T(8,128)S(1)}) custom-call(f32[5,64,1024]{2,1,0:T(8,128)S(1)} %bitcast.7, f32[5,64,1024]{2,1,0:T(8,128)S(1)} %bitcast.8, s32[5]{0:T(128)S(1)} %copy-done.3, s32[64]{0:T(128)S(1)} %copy-done.4, ...), custom_call_target="tpu_custom_call" | custom-call | flops 2621440 | bytes 3932160 | tf_op jit(solution)/shard_map/history/pallas_call | solution.py:294
  22.2 0.9 %collective-permute-done.5.refs_2_ = f32[2,64,128]{2,1,0:T(8,128)S(1)} collective-permute-done((f32[2,64,128]{2,1,0:T(8,128)S(1)}, f32[2,64,128]{2,1,0:T(8,128)S(1)}, u32[]{:S(2)}, u32[]{:S(2)}) %collective-permute-start.5) | collective-permute-done | bytes 65568 | tf_op jit(solution)/shard_map/ppermute | solution.py:480
  23.1 1.9 %collective-permute-done.6.refs_3_ = f32[2,64,128]{2,1,0:T(8,128)S(1)} collective-permute-done((f32[2,64,128]{2,1,0:T(8,128)S(1)}, f32[2,64,128]{2,1,0:T(8,128)S(1)}, u32[]{:S(2)}, u32[]{:S(2)}) %collective-permute-start.6) | collective-permute-done | bytes 65568 | tf_op jit(solution)/shard_map/ppermute | solution.py:480
  24.9 0.8 %collective-permute-done.7.refs_4_ = f32[2,64,128]{2,1,0:T(8,128)S(1)} collective-permute-done((f32[2,64,128]{2,1,0:T(8,128)S(1)}, f32[2,64,128]{2,1,0:T(8,128)S(1)}, u32[]{:S(2)}, u32[]{:S(2)}) %collective-permute-start.7) | collective-permute-done | bytes 65568 | tf_op jit(solution)/shard_map/ppermute | solution.py:480
  25.7 0.0 copy-done.2
  25.7 0.7 %residual.1 = (f32[64,1024]{1,0:T(8,128)S(1)}, f32[32,1,128]{2,1,0:T(1,128)S(1)}) custom-call(f32[4,64,128]{2,1,0:T(8,128)S(1)} %get-tuple-element.25.own.refs_0_, f32[4,64,128]{2,1,0:T(8,128)S(1)} %collective-permute-done.4.swapped.refs_1_, f32[2,64,128]{2,1,0:T(8,128)S(1)} %collective-permute-done.5.refs_2_, ...), custom_call_target="tpu_custom_call" | custom-call | tf_op jit(solution)/shard_map/residual/pallas_call | solution.py:357
  26.4 11.0 %all_to_all.5.refs_0_ = f32[32,1,128]{2,1,0:T(1,128)S(1)} all-to-all(f32[32,1,128]{2,1,0:T(1,128)S(1)} %get-tuple-element.34), channel_id=1, replica_groups=mesh['kgrp'=4,'energy'=8] {'energy','kgrp'}, dimensions={0} | all-to-all | bytes 32768 | tf_op jit(solution)/shard_map/all_to_all | solution.py:486
  37.4 1.0 %mix.1 = f32[64,1024]{1,0:T(8,128)} custom-call(f32[32,1,128]{2,1,0:T(1,128)S(1)} %all_to_all.5.refs_0_, f32[64,1024]{1,0:T(8,128)S(1)} %get-tuple-element.35.refs_1_, f32[5,64,1024]{2,1,0:T(8,128)S(1)} %get-tuple-element.36.refs_2_), custom_call_target="tpu_custom_call" | custom-call | tf_op jit(solution)/shard_map/mix/pallas_call | solution.py:436
  (2 shorter events, 0.0 us)
Async XLA Ops:
  0.0 20.7 %copy-start.8 = (s32[2]{0:T(128)S(1)}, s32[2]{0:T(128)}, u32[]{:S(2)}) copy-start(s32[2]{0:T(128)} %refs_7_.1) | copy-start | bytes 28
  0.0 20.7 %copy-start.7 = (f32[2]{0:T(128)S(1)}, f32[2]{0:T(128)}, u32[]{:S(2)}) copy-start(f32[2]{0:T(128)} %refs_6_.1) | copy-start | bytes 28
  0.0 20.7 %copy-start.6 = (f32[2]{0:T(128)S(1)}, f32[2]{0:T(128)}, u32[]{:S(2)}) copy-start(f32[2]{0:T(128)} %refs_5_.1) | copy-start | bytes 28
  0.0 20.7 %copy-start.5 = (f32[4]{0:T(128)S(1)}, f32[4]{0:T(128)}, u32[]{:S(2)}) copy-start(f32[4]{0:T(128)} %refs_4_.1) | copy-start | bytes 52
  0.0 20.7 %copy-start.4 = (s32[64]{0:T(128)S(1)}, s32[64]{0:T(128)}, u32[]{:S(2)}) copy-start(s32[64]{0:T(128)} %refs_3_.3) | copy-start | bytes 772
  0.0 20.7 %copy-start.3 = (s32[5]{0:T(128)S(1)}, s32[5]{0:T(128)}, u32[]{:S(2)}) copy-start(s32[5]{0:T(128)} %refs_2_.1) | copy-start | bytes 64
  0.0 20.7 %copy-start.1 = (f32[5,2,2,2,8,1024]{5,4,3,2,1,0:T(8,128)S(1)}, f32[5,2,2,2,8,1024]{5,4,3,2,1,0:T(8,128)}, u32[]{:S(2)}) copy-start(f32[5,2,2,2,8,1024]{5,4,3,2,1,0:T(8,128)} %param.15) | copy-start | bytes 3932164
  0.0 20.7 %copy-start = (f32[5,2,2,2,8,1024]{5,4,3,2,1,0:T(8,128)S(1)}, f32[5,2,2,2,8,1024]{5,4,3,2,1,0:T(8,128)}, u32[]{:S(2)}) copy-start(f32[5,2,2,2,8,1024]{5,4,3,2,1,0:T(8,128)} %param.14) | copy-start | bytes 3932164
  1.2 7.4 %collective-permute-start = (f32[4,64,128]{2,1,0:T(8,128)S(1)}, f32[4,64,128]{2,1,0:T(8,128)S(1)}, u32[]{:S(2)}, u32[]{:S(2)}) collective-permute-start(f32[4,64,128]{2,1,0:T(8,128)S(1)} %bitcast.9), channel_id=1, source_target_pairs={{0,8},{8,0},{16,24},{24,16},{1,9},{9,1},{17,25},{25,17},{2,10},{10... | collective-permute-start | bytes 393224 | tf_op jit(solution)/shard_map/ppermute | solution.py:238
  5.5 7.4 %collective-permute-start.3 = (f32[4,64,128]{2,1,0:T(8,128)S(1)}, f32[4,64,128]{2,1,0:T(8,128)S(1)}, u32[]{:S(2)}, u32[]{:S(2)}) collective-permute-start(f32[4,64,128]{2,1,0:T(8,128)S(1)} %get-tuple-element.21._), channel_id=1, source_target_pairs={{0,24},{8,16},{16,8},{24,0},{1,25},{9,17},{17,9},{25,1},{2,26},{10... | collective-permute-start | bytes 393224 | tf_op jit(solution)/shard_map/ppermute | solution.py:238
  7.1 7.2 %collective-permute-start.2 = (f32[4,64,128]{2,1,0:T(8,128)S(1)}, f32[4,64,128]{2,1,0:T(8,128)S(1)}, u32[]{:S(2)}, u32[]{:S(2)}) collective-permute-start(f32[4,64,128]{2,1,0:T(8,128)S(1)} %get-tuple-element.21._), channel_id=1, source_target_pairs={{0,8},{8,0},{16,24},{24,16},{1,9},{9,1},{17,25},{25,17},{2,10},{10... | collective-permute-start | bytes 393224 | tf_op jit(solution)/shard_map/ppermute | solution.py:238
  8.6 5.9 %collective-permute-start.1 = (f32[4,64,128]{2,1,0:T(8,128)S(1)}, f32[4,64,128]{2,1,0:T(8,128)S(1)}, u32[]{:S(2)}, u32[]{:S(2)}) collective-permute-start(f32[4,64,128]{2,1,0:T(8,128)S(1)} %hold.1), channel_id=1, source_target_pairs={{0,16},{8,24},{16,0},{24,8},{1,17},{9,25},{17,1},{25,9},{2,18},{10... | collective-permute-start | bytes 393224 | tf_op jit(solution)/shard_map/ppermute | solution.py:238
  14.8 1.4 %collective-permute-start.4 = (f32[4,64,128]{2,1,0:T(8,128)S(1)}, f32[4,64,128]{2,1,0:T(8,128)S(1)}, u32[]{:S(2)}, u32[]{:S(2)}) collective-permute-start(f32[4,64,128]{2,1,0:T(8,128)S(1)} %get-tuple-element.26), channel_id=1, source_target_pairs={{0,1},{1,0},{2,3},{3,2},{4,5},{5,4},{6,7},{7,6},{8,9},{9,8},{10,11... | collective-permute-start | bytes 393224 | tf_op jit(solution)/shard_map/ppermute | solution.py:480
  16.2 6.9 %collective-permute-start.5 = (f32[2,64,128]{2,1,0:T(8,128)S(1)}, f32[2,64,128]{2,1,0:T(8,128)S(1)}, u32[]{:S(2)}, u32[]{:S(2)}) collective-permute-start(f32[2,64,128]{2,1,0:T(8,128)S(1)} %get-tuple-element.27), channel_id=1, source_target_pairs={{0,6},{1,7},{2,4},{3,5},{4,2},{5,3},{6,0},{7,1},{8,14},{9,15},{10,... | collective-permute-start | bytes 196616 | tf_op jit(solution)/shard_map/ppermute | solution.py:480
  19.9 5.1 %collective-permute-start.6 = (f32[2,64,128]{2,1,0:T(8,128)S(1)}, f32[2,64,128]{2,1,0:T(8,128)S(1)}, u32[]{:S(2)}, u32[]{:S(2)}) collective-permute-start(f32[2,64,128]{2,1,0:T(8,128)S(1)} %get-tuple-element.28), channel_id=1, source_target_pairs={{0,2},{1,3},{2,0},{3,1},{4,6},{5,7},{6,4},{7,5},{8,10},{9,11},{10,... | collective-permute-start | bytes 196616 | tf_op jit(solution)/shard_map/ppermute | solution.py:480
  19.9 5.9 %collective-permute-start.7 = (f32[2,64,128]{2,1,0:T(8,128)S(1)}, f32[2,64,128]{2,1,0:T(8,128)S(1)}, u32[]{:S(2)}, u32[]{:S(2)}) collective-permute-start(f32[2,64,128]{2,1,0:T(8,128)S(1)} %get-tuple-element.29), channel_id=1, source_target_pairs={{0,4},{1,5},{2,6},{3,7},{4,0},{5,1},{6,2},{7,3},{8,12},{9,13},{10,... | collective-permute-start | bytes 196616 | tf_op jit(solution)/shard_map/ppermute | solution.py:480
  20.7 5.0 %copy-start.2 = (f32[2,2,2,8,1024]{4,3,2,1,0:T(8,128)S(1)}, f32[2,2,2,8,1024]{4,3,2,1,0:T(8,128)}, u32[]{:S(2)}) copy-start(f32[2,2,2,8,1024]{4,3,2,1,0:T(8,128)} %param.13) | copy-start | bytes 786436

commit v20 on v17

--- a/solution.py
+++ b/solution.py
@@ -188,7 +188,7 @@
 def chip_order(parts):
     chips = parts // 2
     half = chips // 2
-    return [*range(1, half), *range(half + 1, chips), half] if chips > 1 else []
+    return [*range(half + 1, chips), half, *range(1, half)] if chips > 1 else []
 
 
 def join_kernel(own, swapped, *out):

time: 40.1 us -> 38.8 us (0.968)
  waiting for transfers between devices: 10.3 us -> 8.97 us
    ppermute x4, waiting for transfers between devices: 6.24 us -> 4.94 us  [per_device(): lax.ppermute(block, 'energy', [(e, e ^ m) for e in range(parts)])]
where the time goes in v20:
time: 38.8 us; the launch traced here: 38.7 us
  starting transfers between devices  11.5 us (30%)
  blocking collectives  10.9 us (28%)
  waiting for transfers between devices  8.97 us (23%)
  Pallas kernels  4.6 us (12%)
  local copies, waits for them, and re-layouts  2.52 us (6%)
    all_to_all x1, blocking collectives, per_device(): lax.all_to_all(lines, ('energy', 'kgrp'), split_axis=0, concat_axis=0, ti...  10.9 us
    ppermute x4, starting transfers between devices, smear(): lax.ppermute(block, 'kgrp', [(i, i ^ flip) for i in range(groups)])  7 us
    ppermute x4, waiting for transfers between devices, per_device(): lax.ppermute(block, 'energy', [(e, e ^ m) for e in range(parts)])  4.94 us
    ppermute x4, starting transfers between devices, per_device(): lax.ppermute(block, 'energy', [(e, e ^ m) for e in range(parts)])  4.52 us
    ppermute x4, waiting for transfers between devices, smear(): lax.ppermute(block, 'kgrp', [(i, i ^ flip) for i in range(groups)])  4.04 us
    pallas_call x1, Pallas kernels, history(): pl.pallas_call(lambda *refs: history_kernel(rows, *refs), out_shape=(jax....  1.43 us
    unnamed x22, local copies, waits for them, and re-layouts  1.38 us
    slice x1, local copies, waits for them, and re-layouts, smear(): head, tail = (own[:half], own[half:])  1.14 us
  transfers between devices with their start and end apart: 8, of which 6 were waited for; matrix products, arithmetic and copies ran while one was open for 0% of the time, Pallas kernels for 7%

profile of v20, /device:TPU:0, one launch (start us, length us, event | category | flops | bytes accessed | tf_op | source)
XLA Modules:
  0.0 38.7 jit_solution(8089612775550032243)
XLA Ops:
  0.0 0.0 copy-start.1
  0.0 0.0 copy-start
  0.0 1.1 %fusion = (f32[1,2,2,64,128]{4,3,2,1,0:T(8,128)S(1)}, f32[1,2,2,64,128]{4,3,2,1,0:T(8,128)S(1)}) fusion(f32[2,2,2,64,128]{4,3,2,1,0:T(8,128)} %param.12), kind=kLoop, calls=%fused_computation | loop fusion | bytes 524288 | tf_op jit(solution)/shard_map/slice | solution.py:240
  1.1 3.0 %collective-permute-start = (f32[4,64,128]{2,1,0:T(8,128)S(1)}, f32[4,64,128]{2,1,0:T(8,128)S(1)}, u32[]{:S(2)}, u32[]{:S(2)}) collective-permute-start(f32[4,64,128]{2,1,0:T(8,128)S(1)} %bitcast.11), channel_id=1, source_target_pairs={{0,8},{8,0},{16,24},{24,16},{1,9},{9,1},{17,25},{25,17},{2,10},{10... | collective-permute-start | bytes 393224 | tf_op jit(solution)/shard_map/ppermute | solution.py:238
  4.1 1.5 %collective-permute-start.3 = (f32[4,64,128]{2,1,0:T(8,128)S(1)}, f32[4,64,128]{2,1,0:T(8,128)S(1)}, u32[]{:S(2)}, u32[]{:S(2)}) collective-permute-start(f32[4,64,128]{2,1,0:T(8,128)S(1)} %bitcast.9), channel_id=1, source_target_pairs={{0,24},{8,16},{16,8},{24,0},{1,25},{9,17},{17,9},{25,1},{2,26},{10... | collective-permute-start | bytes 393224 | tf_op jit(solution)/shard_map/ppermute | solution.py:238
  5.6 0.0 copy-start.3
  5.6 0.7 %copy-done.3 = s32[64,5]{0,1:T(8,128)S(1)} copy-done((s32[64,5]{0,1:T(8,128)S(1)}, s32[64,5]{0,1:T(8,128)}, u32[]{:S(2)}) %copy-start.3) | copy-done | bytes 1304
  6.3 0.0 copy-start.4
  6.3 0.7 %copy-done.4 = f32[5]{0:T(128)S(1)} copy-done((f32[5]{0:T(128)S(1)}, f32[5]{0:T(128)}, u32[]{:S(2)}) %copy-start.4) | copy-done | bytes 44
  7.0 0.0 copy-start.5
  7.0 0.0 copy-start.6
  7.0 0.0 copy-start.7
  7.0 0.0 copy-start.8
  7.0 0.0 copy-start.9
  7.0 0.0 copy-start.10
  7.0 1.1 %prepare.1 = (bf16[64,128]{1,0:T(8,128)(2,1)S(1)}, bf16[64,128]{1,0:T(8,128)(2,1)S(1)}, f32[8,64,128]{2,1,0:T(8,128)S(1)}, f32[4,64,128]{2,1,0:T(8,128)S(1)}) custom-call(f32[4,64,128]{2,1,0:T(8,128)S(1)} %bitcast.12, f32[4,64,128]{2,1,0:T(8,128)S(1)} %bitcast.10, s32[5,64]{1,0:T(8,128)S(1)} %bitcast.14, f32[5]{0:T(128)S(1)} %copy-done.4), custom_call_target="tpu_custom_call" | custom-call | flops 25165824 | bytes 524288 | tf_op jit(solution)/shard_map/prepare/pallas_call | solution.py:85
  8.1 1.6 %collective-permute-start.2 = (f32[4,64,128]{2,1,0:T(8,128)S(1)}, f32[4,64,128]{2,1,0:T(8,128)S(1)}, u32[]{:S(2)}, u32[]{:S(2)}) collective-permute-start(f32[4,64,128]{2,1,0:T(8,128)S(1)} %get-tuple-element.21._), channel_id=1, source_target_pairs={{0,8},{8,0},{16,24},{24,16},{1,9},{9,1},{17,25},{25,17},{2,10},{10... | collective-permute-start | bytes 393224 | tf_op jit(solution)/shard_map/ppermute | solution.py:238
  9.7 0.0 collective-permute-done.block.refs_0_
  9.7 0.9 %collective-permute-start.1 = (f32[4,64,128]{2,1,0:T(8,128)S(1)}, f32[4,64,128]{2,1,0:T(8,128)S(1)}, u32[]{:S(2)}, u32[]{:S(2)}) collective-permute-start(f32[4,64,128]{2,1,0:T(8,128)S(1)} %hold.1), channel_id=1, source_target_pairs={{0,16},{8,24},{16,0},{24,8},{1,17},{9,25},{17,1},{25,9},{2,18},{10... | collective-permute-start | bytes 393224 | tf_op jit(solution)/shard_map/ppermute | solution.py:238
  10.6 2.2 %collective-permute-done.3.refs_1_ = f32[4,64,128]{2,1,0:T(8,128)S(1)} collective-permute-done((f32[4,64,128]{2,1,0:T(8,128)S(1)}, f32[4,64,128]{2,1,0:T(8,128)S(1)}, u32[]{:S(2)}, u32[]{:S(2)}) %collective-permute-start.3) | collective-permute-done | bytes 131104 | tf_op jit(solution)/shard_map/ppermute | solution.py:238
  12.8 0.5 %collective-permute-done.2.refs_0_ = f32[4,64,128]{2,1,0:T(8,128)S(1)} collective-permute-done((f32[4,64,128]{2,1,0:T(8,128)S(1)}, f32[4,64,128]{2,1,0:T(8,128)S(1)}, u32[]{:S(2)}, u32[]{:S(2)}) %collective-permute-start.2) | collective-permute-done | bytes 131104 | tf_op jit(solution)/shard_map/ppermute | solution.py:238
  13.3 0.2 add_sides.1.refs_5_
  13.5 1.4 %collective-permute-done.1.refs_1_ = f32[4,64,128]{2,1,0:T(8,128)S(1)} collective-permute-done((f32[4,64,128]{2,1,0:T(8,128)S(1)}, f32[4,64,128]{2,1,0:T(8,128)S(1)}, u32[]{:S(2)}, u32[]{:S(2)}) %collective-permute-start.1) | collective-permute-done | bytes 131104 | tf_op jit(solution)/shard_map/ppermute | solution.py:238
  14.9 0.2 finish.1
  15.1 0.1 collective-permute-start.4
  15.2 1.3 %collective-permute-done.4.swapped.refs_1_ = f32[4,64,128]{2,1,0:T(8,128)S(1)} collective-permute-done((f32[4,64,128]{2,1,0:T(8,128)S(1)}, f32[4,64,128]{2,1,0:T(8,128)S(1)}, u32[]{:S(2)}, u32[]{:S(2)}) %collective-permute-start.4) | collective-permute-done | bytes 131104 | tf_op jit(solution)/shard_map/ppermute | solution.py:480
  16.5 3.7 %collective-permute-start.5 = (f32[2,64,128]{2,1,0:T(8,128)S(1)}, f32[2,64,128]{2,1,0:T(8,128)S(1)}, u32[]{:S(2)}, u32[]{:S(2)}) collective-permute-start(f32[2,64,128]{2,1,0:T(8,128)S(1)} %get-tuple-element.27), channel_id=1, source_target_pairs={{0,6},{1,7},{2,4},{3,5},{4,2},{5,3},{6,0},{7,1},{8,14},{9,15},{10,... | collective-permute-start | bytes 196616 | tf_op jit(solution)/shard_map/ppermute | solution.py:480
  20.2 0.0 collective-permute-start.6
  20.2 0.8 %collective-permute-start.7 = (f32[2,64,128]{2,1,0:T(8,128)S(1)}, f32[2,64,128]{2,1,0:T(8,128)S(1)}, u32[]{:S(2)}, u32[]{:S(2)}) collective-permute-start(f32[2,64,128]{2,1,0:T(8,128)S(1)} %get-tuple-element.29), channel_id=1, source_target_pairs={{0,2},{1,3},{2,0},{3,1},{4,6},{5,7},{6,4},{7,5},{8,10},{9,11},{10,... | collective-permute-start | bytes 196616 | tf_op jit(solution)/shard_map/ppermute | solution.py:480
  21.0 0.0 copy-done.1
  21.0 0.0 copy-done
  21.0 0.0 copy-done.5
  21.0 0.0 copy-done.6
  21.0 0.0 copy-done.7
  21.0 0.0 copy-done.8
  21.0 0.0 copy-done.9
  21.0 0.0 copy-done.10
  21.0 0.0 copy-start.2
  21.0 1.4 %history.1 = (f32[5,64,1024]{2,1,0:T(8,128)S(1)}, f32[5,64,1024]{2,1,0:T(8,128)S(1)}, f32[1,128]{1,0:T(1,128)S(1)}, f32[5,8,128]{2,1,0:T(8,128)S(1)}, s32[2,8,128]{2,1,0:T(8,128)S(1)}) custom-call(f32[5,64,1024]{2,1,0:T(8,128)S(1)} %bitcast.7, f32[5,64,1024]{2,1,0:T(8,128)S(1)} %bitcast.8, s32[5]{0:T(128)S(1)} %copy-done.5, s32[64]{0:T(128)S(1)} %copy-done.6, ...), custom_call_target="tpu_custom_call" | custom-call | flops 2621440 | bytes 3932160 | tf_op jit(solution)/shard_map/history/pallas_call | solution.py:294
  22.5 0.4 %collective-permute-done.5.refs_2_ = f32[2,64,128]{2,1,0:T(8,128)S(1)} collective-permute-done((f32[2,64,128]{2,1,0:T(8,128)S(1)}, f32[2,64,128]{2,1,0:T(8,128)S(1)}, u32[]{:S(2)}, u32[]{:S(2)}) %collective-permute-start.5) | collective-permute-done | bytes 65568 | tf_op jit(solution)/shard_map/ppermute | solution.py:480
  22.9 3.2 %collective-permute-done.6.refs_3_ = f32[2,64,128]{2,1,0:T(8,128)S(1)} collective-permute-done((f32[2,64,128]{2,1,0:T(8,128)S(1)}, f32[2,64,128]{2,1,0:T(8,128)S(1)}, u32[]{:S(2)}, u32[]{:S(2)}) %collective-permute-start.6) | collective-permute-done | bytes 65568 | tf_op jit(solution)/shard_map/ppermute | solution.py:480
  26.1 0.0 collective-permute-done.7.refs_4_
  26.1 0.0 copy-done.2
  26.1 0.7 %residual.1 = (f32[64,1024]{1,0:T(8,128)S(1)}, f32[32,1,128]{2,1,0:T(1,128)S(1)}) custom-call(f32[4,64,128]{2,1,0:T(8,128)S(1)} %get-tuple-element.25.own.refs_0_, f32[4,64,128]{2,1,0:T(8,128)S(1)} %collective-permute-done.4.swapped.refs_1_, f32[2,64,128]{2,1,0:T(8,128)S(1)} %collective-permute-done.5.refs_2_, ...), custom_call_target="tpu_custom_call" | custom-call | tf_op jit(solution)/shard_map/residual/pallas_call | solution.py:357
  26.8 10.9 %all_to_all.5.refs_0_ = f32[32,1,128]{2,1,0:T(1,128)S(1)} all-to-all(f32[32,1,128]{2,1,0:T(1,128)S(1)} %get-tuple-element.34), channel_id=1, replica_groups=mesh['kgrp'=4,'energy'=8] {'energy','kgrp'}, dimensions={0} | all-to-all | bytes 32768 | tf_op jit(solution)/shard_map/all_to_all | solution.py:486
  37.7 1.0 %mix.1 = f32[64,1024]{1,0:T(8,128)} custom-call(f32[32,1,128]{2,1,0:T(1,128)S(1)} %all_to_all.5.refs_0_, f32[64,1024]{1,0:T(8,128)S(1)} %get-tuple-element.35.refs_1_, f32[5,64,1024]{2,1,0:T(8,128)S(1)} %get-tuple-element.36.refs_2_), custom_call_target="tpu_custom_call" | custom-call | tf_op jit(solution)/shard_map/mix/pallas_call | solution.py:436
  (2 shorter events, 0.0 us)
Async XLA Ops:
  0.0 21.0 %copy-start.1 = (f32[5,2,2,2,8,1024]{5,4,3,2,1,0:T(8,128)S(1)}, f32[5,2,2,2,8,1024]{5,4,3,2,1,0:T(8,128)}, u32[]{:S(2)}) copy-start(f32[5,2,2,2,8,1024]{5,4,3,2,1,0:T(8,128)} %param.15) | copy-start | bytes 3932164
  0.0 21.0 %copy-start = (f32[5,2,2,2,8,1024]{5,4,3,2,1,0:T(8,128)S(1)}, f32[5,2,2,2,8,1024]{5,4,3,2,1,0:T(8,128)}, u32[]{:S(2)}) copy-start(f32[5,2,2,2,8,1024]{5,4,3,2,1,0:T(8,128)} %param.14) | copy-start | bytes 3932164
  1.1 8.5 %collective-permute-start = (f32[4,64,128]{2,1,0:T(8,128)S(1)}, f32[4,64,128]{2,1,0:T(8,128)S(1)}, u32[]{:S(2)}, u32[]{:S(2)}) collective-permute-start(f32[4,64,128]{2,1,0:T(8,128)S(1)} %bitcast.11), channel_id=1, source_target_pairs={{0,8},{8,0},{16,24},{24,16},{1,9},{9,1},{17,25},{25,17},{2,10},{10... | collective-permute-start | bytes 393224 | tf_op jit(solution)/shard_map/ppermute | solution.py:238
  4.1 8.7 %collective-permute-start.3 = (f32[4,64,128]{2,1,0:T(8,128)S(1)}, f32[4,64,128]{2,1,0:T(8,128)S(1)}, u32[]{:S(2)}, u32[]{:S(2)}) collective-permute-start(f32[4,64,128]{2,1,0:T(8,128)S(1)} %bitcast.9), channel_id=1, source_target_pairs={{0,24},{8,16},{16,8},{24,0},{1,25},{9,17},{17,9},{25,1},{2,26},{10... | collective-permute-start | bytes 393224 | tf_op jit(solution)/shard_map/ppermute | solution.py:238
  5.6 0.7 %copy-start.3 = (s32[64,5]{0,1:T(8,128)S(1)}, s32[64,5]{0,1:T(8,128)}, u32[]{:S(2)}) copy-start(s32[64,5]{0,1:T(8,128)} %param.17) | copy-start | bytes 3844
  6.3 0.7 %copy-start.4 = (f32[5]{0:T(128)S(1)}, f32[5]{0:T(128)}, u32[]{:S(2)}) copy-start(f32[5]{0:T(128)} %refs_3_.2) | copy-start | bytes 64
  7.0 14.0 %copy-start.5 = (s32[5]{0:T(128)S(1)}, s32[5]{0:T(128)}, u32[]{:S(2)}) copy-start(s32[5]{0:T(128)} %refs_2_.1) | copy-start | bytes 64
  7.0 14.0 %copy-start.6 = (s32[64]{0:T(128)S(1)}, s32[64]{0:T(128)}, u32[]{:S(2)}) copy-start(s32[64]{0:T(128)} %refs_3_.3) | copy-start | bytes 772
  7.0 14.0 %copy-start.7 = (f32[4]{0:T(128)S(1)}, f32[4]{0:T(128)}, u32[]{:S(2)}) copy-start(f32[4]{0:T(128)} %refs_4_.1) | copy-start | bytes 52
  7.0 14.0 %copy-start.8 = (f32[2]{0:T(128)S(1)}, f32[2]{0:T(128)}, u32[]{:S(2)}) copy-start(f32[2]{0:T(128)} %refs_5_.1) | copy-start | bytes 28
  7.0 14.0 %copy-start.9 = (f32[2]{0:T(128)S(1)}, f32[2]{0:T(128)}, u32[]{:S(2)}) copy-start(f32[2]{0:T(128)} %refs_6_.1) | copy-start | bytes 28
  7.0 14.0 %copy-start.10 = (s32[2]{0:T(128)S(1)}, s32[2]{0:T(128)}, u32[]{:S(2)}) copy-start(s32[2]{0:T(128)} %refs_7_.1) | copy-start | bytes 28
  8.1 5.1 %collective-permute-start.2 = (f32[4,64,128]{2,1,0:T(8,128)S(1)}, f32[4,64,128]{2,1,0:T(8,128)S(1)}, u32[]{:S(2)}, u32[]{:S(2)}) collective-permute-start(f32[4,64,128]{2,1,0:T(8,128)S(1)} %get-tuple-element.21._), channel_id=1, source_target_pairs={{0,8},{8,0},{16,24},{24,16},{1,9},{9,1},{17,25},{25,17},{2,10},{10... | collective-permute-start | bytes 393224 | tf_op jit(solution)/shard_map/ppermute | solution.py:238
  9.7 5.2 %collective-permute-start.1 = (f32[4,64,128]{2,1,0:T(8,128)S(1)}, f32[4,64,128]{2,1,0:T(8,128)S(1)}, u32[]{:S(2)}, u32[]{:S(2)}) collective-permute-start(f32[4,64,128]{2,1,0:T(8,128)S(1)} %hold.1), channel_id=1, source_target_pairs={{0,16},{8,24},{16,0},{24,8},{1,17},{9,25},{17,1},{25,9},{2,18},{10... | collective-permute-start | bytes 393224 | tf_op jit(solution)/shard_map/ppermute | solution.py:238
  15.1 1.4 %collective-permute-start.4 = (f32[4,64,128]{2,1,0:T(8,128)S(1)}, f32[4,64,128]{2,1,0:T(8,128)S(1)}, u32[]{:S(2)}, u32[]{:S(2)}) collective-permute-start(f32[4,64,128]{2,1,0:T(8,128)S(1)} %get-tuple-element.26), channel_id=1, source_target_pairs={{0,1},{1,0},{2,3},{3,2},{4,5},{5,4},{6,7},{7,6},{8,9},{9,8},{10,11... | collective-permute-start | bytes 393224 | tf_op jit(solution)/shard_map/ppermute | solution.py:480
  16.5 6.3 %collective-permute-start.5 = (f32[2,64,128]{2,1,0:T(8,128)S(1)}, f32[2,64,128]{2,1,0:T(8,128)S(1)}, u32[]{:S(2)}, u32[]{:S(2)}) collective-permute-start(f32[2,64,128]{2,1,0:T(8,128)S(1)} %get-tuple-element.27), channel_id=1, source_target_pairs={{0,6},{1,7},{2,4},{3,5},{4,2},{5,3},{6,0},{7,1},{8,14},{9,15},{10,... | collective-permute-start | bytes 196616 | tf_op jit(solution)/shard_map/ppermute | solution.py:480
  20.2 5.9 %collective-permute-start.6 = (f32[2,64,128]{2,1,0:T(8,128)S(1)}, f32[2,64,128]{2,1,0:T(8,128)S(1)}, u32[]{:S(2)}, u32[]{:S(2)}) collective-permute-start(f32[2,64,128]{2,1,0:T(8,128)S(1)} %get-tuple-element.28), channel_id=1, source_target_pairs={{0,4},{1,5},{2,6},{3,7},{4,0},{5,1},{6,2},{7,3},{8,12},{9,13},{10,... | collective-permute-start | bytes 196616 | tf_op jit(solution)/shard_map/ppermute | solution.py:480
  20.2 5.9 %collective-permute-start.7 = (f32[2,64,128]{2,1,0:T(8,128)S(1)}, f32[2,64,128]{2,1,0:T(8,128)S(1)}, u32[]{:S(2)}, u32[]{:S(2)}) collective-permute-start(f32[2,64,128]{2,1,0:T(8,128)S(1)} %get-tuple-element.29), channel_id=1, source_target_pairs={{0,2},{1,3},{2,0},{3,1},{4,6},{5,7},{6,4},{7,5},{8,10},{9,11},{10,... | collective-permute-start | bytes 196616 | tf_op jit(solution)/shard_map/ppermute | solution.py:480
  21.0 5.1 %copy-start.2 = (f32[2,2,2,8,1024]{4,3,2,1,0:T(8,128)S(1)}, f32[2,2,2,8,1024]{4,3,2,1,0:T(8,128)}, u32[]{:S(2)}) copy-start(f32[2,2,2,8,1024]{4,3,2,1,0:T(8,128)} %param.13) | copy-start | bytes 786436
